TPU v7x, 32 devices: a whole 2x2x4 slice. The times are simulated.
32 devices in a mesh: clip: 8 (over z, x), band: 4 (over y, core).
Axes of the slice: x: 2, y: 2, z: 4, core: 2. Of those that a mesh axis runs over, the one named last changes fastest.
Arguments:
- visible: bfloat16 [128, 128, 768], P(('clip', 'band')), may hold values from -6 to 6
- keep_index: int32 [128, 128], P(('clip', 'band')), may hold values from 0 to 511, as said below
- visible_count: int32 [128], P(('clip', 'band')), may hold values from 52 to 128, as said below
- enc_gain1: bfloat16 [768], P(('clip', 'band')), may hold values from 0.5 to 1.5
- enc_shift1: bfloat16 [768], P(('clip', 'band')), may hold values from -4 to 4
- enc_qkv: bfloat16 [768, 2304], P(('clip', 'band')), may hold values from -0.21875 to 0.21875
- enc_out: bfloat16 [768, 768], P(('clip', 'band')), may hold values from -0.625 to 0.625
- enc_gain2: bfloat16 [768], P(('clip', 'band')), may hold values from 0.5 to 1.5
- enc_shift2: bfloat16 [768], P(('clip', 'band')), may hold values from -4 to 4
- enc_up: bfloat16 [768, 3072], P(('clip', 'band')), may hold values from -0.21875 to 0.21875
- enc_down: bfloat16 [3072, 768], P(('clip', 'band')), may hold values from -0.15625 to 0.15625
- proj: bfloat16 [768, 512], P(('clip', 'band')), may hold values from -0.4375 to 0.4375
- mask_token: bfloat16 [512], P(('clip', 'band')), may hold values from -6 to 6
- dec_gain1: bfloat16 [512], P(('clip', 'band')), may hold values from 0.5 to 1.5
- dec_shift1: bfloat16 [512], P(('clip', 'band')), may hold values from -4 to 4
- dec_qkv: bfloat16 [512, 1536], P(('clip', 'band')), may hold values from -0.25 to 0.25
- dec_out: bfloat16 [512, 512], P(('clip', 'band')), may hold values from -0.5 to 0.5
- dec_gain2: bfloat16 [512], P(('clip', 'band')), may hold values from 0.5 to 1.5
- dec_shift2: bfloat16 [512], P(('clip', 'band')), may hold values from -4 to 4
- dec_up: bfloat16 [512, 2048], P(('clip', 'band')), may hold values from -0.25 to 0.25
- dec_down: bfloat16 [2048, 512], P(('clip', 'band')), may hold values from -0.1875 to 0.1875
- cotangent: bfloat16 [32, 8, 64, 4, 512], P(('clip', 'band')), may hold values from -6 to 6
Outputs:
- decoded: bfloat16 [32, 8, 64, 4, 512], P(('clip', 'band'))
- visible_grad: bfloat16 [128, 128, 768], P(('clip', 'band'))
- enc_gain1_grad: float32 [768], replicated
- enc_shift1_grad: float32 [768], replicated
- enc_qkv_grad: float32 [768, 2304], replicated
- enc_out_grad: float32 [768, 768], replicated
- enc_gain2_grad: float32 [768], replicated
- enc_shift2_grad: float32 [768], replicated
- enc_up_grad: float32 [768, 3072], replicated
- enc_down_grad: float32 [3072, 768], replicated
- proj_grad: float32 [768, 512], replicated
- mask_token_grad: float32 [512], replicated
- dec_gain1_grad: float32 [512], replicated
- dec_shift1_grad: float32 [512], replicated
- dec_qkv_grad: float32 [512, 1536], replicated
- dec_out_grad: float32 [512, 512], replicated
- dec_gain2_grad: float32 [512], replicated
- dec_shift2_grad: float32 [512], replicated
- dec_up_grad: float32 [512, 2048], replicated
- dec_down_grad: float32 [2048, 512], replicated
Inputs may be any that keep to these rules, and one draw needn't show every extreme that they name: `keep_index`: within a clip the 128 entries are distinct patch numbers; the first visible_count of them are the visible patches. `visible_count`: the 4 clips of each encoder device include one with exactly 128 visible patches.
All inputs are finite; a program needn't handle non-finite values.
Results may differ from a plain program's by a relative error of at most 0.02.
Values may be sent and summed in bfloat16 or wider, within the bound.
No kernel may reach another device: no remote copies, remote signals or barrier semaphores. Data moves between devices by JAX's collectives and lax.ppermute only.
A program may use at most 320 MiB of HBM per device.

v0:
```python
import math

import jax
import jax.numpy as jnp
from jax import lax
from jax.sharding import PartitionSpec as P

HEADS_ENC = 12
D_DEC = 512
HEADS_DEC = 16
TIME = 64
FREQ = 8
WINDOW = 4
SHIFT = 2


norm_eps = 1e-06
neg_fill = -1e30


def layer_norm(inputs, gain_vec, shift_vec):
    centre = jnp.mean(inputs, axis=-1, keepdims=True)
    centred = inputs - centre
    spread = jnp.mean(centred * centred, axis=-1, keepdims=True)
    return centred * lax.rsqrt(spread + norm_eps) * gain_vec + shift_vec


def position_table(places):
    half_width = D_DEC // 2
    omega_vec = jnp.exp(
        jnp.arange(half_width, dtype=jnp.float32) * (-math.log(10000.0) / half_width)
    )
    angles = places.astype(jnp.float32)[..., None] * omega_vec
    return jnp.concatenate([jnp.sin(angles), jnp.cos(angles)], axis=-1)


def forward_dot(operand, weight):
    return jnp.einsum("nd,de->ne", operand, weight, preferred_element_type=jnp.float32)


def backward_dot(gradient, weight):
    return jnp.einsum("ne,de->nd", gradient, weight, preferred_element_type=jnp.float32)


def weight_dot(operand, gradient):
    return jnp.einsum("nd,ne->de", operand, gradient, preferred_element_type=jnp.float32)


def exact_gelu(inputs):
    return jax.nn.gelu(inputs, approximate=False)


def block_forward(inputs, weights, head_count, allowed):
    batch_size, length, model_width = inputs.shape
    head_dim = model_width // head_count
    flat_rows = inputs.reshape(-1, model_width)
    normed, norm_back_one = jax.vjp(
        layer_norm, flat_rows, weights[0].astype(jnp.float32), weights[1].astype(jnp.float32)
    )
    normed = normed.astype(jnp.bfloat16)
    qkv_rows = (
        forward_dot(normed, weights[2])
        .astype(jnp.bfloat16)
        .reshape(batch_size, length, 3, head_count, head_dim)
    )
    queries, key_heads, values = (qkv_rows[:, :, 0], qkv_rows[:, :, 1], qkv_rows[:, :, 2])
    raw_scores = jnp.einsum(
        "bqhd,bkhd->bhqk", queries, key_heads, preferred_element_type=jnp.float32
    )
    scores = jnp.where(allowed, raw_scores * head_dim ** (-0.5), neg_fill)
    row_top = jnp.max(scores, axis=-1, keepdims=True)
    exp_scores = jnp.exp(scores - row_top)
    row_total = jnp.sum(exp_scores, axis=-1, keepdims=True)
    attn_prob = exp_scores / row_total
    log_total = row_top + jnp.log(row_total)
    mixed_heads = jnp.einsum(
        "bhqk,bkhd->bqhd",
        attn_prob.astype(jnp.bfloat16),
        values,
        preferred_element_type=jnp.float32,
    )
    mixed_heads = mixed_heads.astype(jnp.bfloat16).reshape(-1, model_width)
    middle = flat_rows + forward_dot(mixed_heads, weights[3])
    normed_two, norm_back_two = jax.vjp(
        layer_norm, middle, weights[4].astype(jnp.float32), weights[5].astype(jnp.float32)
    )
    normed_two = normed_two.astype(jnp.bfloat16)
    pre_gelu = forward_dot(normed_two, weights[6])
    hidden = exact_gelu(pre_gelu).astype(jnp.bfloat16)
    output = middle + forward_dot(hidden, weights[7])
    stored = (
        norm_back_one,
        normed,
        queries,
        key_heads,
        values,
        log_total,
        mixed_heads,
        norm_back_two,
        normed_two,
        pre_gelu,
        hidden,
    )
    return (output.reshape(inputs.shape), stored)


def block_backward(cotangent_in, stored, weights, head_count, allowed):
    (
        norm_back_one,
        normed,
        queries,
        key_heads,
        values,
        log_total,
        mixed_heads,
        norm_back_two,
        normed_two,
        pre_gelu,
        hidden,
    ) = stored
    batch_size, length, model_width = cotangent_in.shape
    head_dim = model_width // head_count
    upstream = cotangent_in.reshape(-1, model_width)
    upstream_low = upstream.astype(jnp.bfloat16)
    grad_down = weight_dot(hidden, upstream_low)
    grad_hidden = backward_dot(upstream_low, weights[7])
    gelu_back = jax.vjp(exact_gelu, pre_gelu)[1]
    grad_pre = gelu_back(grad_hidden)[0].astype(jnp.bfloat16)
    grad_up = weight_dot(normed_two, grad_pre)
    from_norm_two, grad_gain_two, grad_shift_two = norm_back_two(backward_dot(grad_pre, weights[6]))
    grad_middle = upstream + from_norm_two
    middle_low = grad_middle.astype(jnp.bfloat16)
    grad_out = weight_dot(mixed_heads, middle_low)
    grad_mixed = (
        backward_dot(middle_low, weights[3])
        .astype(jnp.bfloat16)
        .reshape(batch_size, length, head_count, head_dim)
    )
    raw_scores = jnp.einsum(
        "bqhd,bkhd->bhqk", queries, key_heads, preferred_element_type=jnp.float32
    )
    scores = jnp.where(allowed, raw_scores * head_dim ** (-0.5), neg_fill)
    attn_prob = jnp.exp(scores - log_total)
    grad_prob = jnp.einsum(
        "bqhd,bkhd->bhqk", grad_mixed, values, preferred_element_type=jnp.float32
    )
    grad_values = jnp.einsum(
        "bhqk,bqhd->bkhd",
        attn_prob.astype(jnp.bfloat16),
        grad_mixed,
        preferred_element_type=jnp.float32,
    )
    grad_scores = attn_prob * (grad_prob - jnp.sum(attn_prob * grad_prob, axis=-1, keepdims=True))
    grad_raw = (grad_scores * head_dim ** (-0.5)).astype(jnp.bfloat16)
    grad_queries = jnp.einsum(
        "bhqk,bkhd->bqhd", grad_raw, key_heads, preferred_element_type=jnp.float32
    )
    grad_keys = jnp.einsum("bhqk,bqhd->bkhd", grad_raw, queries, preferred_element_type=jnp.float32)
    grad_qkv_rows = (
        jnp.stack([grad_queries, grad_keys, grad_values], axis=2)
        .astype(jnp.bfloat16)
        .reshape(-1, 3 * model_width)
    )
    grad_qkv = weight_dot(normed, grad_qkv_rows)
    from_norm_one, grad_gain_one, grad_shift_one = norm_back_one(
        backward_dot(grad_qkv_rows, weights[2])
    )
    grad_inputs = grad_middle + from_norm_one
    return (
        grad_inputs.reshape(cotangent_in.shape),
        (
            grad_gain_one,
            grad_shift_one,
            grad_qkv,
            grad_out,
            grad_gain_two,
            grad_shift_two,
            grad_up,
            grad_down,
        ),
    )


def shards(
    visible,
    keep_index,
    visible_count,
    enc_gain1,
    enc_shift1,
    enc_qkv,
    enc_out,
    enc_gain2,
    enc_shift2,
    enc_up,
    enc_down,
    proj,
    mask_token,
    dec_gain1,
    dec_shift1,
    dec_qkv,
    dec_out,
    dec_gain2,
    dec_shift2,
    dec_up,
    dec_down,
    cotangent,
):
    enc_weights = (
        lax.all_gather(enc_gain1, ("clip", "band"), axis=0, tiled=True),
        lax.all_gather(enc_shift1, ("clip", "band"), axis=0, tiled=True),
        lax.all_gather(enc_qkv, ("clip", "band"), axis=0, tiled=True),
        lax.all_gather(enc_out, ("clip", "band"), axis=0, tiled=True),
        lax.all_gather(enc_gain2, ("clip", "band"), axis=0, tiled=True),
        lax.all_gather(enc_shift2, ("clip", "band"), axis=0, tiled=True),
        lax.all_gather(enc_up, ("clip", "band"), axis=0, tiled=True),
        lax.all_gather(enc_down, ("clip", "band"), axis=0, tiled=True),
    )
    dec_all = (
        lax.all_gather(proj, ("clip", "band"), axis=0, tiled=True),
        lax.all_gather(mask_token, ("clip", "band"), axis=0, tiled=True),
        lax.all_gather(dec_gain1, ("clip", "band"), axis=0, tiled=True),
        lax.all_gather(dec_shift1, ("clip", "band"), axis=0, tiled=True),
        lax.all_gather(dec_qkv, ("clip", "band"), axis=0, tiled=True),
        lax.all_gather(dec_out, ("clip", "band"), axis=0, tiled=True),
        lax.all_gather(dec_gain2, ("clip", "band"), axis=0, tiled=True),
        lax.all_gather(dec_shift2, ("clip", "band"), axis=0, tiled=True),
        lax.all_gather(dec_up, ("clip", "band"), axis=0, tiled=True),
        lax.all_gather(dec_down, ("clip", "band"), axis=0, tiled=True),
    )
    weight_proj = dec_all[1 - 1]
    token_vec = dec_all[1].astype(jnp.float32)
    dec_weights = dec_all[2:]
    clip_count, slot_total, enc_width = visible.shape
    dec_width = weight_proj.shape[1]
    half_clips = clip_count // 2
    band_height = FREQ // 2
    slot_ids = jnp.arange(slot_total)
    valid_rows = slot_ids[None, :] < visible_count[:, None]
    enc_allowed = valid_rows[:, None, None, :]
    encoded, enc_stored = block_forward(
        visible.astype(jnp.float32), enc_weights, HEADS_ENC, enc_allowed
    )
    enc_inputs = encoded.reshape(-1, enc_width).astype(jnp.bfloat16)
    sent_rows = (
        forward_dot(enc_inputs, weight_proj)
        .astype(jnp.bfloat16)
        .reshape(clip_count, slot_total, dec_width)
    )
    rolled_time = (keep_index // FREQ + TIME - SHIFT) % TIME
    rolled_freq = (keep_index % FREQ + FREQ - SHIFT) % FREQ
    target_band = rolled_freq // band_height
    slot_index = rolled_time * band_height + rolled_freq % band_height
    band_ids = jnp.arange(2)
    chosen = valid_rows[:, None, :] & (target_band[:, None, :] == band_ids[None, :, None])
    chosen = chosen.reshape(2, half_clips, 2, slot_total).transpose(0, 2, 1, 3)
    outgoing = jnp.where(
        chosen[..., None],
        sent_rows.reshape(2, 1, half_clips, slot_total, dec_width),
        jnp.zeros((), jnp.bfloat16),
    )
    outgoing = outgoing.reshape(4, half_clips, slot_total, dec_width)
    slot_out = jnp.where(chosen, slot_index.reshape(2, 1, half_clips, slot_total), -1).astype(
        jnp.bfloat16
    )
    slot_out = slot_out.reshape(4, half_clips, slot_total)
    arrived, arrived_slot = (
        lax.all_to_all(outgoing, "band", split_axis=0, concat_axis=0, tiled=True),
        lax.all_to_all(slot_out, "band", split_axis=0, concat_axis=0, tiled=True),
    )
    half_total = 4 * half_clips
    arrived_rows = arrived.reshape(half_total, slot_total, dec_width)
    arrived_index = arrived_slot.reshape(half_total, slot_total).astype(jnp.int32)
    cell_count = TIME * band_height
    places = jnp.arange(cell_count)
    onehot = (arrived_index[:, :, None] == places[None, None, :]).astype(jnp.bfloat16)
    grid_rows = jnp.einsum("mic,mid->mcd", onehot, arrived_rows, preferred_element_type=jnp.float32)
    seen_mask = jnp.sum(onehot.astype(jnp.float32), axis=1)[:, :, None]
    band_pick = lax.axis_index("band") % 2
    cell_time = places // band_height
    cell_freq = band_pick * band_height + places % band_height
    patch_number = (cell_time + SHIFT) % TIME * FREQ + (cell_freq + SHIFT) % FREQ
    filled = seen_mask * grid_rows + (1.0 - seen_mask) * token_vec + position_table(patch_number)
    labels = (cell_time >= TIME - SHIFT).astype(jnp.int32) * 2 + (cell_freq >= FREQ - SHIFT).astype(
        jnp.int32
    )
    labels = labels.reshape(-1, WINDOW * WINDOW)
    allowed_one = labels[:, :, None] == labels[:, None, :]
    dec_allowed = jnp.tile(allowed_one, (half_total, 1, 1))[:, None]
    decoded, dec_stored = block_forward(
        filled.reshape(-1, WINDOW * WINDOW, dec_width), dec_weights, HEADS_DEC, dec_allowed
    )
    decoded_out = decoded.reshape(cotangent.shape).astype(jnp.bfloat16)
    grad_filled, dec_grads = block_backward(
        cotangent.astype(jnp.float32).reshape(-1, WINDOW * WINDOW, dec_width),
        dec_stored,
        dec_weights,
        HEADS_DEC,
        dec_allowed,
    )
    grad_filled = grad_filled.reshape(half_total, cell_count, dec_width)
    grad_token = jnp.sum((1.0 - seen_mask) * grad_filled, axis=(0, 1))
    safe_index = jnp.maximum(arrived_index, 0)
    picked = jax.vmap(lambda grid_one, index_one: grid_one[index_one])(grad_filled, safe_index)
    returning = jnp.where((arrived_index >= 0)[:, :, None], picked, 0.0).astype(jnp.bfloat16)
    returning = returning.reshape(4, half_clips, slot_total, dec_width)
    coming = lax.all_to_all(returning, "band", split_axis=0, concat_axis=0, tiled=True)
    grad_sent = jnp.sum(
        coming.astype(jnp.float32).reshape(2, 2, half_clips, slot_total, dec_width), axis=1
    )
    grad_sent = grad_sent.astype(jnp.bfloat16).reshape(-1, dec_width)
    grad_proj = weight_dot(enc_inputs, grad_sent)
    grad_encoded = backward_dot(grad_sent, weight_proj)
    dec_share = (
        lax.psum_scatter(grad_proj, ("clip", "band"), scatter_dimension=0, tiled=True),
        lax.psum_scatter(grad_token, ("clip", "band"), scatter_dimension=0, tiled=True),
        lax.psum_scatter(dec_grads[0], ("clip", "band"), scatter_dimension=0, tiled=True),
        lax.psum_scatter(dec_grads[1], ("clip", "band"), scatter_dimension=0, tiled=True),
        lax.psum_scatter(dec_grads[2], ("clip", "band"), scatter_dimension=0, tiled=True),
        lax.psum_scatter(dec_grads[3], ("clip", "band"), scatter_dimension=0, tiled=True),
        lax.psum_scatter(dec_grads[4], ("clip", "band"), scatter_dimension=0, tiled=True),
        lax.psum_scatter(dec_grads[5], ("clip", "band"), scatter_dimension=0, tiled=True),
        lax.psum_scatter(dec_grads[6], ("clip", "band"), scatter_dimension=0, tiled=True),
        lax.psum_scatter(dec_grads[7], ("clip", "band"), scatter_dimension=0, tiled=True),
    )
    dec_total = (
        lax.all_gather(
            dec_share[0].astype(jnp.bfloat16), ("clip", "band"), axis=0, tiled=True
        ).astype(jnp.float32),
        lax.all_gather(
            dec_share[1].astype(jnp.bfloat16), ("clip", "band"), axis=0, tiled=True
        ).astype(jnp.float32),
        lax.all_gather(
            dec_share[2].astype(jnp.bfloat16), ("clip", "band"), axis=0, tiled=True
        ).astype(jnp.float32),
        lax.all_gather(
            dec_share[3].astype(jnp.bfloat16), ("clip", "band"), axis=0, tiled=True
        ).astype(jnp.float32),
        lax.all_gather(
            dec_share[4].astype(jnp.bfloat16), ("clip", "band"), axis=0, tiled=True
        ).astype(jnp.float32),
        lax.all_gather(
            dec_share[5].astype(jnp.bfloat16), ("clip", "band"), axis=0, tiled=True
        ).astype(jnp.float32),
        lax.all_gather(
            dec_share[6].astype(jnp.bfloat16), ("clip", "band"), axis=0, tiled=True
        ).astype(jnp.float32),
        lax.all_gather(
            dec_share[7].astype(jnp.bfloat16), ("clip", "band"), axis=0, tiled=True
        ).astype(jnp.float32),
        lax.all_gather(
            dec_share[8].astype(jnp.bfloat16), ("clip", "band"), axis=0, tiled=True
        ).astype(jnp.float32),
        lax.all_gather(
            dec_share[9].astype(jnp.bfloat16), ("clip", "band"), axis=0, tiled=True
        ).astype(jnp.float32),
    )
    grad_visible, enc_grads = block_backward(
        grad_encoded.reshape(clip_count, slot_total, enc_width),
        enc_stored,
        enc_weights,
        HEADS_ENC,
        enc_allowed,
    )
    enc_share = (
        lax.psum_scatter(enc_grads[0], ("clip", "band"), scatter_dimension=0, tiled=True),
        lax.psum_scatter(enc_grads[1], ("clip", "band"), scatter_dimension=0, tiled=True),
        lax.psum_scatter(enc_grads[2], ("clip", "band"), scatter_dimension=0, tiled=True),
        lax.psum_scatter(enc_grads[3], ("clip", "band"), scatter_dimension=0, tiled=True),
        lax.psum_scatter(enc_grads[4], ("clip", "band"), scatter_dimension=0, tiled=True),
        lax.psum_scatter(enc_grads[5], ("clip", "band"), scatter_dimension=0, tiled=True),
        lax.psum_scatter(enc_grads[6], ("clip", "band"), scatter_dimension=0, tiled=True),
        lax.psum_scatter(enc_grads[7], ("clip", "band"), scatter_dimension=0, tiled=True),
    )
    enc_total = (
        lax.all_gather(
            enc_share[0].astype(jnp.bfloat16), ("clip", "band"), axis=0, tiled=True
        ).astype(jnp.float32),
        lax.all_gather(
            enc_share[1].astype(jnp.bfloat16), ("clip", "band"), axis=0, tiled=True
        ).astype(jnp.float32),
        lax.all_gather(
            enc_share[2].astype(jnp.bfloat16), ("clip", "band"), axis=0, tiled=True
        ).astype(jnp.float32),
        lax.all_gather(
            enc_share[3].astype(jnp.bfloat16), ("clip", "band"), axis=0, tiled=True
        ).astype(jnp.float32),
        lax.all_gather(
            enc_share[4].astype(jnp.bfloat16), ("clip", "band"), axis=0, tiled=True
        ).astype(jnp.float32),
        lax.all_gather(
            enc_share[5].astype(jnp.bfloat16), ("clip", "band"), axis=0, tiled=True
        ).astype(jnp.float32),
        lax.all_gather(
            enc_share[6].astype(jnp.bfloat16), ("clip", "band"), axis=0, tiled=True
        ).astype(jnp.float32),
        lax.all_gather(
            enc_share[7].astype(jnp.bfloat16), ("clip", "band"), axis=0, tiled=True
        ).astype(jnp.float32),
    )
    return (
        decoded_out,
        grad_visible.astype(jnp.bfloat16),
        enc_total[0],
        enc_total[1],
        enc_total[2],
        enc_total[3],
        enc_total[4],
        enc_total[5],
        enc_total[6],
        enc_total[7],
        dec_total[0],
        dec_total[1],
        dec_total[2],
        dec_total[3],
        dec_total[4],
        dec_total[5],
        dec_total[6],
        dec_total[7],
        dec_total[8],
        dec_total[9],
    )


def solution(mesh):
    return jax.shard_map(
        shards,
        mesh=mesh,
        in_specs=(
            P(("clip", "band"), None, None),
            P(("clip", "band"), None),
            P(("clip", "band")),
            P(("clip", "band")),
            P(("clip", "band")),
            P(("clip", "band"), None),
            P(("clip", "band"), None),
            P(("clip", "band")),
            P(("clip", "band")),
            P(("clip", "band"), None),
            P(("clip", "band"), None),
            P(("clip", "band"), None),
            P(("clip", "band")),
            P(("clip", "band")),
            P(("clip", "band")),
            P(("clip", "band"), None),
            P(("clip", "band"), None),
            P(("clip", "band")),
            P(("clip", "band")),
            P(("clip", "band"), None),
            P(("clip", "band"), None),
            P(("clip", "band"), None, None, None, None),
        ),
        out_specs=(
            P(("clip", "band"), None, None, None, None),
            P(("clip", "band"), None, None),
            P(),
            P(),
            P(),
            P(),
            P(),
            P(),
            P(),
            P(),
            P(),
            P(),
            P(),
            P(),
            P(),
            P(),
            P(),
            P(),
            P(),
            P(),
        ),
        check_vma=False,
    )
```

profile of v0, /device:TPU:0, one launch (start us, length us, event | category | flops | bytes accessed | tf_op | source)
XLA Modules:
  0.0 2363.7 jit_solution(2826416864602446592)
XLA Ops:
  26.8 42.0 %all-reduce.29 = (bf16[768]{0:T(1024)(128)(2,1)S(1)}, bf16[768]{0:T(1024)(128)(2,1)S(1)}, bf16[768]{0:T(1024)(128)(2,1)S(1)}, bf16[768]{0:T(1024)(128)(2,1)S(1)}...) all-reduce(bf16[768]{0:T(1024)(128)(2,1)S(1)} %dynamic-update-slice, ...), channel_id=1, replica_groups=mesh['clip'=8,'band'=4] {'clip','band'}, use_global_device_ids=true, to_apply=%add.1 | all-reduce | flops 5632 | bytes 22528
  71.7 45.9 %all_gather.116 = bf16[768,512]{1,0:T(8,128)(2,1)} all-gather(bf16[24,512]{1,0:T(8,128)(2,1)} %param.33), channel_id=1, replica_groups=mesh['clip'=8,'band'=4] {'clip','band'}, dimensions={0}, use_global_device_ids=true | all-gather | bytes 811008 | tf_op jit(solution)/shard_map/all_gather | solution.py:219
  117.7 41.5 %all_gather.121 = bf16[512,512]{1,0:T(8,128)(2,1)} all-gather(bf16[16,512]{1,0:T(8,128)(2,1)} %param.38), channel_id=1, replica_groups=mesh['clip'=8,'band'=4] {'clip','band'}, dimensions={0}, use_global_device_ids=true | all-gather | bytes 540672 | tf_op jit(solution)/shard_map/all_gather | solution.py:224
  184.7 11.2 all-gather.19.cloned.1.call-done
  195.9 19.8 multiply_convert_fusion.1
  215.7 45.4 %all-gather.21.cloned.1.call-done = bf16[3072,768]{1,0:T(8,128)(2,1)} async-done(((bf16[96,768]{1,0:T(8,128)(2,1)}), bf16[3072,768]{1,0:T(8,128)(2,1)}) %all-gather.21.cloned.1.call-update) | async-done | bytes 4718608 | tf_op jit(solution)/shard_map/all_gather | solution.py:216
  274.5 12.6 all-to-all-done.1
  292.0 25.6 %all-gather.23.cloned.1.call-done = bf16[512,1536]{1,0:T(8,128)(2,1)} async-done(((bf16[16,1536]{1,0:T(8,128)(2,1)}), bf16[512,1536]{1,0:T(8,128)(2,1)}) %all-gather.23.cloned.1.call-update) | async-done | bytes 1572880 | tf_op jit(solution)/shard_map/all_gather | solution.py:223
  324.4 27.8 %reshape.584 = bf16[128,16,3,16,32]{4,3,2,1,0:T(8,128)(2,1)} reshape(bf16[2048,1536]{1,0:T(8,128)(2,1)} %convolution_convert_fusion) | data formatting | bytes 12582912 | tf_op jit(solution)/shard_map/reshape | solution.py:64
  352.1 17.5 fusion.148
  369.7 13.6 fusion.8
  383.2 12.4 copy.114
  399.1 12.0 copy.115
  411.1 13.5 convert_bitcast_fusion
  435.5 11.2 reshape.585
  454.6 44.5 %multiply_convert_fusion = (bf16[2048,2048]{1,0:T(8,128)(2,1)}, f32[2048,2048]{1,0:T(8,128)}, f32[2048,2048]{1,0:T(8,128)}) fusion(bf16[512,2048]{1,0:T(8,128)(2,1)} %all-gather.25.cloned.1.call-done, f32[2048,512]{1,0:T(8,128)} %copy-done.5, f32[512]{0:T(512)S(1)} %copy-done.93, f32[512]{0:T(512)S(1)} %copy-done.90, f32[2048]{0:T(1024)S(1)} %fusion.106, ...), kind=kOutput, calls=%fused_computation.6 | convolution fusion | flops 4572839936 | bytes 48254976 | tf_op jit(solution)/shard_map/nd,de->ne/dot_general | solution.py:38
  499.0 19.0 add_convert_fusion
  518.0 11.9 multiply_reduce_fusion
  543.4 13.8 fusion.9
  557.2 13.7 copy.119
  574.1 11.9 copy.121
  595.8 13.7 convolution_bitcast_fusion.1
  619.4 11.0 copy.125
  630.4 12.1 copy.123
  642.5 13.7 convolution_bitcast_fusion
  672.7 33.8 %copy.127 = bf16[128,16,3,16,32]{4,3,2,1,0:T(8,128)(2,1)} copy(bf16[128,16,3,16,32]{0,4,3,2,1:T(8,128)(2,1)} %maximum_convert_fusion) | data formatting | bytes 12582912 | tf_op jit(solution)/shard_map/convert_element_type | solution.py:161
  706.6 33.1 %convert_element_type.384 = bf16[2048,1536]{1,0:T(8,128)(2,1)} reshape(bf16[128,16,3,16,32]{4,3,2,1,0:T(8,128)(2,1)} %copy.127) | data formatting | bytes 12582912 | tf_op jit(solution)/shard_map/convert_element_type | solution.py:161
  760.3 17.5 all_to_all.15
  805.8 11.6 fusion.140
  894.7 105.4 %reduce-scatter.20.cloned.1.call-done = f32[16,1536]{1,0:T(8,128)} async-done(((f32[512,1536]{1,0:T(8,128)}), f32[16,1536]{1,0:T(8,128)}) %reduce-scatter.20.cloned.1.call-update) | async-done | bytes 98320 | tf_op jit(solution)/shard_map/reduce_scatter | solution.py:318
  1001.6 141.2 %reduce-scatter.24.cloned.1.call-done = f32[16,2048]{1,0:T(8,128)} async-done(((f32[512,2048]{1,0:T(8,128)}), f32[16,2048]{1,0:T(8,128)}) %reduce-scatter.24.cloned.1.call-update) | async-done | bytes 131088 | tf_op jit(solution)/shard_map/reduce_scatter | solution.py:322
  1144.4 137.8 %reduce-scatter.26.cloned.1.call-done = f32[64,512]{1,0:T(8,128)} async-done(((f32[2048,512]{1,0:T(8,128)}), f32[64,512]{1,0:T(8,128)}) %reduce-scatter.26.cloned.1.call-update) | async-done | bytes 131088 | tf_op jit(solution)/shard_map/reduce_scatter | solution.py:323
  1283.9 120.5 %reduce-scatter.10.cloned.1.call-done = f32[24,2304]{1,0:T(8,128)} async-done(((f32[768,2304]{1,0:T(8,128)}), f32[24,2304]{1,0:T(8,128)}) %reduce-scatter.10.cloned.1.call-update) | async-done | bytes 221200 | tf_op jit(solution)/shard_map/reduce_scatter | solution.py:367
  1406.0 139.7 %reduce-scatter.14.cloned.1.call-done = f32[24,3072]{1,0:T(8,128)} async-done(((f32[768,3072]{1,0:T(8,128)}), f32[24,3072]{1,0:T(8,128)}) %reduce-scatter.14.cloned.1.call-update) | async-done | bytes 294928 | tf_op jit(solution)/shard_map/reduce_scatter | solution.py:371
  1547.5 140.3 %reduce-scatter.16.cloned.1.call-done = f32[96,768]{1,0:T(8,128)} async-done(((f32[3072,768]{1,0:T(8,128)}), f32[96,768]{1,0:T(8,128)}) %reduce-scatter.16.cloned.1.call-update) | async-done | bytes 294928 | tf_op jit(solution)/shard_map/reduce_scatter | solution.py:372
  1708.3 40.5 %all-reduce.27 = (bf16[768]{0:T(1024)(128)(2,1)S(1)}, bf16[768]{0:T(1024)(128)(2,1)S(1)}, bf16[768]{0:T(1024)(128)(2,1)S(1)}, bf16[768]{0:T(1024)(128)(2,1)S(1)}...) all-reduce(f32[768]{0:T(1024)S(1)} %get-tuple-element.28, ...), channel_id=2, replica_groups=mesh['clip'=8,'band'=4] {'clip','band'}, use_global_device_ids=true, to_apply=%region_25.26.clone | all-reduce | flops 5632 | bytes 33792
  1751.4 39.7 %all-reduce.28 = (bf16[768]{0:T(1024)(128)(2,1)S(1)}, bf16[768]{0:T(1024)(128)(2,1)S(1)}, bf16[768]{0:T(1024)(128)(2,1)S(1)}, bf16[768]{0:T(1024)(128)(2,1)S(1)}...) all-reduce(bf16[768]{0:T(1024)(128)(2,1)S(1)} %dynamic-update-slice, ...), channel_id=1, replica_groups=mesh['clip'=8,'band'=4] {'clip','band'}, use_global_device_ids=true, to_apply=%add.9 | all-reduce | flops 5632 | bytes 22528
  1799.2 25.3 %reduce-scatter.22.cloned.1.call-done = f32[16,512]{1,0:T(8,128)} async-done(((f32[512,512]{1,0:T(8,128)}), f32[16,512]{1,0:T(8,128)}) %reduce-scatter.22.cloned.1.call-update) | async-done | bytes 32784 | tf_op jit(solution)/shard_map/reduce_scatter | solution.py:319
  1825.2 37.7 %all_gather.139 = bf16[512,512]{1,0:T(8,128)(2,1)S(1)} all-gather(bf16[16,512]{1,0:T(8,128)(2,1)S(1)} %convert_element_type.428), channel_id=1, replica_groups=mesh['clip'=8,'band'=4] {'clip','band'}, dimensions={0}, use_global_device_ids=true | all-gather | bytes 540672 | tf_op jit(solution)/shard_map/all_gather | solution.py:341
  1864.1 60.0 %reduce-scatter.18.cloned.1.call-done = f32[24,512]{1,0:T(8,128)} async-done(((f32[768,512]{1,0:T(8,128)}), f32[24,512]{1,0:T(8,128)}) %reduce-scatter.18.cloned.1.call-update) | async-done | bytes 49168 | tf_op jit(solution)/shard_map/reduce_scatter | solution.py:314
  1924.9 41.8 %all_gather.134 = bf16[768,512]{1,0:T(8,128)(2,1)S(1)} all-gather(bf16[24,512]{1,0:T(8,128)(2,1)S(1)} %convert_element_type.416), channel_id=1, replica_groups=mesh['clip'=8,'band'=4] {'clip','band'}, dimensions={0}, use_global_device_ids=true | all-gather | bytes 811008 | tf_op jit(solution)/shard_map/all_gather | solution.py:326
  1968.1 12.3 all-gather.31.cloned.1.call-done
  1983.3 54.3 %all-gather.37.cloned.1.call-done = bf16[512,1536]{1,0:T(8,128)(2,1)} async-done(((bf16[16,1536]{1,0:T(8,128)(2,1)}), bf16[512,1536]{1,0:T(8,128)(2,1)}) %all-gather.37.cloned.1.call-update) | async-done | bytes 1572880 | tf_op jit(solution)/shard_map/all_gather | solution.py:338
  2041.1 55.7 %all-gather.39.cloned.1.call-done = bf16[512,2048]{1,0:T(8,128)(2,1)} async-done(((bf16[16,2048]{1,0:T(8,128)(2,1)}), bf16[512,2048]{1,0:T(8,128)(2,1)}) %all-gather.39.cloned.1.call-update) | async-done | bytes 2097168 | tf_op jit(solution)/shard_map/all_gather | solution.py:350
  2100.9 54.3 %all-gather.41.cloned.1.call-done = bf16[2048,512]{1,0:T(8,128)(2,1)} async-done(((bf16[64,512]{1,0:T(8,128)(2,1)}), bf16[2048,512]{1,0:T(8,128)(2,1)}) %all-gather.41.cloned.1.call-update) | async-done | bytes 2097168 | tf_op jit(solution)/shard_map/all_gather | solution.py:353
  2159.3 58.7 %all-gather.29.cloned.1.call-done = bf16[768,2304]{1,0:T(8,128)(2,1)} async-done(((bf16[24,2304]{1,0:T(8,128)(2,1)}), bf16[768,2304]{1,0:T(8,128)(2,1)}) %all-gather.29.cloned.1.call-update) | async-done | bytes 3538960 | tf_op jit(solution)/shard_map/all_gather | solution.py:381
  2223.5 60.8 %all-gather.33.cloned.1.call-done = bf16[768,3072]{1,0:T(8,128)(2,1)} async-done(((bf16[24,3072]{1,0:T(8,128)(2,1)}), bf16[768,3072]{1,0:T(8,128)(2,1)}) %all-gather.33.cloned.1.call-update) | async-done | bytes 4718608 | tf_op jit(solution)/shard_map/all_gather | solution.py:393
  2291.7 58.4 %all-gather.35.cloned.1.call-done = bf16[3072,768]{1,0:T(8,128)(2,1)} async-done(((bf16[96,768]{1,0:T(8,128)(2,1)}), bf16[3072,768]{1,0:T(8,128)(2,1)}) %all-gather.35.cloned.1.call-update) | async-done | bytes 4718608 | tf_op jit(solution)/shard_map/all_gather | solution.py:396
  (453 shorter events, 350.2 us)
Async XLA Ops:
  7.2 153.0 %copy-start.9 = (bf16[4,128,768]{2,1,0:T(8,128)(2,1)S(1)}, bf16[4,128,768]{2,1,0:T(8,128)(2,1)}, u32[]{:S(2)}) copy-start(bf16[4,128,768]{2,1,0:T(8,128)(2,1)} %param.22) | copy-start | bytes 2359300
  7.2 156.9 %copy-start.36 = (bf16[1,8,64,4,512]{4,3,2,1,0:T(4,128)(2,1)S(1)}, bf16[1,8,64,4,512]{4,3,2,1,0:T(4,128)(2,1)}, u32[]{:S(2)}) copy-start(bf16[1,8,64,4,512]{4,3,2,1,0:T(4,128)(2,1)} %param.43) | copy-start | bytes 6291460
  7.2 159.4 %all-gather.15.cloned.1.call-start = ((), (), s32[]{:S(2)}) async-start(), calls=%async_computation.12 | async-start | bytes 3649536 | tf_op jit(solution)/shard_map/all_gather | solution.py:211
  7.9 174.0 %all-gather.17.cloned.1.call-start = ((), (), s32[]{:S(2)}) async-start(), calls=%async_computation.13 | async-start | bytes 1216512 | tf_op jit(solution)/shard_map/all_gather | solution.py:212
  8.7 187.2 %all-gather.19.cloned.1.call-start = ((), (), s32[]{:S(2)}) async-start(), calls=%async_computation.14 | async-start | bytes 4866048 | tf_op jit(solution)/shard_map/all_gather | solution.py:215
  9.4 251.6 %all-gather.21.cloned.1.call-start = ((), (), s32[]{:S(2)}) async-start(), calls=%async_computation.15 | async-start | bytes 4866048 | tf_op jit(solution)/shard_map/all_gather | solution.py:216
  10.0 307.7 %all-gather.23.cloned.1.call-start = ((), (), s32[]{:S(2)}) async-start(), calls=%async_computation.16 | async-start | bytes 1622016 | tf_op jit(solution)/shard_map/all_gather | solution.py:223
  10.6 443.9 %all-gather.25.cloned.1.call-start = ((), (), s32[]{:S(2)}) async-start(), calls=%async_computation.17 | async-start | bytes 2162688 | tf_op jit(solution)/shard_map/all_gather | solution.py:227
  13.4 152.9 %all-to-all-start = ((bf16[4,2,128]{2,1,0:T(2,128)(2,1)}), bf16[4,2,128]{2,1,0:T(2,128)(2,1)S(1)}, u32[]{:S(2)}, u32[]{:S(2)}) async-start(bf16[4,2,128]{2,1,0:T(2,128)(2,1)} %get-tuple-element.70), calls=%async_computation | async-start | bytes 4096 | tf_op jit(solution)/shard_map/all_to_all | solution.py:268
  17.7 481.3 %all-gather.27.cloned.1.call-start = ((), (), s32[]{:S(2)}) async-start(), calls=%async_computation.18 | async-start | bytes 2162688 | tf_op jit(solution)/shard_map/all_gather | solution.py:228
  68.8 93.6 %copy-start.53 = (f32[768]{0:T(1024)}, f32[768]{0:T(1024)S(1)}, u32[]{:S(2)}) copy-start(f32[768]{0:T(1024)S(1)} %convert_element_type.348) | copy-start | bytes 9220
  68.8 93.6 %copy-start.65 = (f32[768]{0:T(1024)}, f32[768]{0:T(1024)S(1)}, u32[]{:S(2)}) copy-start(f32[768]{0:T(1024)S(1)} %convert_element_type.349) | copy-start | bytes 9220
  70.1 92.2 %copy-start.77 = (f32[4,128]{1,0:T(4,128)}, f32[4,128]{1,0:T(4,128)S(1)}, u32[]{:S(2)}) copy-start(f32[4,128]{1,0:T(4,128)S(1)} %get-tuple-element.91) | copy-start | bytes 6148
  70.1 92.2 %copy-start.67 = (f32[512]{0:T(512)}, f32[512]{0:T(512)S(1)}, u32[]{:S(2)}) copy-start(f32[512]{0:T(512)S(1)} %get-tuple-element.90) | copy-start | bytes 6148
  71.7 46.0 %copy-start.73 = (f32[4,128]{1,0:T(4,128)}, f32[4,128]{1,0:T(4,128)S(1)}, u32[]{:S(2)}) copy-start(f32[4,128]{1,0:T(4,128)S(1)} %fusion.54) | copy-start | bytes 6148
  71.7 90.7 %copy-start.69 = (f32[512]{0:T(512)}, f32[512]{0:T(512)S(1)}, u32[]{:S(2)}) copy-start(f32[512]{0:T(512)S(1)} %bitcast_rsqrt_fusion) | copy-start | bytes 6148
  162.3 33.6 %copy-start.85 = (f32[768]{0:T(1024)}, f32[768]{0:T(1024)S(1)}, u32[]{:S(2)}) copy-start(f32[768]{0:T(1024)S(1)} %convert_element_type.355) | copy-start | bytes 9220
  162.3 33.6 %copy-start.91 = (f32[768]{0:T(1024)}, f32[768]{0:T(1024)S(1)}, u32[]{:S(2)}) copy-start(f32[768]{0:T(1024)S(1)} %convert_element_type.356) | copy-start | bytes 9220
  162.3 128.6 %copy-start.75 = (f32[512]{0:T(512)}, f32[512]{0:T(512)S(1)}, u32[]{:S(2)}) copy-start(f32[512]{0:T(512)S(1)} %convert_element_type.363) | copy-start | bytes 6148
  162.4 128.5 %copy-start.81 = (f32[512]{0:T(512)}, f32[512]{0:T(512)S(1)}, u32[]{:S(2)}) copy-start(f32[512]{0:T(512)S(1)} %convert_element_type.364) | copy-start | bytes 6148
  163.0 234.2 %copy-start.44 = (pred[128,16,16]{0,2,1:T(8,128)(4,1)}, pred[128,16,16]{0,2,1:T(8,128)(4,1)S(1)}, u32[]{:S(2)}) copy-start(pred[128,16,16]{0,2,1:T(8,128)(4,1)S(1)} %tile.9) | copy-start | bytes 98308
  184.3 76.7 %copy-start.22 = (f32[512,768]{1,0:T(8,128)}, f32[512,768]{1,0:T(8,128)S(1)}, u32[]{:S(2)}) copy-start(f32[512,768]{1,0:T(8,128)S(1)} %get-tuple-element.97) | copy-start | bytes 4718596
  184.4 31.3 %copy-start.79 = (f32[512]{0:T(512)}, f32[512]{0:T(512)S(1)}, u32[]{:S(2)}) copy-start(f32[512]{0:T(512)S(1)} %broadcast_multiply_fusion.2) | copy-start | bytes 6148
  269.1 18.0 all-to-all-start.1
  272.6 620.5 %reduce-scatter.12.cloned.1.call-start = ((), (), s32[]{:S(2)}) async-start(), calls=%async_computation.21 | async-start | bytes 2433024 | tf_op jit(solution)/shard_map/reduce_scatter | solution.py:368
  290.3 34.0 %copy-start.61 = (f32[2048]{0:T(1024)}, f32[2048]{0:T(1024)S(1)}, u32[]{:S(2)}) copy-start(f32[2048]{0:T(1024)S(1)} %rsqrt.48) | copy-start | bytes 24580
  290.9 33.5 %copy-start.63 = (f32[1,2,8,128]{3,1,2,0:T(2,128)}, f32[1,2,8,128]{3,1,2,0:T(2,128)S(1)}, u32[]{:S(2)}) copy-start(f32[1,2,8,128]{3,1,2,0:T(2,128)S(1)} %copy.146) | copy-start | bytes 24580
  454.5 44.5 %copy-start.11 = (bf16[2048,512]{1,0:T(8,128)(2,1)S(1)}, bf16[2048,512]{1,0:T(8,128)(2,1)}, u32[]{:S(2)}) copy-start(bf16[2048,512]{1,0:T(8,128)(2,1)} %reshape_reshape.15) | copy-start | bytes 6291460
  706.6 33.1 %copy-start.62 = (f32[2048]{0:T(1024)S(1)}, f32[2048]{0:T(1024)}, u32[]{:S(2)}) copy-start(f32[2048]{0:T(1024)} %copy-done.61) | copy-start | bytes 24580
  706.6 33.1 %copy-start.64 = (f32[1,2,8,128]{3,1,2,0:T(2,128)S(1)}, f32[1,2,8,128]{3,1,2,0:T(2,128)}, u32[]{:S(2)}) copy-start(f32[1,2,8,128]{3,1,2,0:T(2,128)} %copy-done.63) | copy-start | bytes 24580
  706.6 33.1 %copy-start.76 = (f32[512]{0:T(512)S(1)}, f32[512]{0:T(512)}, u32[]{:S(2)}) copy-start(f32[512]{0:T(512)} %copy-done.75) | copy-start | bytes 6148
  706.6 33.1 %copy-start.97 = (bf16[512,1536]{1,0:T(8,128)(2,1)S(1)}, bf16[512,1536]{1,0:T(8,128)(2,1)}, u32[]{:S(2)}) copy-start(bf16[512,1536]{1,0:T(8,128)(2,1)} %all-gather.23.cloned.1.call-done) | copy-start | bytes 4718596
  794.8 205.2 %reduce-scatter.20.cloned.1.call-start = ((), (), s32[]{:S(2)}) async-start(), calls=%async_computation.28 | async-start | bytes 3244032 | tf_op jit(solution)/shard_map/reduce_scatter | solution.py:318
  805.6 337.3 %reduce-scatter.24.cloned.1.call-start = ((), (), s32[]{:S(2)}) async-start(), calls=%async_computation.31 | async-start | bytes 4325376 | tf_op jit(solution)/shard_map/reduce_scatter | solution.py:322
  817.5 464.8 %reduce-scatter.26.cloned.1.call-start = ((), (), s32[]{:S(2)}) async-start(), calls=%async_computation.33 | async-start | bytes 4325376 | tf_op jit(solution)/shard_map/reduce_scatter | solution.py:323
  829.0 575.3 %reduce-scatter.10.cloned.1.call-start = ((), (), s32[]{:S(2)}) async-start(), calls=%async_computation.19 | async-start | bytes 7299072 | tf_op jit(solution)/shard_map/reduce_scatter | solution.py:367
  866.2 679.6 %reduce-scatter.14.cloned.1.call-start = ((), (), s32[]{:S(2)}) async-start(), calls=%async_computation.23 | async-start | bytes 9732096 | tf_op jit(solution)/shard_map/reduce_scatter | solution.py:371
  874.8 812.9 %reduce-scatter.16.cloned.1.call-start = ((), (), s32[]{:S(2)}) async-start(), calls=%async_computation.25 | async-start | bytes 9732096 | tf_op jit(solution)/shard_map/reduce_scatter | solution.py:372
  884.5 940.0 %reduce-scatter.22.cloned.1.call-start = ((), (), s32[]{:S(2)}) async-start(), calls=%async_computation.30 | async-start | bytes 1081344 | tf_op jit(solution)/shard_map/reduce_scatter | solution.py:319
  890.0 1034.1 %reduce-scatter.18.cloned.1.call-start = ((), (), s32[]{:S(2)}) async-start(), calls=%async_computation.27 | async-start | bytes 1622016 | tf_op jit(solution)/shard_map/reduce_scatter | solution.py:314
  892.9 1087.5 %all-gather.31.cloned.1.call-start = ((), (), s32[]{:S(2)}) async-start(), calls=%async_computation.22 | async-start | bytes 1216512 | tf_op jit(solution)/shard_map/all_gather | solution.py:384
  894.6 1143.0 %all-gather.37.cloned.1.call-start = ((), (), s32[]{:S(2)}) async-start(), calls=%async_computation.29 | async-start | bytes 1622016 | tf_op jit(solution)/shard_map/all_gather | solution.py:338
  1001.5 1095.2 %all-gather.39.cloned.1.call-start = ((), (), s32[]{:S(2)}) async-start(), calls=%async_computation.32 | async-start | bytes 2162688 | tf_op jit(solution)/shard_map/all_gather | solution.py:350
  1144.4 1010.7 %all-gather.41.cloned.1.call-start = ((), (), s32[]{:S(2)}) async-start(), calls=%async_computation.34 | async-start | bytes 2162688 | tf_op jit(solution)/shard_map/all_gather | solution.py:353
  1283.8 934.2 %all-gather.29.cloned.1.call-start = ((), (), s32[]{:S(2)}) async-start(), calls=%async_computation.20 | async-start | bytes 3649536 | tf_op jit(solution)/shard_map/all_gather | solution.py:381
  1405.9 878.4 %all-gather.33.cloned.1.call-start = ((), (), s32[]{:S(2)}) async-start(), calls=%async_computation.24 | async-start | bytes 4866048 | tf_op jit(solution)/shard_map/all_gather | solution.py:393
  1547.4 802.7 %all-gather.35.cloned.1.call-start = ((), (), s32[]{:S(2)}) async-start(), calls=%async_computation.26 | async-start | bytes 4866048 | tf_op jit(solution)/shard_map/all_gather | solution.py:396
  1701.2 95.2 %copy-start.18 = (f32[512,768]{1,0:T(8,128)S(1)}, f32[512,768]{1,0:T(8,128)}, u32[]{:S(2)}) copy-start(f32[512,768]{1,0:T(8,128)} %copy-done.16) | copy-start | bytes 4718596
  (78 other events, 444.6 us)
Sparse Core Ops, SparseCore 0:
  11.0 63.1 all-gather.14
  77.1 53.1 all-gather.16
  133.2 62.6 all-gather.18
  198.6 62.3 all-gather.20
  263.8 53.8 all-gather.22
  320.4 55.2 all-gather.24
  378.6 55.2 all-gather.26
  794.9 98.1 reduce-scatter.11
  899.4 100.5 reduce-scatter.19
  1002.8 139.9 reduce-scatter.23
  1145.2 137.0 reduce-scatter.25
  1289.3 114.9 reduce-scatter.9
  1410.8 134.8 reduce-scatter.13
  1553.1 134.5 reduce-scatter.15
  1690.4 134.0 reduce-scatter.21
  1831.0 93.0 reduce-scatter.17
  1927.3 53.0 all-gather.30
  1983.6 53.9 all-gather.36
  2041.4 55.2 all-gather.38
  2099.8 55.2 all-gather.40
  2159.0 58.9 all-gather.28
  2222.0 62.3 all-gather.32
  2287.7 62.3 all-gather.34
where the time goes:
time: 2370 us; the launch traced here: 2360 us
  waiting for transfers between devices  1320 us (56%)
  matrix products  321 us (14%)
  blocking collectives  307 us (13%)
  local copies, waits for them, and re-layouts  288 us (12%)
  other arithmetic  98.4 us (4%)
    reduce_scatter x1, waiting for transfers between devices, shards(): lax.psum_scatter(dec_grads[6], ('clip', 'band'), scatter_dimension=0, til...  141 us
    reduce_scatter x1, waiting for transfers between devices, shards(): lax.psum_scatter(enc_grads[7], ('clip', 'band'), scatter_dimension=0, til...  140 us
    reduce_scatter x1, waiting for transfers between devices, shards(): lax.psum_scatter(enc_grads[6], ('clip', 'band'), scatter_dimension=0, til...  140 us
    reduce_scatter x1, waiting for transfers between devices, shards(): lax.psum_scatter(dec_grads[7], ('clip', 'band'), scatter_dimension=0, til...  138 us
    unnamed x3, blocking collectives  122 us
    reduce_scatter x1, waiting for transfers between devices, shards(): lax.psum_scatter(enc_grads[2], ('clip', 'band'), scatter_dimension=0, til...  120 us
    reduce_scatter x1, waiting for transfers between devices, shards(): lax.psum_scatter(dec_grads[2], ('clip', 'band'), scatter_dimension=0, til...  105 us
    dot_general x9, matrix products, forward_dot(): jnp.einsum('nd,de->ne', operand, weight, preferred_element_type=jnp.float32)  98.2 us
  transfers between devices with their start and end apart: 25, of which 20 were waited for; matrix products, arithmetic and copies ran while one was open for 17% of the time, Pallas kernels for 0%

commit v1 on v0

--- a/solution.py
+++ b/solution.py
@@ -181,6 +181,65 @@
     )
 
 
+AXES = ("clip", "band")
+
+
+def split_bits(parts):
+    return parts.bit_length() - 1
+
+
+def bit_order(count):
+    first = [0, 2, 1][: min(count, 3)]
+    first = [b for b in first if b < count]
+    rest = [b for b in range(count - 1, -1, -1) if b not in first]
+    return first + rest
+
+
+def swap_order(order):
+    if len(order) < 3:
+        return order
+    return [order[0], order[2], order[1]] + order[3:]
+
+
+def partner_pairs(total, bit):
+    return [(i, i ^ (1 << bit)) for i in range(total)]
+
+
+def scatter_sum(partial, total, order):
+    me = lax.axis_index(AXES)
+    left = list(range(split_bits(total) - 1, -1, -1))
+    rows = partial.shape[0] // total
+    held = partial.reshape((2,) * len(left) + (rows,) + partial.shape[1:])
+    for bit in order:
+        place = left.index(bit)
+        mine = (me >> bit) & 1
+        keep = lax.dynamic_index_in_dim(held, mine, place, keepdims=False)
+        give = lax.dynamic_index_in_dim(held, 1 - mine, place, keepdims=False).astype(jnp.bfloat16)
+        got = lax.ppermute(give, AXES, partner_pairs(total, bit))
+        held = (keep.astype(jnp.float32) + got.astype(jnp.float32)).astype(jnp.bfloat16)
+        left.remove(bit)
+    return held
+
+
+def gather_rows(shard, total, order):
+    me = lax.axis_index(AXES)
+    have = []
+    held = shard
+    for bit in reversed(order):
+        mine = (me >> bit) & 1
+        got = lax.ppermute(held, AXES, partner_pairs(total, bit))
+        low = jnp.where(mine == 0, held, got)
+        high = jnp.where(mine == 0, got, held)
+        have = sorted(have + [bit], reverse=True)
+        held = jnp.stack([low, high], axis=have.index(bit))
+    return held.reshape((total * shard.shape[0],) + shard.shape[1:])
+
+
+def columns_of(vectors):
+    block = jnp.stack(vectors, axis=1)
+    return jnp.pad(block, ((0, 0), (0, 128 - len(vectors))))
+
+
 def shards(
     visible,
     keep_index,
@@ -205,31 +264,52 @@
     dec_down,
     cotangent,
 ):
+    total = lax.axis_size(AXES)
+    order = bit_order(split_bits(total))
+    order_two = swap_order(order)
+    enc_wide = enc_out.shape[1]
+    dec_wide = dec_out.shape[1]
+    pack_one = jnp.concatenate(
+        [enc_qkv, enc_out, proj, columns_of([enc_gain1, enc_shift1, enc_gain2, enc_shift2])], axis=1
+    )
+    pack_one = gather_rows(pack_one, total, order)
+    whole_up = gather_rows(enc_up, total, order_two)
+    whole_down = gather_rows(enc_down, total, order)
+    enc_vecs = pack_one[:, 4 * enc_wide + dec_wide : 4 * enc_wide + dec_wide + 4].T
     enc_weights = (
-        lax.all_gather(enc_gain1, ("clip", "band"), axis=0, tiled=True),
-        lax.all_gather(enc_shift1, ("clip", "band"), axis=0, tiled=True),
-        lax.all_gather(enc_qkv, ("clip", "band"), axis=0, tiled=True),
-        lax.all_gather(enc_out, ("clip", "band"), axis=0, tiled=True),
-        lax.all_gather(enc_gain2, ("clip", "band"), axis=0, tiled=True),
-        lax.all_gather(enc_shift2, ("clip", "band"), axis=0, tiled=True),
-        lax.all_gather(enc_up, ("clip", "band"), axis=0, tiled=True),
-        lax.all_gather(enc_down, ("clip", "band"), axis=0, tiled=True),
-    )
-    dec_all = (
-        lax.all_gather(proj, ("clip", "band"), axis=0, tiled=True),
-        lax.all_gather(mask_token, ("clip", "band"), axis=0, tiled=True),
-        lax.all_gather(dec_gain1, ("clip", "band"), axis=0, tiled=True),
-        lax.all_gather(dec_shift1, ("clip", "band"), axis=0, tiled=True),
-        lax.all_gather(dec_qkv, ("clip", "band"), axis=0, tiled=True),
-        lax.all_gather(dec_out, ("clip", "band"), axis=0, tiled=True),
-        lax.all_gather(dec_gain2, ("clip", "band"), axis=0, tiled=True),
-        lax.all_gather(dec_shift2, ("clip", "band"), axis=0, tiled=True),
-        lax.all_gather(dec_up, ("clip", "band"), axis=0, tiled=True),
-        lax.all_gather(dec_down, ("clip", "band"), axis=0, tiled=True),
-    )
-    weight_proj = dec_all[1 - 1]
-    token_vec = dec_all[1].astype(jnp.float32)
-    dec_weights = dec_all[2:]
+        enc_vecs[0],
+        enc_vecs[1],
+        pack_one[:, : 3 * enc_wide],
+        pack_one[:, 3 * enc_wide : 4 * enc_wide],
+        enc_vecs[2],
+        enc_vecs[3],
+        whole_up,
+        whole_down,
+    )
+    pack_two = jnp.concatenate(
+        [
+            dec_qkv,
+            dec_out,
+            columns_of([dec_gain1, dec_shift1, dec_gain2, dec_shift2, mask_token]),
+        ],
+        axis=1,
+    )
+    pack_two = gather_rows(pack_two, total, order_two)
+    dec_whole_up = gather_rows(dec_up, total, order)
+    dec_whole_down = gather_rows(dec_down, total, order_two)
+    dec_vecs = pack_two[:, 4 * dec_wide : 4 * dec_wide + 5].T
+    weight_proj = pack_one[:, 4 * enc_wide : 4 * enc_wide + dec_wide]
+    token_vec = dec_vecs[4].astype(jnp.float32)
+    dec_weights = (
+        dec_vecs[0],
+        dec_vecs[1],
+        pack_two[:, : 3 * dec_wide],
+        pack_two[:, 3 * dec_wide : 4 * dec_wide],
+        dec_vecs[2],
+        dec_vecs[3],
+        dec_whole_up,
+        dec_whole_down,
+    )
     clip_count, slot_total, enc_width = visible.shape
     dec_width = weight_proj.shape[1]
     half_clips = clip_count // 2
@@ -310,50 +390,15 @@
     grad_sent = grad_sent.astype(jnp.bfloat16).reshape(-1, dec_width)
     grad_proj = weight_dot(enc_inputs, grad_sent)
     grad_encoded = backward_dot(grad_sent, weight_proj)
-    dec_share = (
-        lax.psum_scatter(grad_proj, ("clip", "band"), scatter_dimension=0, tiled=True),
-        lax.psum_scatter(grad_token, ("clip", "band"), scatter_dimension=0, tiled=True),
-        lax.psum_scatter(dec_grads[0], ("clip", "band"), scatter_dimension=0, tiled=True),
-        lax.psum_scatter(dec_grads[1], ("clip", "band"), scatter_dimension=0, tiled=True),
-        lax.psum_scatter(dec_grads[2], ("clip", "band"), scatter_dimension=0, tiled=True),
-        lax.psum_scatter(dec_grads[3], ("clip", "band"), scatter_dimension=0, tiled=True),
-        lax.psum_scatter(dec_grads[4], ("clip", "band"), scatter_dimension=0, tiled=True),
-        lax.psum_scatter(dec_grads[5], ("clip", "band"), scatter_dimension=0, tiled=True),
-        lax.psum_scatter(dec_grads[6], ("clip", "band"), scatter_dimension=0, tiled=True),
-        lax.psum_scatter(dec_grads[7], ("clip", "band"), scatter_dimension=0, tiled=True),
-    )
-    dec_total = (
-        lax.all_gather(
-            dec_share[0].astype(jnp.bfloat16), ("clip", "band"), axis=0, tiled=True
-        ).astype(jnp.float32),
-        lax.all_gather(
-            dec_share[1].astype(jnp.bfloat16), ("clip", "band"), axis=0, tiled=True
-        ).astype(jnp.float32),
-        lax.all_gather(
-            dec_share[2].astype(jnp.bfloat16), ("clip", "band"), axis=0, tiled=True
-        ).astype(jnp.float32),
-        lax.all_gather(
-            dec_share[3].astype(jnp.bfloat16), ("clip", "band"), axis=0, tiled=True
-        ).astype(jnp.float32),
-        lax.all_gather(
-            dec_share[4].astype(jnp.bfloat16), ("clip", "band"), axis=0, tiled=True
-        ).astype(jnp.float32),
-        lax.all_gather(
-            dec_share[5].astype(jnp.bfloat16), ("clip", "band"), axis=0, tiled=True
-        ).astype(jnp.float32),
-        lax.all_gather(
-            dec_share[6].astype(jnp.bfloat16), ("clip", "band"), axis=0, tiled=True
-        ).astype(jnp.float32),
-        lax.all_gather(
-            dec_share[7].astype(jnp.bfloat16), ("clip", "band"), axis=0, tiled=True
-        ).astype(jnp.float32),
-        lax.all_gather(
-            dec_share[8].astype(jnp.bfloat16), ("clip", "band"), axis=0, tiled=True
-        ).astype(jnp.float32),
-        lax.all_gather(
-            dec_share[9].astype(jnp.bfloat16), ("clip", "band"), axis=0, tiled=True
-        ).astype(jnp.float32),
-    )
+    dec_small = columns_of([dec_grads[0], dec_grads[1], dec_grads[4], dec_grads[5], grad_token])
+    dec_pack = jnp.concatenate([dec_grads[2], dec_grads[3], dec_small], axis=1)
+    dec_pack = scatter_sum(dec_pack, total, order_two)
+    dec_up_sum = scatter_sum(dec_grads[6], total, order)
+    dec_down_sum = scatter_sum(dec_grads[7], total, order_two)
+    dec_pack = gather_rows(dec_pack, total, order_two).astype(jnp.float32)
+    dec_up_sum = gather_rows(dec_up_sum, total, order).astype(jnp.float32)
+    dec_down_sum = gather_rows(dec_down_sum, total, order_two).astype(jnp.float32)
+    dec_vec_sums = dec_pack[:, 4 * dec_wide : 4 * dec_wide + 5].T
     grad_visible, enc_grads = block_backward(
         grad_encoded.reshape(clip_count, slot_total, enc_width),
         enc_stored,
@@ -361,63 +406,36 @@
         HEADS_ENC,
         enc_allowed,
     )
-    enc_share = (
-        lax.psum_scatter(enc_grads[0], ("clip", "band"), scatter_dimension=0, tiled=True),
-        lax.psum_scatter(enc_grads[1], ("clip", "band"), scatter_dimension=0, tiled=True),
-        lax.psum_scatter(enc_grads[2], ("clip", "band"), scatter_dimension=0, tiled=True),
-        lax.psum_scatter(enc_grads[3], ("clip", "band"), scatter_dimension=0, tiled=True),
-        lax.psum_scatter(enc_grads[4], ("clip", "band"), scatter_dimension=0, tiled=True),
-        lax.psum_scatter(enc_grads[5], ("clip", "band"), scatter_dimension=0, tiled=True),
-        lax.psum_scatter(enc_grads[6], ("clip", "band"), scatter_dimension=0, tiled=True),
-        lax.psum_scatter(enc_grads[7], ("clip", "band"), scatter_dimension=0, tiled=True),
-    )
-    enc_total = (
-        lax.all_gather(
-            enc_share[0].astype(jnp.bfloat16), ("clip", "band"), axis=0, tiled=True
-        ).astype(jnp.float32),
-        lax.all_gather(
-            enc_share[1].astype(jnp.bfloat16), ("clip", "band"), axis=0, tiled=True
-        ).astype(jnp.float32),
-        lax.all_gather(
-            enc_share[2].astype(jnp.bfloat16), ("clip", "band"), axis=0, tiled=True
-        ).astype(jnp.float32),
-        lax.all_gather(
-            enc_share[3].astype(jnp.bfloat16), ("clip", "band"), axis=0, tiled=True
-        ).astype(jnp.float32),
-        lax.all_gather(
-            enc_share[4].astype(jnp.bfloat16), ("clip", "band"), axis=0, tiled=True
-        ).astype(jnp.float32),
-        lax.all_gather(
-            enc_share[5].astype(jnp.bfloat16), ("clip", "band"), axis=0, tiled=True
-        ).astype(jnp.float32),
-        lax.all_gather(
-            enc_share[6].astype(jnp.bfloat16), ("clip", "band"), axis=0, tiled=True
-        ).astype(jnp.float32),
-        lax.all_gather(
-            enc_share[7].astype(jnp.bfloat16), ("clip", "band"), axis=0, tiled=True
-        ).astype(jnp.float32),
-    )
+    enc_up_sum = scatter_sum(enc_grads[6], total, order_two)
+    enc_down_sum = scatter_sum(enc_grads[7], total, order)
+    enc_small = columns_of([enc_grads[0], enc_grads[1], enc_grads[4], enc_grads[5]])
+    enc_pack = jnp.concatenate([enc_grads[2], enc_grads[3], grad_proj, enc_small], axis=1)
+    enc_pack = scatter_sum(enc_pack, total, order)
+    enc_up_sum = gather_rows(enc_up_sum, total, order_two).astype(jnp.float32)
+    enc_down_sum = gather_rows(enc_down_sum, total, order).astype(jnp.float32)
+    enc_pack = gather_rows(enc_pack, total, order).astype(jnp.float32)
+    enc_vec_sums = enc_pack[:, 4 * enc_wide + dec_wide : 4 * enc_wide + dec_wide + 4].T
     return (
         decoded_out,
         grad_visible.astype(jnp.bfloat16),
-        enc_total[0],
-        enc_total[1],
-        enc_total[2],
-        enc_total[3],
-        enc_total[4],
-        enc_total[5],
-        enc_total[6],
-        enc_total[7],
-        dec_total[0],
-        dec_total[1],
-        dec_total[2],
-        dec_total[3],
-        dec_total[4],
-        dec_total[5],
-        dec_total[6],
-        dec_total[7],
-        dec_total[8],
-        dec_total[9],
+        enc_vec_sums[0],
+        enc_vec_sums[1],
+        enc_pack[:, : 3 * enc_wide],
+        enc_pack[:, 3 * enc_wide : 4 * enc_wide],
+        enc_vec_sums[2],
+        enc_vec_sums[3],
+        enc_up_sum,
+        enc_down_sum,
+        enc_pack[:, 4 * enc_wide : 4 * enc_wide + dec_wide],
+        dec_vec_sums[4],
+        dec_vec_sums[0],
+        dec_vec_sums[1],
+        dec_pack[:, : 3 * dec_wide],
+        dec_pack[:, 3 * dec_wide : 4 * dec_wide],
+        dec_vec_sums[2],
+        dec_vec_sums[3],
+        dec_up_sum,
+        dec_down_sum,
     )
 
 

time: 2370 us -> 1410 us (0.59)
  waiting for transfers between devices: 1320 us -> 404 us
  blocking collectives: 307 us -> 0 us
  local copies, waits for them, and re-layouts: 288 us -> 411 us
  other arithmetic: 98.4 us -> 216 us
  starting transfers between devices: 9.44 us -> 93.9 us
  matrix products: 321 us -> 273 us
    reduce_scatter x9 -> x0, waiting for transfers between devices: 870 us -> none  [the longest x1 141 us: shards(): lax.psum_scatter(dec_grads[6], ('clip', 'band'), scatter_dimension=0, til...]
    all_gather x14 -> x0, waiting for transfers between devices: 437 us -> none  [the longest x1 60.8 us: shards(): lax.all_gather(enc_share[6].astype(jnp.bfloat16), ('clip', 'band'), axis=...]
    ppermute x0 -> x90, waiting for transfers between devices: none -> 394 us  [the longest x60 251 us: gather_rows(): got = lax.ppermute(held, AXES, partner_pairs(total, bit))]
    all_gather x4 -> x0, blocking collectives: 167 us -> none  [the longest x1 45.9 us: shards(): lax.all_gather(proj, ('clip', 'band'), axis=0, tiled=True)]
    unnamed x3 -> x0, blocking collectives: 122 us -> none
    ppermute x0 -> x90, starting transfers between devices: none -> 82.6 us  [the longest x60 58.2 us: gather_rows(): got = lax.ppermute(held, AXES, partner_pairs(total, bit))]
    another operation x0 -> x118, other arithmetic: none -> 79.7 us  [the longest x2 46.5 us: exact_gelu(): return jax.nn.gelu(inputs, approximate=False)]
    another operation x0 -> x13, local copies, waits for them, and re-layouts: none -> 66.7 us  [the longest x4 63.9 us: exact_gelu(): return jax.nn.gelu(inputs, approximate=False)]
  transfers between devices with their start and end apart: 25 -> 93, of which waited for: 20 -> 50; matrix products, arithmetic and copies ran while one was open for 17% -> 20% of each run, Pallas kernels for 0% -> 0%
where the time goes in v1:
time: 1410 us; the launch traced here: 1400 us
  local copies, waits for them, and re-layouts  411 us (29%)
  waiting for transfers between devices  404 us (29%)
  matrix products  273 us (19%)
  other arithmetic  216 us (15%)
  starting transfers between devices  93.9 us (7%)
    ppermute x60, waiting for transfers between devices, gather_rows(): got = lax.ppermute(held, AXES, partner_pairs(total, bit))  251 us
    ppermute x30, waiting for transfers between devices, scatter_sum(): got = lax.ppermute(give, AXES, partner_pairs(total, bit))  143 us
    convert_element_type x3, local copies, waits for them, and re-layouts, block_backward(): grad_qkv_rows = jnp.stack([grad_queries, grad_keys, grad_values], axis=2)...  68.7 us
    dot_general x9, matrix products, forward_dot(): jnp.einsum('nd,de->ne', operand, weight, preferred_element_type=jnp.float32)  64.4 us
    another operation x4, local copies, waits for them, and re-layouts, exact_gelu(): return jax.nn.gelu(inputs, approximate=False)  63.9 us
    dot_general x9, matrix products, backward_dot(): jnp.einsum('ne,de->nd', gradient, weight, preferred_element_type=jnp.floa...  59.5 us
    ppermute x60, starting transfers between devices, gather_rows(): got = lax.ppermute(held, AXES, partner_pairs(total, bit))  58.2 us
    another operation x2, other arithmetic, exact_gelu(): return jax.nn.gelu(inputs, approximate=False)  46.5 us
  transfers between devices with their start and end apart: 93, of which 50 were waited for; matrix products, arithmetic and copies ran while one was open for 20% of the time, Pallas kernels for 0%

profile of v1, /device:TPU:0, one launch (start us, length us, event | category | flops | bytes accessed | tf_op | source)
XLA Modules:
  0.0 1401.2 jit_solution(13140818589271408174)
XLA Ops:
  46.2 17.2 %collective-permute-done.26 = bf16[2,64,512]{2,1,0:T(8,128)(2,1)S(1)} collective-permute-done((bf16[2,64,512]{2,1,0:T(8,128)(2,1)S(1)}, bf16[2,64,512]{2,1,0:T(8,128)(2,1)S(1)}, u32[]{:S(2)}, u32[]{:S(2)}) %collective-permute-start.26) | collective-permute-done | bytes 131104 | tf_op jit(solution)/shard_map/ppermute | solution.py:230
  63.4 10.4 collective-permute-done.21
  97.7 20.9 %collective-permute-done.28 = bf16[2,2,2,64,512]{4,3,1,0,2:T(8,128)(2,1)S(1)} collective-permute-done((bf16[2,2,2,64,512]{4,3,1,0,2:T(8,128)(2,1)S(1)}, bf16[2,2,2,64,512]{4,3,1,0,2:T(8,128)(2,1)S(1)}, u32[]{:S(2)}, u32[]{:S(2)}) %collective-permute-start.28) | collective-permute-done | bytes 524320 | tf_op jit(solution)/shard_map/ppermute | solution.py:230
  131.3 14.5 %collective-permute-done.2 = bf16[2,2,24,3712]{3,2,1,0:T(8,128)(2,1)S(1)} collective-permute-done((bf16[2,2,24,3712]{3,2,1,0:T(8,128)(2,1)S(1)}, bf16[2,2,24,3712]{3,2,1,0:T(8,128)(2,1)S(1)}, u32[]{:S(2)}, u32[]{:S(2)}) %collective-permute-start.2) | collective-permute-done | bytes 712736 | tf_op jit(solution)/shard_map/ppermute | solution.py:230
  150.3 17.3 %collective-permute-done.8 = bf16[2,2,2,24,3072]{4,3,2,1,0:T(8,128)(2,1)S(1)} collective-permute-done((bf16[2,2,2,24,3072]{4,3,2,1,0:T(8,128)(2,1)S(1)}, bf16[2,2,2,24,3072]{4,3,2,1,0:T(8,128)(2,1)S(1)}, u32[]{:S(2)}, u32[]{:S(2)}) %collective-permute-start.8) | collective-permute-done | bytes 1179680 | tf_op jit(solution)/shard_map/ppermute | solution.py:230
  169.1 13.1 collective-permute-done.3
  211.4 18.4 %multiply_convert_fusion.2 = (bf16[512,3072]{1,0:T(8,128)(2,1)S(1)}, f32[512,3072]{1,0:T(8,128)}, f32[512,3072]{1,0:T(8,128)}) fusion(bf16[768,3072]{1,0:T(8,128)(2,1)S(1)} %bitcast.787, f32[512,768]{1,0:T(8,128)S(1)} %get-tuple-element.210, f32[768]{0:T(1024)S(1)} %get-tuple-element.42, f32[768]{0:T(1024)S(1)} %get-tuple-element.41, f32[512]{0:T(512)S(1)} %fusion.186, ...), kind=kOutput, calls=%fused_computation.68 | convolution fusion | flops 2520121344 | bytes 22030336 | tf_op jit(solution)/shard_map/nd,de->ne/dot_general | solution.py:38
  244.7 10.2 all-to-all-done.1
  265.9 27.7 %reshape.707 = bf16[128,16,3,16,32]{4,3,2,1,0:T(8,128)(2,1)} reshape(bf16[2048,1536]{1,0:T(8,128)(2,1)} %convolution_convert_fusion) | data formatting | bytes 12582912 | tf_op jit(solution)/shard_map/reshape | solution.py:64
  293.7 17.5 %fusion.217 = (bf16[128,16,1,16,32]{4,3,2,1,0:T(8,128)(2,1)}, bf16[128,16,1,16,32]{4,3,2,1,0:T(8,128)(2,1)}, bf16[128,16,1,16,32]{4,3,2,1,0:T(8,128)(2,1)}) fusion(bf16[128,16,3,16,32]{4,3,2,1,0:T(8,128)(2,1)} %reshape.707), kind=kLoop, calls=%fused_computation.648 | loop fusion | bytes 12582912 | tf_op jit(solution)/shard_map/slice | solution.py:66
  311.2 14.6 %fusion.24 = f32[128,16,16,16]{2,3,1,0:T(8,128)} fusion(bf16[128,16,1,16,32]{4,3,2,1,0:T(8,128)(2,1)} %get-tuple-element.66, bf16[128,16,1,16,32]{4,3,2,1,0:T(8,128)(2,1)} %get-tuple-element.65), kind=kOutput, calls=%fused_computation.59 | convolution fusion | flops 33554432 | bytes 6291456 | tf_op jit(solution)/shard_map/bqhd,bkhd->bhqk/dot_general | solution.py:67
  325.8 12.7 copy.396
  341.9 11.8 copy.397
  353.7 13.6 convert_bitcast_fusion
  367.3 10.9 copy.398
  378.2 12.4 reshape.708
  403.2 36.1 %fusion.21 = (f32[2048,2048]{1,0:T(8,128)}, f32[2048,2048]{0,1:T(8,128)}) fusion(f32[2048,2048]{0,1:T(8,128)S(1)} %fusion.212), kind=kLoop, calls=%fused_computation.43 | loop fusion | flops 260046848 | bytes 50331648 | tf_op jit(solution)/shard_map/mul | solution.py:50
  439.3 19.6 %add_convert_fusion.2 = bf16[2048,512]{1,0:T(8,128)(2,1)} fusion(f32[2048,512]{1,0:T(8,128)} %copy-done.3, bf16[2048,512]{1,0:T(8,128)(2,1)} %bitcast.768, f32[2048,2048]{0,1:T(8,128)} %get-tuple-element.69, f32[2048,2048]{0,1:T(8,128)} %copy-done), kind=kOutput, calls=%fused_computation.111 | convolution fusion | flops 4309647360 | bytes 41943040 | tf_op jit(solution)/shard_map/nd,de->ne/dot_general | solution.py:38
  458.9 18.1 %fusion.9 = bf16[2048,2048]{0,1:T(8,128)(2,1)} fusion(f32[2048,2048]{0,1:T(8,128)} %get-tuple-element.69, f32[2048,2048]{0,1:T(8,128)} %copy-done, bf16[2048,512]{1,0:T(8,128)(2,1)} %bitcast.769, bf16[2048,512]{1,0:T(8,128)(2,1)S(1)} %copy-done.13), kind=kOutput, calls=%fused_computation.14 | convolution fusion | flops 4353687552 | bytes 46137344 | tf_op jit(solution)/shard_map/ne,de->nd/dot_general | solution.py:42
  477.1 12.7 multiply_reduce_fusion.1
  504.3 14.0 fusion.25
  518.3 13.7 copy.406
  535.2 11.9 copy.408
  547.1 13.6 convolution_bitcast_fusion.1
  573.0 10.7 fusion.211
  583.7 17.7 %copy.457 = f32[2048,2048]{0,1:T(8,128)} copy(f32[2048,2048]{1,0:T(8,128)} %get-tuple-element.68) | data formatting | bytes 33554432 | tf_op jit(solution)/shard_map/mul | solution.py:50
  601.4 10.7 abs_compare_fusion
  612.1 35.7 %broadcast_subtract_fusion = (f32[2048,2048]{0,1:T(8,128)}, f32[2048,2048]{0,1:T(8,128)}, f32[2048,2048]{0,1:T(8,128)}) fusion(f32[2048,2048]{0,1:T(8,128)} %copy.457), kind=kLoop, calls=%fused_computation.55 | loop fusion | flops 234881024 | bytes 67108864 | tf_op jit(solution)/shard_map/erfc | solution.py:50
  649.9 11.9 copy.410
  661.8 13.7 convolution_bitcast_fusion
  685.3 10.9 copy.412
  696.3 11.3 copy.411
  713.1 33.8 %copy.414 = bf16[128,16,3,16,32]{4,3,2,1,0:T(8,128)(2,1)} copy(bf16[128,16,3,16,32]{0,4,3,2,1:T(8,128)(2,1)} %maximum_convert_fusion) | data formatting | bytes 12582912 | tf_op jit(solution)/shard_map/convert_element_type | solution.py:161
  747.0 32.7 %convert_element_type.677 = bf16[2048,1536]{1,0:T(8,128)(2,1)} reshape(bf16[128,16,3,16,32]{4,3,2,1,0:T(8,128)(2,1)} %copy.414) | data formatting | bytes 12582912 | tf_op jit(solution)/shard_map/convert_element_type | solution.py:161
  820.4 10.9 copy.464
  831.3 17.7 %copy.465 = f32[2048,2048]{1,0:T(8,128)} copy(f32[2048,2048]{0,1:T(8,128)} %get-tuple-element.67) | data formatting | bytes 33554432 | tf_op jit(solution)/shard_map/erfc | solution.py:50
  849.0 17.7 %copy.462 = f32[2048,2048]{1,0:T(8,128)} copy(f32[2048,2048]{0,1:T(8,128)} %get-tuple-element.50) | data formatting | bytes 33554432 | tf_op jit(solution)/shard_map/erfc | solution.py:50
  866.6 17.7 %copy.463 = f32[2048,2048]{1,0:T(8,128)} copy(f32[2048,2048]{0,1:T(8,128)} %get-tuple-element.51) | data formatting | bytes 33554432 | tf_op jit(solution)/shard_map/erfc | solution.py:50
  884.3 23.9 %fusion.3 = bf16[2048,2048]{1,0:T(8,128)(2,1)S(1)} fusion(pred[2048,2048]{1,0:T(8,128)(4,1)} %copy.464, f32[2048,2048]{1,0:T(8,128)} %copy.465, f32[2048,2048]{1,0:T(8,128)} %copy.462, f32[2048,2048]{1,0:T(8,128)} %copy.463, f32[2048,2048]{0,1:T(8,128)} %copy-done), kind=kLoop, calls=%fused_computation.6 | loop fusion | flops 33554432 | bytes 79691776 | tf_op jit(solution)/shard_map/convert_element_type | solution.py:89
  1016.9 10.8 collective-permute-done.61
  1155.6 37.0 %collective-permute-done.42 = bf16[2,2,24,3072]{3,2,1,0:T(8,128)(2,1)S(1)} collective-permute-done((bf16[2,2,24,3072]{3,2,1,0:T(8,128)(2,1)S(1)}, bf16[2,2,24,3072]{3,2,1,0:T(8,128)(2,1)S(1)}, u32[]{:S(2)}, u32[]{:S(2)}) %collective-permute-start.42) | collective-permute-done | bytes 589856 | tf_op jit(solution)/shard_map/ppermute | solution.py:218
  1198.3 16.5 %collective-permute-done.43 = bf16[2,24,3072]{2,1,0:T(8,128)(2,1)S(1)} collective-permute-done((bf16[2,24,3072]{2,1,0:T(8,128)(2,1)S(1)}, bf16[2,24,3072]{2,1,0:T(8,128)(2,1)S(1)}, u32[]{:S(2)}, u32[]{:S(2)}) %collective-permute-start.43) | collective-permute-done | bytes 294944 | tf_op jit(solution)/shard_map/ppermute | solution.py:218
  1235.8 22.5 %collective-permute-done.46 = bf16[2,24,3072]{2,1,0:T(8,128)(2,1)S(1)} collective-permute-done((bf16[2,24,3072]{2,1,0:T(8,128)(2,1)S(1)}, bf16[2,24,3072]{2,1,0:T(8,128)(2,1)S(1)}, u32[]{:S(2)}, u32[]{:S(2)}) %collective-permute-start.46) | collective-permute-done | bytes 294944 | tf_op jit(solution)/shard_map/ppermute | solution.py:230
  1258.3 13.8 collective-permute-done.33
  1287.8 13.8 collective-permute-done.36
  1306.1 14.7 %collective-permute-done.37 = bf16[2,2,24,3712]{3,2,1,0:T(8,128)(2,1)S(1)} collective-permute-done((bf16[2,2,24,3712]{3,2,1,0:T(8,128)(2,1)S(1)}, bf16[2,2,24,3712]{3,2,1,0:T(8,128)(2,1)S(1)}, u32[]{:S(2)}, u32[]{:S(2)}) %collective-permute-start.37) | collective-permute-done | bytes 712736 | tf_op jit(solution)/shard_map/ppermute | solution.py:230
  1322.9 21.7 %collective-permute-done.48 = bf16[2,2,2,24,3072]{4,3,2,1,0:T(8,128)(2,1)S(1)} collective-permute-done((bf16[2,2,2,24,3072]{4,3,2,1,0:T(8,128)(2,1)S(1)}, bf16[2,2,2,24,3072]{4,3,2,1,0:T(8,128)(2,1)S(1)}, u32[]{:S(2)}, u32[]{:S(2)}) %collective-permute-start.48) | collective-permute-done | bytes 1179680 | tf_op jit(solution)/shard_map/ppermute | solution.py:230
  1347.4 14.4 %collective-permute-done.38 = bf16[2,2,2,24,3712]{4,3,2,1,0:T(8,128)(2,1)S(1)} collective-permute-done((bf16[2,2,2,24,3712]{4,3,2,1,0:T(8,128)(2,1)S(1)}, bf16[2,2,2,24,3712]{4,3,2,1,0:T(8,128)(2,1)S(1)}, u32[]{:S(2)}, u32[]{:S(2)}) %collective-permute-start.38) | collective-permute-done | bytes 1425440 | tf_op jit(solution)/shard_map/ppermute | solution.py:230
  (763 shorter events, 572.0 us)
Async XLA Ops:
  2.5 37.2 %collective-permute-start.15 = (bf16[16,2176]{1,0:T(8,128)(2,1)S(1)}, bf16[16,2176]{1,0:T(8,128)(2,1)S(1)}, u32[]{:S(2)}, u32[]{:S(2)}) collective-permute-start(bf16[16,2176]{1,0:T(8,128)(2,1)S(1)} %fusion.167), channel_id=1, source_target_pairs={{0,8},{1,9},{2,10},{3,11},{4,12},{5,13},{6,14},{7,15},{8,0},{9,1},... | collective-permute-start | bytes 208904 | tf_op jit(solution)/shard_map/ppermute | solution.py:230
  7.8 21.3 %all-to-all-start = ((bf16[4,2,128]{2,1,0:T(2,128)(2,1)}), bf16[4,2,128]{2,1,0:T(2,128)(2,1)S(1)}, u32[]{:S(2)}, u32[]{:S(2)}) async-start(bf16[4,2,128]{2,1,0:T(2,128)(2,1)} %get-tuple-element.60), calls=%async_computation | async-start | bytes 4096 | tf_op jit(solution)/shard_map/all_to_all | solution.py:348
  12.8 30.3 %collective-permute-start = (bf16[24,3712]{1,0:T(8,128)(2,1)S(1)}, bf16[24,3712]{1,0:T(8,128)(2,1)S(1)}, u32[]{:S(2)}, u32[]{:S(2)}) collective-permute-start(bf16[24,3712]{1,0:T(8,128)(2,1)S(1)} %fusion.162), channel_id=1, source_target_pairs={{0,8},{1,9},{2,10},{3,11},{4,12},{5,13},{6,14},{7,15},{8,0},{9,1},... | collective-permute-start | bytes 534536 | tf_op jit(solution)/shard_map/ppermute | solution.py:230
  12.9 27.0 %collective-permute-start.5 = (bf16[24,3072]{1,0:T(8,128)(2,1)}, bf16[24,3072]{1,0:T(8,128)(2,1)S(1)}, u32[]{:S(2)}, u32[]{:S(2)}) collective-permute-start(bf16[24,3072]{1,0:T(8,128)(2,1)} %param.31), channel_id=1, source_target_pairs={{0,8},{1,9},{2,10},{3,11},{4,12},{5,13},{6,14},{7,15},{8,0},{9,1},... | collective-permute-start | bytes 442376 | tf_op jit(solution)/shard_map/ppermute | solution.py:230
  14.9 28.1 %collective-permute-start.10 = (bf16[96,768]{1,0:T(8,128)(2,1)}, bf16[96,768]{1,0:T(8,128)(2,1)S(1)}, u32[]{:S(2)}, u32[]{:S(2)}) collective-permute-start(bf16[96,768]{1,0:T(8,128)(2,1)} %param.32), channel_id=1, source_target_pairs={{0,8},{1,9},{2,10},{3,11},{4,12},{5,13},{6,14},{7,15},{8,0},{9,1},... | collective-permute-start | bytes 442376 | tf_op jit(solution)/shard_map/ppermute | solution.py:230
  36.6 26.8 %collective-permute-start.26 = (bf16[2,64,512]{2,1,0:T(8,128)(2,1)S(1)}, bf16[2,64,512]{2,1,0:T(8,128)(2,1)S(1)}, u32[]{:S(2)}, u32[]{:S(2)}) collective-permute-start(bf16[2,64,512]{2,1,0:T(8,128)(2,1)S(1)} %pad_maximum_fusion.52), channel_id=1, source_target_pairs={{0,16},{1,17},{2,18},{3,19},{4,20},{5,21},{6,22},{7,23},{8,24},{9,... | collective-permute-start | bytes 393224 | tf_op jit(solution)/shard_map/ppermute | solution.py:230
  39.7 34.1 %collective-permute-start.21 = (bf16[2,16,2048]{2,1,0:T(8,128)(2,1)S(1)}, bf16[2,16,2048]{2,1,0:T(8,128)(2,1)S(1)}, u32[]{:S(2)}, u32[]{:S(2)}) collective-permute-start(bf16[2,16,2048]{2,1,0:T(8,128)(2,1)S(1)} %pad_maximum_fusion.51), channel_id=1, source_target_pairs={{0,16},{1,17},{2,18},{3,19},{4,20},{5,21},{6,22},{7,23},{8,24},{9,... | collective-permute-start | bytes 393224 | tf_op jit(solution)/shard_map/ppermute | solution.py:230
  39.9 36.9 %collective-permute-start.16 = (bf16[2,16,2176]{2,1,0:T(8,128)(2,1)S(1)}, bf16[2,16,2176]{2,1,0:T(8,128)(2,1)S(1)}, u32[]{:S(2)}, u32[]{:S(2)}) collective-permute-start(bf16[2,16,2176]{2,1,0:T(8,128)(2,1)S(1)} %pad_maximum_fusion.49), channel_id=1, source_target_pairs={{0,16},{1,17},{2,18},{3,19},{4,20},{5,21},{6,22},{7,23},{8,24},{9,... | collective-permute-start | bytes 417800 | tf_op jit(solution)/shard_map/ppermute | solution.py:230
  42.9 40.2 %collective-permute-start.6 = (bf16[2,24,3072]{2,1,0:T(8,128)(2,1)S(1)}, bf16[2,24,3072]{2,1,0:T(8,128)(2,1)S(1)}, u32[]{:S(2)}, u32[]{:S(2)}) collective-permute-start(bf16[2,24,3072]{2,1,0:T(8,128)(2,1)S(1)} %pad_maximum_fusion.39), channel_id=1, source_target_pairs={{0,16},{1,17},{2,18},{3,19},{4,20},{5,21},{6,22},{7,23},{8,24},{9,... | collective-permute-start | bytes 884744 | tf_op jit(solution)/shard_map/ppermute | solution.py:230
  43.1 46.3 %collective-permute-start.11 = (bf16[2,96,768]{2,1,0:T(8,128)(2,1)S(1)}, bf16[2,96,768]{2,1,0:T(8,128)(2,1)S(1)}, u32[]{:S(2)}, u32[]{:S(2)}) collective-permute-start(bf16[2,96,768]{2,1,0:T(8,128)(2,1)S(1)} %pad_maximum_fusion.40), channel_id=1, source_target_pairs={{0,16},{1,17},{2,18},{3,19},{4,20},{5,21},{6,22},{7,23},{8,24},{9,... | collective-permute-start | bytes 884744 | tf_op jit(solution)/shard_map/ppermute | solution.py:230
  63.4 32.6 %collective-permute-start.1 = (bf16[2,24,3712]{2,1,0:T(8,128)(2,1)S(1)}, bf16[2,24,3712]{2,1,0:T(8,128)(2,1)S(1)}, u32[]{:S(2)}, u32[]{:S(2)}) collective-permute-start(bf16[2,24,3712]{2,1,0:T(8,128)(2,1)S(1)} %pad_maximum_fusion.37), channel_id=1, source_target_pairs={{0,16},{1,17},{2,18},{3,19},{4,20},{5,21},{6,22},{7,23},{8,24},{9,... | collective-permute-start | bytes 1069064 | tf_op jit(solution)/shard_map/ppermute | solution.py:230
  89.4 31.2 %collective-permute-start.7 = (bf16[2,2,24,3072]{3,2,1,0:T(8,128)(2,1)S(1)}, bf16[2,2,24,3072]{3,2,1,0:T(8,128)(2,1)S(1)}, u32[]{:S(2)}, u32[]{:S(2)}) collective-permute-start(bf16[2,2,24,3072]{3,2,1,0:T(8,128)(2,1)S(1)} %pad_maximum_fusion.26), channel_id=1, source_target_pairs={{0,4},{1,5},{2,6},{3,7},{4,0},{5,1},{6,2},{7,3},{8,12},{9,13},{10,... | collective-permute-start | bytes 1769480 | tf_op jit(solution)/shard_map/ppermute | solution.py:230
  91.1 30.4 %collective-permute-start.12 = (bf16[2,2,96,768]{3,2,1,0:T(8,128)(2,1)S(1)}, bf16[2,2,96,768]{3,2,1,0:T(8,128)(2,1)S(1)}, u32[]{:S(2)}, u32[]{:S(2)}) collective-permute-start(bf16[2,2,96,768]{3,2,1,0:T(8,128)(2,1)S(1)} %pad_maximum_fusion.27), channel_id=1, source_target_pairs={{0,2},{1,3},{2,0},{3,1},{4,6},{5,7},{6,4},{7,5},{8,10},{9,11},{10,... | collective-permute-start | bytes 1769480 | tf_op jit(solution)/shard_map/ppermute | solution.py:230
  92.8 25.8 %collective-permute-start.28 = (bf16[2,2,2,64,512]{4,3,1,0,2:T(8,128)(2,1)S(1)}, bf16[2,2,2,64,512]{4,3,1,0,2:T(8,128)(2,1)S(1)}, u32[]{:S(2)}, u32[]{:S(2)}) collective-permute-start(bf16[2,2,2,64,512]{4,3,1,0,2:T(8,128)(2,1)S(1)} %pad_maximum_fusion.34), channel_id=1, source_target_pairs={{0,2},{1,3},{2,0},{3,1},{4,6},{5,7},{6,4},{7,5},{8,10},{9,11},{10,... | collective-permute-start | bytes 1572872 | tf_op jit(solution)/shard_map/ppermute | solution.py:230
  93.4 26.9 %collective-permute-start.23 = (bf16[2,2,2,16,2048]{4,3,2,1,0:T(8,128)(2,1)S(1)}, bf16[2,2,2,16,2048]{4,3,2,1,0:T(8,128)(2,1)S(1)}, u32[]{:S(2)}, u32[]{:S(2)}) collective-permute-start(bf16[2,2,2,16,2048]{4,3,2,1,0:T(8,128)(2,1)S(1)} %pad_maximum_fusion.33), channel_id=1, source_target_pairs={{0,4},{1,5},{2,6},{3,7},{4,0},{5,1},{6,2},{7,3},{8,12},{9,13},{10,... | collective-permute-start | bytes 1572872 | tf_op jit(solution)/shard_map/ppermute | solution.py:230
  95.9 34.6 %collective-permute-start.18 = (bf16[2,2,2,16,2176]{4,3,2,1,0:T(8,128)(2,1)S(1)}, bf16[2,2,2,16,2176]{4,3,2,1,0:T(8,128)(2,1)S(1)}, u32[]{:S(2)}, u32[]{:S(2)}) collective-permute-start(bf16[2,2,2,16,2176]{4,3,2,1,0:T(8,128)(2,1)S(1)} %pad_maximum_fusion.30), channel_id=1, source_target_pairs={{0,2},{1,3},{2,0},{3,1},{4,6},{5,7},{6,4},{7,5},{8,10},{9,11},{10,... | collective-permute-start | bytes 1671176 | tf_op jit(solution)/shard_map/ppermute | solution.py:230
  118.6 27.2 %collective-permute-start.2 = (bf16[2,2,24,3712]{3,2,1,0:T(8,128)(2,1)S(1)}, bf16[2,2,24,3712]{3,2,1,0:T(8,128)(2,1)S(1)}, u32[]{:S(2)}, u32[]{:S(2)}) collective-permute-start(bf16[2,2,24,3712]{3,2,1,0:T(8,128)(2,1)S(1)} %pad_maximum_fusion.24), channel_id=1, source_target_pairs={{0,2},{1,3},{2,0},{3,1},{4,6},{5,7},{6,4},{7,5},{8,10},{9,11},{10,... | collective-permute-start | bytes 2138120 | tf_op jit(solution)/shard_map/ppermute | solution.py:230
  120.4 28.0 %collective-permute-start.29 = (bf16[2,2,2,2,64,512]{5,4,1,0,2,3:T(8,128)(2,1)S(1)}, bf16[2,2,2,2,64,512]{5,4,1,0,2,3:T(8,128)(2,1)S(1)}, u32[]{:S(2)}, u32[]{:S(2)}) collective-permute-start(bf16[2,2,2,2,64,512]{5,4,1,0,2,3:T(8,128)(2,1)S(1)} %pad_maximum_fusion.21), channel_id=1, source_target_pairs={{0,1},{1,0},{2,3},{3,2},{4,5},{5,4},{6,7},{7,6},{8,9},{9,8},{10,11... | collective-permute-start | bytes 3145736 | tf_op jit(solution)/shard_map/ppermute | solution.py:230
  120.7 25.5 %collective-permute-start.24 = (bf16[2,2,2,2,16,2048]{5,4,3,2,1,0:T(8,128)(2,1)S(1)}, bf16[2,2,2,2,16,2048]{5,4,3,2,1,0:T(8,128)(2,1)S(1)}, u32[]{:S(2)}, u32[]{:S(2)}) collective-permute-start(bf16[2,2,2,2,16,2048]{5,4,3,2,1,0:T(8,128)(2,1)S(1)} %pad_maximum_fusion.20), channel_id=1, source_target_pairs={{0,1},{1,0},{2,3},{3,2},{4,5},{5,4},{6,7},{7,6},{8,9},{9,8},{10,11... | collective-permute-start | bytes 3145736 | tf_op jit(solution)/shard_map/ppermute | solution.py:230
  121.4 46.2 %collective-permute-start.8 = (bf16[2,2,2,24,3072]{4,3,2,1,0:T(8,128)(2,1)S(1)}, bf16[2,2,2,24,3072]{4,3,2,1,0:T(8,128)(2,1)S(1)}, u32[]{:S(2)}, u32[]{:S(2)}) collective-permute-start(bf16[2,2,2,24,3072]{4,3,2,1,0:T(8,128)(2,1)S(1)} %pad_maximum_fusion.14), channel_id=1, source_target_pairs={{0,2},{1,3},{2,0},{3,1},{4,6},{5,7},{6,4},{7,5},{8,10},{9,11},{10,... | collective-permute-start | bytes 3538952 | tf_op jit(solution)/shard_map/ppermute | solution.py:230
  130.6 37.6 %collective-permute-start.13 = (bf16[2,2,2,96,768]{4,3,2,1,0:T(8,128)(2,1)S(1)}, bf16[2,2,2,96,768]{4,3,2,1,0:T(8,128)(2,1)S(1)}, u32[]{:S(2)}, u32[]{:S(2)}) collective-permute-start(bf16[2,2,2,96,768]{4,3,2,1,0:T(8,128)(2,1)S(1)} %pad_maximum_fusion.15), channel_id=1, source_target_pairs={{0,4},{1,5},{2,6},{3,7},{4,0},{5,1},{6,2},{7,3},{8,12},{9,13},{10,... | collective-permute-start | bytes 3538952 | tf_op jit(solution)/shard_map/ppermute | solution.py:230
  145.8 37.0 %collective-permute-start.19 = (bf16[2,2,2,2,16,2176]{5,4,3,2,1,0:T(8,128)(2,1)S(1)}, bf16[2,2,2,2,16,2176]{5,4,3,2,1,0:T(8,128)(2,1)S(1)}, u32[]{:S(2)}, u32[]{:S(2)}) collective-permute-start(bf16[2,2,2,2,16,2176]{5,4,3,2,1,0:T(8,128)(2,1)S(1)} %pad_maximum_fusion.18), channel_id=1, source_target_pairs={{0,1},{1,0},{2,3},{3,2},{4,5},{5,4},{6,7},{7,6},{8,9},{9,8},{10,11... | collective-permute-start | bytes 3342344 | tf_op jit(solution)/shard_map/ppermute | solution.py:230
  146.2 36.0 %collective-permute-start.3 = (bf16[2,2,2,24,3712]{4,3,2,1,0:T(8,128)(2,1)S(1)}, bf16[2,2,2,24,3712]{4,3,2,1,0:T(8,128)(2,1)S(1)}, u32[]{:S(2)}, u32[]{:S(2)}) collective-permute-start(bf16[2,2,2,24,3712]{4,3,2,1,0:T(8,128)(2,1)S(1)} %pad_maximum_fusion.12), channel_id=1, source_target_pairs={{0,4},{1,5},{2,6},{3,7},{4,0},{5,1},{6,2},{7,3},{8,12},{9,13},{10,... | collective-permute-start | bytes 4276232 | tf_op jit(solution)/shard_map/ppermute | solution.py:230
  801.3 115.8 %all-to-all-start.2 = ((bf16[4,2,128,512]{3,2,1,0:T(8,128)(2,1)}), bf16[4,2,128,512]{3,2,1,0:T(8,128)(2,1)S(1)}, u32[]{:S(2)}, u32[]{:S(2)}) async-start(bf16[4,2,128,512]{3,2,1,0:T(8,128)(2,1)} %select_convert_fusion), calls=%async_computation.2 | async-start | bytes 2097152 | tf_op jit(solution)/shard_map/all_to_all | solution.py:386
  817.2 183.4 %collective-permute-start.60 = (bf16[2,2,2,2,16,2176]{5,4,1,0,2,3:T(8,128)(2,1)}, bf16[2,2,2,2,16,2176]{5,4,1,0,2,3:T(8,128)(2,1)}, u32[]{:S(2)}, u32[]{:S(2)}) collective-permute-start(bf16[2,2,2,2,16,2176]{5,4,1,0,2,3:T(8,128)(2,1)} %fusion.116), channel_id=1, source_target_pairs={{0,1},{1,0},{2,3},{3,2},{4,5},{5,4},{6,7},{7,6},{8,9},{9,8},{10,11... | collective-permute-start | bytes 3342344 | tf_op jit(solution)/shard_map/ppermute | solution.py:218
  820.4 175.8 %collective-permute-start.70 = (bf16[2,2,2,2,16,2048]{5,4,1,0,3,2:T(8,128)(2,1)}, bf16[2,2,2,2,16,2048]{5,4,1,0,3,2:T(8,128)(2,1)}, u32[]{:S(2)}, u32[]{:S(2)}) collective-permute-start(bf16[2,2,2,2,16,2048]{5,4,1,0,3,2:T(8,128)(2,1)} %fusion.119), channel_id=1, source_target_pairs={{0,1},{1,0},{2,3},{3,2},{4,5},{5,4},{6,7},{7,6},{8,9},{9,8},{10,11... | collective-permute-start | bytes 3145736 | tf_op jit(solution)/shard_map/ppermute | solution.py:218
  916.6 81.5 %collective-permute-start.80 = (bf16[2,2,2,2,64,512]{5,4,3,2,1,0:T(8,128)(2,1)}, bf16[2,2,2,2,64,512]{5,4,3,2,1,0:T(8,128)(2,1)}, u32[]{:S(2)}, u32[]{:S(2)}) collective-permute-start(bf16[2,2,2,2,64,512]{5,4,3,2,1,0:T(8,128)(2,1)} %fusion.118), channel_id=1, source_target_pairs={{0,1},{1,0},{2,3},{3,2},{4,5},{5,4},{6,7},{7,6},{8,9},{9,8},{10,11... | collective-permute-start | bytes 3145736 | tf_op jit(solution)/shard_map/ppermute | solution.py:218
  984.3 141.2 %collective-permute-start.30 = (bf16[2,2,2,2,24,3712]{5,4,1,0,3,2:T(8,128)(2,1)S(1)}, bf16[2,2,2,2,24,3712]{5,4,1,0,3,2:T(8,128)(2,1)}, u32[]{:S(2)}, u32[]{:S(2)}) collective-permute-start(bf16[2,2,2,2,24,3712]{5,4,1,0,3,2:T(8,128)(2,1)S(1)} %fusion.42), channel_id=1, source_target_pairs={{0,1},{1,0},{2,3},{3,2},{4,5},{5,4},{6,7},{7,6},{8,9},{9,8},{10,11... | collective-permute-start | bytes 8552456 | tf_op jit(solution)/shard_map/ppermute | solution.py:218
  988.6 124.5 %collective-permute-start.40 = (bf16[2,2,2,2,24,3072]{5,4,1,0,2,3:T(8,128)(2,1)}, bf16[2,2,2,2,24,3072]{5,4,1,0,2,3:T(8,128)(2,1)}, u32[]{:S(2)}, u32[]{:S(2)}) collective-permute-start(bf16[2,2,2,2,24,3072]{5,4,1,0,2,3:T(8,128)(2,1)} %fusion.55), channel_id=1, source_target_pairs={{0,1},{1,0},{2,3},{3,2},{4,5},{5,4},{6,7},{7,6},{8,9},{9,8},{10,11... | collective-permute-start | bytes 7077896 | tf_op jit(solution)/shard_map/ppermute | solution.py:218
  996.2 121.3 %collective-permute-start.50 = (bf16[2,2,2,2,96,768]{5,4,1,0,3,2:T(8,128)(2,1)}, bf16[2,2,2,2,96,768]{5,4,1,0,3,2:T(8,128)(2,1)S(1)}, u32[]{:S(2)}, u32[]{:S(2)}) collective-permute-start(bf16[2,2,2,2,96,768]{5,4,1,0,3,2:T(8,128)(2,1)} %fusion.56), channel_id=1, source_target_pairs={{0,1},{1,0},{2,3},{3,2},{4,5},{5,4},{6,7},{7,6},{8,9},{9,8},{10,11... | collective-permute-start | bytes 7077896 | tf_op jit(solution)/shard_map/ppermute | solution.py:218
  1118.9 28.0 %collective-permute-start.41 = (bf16[2,2,2,24,3072]{4,3,1,0,2:T(8,128)(2,1)S(1)}, bf16[2,2,2,24,3072]{4,3,1,0,2:T(8,128)(2,1)}, u32[]{:S(2)}, u32[]{:S(2)}) collective-permute-start(bf16[2,2,2,24,3072]{4,3,1,0,2:T(8,128)(2,1)S(1)} %dynamic-slice_bitcast_fusion.2), channel_id=1, source_target_pairs={{0,2},{1,3},{2,0},{3,1},{4,6},{5,7},{6,4},{7,5},{8,10},{9,11},{10,... | collective-permute-start | bytes 3538952 | tf_op jit(solution)/shard_map/ppermute | solution.py:218
  1122.4 29.6 %collective-permute-start.51 = (bf16[2,2,2,96,768]{4,3,1,0,2:T(8,128)(2,1)S(1)}, bf16[2,2,2,96,768]{4,3,1,0,2:T(8,128)(2,1)}, u32[]{:S(2)}, u32[]{:S(2)}) collective-permute-start(bf16[2,2,2,96,768]{4,3,1,0,2:T(8,128)(2,1)S(1)} %dynamic-slice_bitcast_fusion.1), channel_id=1, source_target_pairs={{0,4},{1,5},{2,6},{3,7},{4,0},{5,1},{6,2},{7,3},{8,12},{9,13},{10,... | collective-permute-start | bytes 3538952 | tf_op jit(solution)/shard_map/ppermute | solution.py:218
  1125.5 25.1 %collective-permute-start.69 = (bf16[2,2,2,2,16,2176]{5,4,3,2,1,0:T(8,128)(2,1)S(1)}, bf16[2,2,2,2,16,2176]{5,4,3,2,1,0:T(8,128)(2,1)}, u32[]{:S(2)}, u32[]{:S(2)}) collective-permute-start(bf16[2,2,2,2,16,2176]{5,4,3,2,1,0:T(8,128)(2,1)S(1)} %pad_maximum_fusion.19), channel_id=1, source_target_pairs={{0,1},{1,0},{2,3},{3,2},{4,5},{5,4},{6,7},{7,6},{8,9},{9,8},{10,11... | collective-permute-start | bytes 3342344 | tf_op jit(solution)/shard_map/ppermute | solution.py:230
  1128.4 67.7 %collective-permute-start.31 = (bf16[2,2,2,24,3712]{4,3,1,0,2:T(8,128)(2,1)S(1)}, bf16[2,2,2,24,3712]{4,3,1,0,2:T(8,128)(2,1)S(1)}, u32[]{:S(2)}, u32[]{:S(2)}) collective-permute-start(bf16[2,2,2,24,3712]{4,3,1,0,2:T(8,128)(2,1)S(1)} %dynamic-slice_bitcast_fusion), channel_id=1, source_target_pairs={{0,4},{1,5},{2,6},{3,7},{4,0},{5,1},{6,2},{7,3},{8,12},{9,13},{10,... | collective-permute-start | bytes 4276232 | tf_op jit(solution)/shard_map/ppermute | solution.py:218
  1148.7 43.9 %collective-permute-start.42 = (bf16[2,2,24,3072]{3,2,1,0:T(8,128)(2,1)S(1)}, bf16[2,2,24,3072]{3,2,1,0:T(8,128)(2,1)S(1)}, u32[]{:S(2)}, u32[]{:S(2)}) collective-permute-start(bf16[2,2,24,3072]{3,2,1,0:T(8,128)(2,1)S(1)} %dynamic-slice_bitcast_fusion.5), channel_id=1, source_target_pairs={{0,4},{1,5},{2,6},{3,7},{4,0},{5,1},{6,2},{7,3},{8,12},{9,13},{10,... | collective-permute-start | bytes 1769480 | tf_op jit(solution)/shard_map/ppermute | solution.py:218
  1153.7 39.2 %collective-permute-start.52 = (bf16[2,2,96,768]{3,2,1,0:T(8,128)(2,1)S(1)}, bf16[2,2,96,768]{3,2,1,0:T(8,128)(2,1)S(1)}, u32[]{:S(2)}, u32[]{:S(2)}) collective-permute-start(bf16[2,2,96,768]{3,2,1,0:T(8,128)(2,1)S(1)} %dynamic-slice_bitcast_fusion.4), channel_id=1, source_target_pairs={{0,2},{1,3},{2,0},{3,1},{4,6},{5,7},{6,4},{7,5},{8,10},{9,11},{10,... | collective-permute-start | bytes 1769480 | tf_op jit(solution)/shard_map/ppermute | solution.py:218
  1192.8 22.1 %collective-permute-start.43 = (bf16[2,24,3072]{2,1,0:T(8,128)(2,1)S(1)}, bf16[2,24,3072]{2,1,0:T(8,128)(2,1)S(1)}, u32[]{:S(2)}, u32[]{:S(2)}) collective-permute-start(bf16[2,24,3072]{2,1,0:T(8,128)(2,1)S(1)} %dynamic-slice_bitcast_fusion.11), channel_id=1, source_target_pairs={{0,16},{1,17},{2,18},{3,19},{4,20},{5,21},{6,22},{7,23},{8,24},{9,... | collective-permute-start | bytes 884744 | tf_op jit(solution)/shard_map/ppermute | solution.py:218
  1193.1 26.8 %collective-permute-start.53 = (bf16[2,96,768]{2,1,0:T(8,128)(2,1)S(1)}, bf16[2,96,768]{2,1,0:T(8,128)(2,1)S(1)}, u32[]{:S(2)}, u32[]{:S(2)}) collective-permute-start(bf16[2,96,768]{2,1,0:T(8,128)(2,1)S(1)} %dynamic-slice_bitcast_fusion.10), channel_id=1, source_target_pairs={{0,16},{1,17},{2,18},{3,19},{4,20},{5,21},{6,22},{7,23},{8,24},{9,... | collective-permute-start | bytes 884744 | tf_op jit(solution)/shard_map/ppermute | solution.py:218
  1196.5 36.6 %collective-permute-start.32 = (bf16[2,2,24,3712]{3,2,1,0:T(8,128)(2,1)S(1)}, bf16[2,2,24,3712]{3,2,1,0:T(8,128)(2,1)S(1)}, u32[]{:S(2)}, u32[]{:S(2)}) collective-permute-start(bf16[2,2,24,3712]{3,2,1,0:T(8,128)(2,1)S(1)} %dynamic-slice_bitcast_fusion.3), channel_id=1, source_target_pairs={{0,2},{1,3},{2,0},{3,1},{4,6},{5,7},{6,4},{7,5},{8,10},{9,11},{10,... | collective-permute-start | bytes 2138120 | tf_op jit(solution)/shard_map/ppermute | solution.py:218
  1230.0 28.3 %collective-permute-start.46 = (bf16[2,24,3072]{2,1,0:T(8,128)(2,1)S(1)}, bf16[2,24,3072]{2,1,0:T(8,128)(2,1)S(1)}, u32[]{:S(2)}, u32[]{:S(2)}) collective-permute-start(bf16[2,24,3072]{2,1,0:T(8,128)(2,1)S(1)} %pad_maximum_fusion.41), channel_id=1, source_target_pairs={{0,16},{1,17},{2,18},{3,19},{4,20},{5,21},{6,22},{7,23},{8,24},{9,... | collective-permute-start | bytes 884744 | tf_op jit(solution)/shard_map/ppermute | solution.py:230
  1232.5 46.6 %collective-permute-start.56 = (bf16[2,96,768]{2,1,0:T(8,128)(2,1)S(1)}, bf16[2,96,768]{2,1,0:T(8,128)(2,1)S(1)}, u32[]{:S(2)}, u32[]{:S(2)}) collective-permute-start(bf16[2,96,768]{2,1,0:T(8,128)(2,1)S(1)} %pad_maximum_fusion.42), channel_id=1, source_target_pairs={{0,16},{1,17},{2,18},{3,19},{4,20},{5,21},{6,22},{7,23},{8,24},{9,... | collective-permute-start | bytes 884744 | tf_op jit(solution)/shard_map/ppermute | solution.py:230
  1233.3 38.8 %collective-permute-start.33 = (bf16[2,24,3712]{2,1,0:T(8,128)(2,1)S(1)}, bf16[2,24,3712]{2,1,0:T(8,128)(2,1)S(1)}, u32[]{:S(2)}, u32[]{:S(2)}) collective-permute-start(bf16[2,24,3712]{2,1,0:T(8,128)(2,1)S(1)} %dynamic-slice_bitcast_fusion.9), channel_id=1, source_target_pairs={{0,16},{1,17},{2,18},{3,19},{4,20},{5,21},{6,22},{7,23},{8,24},{9,... | collective-permute-start | bytes 1069064 | tf_op jit(solution)/shard_map/ppermute | solution.py:218
  1279.3 24.8 %collective-permute-start.57 = (bf16[2,2,96,768]{3,2,1,0:T(8,128)(2,1)S(1)}, bf16[2,2,96,768]{3,2,1,0:T(8,128)(2,1)S(1)}, u32[]{:S(2)}, u32[]{:S(2)}) collective-permute-start(bf16[2,2,96,768]{3,2,1,0:T(8,128)(2,1)S(1)} %pad_maximum_fusion.29), channel_id=1, source_target_pairs={{0,2},{1,3},{2,0},{3,1},{4,6},{5,7},{6,4},{7,5},{8,10},{9,11},{10,... | collective-permute-start | bytes 1769480 | tf_op jit(solution)/shard_map/ppermute | solution.py:230
  1303.0 41.6 %collective-permute-start.48 = (bf16[2,2,2,24,3072]{4,3,2,1,0:T(8,128)(2,1)S(1)}, bf16[2,2,2,24,3072]{4,3,2,1,0:T(8,128)(2,1)S(1)}, u32[]{:S(2)}, u32[]{:S(2)}) collective-permute-start(bf16[2,2,2,24,3072]{4,3,2,1,0:T(8,128)(2,1)S(1)} %pad_maximum_fusion.16), channel_id=1, source_target_pairs={{0,2},{1,3},{2,0},{3,1},{4,6},{5,7},{6,4},{7,5},{8,10},{9,11},{10,... | collective-permute-start | bytes 3538952 | tf_op jit(solution)/shard_map/ppermute | solution.py:230
  1304.3 40.8 %collective-permute-start.58 = (bf16[2,2,2,96,768]{4,3,2,1,0:T(8,128)(2,1)S(1)}, bf16[2,2,2,96,768]{4,3,2,1,0:T(8,128)(2,1)S(1)}, u32[]{:S(2)}, u32[]{:S(2)}) collective-permute-start(bf16[2,2,2,96,768]{4,3,2,1,0:T(8,128)(2,1)S(1)} %pad_maximum_fusion.17), channel_id=1, source_target_pairs={{0,4},{1,5},{2,6},{3,7},{4,0},{5,1},{6,2},{7,3},{8,12},{9,13},{10,... | collective-permute-start | bytes 3538952 | tf_op jit(solution)/shard_map/ppermute | solution.py:230
  1321.1 40.7 %collective-permute-start.38 = (bf16[2,2,2,24,3712]{4,3,2,1,0:T(8,128)(2,1)S(1)}, bf16[2,2,2,24,3712]{4,3,2,1,0:T(8,128)(2,1)S(1)}, u32[]{:S(2)}, u32[]{:S(2)}) collective-permute-start(bf16[2,2,2,24,3712]{4,3,2,1,0:T(8,128)(2,1)S(1)} %pad_maximum_fusion.13), channel_id=1, source_target_pairs={{0,4},{1,5},{2,6},{3,7},{4,0},{5,1},{6,2},{7,3},{8,12},{9,13},{10,... | collective-permute-start | bytes 4276232 | tf_op jit(solution)/shard_map/ppermute | solution.py:230
  1345.0 22.8 %collective-permute-start.49 = (bf16[2,2,2,2,24,3072]{5,4,3,2,1,0:T(8,128)(2,1)S(1)}, bf16[2,2,2,2,24,3072]{5,4,3,2,1,0:T(8,128)(2,1)S(1)}, u32[]{:S(2)}, u32[]{:S(2)}) collective-permute-start(bf16[2,2,2,2,24,3072]{5,4,3,2,1,0:T(8,128)(2,1)S(1)} %pad_maximum_fusion.7), channel_id=1, source_target_pairs={{0,1},{1,0},{2,3},{3,2},{4,5},{5,4},{6,7},{7,6},{8,9},{9,8},{10,11... | collective-permute-start | bytes 7077896 | tf_op jit(solution)/shard_map/ppermute | solution.py:230
  1346.9 26.5 %collective-permute-start.59 = (bf16[2,2,2,2,96,768]{5,4,3,2,1,0:T(8,128)(2,1)}, bf16[2,2,2,2,96,768]{5,4,3,2,1,0:T(8,128)(2,1)}, u32[]{:S(2)}, u32[]{:S(2)}) collective-permute-start(bf16[2,2,2,2,96,768]{5,4,3,2,1,0:T(8,128)(2,1)} %pad_maximum_fusion.8), channel_id=1, source_target_pairs={{0,1},{1,0},{2,3},{3,2},{4,5},{5,4},{6,7},{7,6},{8,9},{9,8},{10,11... | collective-permute-start | bytes 7077896 | tf_op jit(solution)/shard_map/ppermute | solution.py:230
  (174 other events, 1890.0 us)

commit v2 on v1

v2 whole, which is shorter than its diff:
```python
import math

import jax
import jax.numpy as jnp
from jax import lax
from jax.experimental import pallas as pl
from jax.experimental.pallas import tpu as pltpu
from jax.sharding import PartitionSpec as P

HEADS_ENC = 12
D_DEC = 512
HEADS_DEC = 16
TIME = 64
FREQ = 8
WINDOW = 4
SHIFT = 2
norm_eps = 1e-06
neg_fill = -1e30
F32 = jnp.float32
BF16 = jnp.bfloat16
LANES = 128


def mm(a, b):
    return lax.dot_general(a, b, (((1,), (0,)), ((), ())), preferred_element_type=F32)


def mm_t(a, b):
    return lax.dot_general(a, b, (((1,), (1,)), ((), ())), preferred_element_type=F32)


def bmm(a, b):
    return lax.dot_general(a, b, (((2,), (1,)), ((0,), (0,))), preferred_element_type=F32)


def bmm_t(a, b):
    return lax.dot_general(a, b, (((2,), (2,)), ((0,), (0,))), preferred_element_type=F32)


def bmm_l(a, b):
    return lax.dot_general(a, b, (((1,), (1,)), ((0,), (0,))), preferred_element_type=F32)


def normalise(x):
    centre = jnp.mean(x, axis=-1, keepdims=True)
    centred = x - centre
    rstd = lax.rsqrt(jnp.mean(centred * centred, axis=-1, keepdims=True) + norm_eps)
    return centred * rstd, rstd


def norm_back(da, xhat, rstd, gain):
    dag = da * gain
    return rstd * (
        dag
        - jnp.mean(dag, axis=-1, keepdims=True)
        - xhat * jnp.mean(dag * xhat, axis=-1, keepdims=True)
    )


def gelu_parts(u):
    size = jnp.abs(u) * 0.7071067811865476
    bell = jnp.exp(-0.5 * u * u)
    t = 1.0 / (1.0 + 0.3275911 * size)
    poly = 0.530702715
    poly = poly * t - 0.726576013
    poly = poly * t + 0.710706871
    poly = poly * t - 0.142248368
    poly = poly * t + 0.127414796
    tail = poly * t * bell
    cdf = jnp.where(u >= 0, 1.0 - tail, tail)
    return cdf, u * bell * 0.3989422804014327


def segment_sum(x, ones):
    high = x.astype(BF16)
    low = (x - high.astype(F32)).astype(BF16)
    return mm(high, ones) + mm(low, ones)


def window_max(s):
    ahead = s
    behind = s
    for step in (1, 2, 4, 8):
        ahead = jnp.maximum(ahead, pltpu.roll(ahead, step, 1))
        behind = jnp.maximum(behind, pltpu.roll(behind, LANES - step, 1))
    return jnp.maximum(ahead, behind)


def decoder_kernel(
    rows_ref, idx_ref, cot_ref, pos_ref, mask_ref, vec_ref, wqkv_ref, wo_ref, wu_ref, wd_ref,
    out_ref, ret_ref, gqkv_ref, go_ref, gu_ref, gd_ref, gvec_ref,
    acc_qkv, acc_o, acc_u, acc_d, x_s, qkv_s, p_s, o_s, a2_s, a2t_s, dzt_s, da_s, y_s, dqkv_s,
):
    step = pl.program_id(0)
    last = pl.num_programs(0) - 1
    halves, cells, width = cot_ref.shape
    m_rows = halves * cells
    slots = rows_ref.shape[1]
    head_dim = width // HEADS_DEC
    heads_in = LANES // head_dim
    groups = width // LANES
    block = LANES // heads_in
    blocks = m_rows // block
    scale = head_dim ** (-0.5)
    ff = wu_ref.shape[1]
    chunk = 512

    @pl.when(step == 0)
    def _():
        acc_qkv[...] = jnp.zeros_like(acc_qkv)
        acc_o[...] = jnp.zeros_like(acc_o)
        acc_u[...] = jnp.zeros_like(acc_u)
        acc_d[...] = jnp.zeros_like(acc_d)
        gvec_ref[...] = jnp.zeros_like(gvec_ref)

    gain1, shift1 = vec_ref[0:1, :], vec_ref[1:2, :]
    gain2, shift2 = vec_ref[2:3, :], vec_ref[3:4, :]
    token = vec_ref[4:5, :]

    def place_of(h):
        cell = lax.broadcasted_iota(jnp.int32, (cells, slots), 0)
        return cell == idx_ref[h]

    unseen = []
    for h in range(halves):
        place = place_of(h)
        unseen_h = 1.0 - jnp.sum(place.astype(F32), axis=1, keepdims=True)
        unseen.append(unseen_h)
        x_s[h * cells : (h + 1) * cells, :] = (
            mm(place.astype(BF16), rows_ref[h]) + unseen_h * token + pos_ref[...]
        )
    xhat1, rstd1 = normalise(x_s[...])
    a1 = (xhat1 * gain1 + shift1).astype(BF16)
    qkv_s[...] = mm(a1, wqkv_ref[...]).astype(BF16)

    lane = lax.broadcasted_iota(jnp.int32, (1, LANES), 1)
    head_masks = [(lane // head_dim == h) for h in range(heads_in)]
    ones = (
        lax.broadcasted_iota(jnp.int32, (LANES, LANES), 0) // block
        == lax.broadcasted_iota(jnp.int32, (LANES, LANES), 1) // block
    ).astype(BF16)

    def spread(t):
        parts = [t * hm.astype(BF16)[None] for hm in head_masks]
        return jnp.concatenate(parts, axis=1)

    def fold(t):
        out = t[:, 0:block, :]
        for h in range(1, heads_in):
            out = jnp.where(head_masks[h][None], t[:, h * block : (h + 1) * block, :], out)
        return out

    def part(ref, base, g):
        return ref[:, base + g * LANES : base + (g + 1) * LANES].reshape(blocks, block, LANES)

    allowed = jnp.concatenate([mask_ref[...]] * halves, axis=0) > 0.5
    for g in range(groups):
        q3 = part(qkv_s, 0, g)
        k3 = spread(part(qkv_s, width, g))
        v3 = spread(part(qkv_s, 2 * width, g))
        s = bmm_t(q3, k3).reshape(m_rows, LANES) * scale
        s = jnp.where(allowed, s, neg_fill)
        e = jnp.where(allowed, jnp.exp(s - window_max(s)), 0.0)
        p = e / segment_sum(e, ones)
        p_s[:, g * LANES : (g + 1) * LANES] = p
        o = bmm(p.astype(BF16).reshape(blocks, block, LANES), v3)
        o_s[:, g * LANES : (g + 1) * LANES] = o.reshape(m_rows, LANES).astype(BF16)

    x2 = x_s[...] + mm(o_s[...], wo_ref[...])
    xhat2, rstd2 = normalise(x2)
    a2 = (xhat2 * gain2 + shift2).astype(BF16)
    a2_s[...] = a2
    a2t_s[...] = a2.T
    dz = cot_ref[...].reshape(m_rows, width)
    dzt_s[...] = dz.T
    y_s[...] = x2
    da_s[...] = jnp.zeros_like(da_s)

    def ff_body(c, carry):
        at = pl.ds(pl.multiple_of(c * chunk, chunk), chunk)
        wu = wu_ref[:, at]
        wd = wd_ref[at, :]
        dzc = cot_ref[...].reshape(m_rows, width)
        u = mm(a2_s[...], wu)
        dh = mm_t(dzc, wd)
        cdf, bump = gelu_parts(u)
        h = (u * cdf).astype(BF16)
        du = ((cdf + bump) * dh).astype(BF16)
        y_s[...] += mm(h, wd)
        acc_d[:, at] += mm(dzt_s[...], h)
        acc_u[:, at] += mm(a2t_s[...], du)
        da_s[...] += mm_t(du, wu)
        return carry

    lax.fori_loop(0, ff // chunk, ff_body, 0)

    out_ref[...] = y_s[...].reshape(halves, cells, width).astype(BF16)
    da2 = da_s[...]
    gvec_ref[2:3, :] += jnp.sum(da2 * xhat2, axis=0, keepdims=True)
    gvec_ref[3:4, :] += jnp.sum(da2, axis=0, keepdims=True)
    dx2 = cot_ref[...].reshape(m_rows, width).astype(F32) + norm_back(da2, xhat2, rstd2, gain2)
    dy2 = dx2.astype(BF16)
    acc_o[...] += mm(o_s[...].T, dy2)
    do = mm_t(dy2, wo_ref[...]).astype(BF16)

    for g in range(groups):
        cols = slice(g * LANES, (g + 1) * LANES)
        q3 = part(qkv_s, 0, g)
        k3 = spread(part(qkv_s, width, g))
        v3 = spread(part(qkv_s, 2 * width, g))
        do3 = do[:, cols].reshape(blocks, block, LANES)
        p = p_s[:, cols]
        dp = bmm_t(do3, v3).reshape(m_rows, LANES)
        draw = (p * (dp - segment_sum(p * dp, ones)) * scale).astype(BF16)
        draw3 = draw.reshape(blocks, block, LANES)
        dq = bmm(draw3, k3).reshape(m_rows, LANES)
        dk = fold(bmm_l(draw3, q3)).reshape(m_rows, LANES)
        dv = fold(bmm_l(p.astype(BF16).reshape(blocks, block, LANES), do3)).reshape(m_rows, LANES)
        dqkv_s[:, g * LANES : (g + 1) * LANES] = dq.astype(BF16)
        dqkv_s[:, width + g * LANES : width + (g + 1) * LANES] = dk.astype(BF16)
        dqkv_s[:, 2 * width + g * LANES : 2 * width + (g + 1) * LANES] = dv.astype(BF16)

    xhat1, rstd1 = normalise(x_s[...])
    a1 = (xhat1 * gain1 + shift1).astype(BF16)
    dqkv = dqkv_s[...]
    acc_qkv[...] += mm(a1.T, dqkv)
    da1 = mm_t(dqkv, wqkv_ref[...])
    gvec_ref[0:1, :] += jnp.sum(da1 * xhat1, axis=0, keepdims=True)
    gvec_ref[1:2, :] += jnp.sum(da1, axis=0, keepdims=True)
    dx = dx2 + norm_back(da1, xhat1, rstd1, gain1)
    for h in range(halves):
        dx_h = dx[h * cells : (h + 1) * cells, :]
        gvec_ref[4:5, :] += jnp.sum(unseen[h] * dx_h, axis=0, keepdims=True)
        place = place_of(h).astype(F32).T.astype(BF16)
        ret_ref[h] = mm(place, dx_h.astype(BF16)).astype(BF16)

    @pl.when(step == last)
    def _():
        gqkv_ref[...] = acc_qkv[...].astype(BF16)
        go_ref[...] = acc_o[...].astype(BF16)
        gu_ref[...] = acc_u[...].astype(BF16)
        for c in range(ff // chunk):
            gd_ref[c * chunk : (c + 1) * chunk, :] = acc_d[:, c * chunk : (c + 1) * chunk].T.astype(BF16)


def decoder_block(rows, idx, cot, pos, mask, vecs, wqkv, wo, wu, wd):
    n_half, slots, width = rows.shape
    cells = cot.shape[1]
    ff = wu.shape[1]
    halves = 2
    m_rows = halves * cells
    whole = lambda *shape: pl.BlockSpec(shape, lambda i: (0,) * len(shape), pipeline_mode=pl.Buffered(1))
    vm = pltpu.VMEM
    return pl.pallas_call(
        decoder_kernel,
        grid=(n_half // halves,),
        in_specs=[
            pl.BlockSpec((halves, slots, width), lambda i: (i, 0, 0)),
            pl.BlockSpec((halves, 1, slots), lambda i: (i, 0, 0)),
            pl.BlockSpec((halves, cells, width), lambda i: (i, 0, 0)),
            whole(cells, width),
            whole(cells, LANES),
            whole(8, width),
            whole(width, 3 * width),
            whole(width, width),
            whole(width, ff),
            whole(ff, width),
        ],
        out_specs=[
            pl.BlockSpec((halves, cells, width), lambda i: (i, 0, 0)),
            pl.BlockSpec((halves, slots, width), lambda i: (i, 0, 0)),
            whole(width, 3 * width),
            whole(width, width),
            whole(width, ff),
            whole(ff, width),
            whole(8, width),
        ],
        out_shape=[
            jax.ShapeDtypeStruct((n_half, cells, width), BF16),
            jax.ShapeDtypeStruct((n_half, slots, width), BF16),
            jax.ShapeDtypeStruct((width, 3 * width), BF16),
            jax.ShapeDtypeStruct((width, width), BF16),
            jax.ShapeDtypeStruct((width, ff), BF16),
            jax.ShapeDtypeStruct((ff, width), BF16),
            jax.ShapeDtypeStruct((8, width), F32),
        ],
        scratch_shapes=[
            vm((width, 3 * width), F32),
            vm((width, width), F32),
            vm((width, ff), F32),
            vm((width, ff), F32),
            vm((m_rows, width), F32),
            vm((m_rows, 3 * width), BF16),
            vm((m_rows, width), F32),
            vm((m_rows, width), BF16),
            vm((m_rows, width), BF16),
            vm((width, m_rows), BF16),
            vm((width, m_rows), BF16),
            vm((m_rows, width), F32),
            vm((m_rows, width), F32),
            vm((m_rows, 3 * width), BF16),
        ],
        compiler_params=pltpu.CompilerParams(
            dimension_semantics=("arbitrary",), vmem_limit_bytes=58 * 1024 * 1024
        ),
        name="decoder_block",
    )(rows, idx.reshape(n_half, 1, slots), cot, pos, mask, vecs, wqkv, wo, wu, wd)


def enc_spread(t, head_masks):
    return jnp.concatenate([t * hm.astype(BF16)[None] for hm in head_masks], axis=1)


def enc_heads(width):
    head_dim = width // HEADS_ENC
    lane = lax.broadcasted_iota(jnp.int32, (1, LANES), 1)
    return head_dim, [(lane // head_dim == h) for h in range(LANES // head_dim)]


def enc_attend_kernel(x_ref, mask_ref, vec_ref, wqkv_ref, wo_ref, qkv_ref, p_ref, o_ref, x2_ref):
    clips, slots, width = x_ref.shape
    m_rows = clips * slots
    head_dim, head_masks = enc_heads(width)
    scale = head_dim ** (-0.5)
    x = x_ref[...].reshape(m_rows, width).astype(F32)
    xhat, rstd = normalise(x)
    a1 = (xhat * vec_ref[0:1, :] + vec_ref[1:2, :]).astype(BF16)
    qkv_ref[...] = mm(a1, wqkv_ref[...]).astype(BF16)
    allowed = mask_ref[...] > 0.5
    for g in range(width // LANES):
        cols = lambda part: slice(part * width + g * LANES, part * width + (g + 1) * LANES)
        q3 = qkv_ref[:, cols(0)].reshape(clips, slots, LANES)
        k3 = enc_spread(qkv_ref[:, cols(1)].reshape(clips, slots, LANES), head_masks)
        v3 = enc_spread(qkv_ref[:, cols(2)].reshape(clips, slots, LANES), head_masks)
        s = bmm_t(q3, k3) * scale
        for h in range(len(head_masks)):
            sh = jnp.where(allowed, s[:, :, h * slots : (h + 1) * slots], neg_fill)
            e = jnp.exp(sh - jnp.max(sh, axis=-1, keepdims=True))
            e = e / jnp.sum(e, axis=-1, keepdims=True)
            at = (g * len(head_masks) + h) * slots
            p_ref[:, at : at + slots] = e.reshape(m_rows, slots).astype(BF16)
        span = len(head_masks) * slots
        p3 = p_ref[:, g * span : (g + 1) * span].reshape(clips, slots, span)
        o_ref[:, cols(0)] = bmm(p3, v3).reshape(m_rows, LANES).astype(BF16)
    x2_ref[...] = x_ref[...].reshape(m_rows, width).astype(F32) + mm(o_ref[...], wo_ref[...])


def enc_feed_kernel(
    x2_ref, vec_ref, wu_ref, wd_ref, proj_ref, sent_ref, enc_ref, h_ref, gp_ref, a2_s, y_s
):
    ff = wu_ref.shape[1]
    chunk = 512
    xhat, rstd = normalise(x2_ref[...])
    a2_s[...] = (xhat * vec_ref[2:3, :] + vec_ref[3:4, :]).astype(BF16)
    y_s[...] = x2_ref[...]

    def body(c, carry):
        at = pl.ds(pl.multiple_of(c * chunk, chunk), chunk)
        u = mm(a2_s[...], wu_ref[:, at])
        cdf, bump = gelu_parts(u)
        h = (u * cdf).astype(BF16)
        h_ref[:, at] = h
        gp_ref[:, at] = (cdf + bump).astype(BF16)
        y_s[...] += mm(h, wd_ref[at, :])
        return carry

    lax.fori_loop(0, ff // chunk, body, 0)
    encoded = y_s[...].astype(BF16)
    enc_ref[...] = encoded
    sent_ref[...] = mm(encoded, proj_ref[...]).astype(BF16)


def enc_feed_back_kernel(
    dsent_ref, enc_ref, proj_ref, h_ref, gp_ref, x2_ref, vec_ref, wu_ref, wd_ref,
    gproj_ref, gu_ref, gd_ref, dx2_ref, gvec_ref,
    a2t_s, dz_s, dzt_s, da_s,
):
    ff = wu_ref.shape[1]
    chunk = 512
    gain2 = vec_ref[2:3, :]
    dsent = dsent_ref[...]
    gproj_ref[...] = mm(enc_ref[...].T, dsent).astype(BF16)
    dy = mm_t(dsent, proj_ref[...])
    dx2_ref[...] = dy
    dz = dy.astype(BF16)
    dz_s[...] = dz
    dzt_s[...] = dz.T
    xhat, rstd = normalise(x2_ref[...])
    a2t_s[...] = (xhat * gain2 + vec_ref[3:4, :]).astype(BF16).T
    da_s[...] = jnp.zeros_like(da_s)

    def body(c, carry):
        at = pl.ds(pl.multiple_of(c * chunk, chunk), chunk)
        dh = mm_t(dz_s[...], wd_ref[at, :])
        du = (gp_ref[:, at].astype(F32) * dh).astype(BF16)
        gd_ref[at, :] = mm(dzt_s[...], h_ref[:, at]).T.astype(BF16)
        gu_ref[:, at] = mm(a2t_s[...], du).astype(BF16)
        da_s[...] += mm_t(du, wu_ref[:, at])
        return carry

    lax.fori_loop(0, ff // chunk, body, 0)
    da = da_s[...]
    xhat, rstd = normalise(x2_ref[...])
    gvec_ref[...] = jnp.zeros_like(gvec_ref)
    gvec_ref[2:3, :] = jnp.sum(da * xhat, axis=0, keepdims=True)
    gvec_ref[3:4, :] = jnp.sum(da, axis=0, keepdims=True)
    dx2_ref[...] += norm_back(da, xhat, rstd, gain2)


def enc_attend_back_kernel(
    dx2_ref, o_ref, qkv_ref, p_ref, x_ref, vec_ref, wqkv_ref, wo_ref,
    gqkv_ref, go_ref, dvis_ref, gvec_ref,
    do_s, dqkv_s,
):
    clips, slots, width = x_ref.shape
    m_rows = clips * slots
    head_dim, head_masks = enc_heads(width)
    count = len(head_masks)
    scale = head_dim ** (-0.5)
    gain1, shift1 = vec_ref[0:1, :], vec_ref[1:2, :]
    dy2 = dx2_ref[...].astype(BF16)
    go_ref[...] = mm(o_ref[...].T, dy2).astype(BF16)
    do_s[...] = mm_t(dy2, wo_ref[...]).astype(BF16)

    def fold(t):
        out = t[:, 0:slots, :]
        for h in range(1, count):
            out = jnp.where(head_masks[h][None], t[:, h * slots : (h + 1) * slots, :], out)
        return out.reshape(m_rows, LANES).astype(BF16)

    for g in range(width // LANES):
        cols = lambda part: slice(part * width + g * LANES, part * width + (g + 1) * LANES)
        q3 = qkv_ref[:, cols(0)].reshape(clips, slots, LANES)
        k3 = enc_spread(qkv_ref[:, cols(1)].reshape(clips, slots, LANES), head_masks)
        v3 = enc_spread(qkv_ref[:, cols(2)].reshape(clips, slots, LANES), head_masks)
        do3 = do_s[:, cols(0)].reshape(clips, slots, LANES)
        span = count * slots
        p3 = p_ref[:, g * span : (g + 1) * span].reshape(clips, slots, span)
        dp = bmm_t(do3, v3)
        parts = []
        for h in range(count):
            hs = slice(h * slots, (h + 1) * slots)
            ph = p3[:, :, hs].astype(F32)
            dph = dp[:, :, hs]
            mean = jnp.sum(ph * dph, axis=-1, keepdims=True)
            parts.append((ph * (dph - mean) * scale).astype(BF16))
        draw3 = jnp.concatenate(parts, axis=2)
        dqkv_s[:, cols(0)] = bmm(draw3, k3).reshape(m_rows, LANES).astype(BF16)
        dqkv_s[:, cols(1)] = fold(bmm_l(draw3, q3))
        dqkv_s[:, cols(2)] = fold(bmm_l(p3, do3))

    x = x_ref[...].reshape(m_rows, width).astype(F32)
    xhat, rstd = normalise(x)
    a1t = (xhat * gain1 + shift1).astype(BF16).T
    gqkv_ref[...] = mm(a1t, dqkv_s[...]).astype(BF16)
    da = mm_t(dqkv_s[...], wqkv_ref[...])
    gvec_ref[...] = jnp.zeros_like(gvec_ref)
    gvec_ref[0:1, :] = jnp.sum(da * xhat, axis=0, keepdims=True)
    gvec_ref[1:2, :] = jnp.sum(da, axis=0, keepdims=True)
    dx = dx2_ref[...] + norm_back(da, xhat, rstd, gain1)
    dvis_ref[...] = dx.reshape(clips, slots, width).astype(BF16)


def whole_call(kernel, outs, scratch, name, *args):
    return pl.pallas_call(
        kernel,
        out_shape=[jax.ShapeDtypeStruct(s, d) for s, d in outs],
        scratch_shapes=[pltpu.VMEM(s, d) for s, d in scratch],
        compiler_params=pltpu.CompilerParams(vmem_limit_bytes=58 * 1024 * 1024),
        name=name,
    )(*args)


def enc_attend(x, mask, vecs, wqkv, wo):
    clips, slots, width = x.shape
    m = clips * slots
    outs = [((m, 3 * width), BF16), ((m, HEADS_ENC * slots), BF16), ((m, width), BF16), ((m, width), F32)]
    return whole_call(enc_attend_kernel, outs, [], "enc_attend", x, mask, vecs, wqkv, wo)


def enc_feed(x2, vecs, wu, wd, proj):
    m, width = x2.shape
    ff = wu.shape[1]
    outs = [((m, proj.shape[1]), BF16), ((m, width), BF16), ((m, ff), BF16), ((m, ff), BF16)]
    scratch = [((m, width), BF16), ((m, width), F32)]
    return whole_call(enc_feed_kernel, outs, scratch, "enc_feed", x2, vecs, wu, wd, proj)


def enc_feed_back(dsent, enc, proj, h, gp, x2, vecs, wu, wd):
    m, width = x2.shape
    ff = wu.shape[1]
    outs = [(proj.shape, BF16), (wu.shape, BF16), (wd.shape, BF16), ((m, width), F32), ((8, width), F32)]
    scratch = [((width, m), BF16), ((m, width), BF16), ((width, m), BF16), ((m, width), F32)]
    return whole_call(
        enc_feed_back_kernel, outs, scratch, "enc_feed_back", dsent, enc, proj, h, gp, x2, vecs, wu, wd
    )


def enc_attend_back(dx2, o, qkv, p, x, vecs, wqkv, wo):
    m, width = dx2.shape
    outs = [(wqkv.shape, BF16), (wo.shape, BF16), (x.shape, BF16), ((8, width), F32)]
    scratch = [((m, width), BF16), ((m, 3 * width), BF16)]
    return whole_call(
        enc_attend_back_kernel, outs, scratch, "enc_attend_back", dx2, o, qkv, p, x, vecs, wqkv, wo
    )


AXES = ("clip", "band")


def split_bits(parts):
    return parts.bit_length() - 1


def bit_order(count):
    first = [b for b in (0, 2, 1) if b < count]
    rest = [b for b in range(count - 1, -1, -1) if b not in first]
    return first + rest


def swap_order(order):
    if len(order) < 3:
        return order
    return [order[0], order[2], order[1]] + order[3:]


def partner_pairs(total, bit):
    return [(i, i ^ (1 << bit)) for i in range(total)]


def scatter_sum(partial, total, order):
    me = lax.axis_index(AXES)
    left = list(range(split_bits(total) - 1, -1, -1))
    rows = partial.shape[0] // total
    held = partial.reshape((2,) * len(left) + (rows,) + partial.shape[1:])
    for bit in order:
        place = left.index(bit)
        mine = (me >> bit) & 1
        keep = lax.dynamic_index_in_dim(held, mine, place, keepdims=False)
        give = lax.dynamic_index_in_dim(held, 1 - mine, place, keepdims=False)
        got = lax.ppermute(give, AXES, partner_pairs(total, bit))
        held = (keep.astype(F32) + got.astype(F32)).astype(BF16)
        left.remove(bit)
    return held


def gather_rows(shard, total, order):
    me = lax.axis_index(AXES)
    have = []
    held = shard
    for bit in reversed(order):
        mine = (me >> bit) & 1
        got = lax.ppermute(held, AXES, partner_pairs(total, bit))
        low = jnp.where(mine == 0, held, got)
        high = jnp.where(mine == 0, got, held)
        have = sorted(have + [bit], reverse=True)
        held = jnp.stack([low, high], axis=have.index(bit))
    return held.reshape((total * shard.shape[0],) + shard.shape[1:])


def columns_of(vectors):
    block = jnp.stack(vectors, axis=1)
    return jnp.pad(block, ((0, 0), (0, LANES - len(vectors)))).astype(BF16)


def rows_of(block, count):
    vectors = block[:, :count].T.astype(F32)
    return jnp.pad(vectors, ((0, 8 - count), (0, 0)))


def position_table(places):
    half_width = D_DEC // 2
    omega_vec = jnp.exp(
        jnp.arange(half_width, dtype=F32) * (-math.log(10000.0) / half_width)
    )
    angles = places.astype(F32)[..., None] * omega_vec
    return jnp.concatenate([jnp.sin(angles), jnp.cos(angles)], axis=-1)


def shards(
    visible,
    keep_index,
    visible_count,
    enc_gain1,
    enc_shift1,
    enc_qkv,
    enc_out,
    enc_gain2,
    enc_shift2,
    enc_up,
    enc_down,
    proj,
    mask_token,
    dec_gain1,
    dec_shift1,
    dec_qkv,
    dec_out,
    dec_gain2,
    dec_shift2,
    dec_up,
    dec_down,
    cotangent,
):
    total = lax.axis_size(AXES)
    order = bit_order(split_bits(total))
    order_two = swap_order(order)
    enc_wide = enc_out.shape[1]
    dec_wide = dec_out.shape[1]
    pack_one = jnp.concatenate(
        [enc_qkv, enc_out, proj, columns_of([enc_gain1, enc_shift1, enc_gain2, enc_shift2])], axis=1
    )
    pack_one = gather_rows(pack_one, total, order)
    whole_up = gather_rows(enc_up, total, order_two)
    whole_down = gather_rows(enc_down, total, order)
    enc_vecs = rows_of(pack_one[:, 4 * enc_wide + dec_wide :], 4)
    whole_qkv = pack_one[:, : 3 * enc_wide]
    whole_out = pack_one[:, 3 * enc_wide : 4 * enc_wide]
    whole_proj = pack_one[:, 4 * enc_wide : 4 * enc_wide + dec_wide]
    pack_two = jnp.concatenate(
        [
            dec_qkv,
            dec_out,
            columns_of([dec_gain1, dec_shift1, dec_gain2, dec_shift2, mask_token]),
        ],
        axis=1,
    )
    pack_two = gather_rows(pack_two, total, order_two)
    dec_whole_up = gather_rows(dec_up, total, order)
    dec_whole_down = gather_rows(dec_down, total, order_two)
    dec_vecs = rows_of(pack_two[:, 4 * dec_wide :], 5)

    clip_count, slot_total, _ = visible.shape
    half_clips = clip_count // 2
    band_height = FREQ // 2
    slot_ids = jnp.arange(slot_total)
    valid_rows = slot_ids[None, :] < visible_count[:, None]
    valid_mask = valid_rows.astype(F32)[:, None, :]
    qkv, probs, mixed, middle = enc_attend(visible, valid_mask, enc_vecs, whole_qkv, whole_out)
    sent_rows, encoded, hidden, slope = enc_feed(middle, enc_vecs, whole_up, whole_down, whole_proj)
    sent_rows = sent_rows.reshape(clip_count, slot_total, dec_wide)

    rolled_time = (keep_index // FREQ + TIME - SHIFT) % TIME
    rolled_freq = (keep_index % FREQ + FREQ - SHIFT) % FREQ
    target_band = rolled_freq // band_height
    slot_index = rolled_time * band_height + rolled_freq % band_height
    band_ids = jnp.arange(2)
    chosen = valid_rows[:, None, :] & (target_band[:, None, :] == band_ids[None, :, None])
    chosen = chosen.reshape(2, half_clips, 2, slot_total).transpose(0, 2, 1, 3)
    outgoing = jnp.where(
        chosen[..., None],
        sent_rows.reshape(2, 1, half_clips, slot_total, dec_wide),
        jnp.zeros((), BF16),
    )
    outgoing = outgoing.reshape(4, half_clips, slot_total, dec_wide)
    slot_out = jnp.where(chosen, slot_index.reshape(2, 1, half_clips, slot_total), -1).astype(BF16)
    slot_out = slot_out.reshape(4, half_clips, slot_total)
    arrived = lax.all_to_all(outgoing, "band", split_axis=0, concat_axis=0, tiled=True)
    arrived_slot = lax.all_to_all(slot_out, "band", split_axis=0, concat_axis=0, tiled=True)
    half_total = 4 * half_clips
    arrived_rows = arrived.reshape(half_total, slot_total, dec_wide)
    arrived_index = arrived_slot.reshape(half_total, slot_total).astype(jnp.int32)

    cell_count = TIME * band_height
    places = jnp.arange(cell_count)
    band_pick = lax.axis_index("band") % 2
    cell_freq = band_pick * band_height + places % band_height
    patch_number = (places // band_height + SHIFT) % TIME * FREQ + (cell_freq + SHIFT) % FREQ
    span = LANES * D_DEC // (HEADS_DEC * LANES)
    query = places[:, None]
    key = query // span * span + jnp.arange(LANES)[None, :] % span

    def label(cell):
        late = cell // band_height >= TIME - SHIFT
        high = band_pick * band_height + cell % band_height >= FREQ - SHIFT
        return late.astype(jnp.int32) * 2 + high.astype(jnp.int32)

    cells_in = WINDOW * WINDOW
    allowed = (query // cells_in == key // cells_in) & (label(query) == label(key))
    decoded, returning, g_dqkv, g_dout, g_dup, g_ddown, g_dvec = decoder_block(
        arrived_rows,
        arrived_index,
        cotangent.reshape(half_total, cell_count, dec_wide),
        position_table(patch_number),
        allowed.astype(F32),
        dec_vecs,
        pack_two[:, : 3 * dec_wide],
        pack_two[:, 3 * dec_wide : 4 * dec_wide],
        dec_whole_up,
        dec_whole_down,
    )
    decoded_out = decoded.reshape(cotangent.shape)

    returning = returning.reshape(4, half_clips, slot_total, dec_wide)
    coming = lax.all_to_all(returning, "band", split_axis=0, concat_axis=0, tiled=True)
    grad_sent = jnp.sum(coming.astype(F32).reshape(2, 2, half_clips, slot_total, dec_wide), axis=1)
    grad_sent = grad_sent.astype(BF16).reshape(-1, dec_wide)

    dec_pack = jnp.concatenate([g_dqkv, g_dout, columns_of([g_dvec[i] for i in range(5)])], axis=1)
    dec_pack = scatter_sum(dec_pack, total, order_two)
    dec_up_sum = scatter_sum(g_dup, total, order)
    dec_down_sum = scatter_sum(g_ddown, total, order_two)
    dec_pack = gather_rows(dec_pack, total, order_two).astype(F32)
    dec_up_sum = gather_rows(dec_up_sum, total, order).astype(F32)
    dec_down_sum = gather_rows(dec_down_sum, total, order_two).astype(F32)
    dec_vec_sums = rows_of(dec_pack[:, 4 * dec_wide :], 5)

    g_proj, g_eup, g_edown, grad_middle, g_evec2 = enc_feed_back(
        grad_sent, encoded, whole_proj, hidden, slope, middle, enc_vecs, whole_up, whole_down
    )
    enc_up_sum = scatter_sum(g_eup, total, order_two)
    enc_down_sum = scatter_sum(g_edown, total, order)
    g_eqkv, g_eout, grad_visible, g_evec1 = enc_attend_back(
        grad_middle, mixed, qkv, probs, visible, enc_vecs, whole_qkv, whole_out
    )
    g_evec = g_evec1 + g_evec2
    enc_pack = jnp.concatenate(
        [g_eqkv, g_eout, g_proj, columns_of([g_evec[i] for i in range(4)])], axis=1
    )
    enc_pack = scatter_sum(enc_pack, total, order)
    enc_up_sum = gather_rows(enc_up_sum, total, order_two).astype(F32)
    enc_down_sum = gather_rows(enc_down_sum, total, order).astype(F32)
    enc_pack = gather_rows(enc_pack, total, order).astype(F32)
    enc_vec_sums = rows_of(enc_pack[:, 4 * enc_wide + dec_wide :], 4)
    return (
        decoded_out,
        grad_visible,
        enc_vec_sums[0],
        enc_vec_sums[1],
        enc_pack[:, : 3 * enc_wide],
        enc_pack[:, 3 * enc_wide : 4 * enc_wide],
        enc_vec_sums[2],
        enc_vec_sums[3],
        enc_up_sum,
        enc_down_sum,
        enc_pack[:, 4 * enc_wide : 4 * enc_wide + dec_wide],
        dec_vec_sums[4],
        dec_vec_sums[0],
        dec_vec_sums[1],
        dec_pack[:, : 3 * dec_wide],
        dec_pack[:, 3 * dec_wide : 4 * dec_wide],
        dec_vec_sums[2],
        dec_vec_sums[3],
        dec_up_sum,
        dec_down_sum,
    )


def solution(mesh):
    return jax.shard_map(
        shards,
        mesh=mesh,
        in_specs=(
            P(("clip", "band"), None, None),
            P(("clip", "band"), None),
            P(("clip", "band")),
            P(("clip", "band")),
            P(("clip", "band")),
            P(("clip", "band"), None),
            P(("clip", "band"), None),
            P(("clip", "band")),
            P(("clip", "band")),
            P(("clip", "band"), None),
            P(("clip", "band"), None),
            P(("clip", "band"), None),
            P(("clip", "band")),
            P(("clip", "band")),
            P(("clip", "band")),
            P(("clip", "band"), None),
            P(("clip", "band"), None),
            P(("clip", "band")),
            P(("clip", "band")),
            P(("clip", "band"), None),
            P(("clip", "band"), None),
            P(("clip", "band"), None, None, None, None),
        ),
        out_specs=(
            P(("clip", "band"), None, None, None, None),
            P(("clip", "band"), None, None),
            P(),
            P(),
            P(),
            P(),
            P(),
            P(),
            P(),
            P(),
            P(),
            P(),
            P(),
            P(),
            P(),
            P(),
            P(),
            P(),
            P(),
            P(),
        ),
        check_vma=False,
    )
```

time: 1410 us -> 823 us (0.58)
  local copies, waits for them, and re-layouts: 411 us -> 67.6 us
  matrix products: 273 us -> 0 us
  Pallas kernels: 0 us -> 181 us
  other arithmetic: 216 us -> 57.1 us
    dot_general x40 -> x0, matrix products: 273 us -> none  [the longest x9 64.4 us: forward_dot(): jnp.einsum('nd,de->ne', operand, weight, preferred_element_type=jnp.float32)]
    pallas_call x0 -> x5, Pallas kernels: none -> 181 us  [the longest x1 115 us: decoder_block(): pl.pallas_call(decoder_kernel, grid=(n_half // halves,), in_specs=[pl.Blo...]
    convert_element_type x23 -> x8, local copies, waits for them, and re-layouts: 153 us -> 19.7 us  [the longest x1 5.15 us: shards(): enc_pack = gather_rows(enc_pack, total, order).astype(F32)]
    another operation x11 -> x0, local copies, waits for them, and re-layouts: 101 us -> none  [the longest x4 63.9 us: exact_gelu(): return jax.nn.gelu(inputs, approximate=False)]
    convert_element_type x48 -> x39, other arithmetic: 68 us -> 19.3 us  [the longest x30 9.96 us: scatter_sum(): held = (keep.astype(F32) + got.astype(F32)).astype(BF16)]
    reshape x5 -> x2, local copies, waits for them, and re-layouts: 53 us -> 6.14 us  [the longest x1 4.11 us: shards(): decoded_out = decoded.reshape(cotangent.shape)]
    another operation x2, other arithmetic: 46.5 us -> 0.75 us  [exact_gelu(): return jax.nn.gelu(inputs, approximate=False)]
    mul x3 -> x0, other arithmetic: 37.6 us -> none  [the longest x1 36.1 us: exact_gelu(): return jax.nn.gelu(inputs, approximate=False)]
  transfers between devices with their start and end apart: 93 -> 93, of which waited for: 50 -> 53; matrix products, arithmetic and copies ran while one was open for 20% -> 12% of each run, Pallas kernels for 0% -> 8%
where the time goes in v2:
time: 823 us; the launch traced here: 813 us
  waiting for transfers between devices  404 us (49%)
  Pallas kernels  181 us (22%)
  starting transfers between devices  100 us (12%)
  local copies, waits for them, and re-layouts  67.6 us (8%)
  other arithmetic  57.1 us (7%)
    ppermute x60, waiting for transfers between devices, gather_rows(): got = lax.ppermute(held, AXES, partner_pairs(total, bit))  256 us
    ppermute x30, waiting for transfers between devices, scatter_sum(): got = lax.ppermute(give, AXES, partner_pairs(total, bit))  129 us
    pallas_call x1, Pallas kernels, decoder_block(): pl.pallas_call(decoder_kernel, grid=(n_half // halves,), in_specs=[pl.Blo...  115 us
    pallas_call x4, Pallas kernels, whole_call(): pl.pallas_call(kernel, out_shape=[jax.ShapeDtypeStruct(s, d) for s, d in...  65.9 us
    ppermute x60, starting transfers between devices, gather_rows(): got = lax.ppermute(held, AXES, partner_pairs(total, bit))  64.9 us
    ppermute x30, starting transfers between devices, scatter_sum(): got = lax.ppermute(give, AXES, partner_pairs(total, bit))  23.5 us
    another operation x114, other arithmetic, gather_rows(): held = jnp.stack([low, high], axis=have.index(bit))  22.4 us
  transfers between devices with their start and end apart: 93, of which 53 were waited for; matrix products, arithmetic and copies ran while one was open for 12% of the time, Pallas kernels for 8%

profile of v2, /device:TPU:0, one launch (start us, length us, event | category | flops | bytes accessed | tf_op | source)
XLA Modules:
  0.0 812.8 jit_solution(16301765299067965563)
XLA Ops:
  3.1 4.2 all-to-all-start.1
  36.5 18.3 %collective-permute-done.26 = bf16[2,64,512]{2,1,0:T(8,128)(2,1)S(1)} collective-permute-done((bf16[2,64,512]{2,1,0:T(8,128)(2,1)S(1)}, bf16[2,64,512]{2,1,0:T(8,128)(2,1)S(1)}, u32[]{:S(2)}, u32[]{:S(2)}) %collective-permute-start.26) | collective-permute-done | bytes 131104 | tf_op jit(solution)/shard_map/ppermute | solution.py:553
  57.8 5.9 collective-permute-start.27
  63.8 8.0 collective-permute-done.6
  74.0 4.1 collective-permute-done.11
  86.9 15.9 %collective-permute-done.23 = bf16[2,2,2,16,2048]{4,3,1,0,2:T(8,128)(2,1)S(1)} collective-permute-done((bf16[2,2,2,16,2048]{4,3,1,0,2:T(8,128)(2,1)S(1)}, bf16[2,2,2,16,2048]{4,3,1,0,2:T(8,128)(2,1)S(1)}, u32[]{:S(2)}, u32[]{:S(2)}) %collective-permute-start.23) | collective-permute-done | bytes 524320 | tf_op jit(solution)/shard_map/ppermute | solution.py:553
  111.2 8.7 %collective-permute-done.18 = bf16[2,2,2,16,2176]{4,3,1,0,2:T(8,128)(2,1)S(1)} collective-permute-done((bf16[2,2,2,16,2176]{4,3,1,0,2:T(8,128)(2,1)S(1)}, bf16[2,2,2,16,2176]{4,3,1,0,2:T(8,128)(2,1)S(1)}, u32[]{:S(2)}, u32[]{:S(2)}) %collective-permute-start.18) | collective-permute-done | bytes 557088 | tf_op jit(solution)/shard_map/ppermute | solution.py:553
  121.1 14.0 %collective-permute-done.2 = bf16[2,2,24,3712]{3,2,1,0:T(8,128)(2,1)S(1)} collective-permute-done((bf16[2,2,24,3712]{3,2,1,0:T(8,128)(2,1)S(1)}, bf16[2,2,24,3712]{3,2,1,0:T(8,128)(2,1)S(1)}, u32[]{:S(2)}, u32[]{:S(2)}) %collective-permute-start.2) | collective-permute-done | bytes 712736 | tf_op jit(solution)/shard_map/ppermute | solution.py:553
  135.5 21.2 %collective-permute-done.8 = bf16[2,2,2,24,3072]{4,3,1,0,2:T(8,128)(2,1)S(1)} collective-permute-done((bf16[2,2,2,24,3072]{4,3,1,0,2:T(8,128)(2,1)S(1)}, bf16[2,2,2,24,3072]{4,3,1,0,2:T(8,128)(2,1)S(1)}, u32[]{:S(2)}, u32[]{:S(2)}) %collective-permute-start.8) | collective-permute-done | bytes 1179680 | tf_op jit(solution)/shard_map/ppermute | solution.py:553
  158.1 28.2 %collective-permute-done.3 = bf16[2,2,2,24,3712]{4,3,1,0,2:T(8,128)(2,1)S(1)} collective-permute-done((bf16[2,2,2,24,3712]{4,3,1,0,2:T(8,128)(2,1)S(1)}, bf16[2,2,2,24,3712]{4,3,1,0,2:T(8,128)(2,1)S(1)}, u32[]{:S(2)}, u32[]{:S(2)}) %collective-permute-start.3) | collective-permute-done | bytes 1425440 | tf_op jit(solution)/shard_map/ppermute | solution.py:553
  207.9 9.9 %enc_attend.1 = (bf16[512,2304]{1,0:T(8,128)(2,1)}, bf16[512,1536]{1,0:T(8,128)(2,1)}, bf16[512,768]{1,0:T(8,128)(2,1)}, f32[512,768]{1,0:T(8,128)}) custom-call(bf16[4,128,768]{2,1,0:T(8,128)(2,1)} %x_ref.3, f32[4,1,128]{2,1,0:T(1,128)} %compare_convert_fusion.mask_ref, f32[8,768]{1,0:T(8,128)} %copy.148.vec_ref, bf16[768,2304]{1,0:T(8,128)(2,1)} %slice.155.wqkv_ref, ...), custom_call_target="tpu_custom_call" | custom-call | tf_op jit(solution)/shard_map/enc_attend/pallas_call | solution.py:465
  217.8 18.5 %enc_feed.1 = (bf16[512,512]{1,0:T(8,128)(2,1)}, bf16[512,768]{1,0:T(8,128)(2,1)}, bf16[512,3072]{1,0:T(8,128)(2,1)}, bf16[512,3072]{1,0:T(8,128)(2,1)}) custom-call(f32[512,768]{1,0:T(8,128)} %get-tuple-element.44.x2_ref, f32[8,768]{1,0:T(8,128)} %copy.148.vec_ref, bf16[768,3072]{1,0:T(8,128)(2,1)} %bitcast.486, bf16[3072,768]{1,0:T(8,128)(2,1)} %bitcast.488, ...), custom_call_target="tpu_custom_call" | custom-call | tf_op jit(solution)/shard_map/enc_feed/pallas_call | solution.py:465
  245.6 10.9 %all-to-all-done = bf16[4,2,128,512]{3,2,1,0:T(8,128)(2,1)S(1)} async-done(((bf16[4,2,128,512]{3,2,1,0:T(8,128)(2,1)}), bf16[4,2,128,512]{3,2,1,0:T(8,128)(2,1)S(1)}, u32[]{:S(2)}, u32[]{:S(2)}) %all-to-all-start) | async-done | bytes 1048608 | tf_op jit(solution)/shard_map/all_to_all | solution.py:657
  257.5 114.8 %decoder_block.1 = (bf16[8,256,512]{2,1,0:T(8,128)(2,1)}, bf16[8,128,512]{2,1,0:T(8,128)(2,1)}, bf16[512,1536]{1,0:T(8,128)(2,1)}, bf16[512,512]{1,0:T(8,128)(2,...) custom-call(bf16[8,128,512]{2,1,0:T(8,128)(2,1)} %bitcast.512, ...), custom_call_target="tpu_custom_call" | custom-call | tf_op jit(solution)/shard_map/decoder_block/pallas_call | solution.py:254
  372.3 4.1 reshape.442
  376.5 4.3 all-to-all-start.2
  387.1 8.2 %all-to-all-done.2 = bf16[4,2,128,512]{3,2,1,0:T(8,128)(2,1)} async-done(((bf16[4,2,128,512]{3,2,1,0:T(8,128)(2,1)}), bf16[4,2,128,512]{3,2,1,0:T(8,128)(2,1)}, u32[]{:S(2)}, u32[]{:S(2)}) %all-to-all-start.2) | async-done | bytes 1048608 | tf_op jit(solution)/shard_map/all_to_all | solution.py:694
  397.6 23.3 %enc_feed_back.1 = (bf16[768,512]{1,0:T(8,128)(2,1)}, bf16[768,3072]{1,0:T(8,128)(2,1)}, bf16[3072,768]{1,0:T(8,128)(2,1)}, f32[512,768]{1,0:T(8,128)}, f32[8,768]{1,0:T(8,128)}) custom-call(bf16[512,512]{1,0:T(8,128)(2,1)} %bitcast.518, bf16[512,768]{1,0:T(8,128)(2,1)} %get-tuple-element.48.enc_ref, bf16[768,512]{1,0:T(8,128)(2,1)} %slice.157.proj_ref, ...), custom_call_target="tpu_custom_call" | custom-call | tf_op jit(solution)/shard_map/enc_feed_back/pallas_call | solution.py:465
  420.9 14.2 %enc_attend_back.1 = (bf16[768,2304]{1,0:T(8,128)(2,1)}, bf16[768,768]{1,0:T(8,128)(2,1)}, bf16[4,128,768]{2,1,0:T(8,128)(2,1)}, f32[8,768]{1,0:T(8,128)}) custom-call(f32[512,768]{1,0:T(8,128)} %get-tuple-element.51.dx2_ref, bf16[512,768]{1,0:T(8,128)(2,1)} %get-tuple-element.52.o_ref, bf16[512,2304]{1,0:T(8,128)(2,1)} %get-tuple-element.53.qkv_ref, ...), custom_call_target="tpu_custom_call" | custom-call | tf_op jit(solution)/shard_map/enc_attend_back/pallas_call | solution.py:465
  450.8 9.4 %collective-permute-done.71 = bf16[2,2,2,16,2048]{4,3,1,0,2:T(8,128)(2,1)S(1)} collective-permute-done((bf16[2,2,2,16,2048]{4,3,1,0,2:T(8,128)(2,1)S(1)}, bf16[2,2,2,16,2048]{4,3,1,0,2:T(8,128)(2,1)S(1)}, u32[]{:S(2)}, u32[]{:S(2)}) %collective-permute-start.71) | collective-permute-done | bytes 524320 | tf_op jit(solution)/shard_map/ppermute | solution.py:541
  463.5 12.3 %collective-permute-done.61 = bf16[2,2,2,16,2176]{4,3,1,0,2:T(8,128)(2,1)S(1)} collective-permute-done((bf16[2,2,2,16,2176]{4,3,1,0,2:T(8,128)(2,1)S(1)}, bf16[2,2,2,16,2176]{4,3,1,0,2:T(8,128)(2,1)S(1)}, u32[]{:S(2)}, u32[]{:S(2)}) %collective-permute-start.61) | collective-permute-done | bytes 557088 | tf_op jit(solution)/shard_map/ppermute | solution.py:541
  482.9 5.3 collective-permute-done.62
  491.3 8.5 %collective-permute-done.83 = bf16[2,64,512]{2,1,0:T(8,128)(2,1)S(1)} collective-permute-done((bf16[2,64,512]{2,1,0:T(8,128)(2,1)S(1)}, bf16[2,64,512]{2,1,0:T(8,128)(2,1)S(1)}, u32[]{:S(2)}, u32[]{:S(2)}) %collective-permute-start.83) | collective-permute-done | bytes 131104 | tf_op jit(solution)/shard_map/ppermute | solution.py:541
  499.9 4.2 collective-permute-done.74
  504.1 4.7 collective-permute-done.84
  517.6 4.1 collective-permute-done.65
  525.6 6.2 collective-permute-done.86
  534.5 3.7 collective-permute-done.77
  543.7 4.8 collective-permute-done.67
  549.3 7.9 collective-permute-done.78
  561.7 8.4 %collective-permute-done.68 = bf16[2,2,2,16,2176]{4,3,1,0,2:T(8,128)(2,1)S(1)} collective-permute-done((bf16[2,2,2,16,2176]{4,3,1,0,2:T(8,128)(2,1)S(1)}, bf16[2,2,2,16,2176]{4,3,1,0,2:T(8,128)(2,1)S(1)}, u32[]{:S(2)}, u32[]{:S(2)}) %collective-permute-start.68) | collective-permute-done | bytes 557088 | tf_op jit(solution)/shard_map/ppermute | solution.py:553
  578.5 10.0 %collective-permute-done.51 = bf16[2,2,2,96,768]{4,3,1,0,2:T(8,128)(2,1)S(1)} collective-permute-done((bf16[2,2,2,96,768]{4,3,1,0,2:T(8,128)(2,1)S(1)}, bf16[2,2,2,96,768]{4,3,1,0,2:T(8,128)(2,1)S(1)}, u32[]{:S(2)}, u32[]{:S(2)}) %collective-permute-start.51) | collective-permute-done | bytes 1179680 | tf_op jit(solution)/shard_map/ppermute | solution.py:541
  590.6 8.3 %collective-permute-done.41 = bf16[2,2,2,24,3072]{4,3,1,0,2:T(8,128)(2,1)S(1)} collective-permute-done((bf16[2,2,2,24,3072]{4,3,1,0,2:T(8,128)(2,1)S(1)}, bf16[2,2,2,24,3072]{4,3,1,0,2:T(8,128)(2,1)S(1)}, u32[]{:S(2)}, u32[]{:S(2)}) %collective-permute-start.41) | collective-permute-done | bytes 1179680 | tf_op jit(solution)/shard_map/ppermute | solution.py:541
  600.9 6.7 collective-permute-done.52
  607.9 22.9 %collective-permute-done.42 = bf16[2,2,24,3072]{3,2,1,0:T(8,128)(2,1)S(1)} collective-permute-done((bf16[2,2,24,3072]{3,2,1,0:T(8,128)(2,1)S(1)}, bf16[2,2,24,3072]{3,2,1,0:T(8,128)(2,1)S(1)}, u32[]{:S(2)}, u32[]{:S(2)}) %collective-permute-start.42) | collective-permute-done | bytes 589856 | tf_op jit(solution)/shard_map/ppermute | solution.py:541
  633.2 5.3 collective-permute-start.54
  638.5 7.8 collective-permute-done.43
  662.9 21.6 %collective-permute-done.56 = bf16[2,96,768]{2,1,0:T(8,128)(2,1)S(1)} collective-permute-done((bf16[2,96,768]{2,1,0:T(8,128)(2,1)S(1)}, bf16[2,96,768]{2,1,0:T(8,128)(2,1)S(1)}, u32[]{:S(2)}, u32[]{:S(2)}) %collective-permute-start.56) | collective-permute-done | bytes 294944 | tf_op jit(solution)/shard_map/ppermute | solution.py:553
  686.5 9.6 %collective-permute-done.33 = bf16[2,24,3712]{2,1,0:T(8,128)(2,1)S(1)} collective-permute-done((bf16[2,24,3712]{2,1,0:T(8,128)(2,1)S(1)}, bf16[2,24,3712]{2,1,0:T(8,128)(2,1)S(1)}, u32[]{:S(2)}, u32[]{:S(2)}) %collective-permute-start.33) | collective-permute-done | bytes 356384 | tf_op jit(solution)/shard_map/ppermute | solution.py:541
  697.1 4.7 collective-permute-done.34
  712.0 12.4 %collective-permute-done.36 = bf16[2,24,3712]{2,1,0:T(8,128)(2,1)S(1)} collective-permute-done((bf16[2,24,3712]{2,1,0:T(8,128)(2,1)S(1)}, bf16[2,24,3712]{2,1,0:T(8,128)(2,1)S(1)}, u32[]{:S(2)}, u32[]{:S(2)}) %collective-permute-start.36) | collective-permute-done | bytes 356384 | tf_op jit(solution)/shard_map/ppermute | solution.py:553
  726.9 16.6 %collective-permute-done.37 = bf16[2,2,24,3712]{3,2,1,0:T(8,128)(2,1)S(1)} collective-permute-done((bf16[2,2,24,3712]{3,2,1,0:T(8,128)(2,1)S(1)}, bf16[2,2,24,3712]{3,2,1,0:T(8,128)(2,1)S(1)}, u32[]{:S(2)}, u32[]{:S(2)}) %collective-permute-start.37) | collective-permute-done | bytes 712736 | tf_op jit(solution)/shard_map/ppermute | solution.py:553
  747.0 19.9 %collective-permute-done.48 = bf16[2,2,2,24,3072]{4,3,1,0,2:T(8,128)(2,1)S(1)} collective-permute-done((bf16[2,2,2,24,3072]{4,3,1,0,2:T(8,128)(2,1)S(1)}, bf16[2,2,2,24,3072]{4,3,1,0,2:T(8,128)(2,1)S(1)}, u32[]{:S(2)}, u32[]{:S(2)}) %collective-permute-start.48) | collective-permute-done | bytes 1179680 | tf_op jit(solution)/shard_map/ppermute | solution.py:553
  767.4 6.0 collective-permute-done.38
  780.3 4.4 copy.165
  787.2 4.8 copy.168
  794.4 5.0 maximum_convert_fusion
  799.3 5.1 copy.162
  (441 shorter events, 222.7 us)
Async XLA Ops:
  3.1 20.0 %all-to-all-start.1 = ((bf16[4,2,128]{2,1,0:T(2,128)(2,1)}), bf16[4,2,128]{2,1,0:T(2,128)(2,1)S(1)}, u32[]{:S(2)}, u32[]{:S(2)}) async-start(bf16[4,2,128]{2,1,0:T(2,128)(2,1)} %get-tuple-element.77), calls=%async_computation.1 | async-start | bytes 4096 | tf_op jit(solution)/shard_map/all_to_all | solution.py:658
  26.9 27.9 %collective-permute-start.26 = (bf16[2,64,512]{2,1,0:T(8,128)(2,1)S(1)}, bf16[2,64,512]{2,1,0:T(8,128)(2,1)S(1)}, u32[]{:S(2)}, u32[]{:S(2)}) collective-permute-start(bf16[2,64,512]{2,1,0:T(8,128)(2,1)S(1)} %pad_maximum_fusion.52), channel_id=1, source_target_pairs={{0,16},{1,17},{2,18},{3,19},{4,20},{5,21},{6,22},{7,23},{8,24},{9,... | collective-permute-start | bytes 393224 | tf_op jit(solution)/shard_map/ppermute | solution.py:553
  27.1 30.7 %collective-permute-start.16 = (bf16[2,16,2176]{2,1,0:T(8,128)(2,1)S(1)}, bf16[2,16,2176]{2,1,0:T(8,128)(2,1)S(1)}, u32[]{:S(2)}, u32[]{:S(2)}) collective-permute-start(bf16[2,16,2176]{2,1,0:T(8,128)(2,1)S(1)} %pad_maximum_fusion.49), channel_id=1, source_target_pairs={{0,16},{1,17},{2,18},{3,19},{4,20},{5,21},{6,22},{7,23},{8,24},{9,... | collective-permute-start | bytes 417800 | tf_op jit(solution)/shard_map/ppermute | solution.py:553
  30.1 41.6 %collective-permute-start.6 = (bf16[2,24,3072]{2,1,0:T(8,128)(2,1)S(1)}, bf16[2,24,3072]{2,1,0:T(8,128)(2,1)S(1)}, u32[]{:S(2)}, u32[]{:S(2)}) collective-permute-start(bf16[2,24,3072]{2,1,0:T(8,128)(2,1)S(1)} %pad_maximum_fusion.39), channel_id=1, source_target_pairs={{0,16},{1,17},{2,18},{3,19},{4,20},{5,21},{6,22},{7,23},{8,24},{9,... | collective-permute-start | bytes 884744 | tf_op jit(solution)/shard_map/ppermute | solution.py:553
  33.3 44.7 %collective-permute-start.11 = (bf16[2,96,768]{2,1,0:T(8,128)(2,1)S(1)}, bf16[2,96,768]{2,1,0:T(8,128)(2,1)S(1)}, u32[]{:S(2)}, u32[]{:S(2)}) collective-permute-start(bf16[2,96,768]{2,1,0:T(8,128)(2,1)S(1)} %pad_maximum_fusion.40), channel_id=1, source_target_pairs={{0,16},{1,17},{2,18},{3,19},{4,20},{5,21},{6,22},{7,23},{8,24},{9,... | collective-permute-start | bytes 884744 | tf_op jit(solution)/shard_map/ppermute | solution.py:553
  33.9 50.9 %collective-permute-start.1 = (bf16[2,24,3712]{2,1,0:T(8,128)(2,1)S(1)}, bf16[2,24,3712]{2,1,0:T(8,128)(2,1)S(1)}, u32[]{:S(2)}, u32[]{:S(2)}) collective-permute-start(bf16[2,24,3712]{2,1,0:T(8,128)(2,1)S(1)} %pad_maximum_fusion.37), channel_id=1, source_target_pairs={{0,16},{1,17},{2,18},{3,19},{4,20},{5,21},{6,22},{7,23},{8,24},{9,... | collective-permute-start | bytes 1069064 | tf_op jit(solution)/shard_map/ppermute | solution.py:553
  54.8 25.5 %collective-permute-start.22 = (bf16[2,2,16,2048]{3,2,1,0:T(8,128)(2,1)S(1)}, bf16[2,2,16,2048]{3,2,1,0:T(8,128)(2,1)S(1)}, u32[]{:S(2)}, u32[]{:S(2)}) collective-permute-start(bf16[2,2,16,2048]{3,2,1,0:T(8,128)(2,1)S(1)} %pad_maximum_fusion.45), channel_id=1, source_target_pairs={{0,2},{1,3},{2,0},{3,1},{4,6},{5,7},{6,4},{7,5},{8,10},{9,11},{10,... | collective-permute-start | bytes 786440 | tf_op jit(solution)/shard_map/ppermute | solution.py:553
  57.8 24.8 %collective-permute-start.27 = (bf16[2,2,64,512]{3,2,1,0:T(8,128)(2,1)S(1)}, bf16[2,2,64,512]{3,2,1,0:T(8,128)(2,1)S(1)}, u32[]{:S(2)}, u32[]{:S(2)}) collective-permute-start(bf16[2,2,64,512]{3,2,1,0:T(8,128)(2,1)S(1)} %pad_maximum_fusion.46), channel_id=1, source_target_pairs={{0,4},{1,5},{2,6},{3,7},{4,0},{5,1},{6,2},{7,3},{8,12},{9,13},{10,... | collective-permute-start | bytes 786440 | tf_op jit(solution)/shard_map/ppermute | solution.py:553
  78.1 30.1 %collective-permute-start.7 = (bf16[2,2,24,3072]{3,2,1,0:T(8,128)(2,1)S(1)}, bf16[2,2,24,3072]{3,2,1,0:T(8,128)(2,1)S(1)}, u32[]{:S(2)}, u32[]{:S(2)}) collective-permute-start(bf16[2,2,24,3072]{3,2,1,0:T(8,128)(2,1)S(1)} %pad_maximum_fusion.26), channel_id=1, source_target_pairs={{0,4},{1,5},{2,6},{3,7},{4,0},{5,1},{6,2},{7,3},{8,12},{9,13},{10,... | collective-permute-start | bytes 1769480 | tf_op jit(solution)/shard_map/ppermute | solution.py:553
  80.3 28.7 %collective-permute-start.12 = (bf16[2,2,96,768]{3,2,1,0:T(8,128)(2,1)S(1)}, bf16[2,2,96,768]{3,2,1,0:T(8,128)(2,1)S(1)}, u32[]{:S(2)}, u32[]{:S(2)}) collective-permute-start(bf16[2,2,96,768]{3,2,1,0:T(8,128)(2,1)S(1)} %pad_maximum_fusion.27), channel_id=1, source_target_pairs={{0,2},{1,3},{2,0},{3,1},{4,6},{5,7},{6,4},{7,5},{8,10},{9,11},{10,... | collective-permute-start | bytes 1769480 | tf_op jit(solution)/shard_map/ppermute | solution.py:553
  82.6 20.2 %collective-permute-start.23 = (bf16[2,2,2,16,2048]{4,3,1,0,2:T(8,128)(2,1)S(1)}, bf16[2,2,2,16,2048]{4,3,1,0,2:T(8,128)(2,1)S(1)}, u32[]{:S(2)}, u32[]{:S(2)}) collective-permute-start(bf16[2,2,2,16,2048]{4,3,1,0,2:T(8,128)(2,1)S(1)} %pad_maximum_fusion.33), channel_id=1, source_target_pairs={{0,4},{1,5},{2,6},{3,7},{4,0},{5,1},{6,2},{7,3},{8,12},{9,13},{10,... | collective-permute-start | bytes 1572872 | tf_op jit(solution)/shard_map/ppermute | solution.py:553
  82.8 25.2 %collective-permute-start.28 = (bf16[2,2,2,64,512]{4,3,1,0,2:T(8,128)(2,1)S(1)}, bf16[2,2,2,64,512]{4,3,1,0,2:T(8,128)(2,1)S(1)}, u32[]{:S(2)}, u32[]{:S(2)}) collective-permute-start(bf16[2,2,2,64,512]{4,3,1,0,2:T(8,128)(2,1)S(1)} %pad_maximum_fusion.34), channel_id=1, source_target_pairs={{0,2},{1,3},{2,0},{3,1},{4,6},{5,7},{6,4},{7,5},{8,10},{9,11},{10,... | collective-permute-start | bytes 1572872 | tf_op jit(solution)/shard_map/ppermute | solution.py:553
  84.8 35.1 %collective-permute-start.18 = (bf16[2,2,2,16,2176]{4,3,1,0,2:T(8,128)(2,1)S(1)}, bf16[2,2,2,16,2176]{4,3,1,0,2:T(8,128)(2,1)S(1)}, u32[]{:S(2)}, u32[]{:S(2)}) collective-permute-start(bf16[2,2,2,16,2176]{4,3,1,0,2:T(8,128)(2,1)S(1)} %pad_maximum_fusion.30), channel_id=1, source_target_pairs={{0,2},{1,3},{2,0},{3,1},{4,6},{5,7},{6,4},{7,5},{8,10},{9,11},{10,... | collective-permute-start | bytes 1671176 | tf_op jit(solution)/shard_map/ppermute | solution.py:553
  102.8 32.4 %collective-permute-start.2 = (bf16[2,2,24,3712]{3,2,1,0:T(8,128)(2,1)S(1)}, bf16[2,2,24,3712]{3,2,1,0:T(8,128)(2,1)S(1)}, u32[]{:S(2)}, u32[]{:S(2)}) collective-permute-start(bf16[2,2,24,3712]{3,2,1,0:T(8,128)(2,1)S(1)} %pad_maximum_fusion.24), channel_id=1, source_target_pairs={{0,2},{1,3},{2,0},{3,1},{4,6},{5,7},{6,4},{7,5},{8,10},{9,11},{10,... | collective-permute-start | bytes 2138120 | tf_op jit(solution)/shard_map/ppermute | solution.py:553
  108.0 78.9 %collective-permute-start.24 = (bf16[2,2,2,2,16,2048]{5,4,1,0,3,2:T(8,128)(2,1)S(1)}, bf16[2,2,2,2,16,2048]{5,4,1,0,3,2:T(8,128)(2,1)S(1)}, u32[]{:S(2)}, u32[]{:S(2)}) collective-permute-start(bf16[2,2,2,2,16,2048]{5,4,1,0,3,2:T(8,128)(2,1)S(1)} %pad_maximum_fusion.20), channel_id=1, source_target_pairs={{0,1},{1,0},{2,3},{3,2},{4,5},{5,4},{6,7},{7,6},{8,9},{9,8},{10,11... | collective-permute-start | bytes 3145736 | tf_op jit(solution)/shard_map/ppermute | solution.py:553
  108.2 81.1 %collective-permute-start.29 = (bf16[2,2,2,2,64,512]{5,4,1,0,2,3:T(8,128)(2,1)S(1)}, bf16[2,2,2,2,64,512]{5,4,1,0,2,3:T(8,128)(2,1)S(1)}, u32[]{:S(2)}, u32[]{:S(2)}) collective-permute-start(bf16[2,2,2,2,64,512]{5,4,1,0,2,3:T(8,128)(2,1)S(1)} %pad_maximum_fusion.21), channel_id=1, source_target_pairs={{0,1},{1,0},{2,3},{3,2},{4,5},{5,4},{6,7},{7,6},{8,9},{9,8},{10,11... | collective-permute-start | bytes 3145736 | tf_op jit(solution)/shard_map/ppermute | solution.py:553
  108.9 47.8 %collective-permute-start.8 = (bf16[2,2,2,24,3072]{4,3,1,0,2:T(8,128)(2,1)S(1)}, bf16[2,2,2,24,3072]{4,3,1,0,2:T(8,128)(2,1)S(1)}, u32[]{:S(2)}, u32[]{:S(2)}) collective-permute-start(bf16[2,2,2,24,3072]{4,3,1,0,2:T(8,128)(2,1)S(1)} %pad_maximum_fusion.14), channel_id=1, source_target_pairs={{0,2},{1,3},{2,0},{3,1},{4,6},{5,7},{6,4},{7,5},{8,10},{9,11},{10,... | collective-permute-start | bytes 3538952 | tf_op jit(solution)/shard_map/ppermute | solution.py:553
  119.9 37.7 %collective-permute-start.13 = (bf16[2,2,2,96,768]{4,3,1,0,2:T(8,128)(2,1)S(1)}, bf16[2,2,2,96,768]{4,3,1,0,2:T(8,128)(2,1)S(1)}, u32[]{:S(2)}, u32[]{:S(2)}) collective-permute-start(bf16[2,2,2,96,768]{4,3,1,0,2:T(8,128)(2,1)S(1)} %pad_maximum_fusion.15), channel_id=1, source_target_pairs={{0,4},{1,5},{2,6},{3,7},{4,0},{5,1},{6,2},{7,3},{8,12},{9,13},{10,... | collective-permute-start | bytes 3538952 | tf_op jit(solution)/shard_map/ppermute | solution.py:553
  135.2 106.9 %collective-permute-start.19 = (bf16[2,2,2,2,16,2176]{5,4,1,0,2,3:T(8,128)(2,1)}, bf16[2,2,2,2,16,2176]{5,4,1,0,2,3:T(8,128)(2,1)S(1)}, u32[]{:S(2)}, u32[]{:S(2)}) collective-permute-start(bf16[2,2,2,2,16,2176]{5,4,1,0,2,3:T(8,128)(2,1)} %pad_maximum_fusion.18), channel_id=1, source_target_pairs={{0,1},{1,0},{2,3},{3,2},{4,5},{5,4},{6,7},{7,6},{8,9},{9,8},{10,11... | collective-permute-start | bytes 3342344 | tf_op jit(solution)/shard_map/ppermute | solution.py:553
  156.7 29.5 %collective-permute-start.3 = (bf16[2,2,2,24,3712]{4,3,1,0,2:T(8,128)(2,1)S(1)}, bf16[2,2,2,24,3712]{4,3,1,0,2:T(8,128)(2,1)S(1)}, u32[]{:S(2)}, u32[]{:S(2)}) collective-permute-start(bf16[2,2,2,24,3712]{4,3,1,0,2:T(8,128)(2,1)S(1)} %pad_maximum_fusion.12), channel_id=1, source_target_pairs={{0,4},{1,5},{2,6},{3,7},{4,0},{5,1},{6,2},{7,3},{8,12},{9,13},{10,... | collective-permute-start | bytes 4276232 | tf_op jit(solution)/shard_map/ppermute | solution.py:553
  157.6 33.6 %collective-permute-start.9 = (bf16[2,2,2,2,24,3072]{5,4,1,0,2,3:T(8,128)(2,1)S(1)}, bf16[2,2,2,2,24,3072]{5,4,1,0,2,3:T(8,128)(2,1)}, u32[]{:S(2)}, u32[]{:S(2)}) collective-permute-start(bf16[2,2,2,2,24,3072]{5,4,1,0,2,3:T(8,128)(2,1)S(1)} %pad_maximum_fusion.5), channel_id=1, source_target_pairs={{0,1},{1,0},{2,3},{3,2},{4,5},{5,4},{6,7},{7,6},{8,9},{9,8},{10,11... | collective-permute-start | bytes 7077896 | tf_op jit(solution)/shard_map/ppermute | solution.py:553
  376.5 18.8 %all-to-all-start.2 = ((bf16[4,2,128,512]{3,2,1,0:T(8,128)(2,1)}), bf16[4,2,128,512]{3,2,1,0:T(8,128)(2,1)}, u32[]{:S(2)}, u32[]{:S(2)}) async-start(bf16[4,2,128,512]{3,2,1,0:T(8,128)(2,1)} %bitcast.86), calls=%async_computation.2 | async-start | bytes 2097152 | tf_op jit(solution)/shard_map/all_to_all | solution.py:694
  382.4 66.4 %collective-permute-start.60 = (bf16[2,2,2,2,16,2176]{5,4,1,0,2,3:T(8,128)(2,1)}, bf16[2,2,2,2,16,2176]{5,4,1,0,2,3:T(8,128)(2,1)}, u32[]{:S(2)}, u32[]{:S(2)}) collective-permute-start(bf16[2,2,2,2,16,2176]{5,4,1,0,2,3:T(8,128)(2,1)} %bitcast.479), channel_id=1, source_target_pairs={{0,1},{1,0},{2,3},{3,2},{4,5},{5,4},{6,7},{7,6},{8,9},{9,8},{10,11... | collective-permute-start | bytes 3342344 | tf_op jit(solution)/shard_map/ppermute | solution.py:541
  384.5 59.5 %collective-permute-start.70 = (bf16[2,2,2,2,16,2048]{5,4,1,0,3,2:T(8,128)(2,1)}, bf16[2,2,2,2,16,2048]{5,4,1,0,3,2:T(8,128)(2,1)}, u32[]{:S(2)}, u32[]{:S(2)}) collective-permute-start(bf16[2,2,2,2,16,2048]{5,4,1,0,3,2:T(8,128)(2,1)} %bitcast.481), channel_id=1, source_target_pairs={{0,1},{1,0},{2,3},{3,2},{4,5},{5,4},{6,7},{7,6},{8,9},{9,8},{10,11... | collective-permute-start | bytes 3145736 | tf_op jit(solution)/shard_map/ppermute | solution.py:541
  386.6 59.6 %collective-permute-start.80 = (bf16[2,2,2,2,64,512]{5,4,1,0,2,3:T(8,128)(2,1)}, bf16[2,2,2,2,64,512]{5,4,1,0,2,3:T(8,128)(2,1)}, u32[]{:S(2)}, u32[]{:S(2)}) collective-permute-start(bf16[2,2,2,2,64,512]{5,4,1,0,2,3:T(8,128)(2,1)} %bitcast.480), channel_id=1, source_target_pairs={{0,1},{1,0},{2,3},{3,2},{4,5},{5,4},{6,7},{7,6},{8,9},{9,8},{10,11... | collective-permute-start | bytes 3145736 | tf_op jit(solution)/shard_map/ppermute | solution.py:541
  440.3 130.4 %collective-permute-start.30 = (bf16[2,2,2,2,24,3712]{5,4,1,0,3,2:T(8,128)(2,1)S(1)}, bf16[2,2,2,2,24,3712]{5,4,1,0,3,2:T(8,128)(2,1)S(1)}, u32[]{:S(2)}, u32[]{:S(2)}) collective-permute-start(bf16[2,2,2,2,24,3712]{5,4,1,0,3,2:T(8,128)(2,1)S(1)} %bitcast.515), channel_id=1, source_target_pairs={{0,1},{1,0},{2,3},{3,2},{4,5},{5,4},{6,7},{7,6},{8,9},{9,8},{10,11... | collective-permute-start | bytes 8552456 | tf_op jit(solution)/shard_map/ppermute | solution.py:541
  444.0 114.2 %collective-permute-start.50 = (bf16[2,2,2,2,96,768]{5,4,1,0,3,2:T(8,128)(2,1)S(1)}, bf16[2,2,2,2,96,768]{5,4,1,0,3,2:T(8,128)(2,1)S(1)}, u32[]{:S(2)}, u32[]{:S(2)}) collective-permute-start(bf16[2,2,2,2,96,768]{5,4,1,0,3,2:T(8,128)(2,1)S(1)} %bitcast.517), channel_id=1, source_target_pairs={{0,1},{1,0},{2,3},{3,2},{4,5},{5,4},{6,7},{7,6},{8,9},{9,8},{10,11... | collective-permute-start | bytes 7077896 | tf_op jit(solution)/shard_map/ppermute | solution.py:541
  444.1 115.5 %collective-permute-start.40 = (bf16[2,2,2,2,24,3072]{5,4,1,0,2,3:T(8,128)(2,1)S(1)}, bf16[2,2,2,2,24,3072]{5,4,1,0,2,3:T(8,128)(2,1)S(1)}, u32[]{:S(2)}, u32[]{:S(2)}) collective-permute-start(bf16[2,2,2,2,24,3072]{5,4,1,0,2,3:T(8,128)(2,1)S(1)} %bitcast.516), channel_id=1, source_target_pairs={{0,1},{1,0},{2,3},{3,2},{4,5},{5,4},{6,7},{7,6},{8,9},{9,8},{10,11... | collective-permute-start | bytes 7077896 | tf_op jit(solution)/shard_map/ppermute | solution.py:541
  490.0 18.8 %collective-permute-start.63 = (bf16[2,16,2176]{2,1,0:T(8,128)(2,1)S(1)}, bf16[2,16,2176]{2,1,0:T(8,128)(2,1)S(1)}, u32[]{:S(2)}, u32[]{:S(2)}) collective-permute-start(bf16[2,16,2176]{2,1,0:T(8,128)(2,1)S(1)} %dynamic-slice_bitcast_fusion.18), channel_id=1, source_target_pairs={{0,16},{1,17},{2,18},{3,19},{4,20},{5,21},{6,22},{7,23},{8,24},{9,... | collective-permute-start | bytes 417800 | tf_op jit(solution)/shard_map/ppermute | solution.py:541
  559.6 28.9 %collective-permute-start.51 = (bf16[2,2,2,96,768]{4,3,1,0,2:T(8,128)(2,1)S(1)}, bf16[2,2,2,96,768]{4,3,1,0,2:T(8,128)(2,1)S(1)}, u32[]{:S(2)}, u32[]{:S(2)}) collective-permute-start(bf16[2,2,2,96,768]{4,3,1,0,2:T(8,128)(2,1)S(1)} %dynamic-slice_bitcast_fusion.1), channel_id=1, source_target_pairs={{0,4},{1,5},{2,6},{3,7},{4,0},{5,1},{6,2},{7,3},{8,12},{9,13},{10,... | collective-permute-start | bytes 3538952 | tf_op jit(solution)/shard_map/ppermute | solution.py:541
  570.0 28.9 %collective-permute-start.41 = (bf16[2,2,2,24,3072]{4,3,1,0,2:T(8,128)(2,1)S(1)}, bf16[2,2,2,24,3072]{4,3,1,0,2:T(8,128)(2,1)S(1)}, u32[]{:S(2)}, u32[]{:S(2)}) collective-permute-start(bf16[2,2,2,24,3072]{4,3,1,0,2:T(8,128)(2,1)S(1)} %dynamic-slice_bitcast_fusion.2), channel_id=1, source_target_pairs={{0,2},{1,3},{2,0},{3,1},{4,6},{5,7},{6,4},{7,5},{8,10},{9,11},{10,... | collective-permute-start | bytes 3538952 | tf_op jit(solution)/shard_map/ppermute | solution.py:541
  570.6 30.0 %collective-permute-start.69 = (bf16[2,2,2,2,16,2176]{5,4,1,0,2,3:T(8,128)(2,1)S(1)}, bf16[2,2,2,2,16,2176]{5,4,1,0,2,3:T(8,128)(2,1)S(1)}, u32[]{:S(2)}, u32[]{:S(2)}) collective-permute-start(bf16[2,2,2,2,16,2176]{5,4,1,0,2,3:T(8,128)(2,1)S(1)} %pad_maximum_fusion.19), channel_id=1, source_target_pairs={{0,1},{1,0},{2,3},{3,2},{4,5},{5,4},{6,7},{7,6},{8,9},{9,8},{10,11... | collective-permute-start | bytes 3342344 | tf_op jit(solution)/shard_map/ppermute | solution.py:553
  571.6 59.5 %collective-permute-start.31 = (bf16[2,2,2,24,3712]{4,3,1,0,2:T(8,128)(2,1)S(1)}, bf16[2,2,2,24,3712]{4,3,1,0,2:T(8,128)(2,1)S(1)}, u32[]{:S(2)}, u32[]{:S(2)}) collective-permute-start(bf16[2,2,2,24,3712]{4,3,1,0,2:T(8,128)(2,1)S(1)} %dynamic-slice_bitcast_fusion), channel_id=1, source_target_pairs={{0,4},{1,5},{2,6},{3,7},{4,0},{5,1},{6,2},{7,3},{8,12},{9,13},{10,... | collective-permute-start | bytes 4276232 | tf_op jit(solution)/shard_map/ppermute | solution.py:541
  589.1 18.5 %collective-permute-start.52 = (bf16[2,2,96,768]{3,2,1,0:T(8,128)(2,1)S(1)}, bf16[2,2,96,768]{3,2,1,0:T(8,128)(2,1)S(1)}, u32[]{:S(2)}, u32[]{:S(2)}) collective-permute-start(bf16[2,2,96,768]{3,2,1,0:T(8,128)(2,1)S(1)} %dynamic-slice_bitcast_fusion.4), channel_id=1, source_target_pairs={{0,2},{1,3},{2,0},{3,1},{4,6},{5,7},{6,4},{7,5},{8,10},{9,11},{10,... | collective-permute-start | bytes 1769480 | tf_op jit(solution)/shard_map/ppermute | solution.py:541
  599.4 31.3 %collective-permute-start.42 = (bf16[2,2,24,3072]{3,2,1,0:T(8,128)(2,1)S(1)}, bf16[2,2,24,3072]{3,2,1,0:T(8,128)(2,1)S(1)}, u32[]{:S(2)}, u32[]{:S(2)}) collective-permute-start(bf16[2,2,24,3072]{3,2,1,0:T(8,128)(2,1)S(1)} %dynamic-slice_bitcast_fusion.5), channel_id=1, source_target_pairs={{0,4},{1,5},{2,6},{3,7},{4,0},{5,1},{6,2},{7,3},{8,12},{9,13},{10,... | collective-permute-start | bytes 1769480 | tf_op jit(solution)/shard_map/ppermute | solution.py:541
  607.8 25.3 %collective-permute-start.53 = (bf16[2,96,768]{2,1,0:T(8,128)(2,1)S(1)}, bf16[2,96,768]{2,1,0:T(8,128)(2,1)S(1)}, u32[]{:S(2)}, u32[]{:S(2)}) collective-permute-start(bf16[2,96,768]{2,1,0:T(8,128)(2,1)S(1)} %dynamic-slice_bitcast_fusion.10), channel_id=1, source_target_pairs={{0,16},{1,17},{2,18},{3,19},{4,20},{5,21},{6,22},{7,23},{8,24},{9,... | collective-permute-start | bytes 884744 | tf_op jit(solution)/shard_map/ppermute | solution.py:541
  631.5 28.6 %collective-permute-start.32 = (bf16[2,2,24,3712]{3,2,1,0:T(8,128)(2,1)S(1)}, bf16[2,2,24,3712]{3,2,1,0:T(8,128)(2,1)S(1)}, u32[]{:S(2)}, u32[]{:S(2)}) collective-permute-start(bf16[2,2,24,3712]{3,2,1,0:T(8,128)(2,1)S(1)} %dynamic-slice_bitcast_fusion.3), channel_id=1, source_target_pairs={{0,2},{1,3},{2,0},{3,1},{4,6},{5,7},{6,4},{7,5},{8,10},{9,11},{10,... | collective-permute-start | bytes 2138120 | tf_op jit(solution)/shard_map/ppermute | solution.py:541
  654.9 29.7 %collective-permute-start.56 = (bf16[2,96,768]{2,1,0:T(8,128)(2,1)S(1)}, bf16[2,96,768]{2,1,0:T(8,128)(2,1)S(1)}, u32[]{:S(2)}, u32[]{:S(2)}) collective-permute-start(bf16[2,96,768]{2,1,0:T(8,128)(2,1)S(1)} %pad_maximum_fusion.42), channel_id=1, source_target_pairs={{0,16},{1,17},{2,18},{3,19},{4,20},{5,21},{6,22},{7,23},{8,24},{9,... | collective-permute-start | bytes 884744 | tf_op jit(solution)/shard_map/ppermute | solution.py:553
  659.7 37.3 %collective-permute-start.46 = (bf16[2,24,3072]{2,1,0:T(8,128)(2,1)S(1)}, bf16[2,24,3072]{2,1,0:T(8,128)(2,1)S(1)}, u32[]{:S(2)}, u32[]{:S(2)}) collective-permute-start(bf16[2,24,3072]{2,1,0:T(8,128)(2,1)S(1)} %pad_maximum_fusion.41), channel_id=1, source_target_pairs={{0,16},{1,17},{2,18},{3,19},{4,20},{5,21},{6,22},{7,23},{8,24},{9,... | collective-permute-start | bytes 884744 | tf_op jit(solution)/shard_map/ppermute | solution.py:553
  660.3 35.9 %collective-permute-start.33 = (bf16[2,24,3712]{2,1,0:T(8,128)(2,1)S(1)}, bf16[2,24,3712]{2,1,0:T(8,128)(2,1)S(1)}, u32[]{:S(2)}, u32[]{:S(2)}) collective-permute-start(bf16[2,24,3712]{2,1,0:T(8,128)(2,1)S(1)} %dynamic-slice_bitcast_fusion.9), channel_id=1, source_target_pairs={{0,16},{1,17},{2,18},{3,19},{4,20},{5,21},{6,22},{7,23},{8,24},{9,... | collective-permute-start | bytes 1069064 | tf_op jit(solution)/shard_map/ppermute | solution.py:541
  684.7 25.7 %collective-permute-start.57 = (bf16[2,2,96,768]{3,2,1,0:T(8,128)(2,1)S(1)}, bf16[2,2,96,768]{3,2,1,0:T(8,128)(2,1)S(1)}, u32[]{:S(2)}, u32[]{:S(2)}) collective-permute-start(bf16[2,2,96,768]{3,2,1,0:T(8,128)(2,1)S(1)} %pad_maximum_fusion.29), channel_id=1, source_target_pairs={{0,2},{1,3},{2,0},{3,1},{4,6},{5,7},{6,4},{7,5},{8,10},{9,11},{10,... | collective-permute-start | bytes 1769480 | tf_op jit(solution)/shard_map/ppermute | solution.py:553
  703.2 23.2 %collective-permute-start.47 = (bf16[2,2,24,3072]{3,2,1,0:T(8,128)(2,1)S(1)}, bf16[2,2,24,3072]{3,2,1,0:T(8,128)(2,1)S(1)}, u32[]{:S(2)}, u32[]{:S(2)}) collective-permute-start(bf16[2,2,24,3072]{3,2,1,0:T(8,128)(2,1)S(1)} %pad_maximum_fusion.28), channel_id=1, source_target_pairs={{0,4},{1,5},{2,6},{3,7},{4,0},{5,1},{6,2},{7,3},{8,12},{9,13},{10,... | collective-permute-start | bytes 1769480 | tf_op jit(solution)/shard_map/ppermute | solution.py:553
  710.6 34.6 %collective-permute-start.58 = (bf16[2,2,2,96,768]{4,3,1,0,2:T(8,128)(2,1)S(1)}, bf16[2,2,2,96,768]{4,3,1,0,2:T(8,128)(2,1)S(1)}, u32[]{:S(2)}, u32[]{:S(2)}) collective-permute-start(bf16[2,2,2,96,768]{4,3,1,0,2:T(8,128)(2,1)S(1)} %pad_maximum_fusion.17), channel_id=1, source_target_pairs={{0,4},{1,5},{2,6},{3,7},{4,0},{5,1},{6,2},{7,3},{8,12},{9,13},{10,... | collective-permute-start | bytes 3538952 | tf_op jit(solution)/shard_map/ppermute | solution.py:553
  724.6 19.0 %collective-permute-start.37 = (bf16[2,2,24,3712]{3,2,1,0:T(8,128)(2,1)S(1)}, bf16[2,2,24,3712]{3,2,1,0:T(8,128)(2,1)S(1)}, u32[]{:S(2)}, u32[]{:S(2)}) collective-permute-start(bf16[2,2,24,3712]{3,2,1,0:T(8,128)(2,1)S(1)} %pad_maximum_fusion.25), channel_id=1, source_target_pairs={{0,2},{1,3},{2,0},{3,1},{4,6},{5,7},{6,4},{7,5},{8,10},{9,11},{10,... | collective-permute-start | bytes 2138120 | tf_op jit(solution)/shard_map/ppermute | solution.py:553
  726.6 40.3 %collective-permute-start.48 = (bf16[2,2,2,24,3072]{4,3,1,0,2:T(8,128)(2,1)S(1)}, bf16[2,2,2,24,3072]{4,3,1,0,2:T(8,128)(2,1)S(1)}, u32[]{:S(2)}, u32[]{:S(2)}) collective-permute-start(bf16[2,2,2,24,3072]{4,3,1,0,2:T(8,128)(2,1)S(1)} %pad_maximum_fusion.16), channel_id=1, source_target_pairs={{0,2},{1,3},{2,0},{3,1},{4,6},{5,7},{6,4},{7,5},{8,10},{9,11},{10,... | collective-permute-start | bytes 3538952 | tf_op jit(solution)/shard_map/ppermute | solution.py:553
  743.9 29.5 %collective-permute-start.38 = (bf16[2,2,2,24,3712]{4,3,1,0,2:T(8,128)(2,1)S(1)}, bf16[2,2,2,24,3712]{4,3,1,0,2:T(8,128)(2,1)S(1)}, u32[]{:S(2)}, u32[]{:S(2)}) collective-permute-start(bf16[2,2,2,24,3712]{4,3,1,0,2:T(8,128)(2,1)S(1)} %pad_maximum_fusion.13), channel_id=1, source_target_pairs={{0,4},{1,5},{2,6},{3,7},{4,0},{5,1},{6,2},{7,3},{8,12},{9,13},{10,... | collective-permute-start | bytes 4276232 | tf_op jit(solution)/shard_map/ppermute | solution.py:553
  747.0 37.6 %collective-permute-start.59 = (bf16[2,2,2,2,96,768]{5,4,1,0,3,2:T(8,128)(2,1)}, bf16[2,2,2,2,96,768]{5,4,1,0,3,2:T(8,128)(2,1)}, u32[]{:S(2)}, u32[]{:S(2)}) collective-permute-start(bf16[2,2,2,2,96,768]{5,4,1,0,3,2:T(8,128)(2,1)} %pad_maximum_fusion.8), channel_id=1, source_target_pairs={{0,1},{1,0},{2,3},{3,2},{4,5},{5,4},{6,7},{7,6},{8,9},{9,8},{10,11... | collective-permute-start | bytes 7077896 | tf_op jit(solution)/shard_map/ppermute | solution.py:553
  774.0 18.1 %collective-permute-start.39 = (bf16[2,2,2,2,24,3712]{5,4,1,0,3,2:T(8,128)(2,1)S(1)}, bf16[2,2,2,2,24,3712]{5,4,1,0,3,2:T(8,128)(2,1)}, u32[]{:S(2)}, u32[]{:S(2)}) collective-permute-start(bf16[2,2,2,2,24,3712]{5,4,1,0,3,2:T(8,128)(2,1)S(1)} %pad_maximum_fusion.4), channel_id=1, source_target_pairs={{0,1},{1,0},{2,3},{3,2},{4,5},{5,4},{6,7},{7,6},{8,9},{9,8},{10,11... | collective-permute-start | bytes 8552456 | tf_op jit(solution)/shard_map/ppermute | solution.py:553
  (66 other events, 624.3 us)

commit v3 on v2

--- a/solution.py
+++ b/solution.py
@@ -1,3 +1,4 @@
+import functools
 import math
 
 import jax
@@ -19,6 +20,7 @@
 F32 = jnp.float32
 BF16 = jnp.bfloat16
 LANES = 128
+VMEM_BYTES = 58 * 1024 * 1024
 
 
 def mm(a, b):
@@ -71,6 +73,16 @@
     return cdf, u * bell * 0.3989422804014327
 
 
+def vectors_of(small_ref):
+    return small_ref[...].astype(F32).T[0:8, :]
+
+
+def columns_of_vectors(vectors):
+    count, width = vectors.shape
+    block = jnp.concatenate([vectors, jnp.zeros((LANES - count, width), F32)], axis=0)
+    return block.T.astype(BF16)
+
+
 def segment_sum(x, ones):
     high = x.astype(BF16)
     low = (x - high.astype(F32)).astype(BF16)
@@ -87,9 +99,10 @@
 
 
 def decoder_kernel(
-    rows_ref, idx_ref, cot_ref, pos_ref, mask_ref, vec_ref, wqkv_ref, wo_ref, wu_ref, wd_ref,
-    out_ref, ret_ref, gqkv_ref, go_ref, gu_ref, gd_ref, gvec_ref,
-    acc_qkv, acc_o, acc_u, acc_d, x_s, qkv_s, p_s, o_s, a2_s, a2t_s, dzt_s, da_s, y_s, dqkv_s,
+    rows_ref, idx_ref, cot_ref, pos_ref, mask_ref, small_ref, wqkv_ref, wo_ref, wu_ref, wd_ref,
+    out_ref, ret_ref, grad_ref,
+    acc_qkv, acc_o, acc_u, acc_d, gvec_ref, vec_ref,
+    x_s, qkv_s, p_s, o_s, a2_s, a2t_s, dzt_s, da_s, y_s, dqkv_s,
 ):
     step = pl.program_id(0)
     last = pl.num_programs(0) - 1
@@ -112,6 +125,7 @@
         acc_u[...] = jnp.zeros_like(acc_u)
         acc_d[...] = jnp.zeros_like(acc_d)
         gvec_ref[...] = jnp.zeros_like(gvec_ref)
+        vec_ref[...] = vectors_of(small_ref)
 
     gain1, shift1 = vec_ref[0:1, :], vec_ref[1:2, :]
     gain2, shift2 = vec_ref[2:3, :], vec_ref[3:4, :]
@@ -236,21 +250,26 @@
 
     @pl.when(step == last)
     def _():
-        gqkv_ref[...] = acc_qkv[...].astype(BF16)
-        go_ref[...] = acc_o[...].astype(BF16)
-        gu_ref[...] = acc_u[...].astype(BF16)
-        for c in range(ff // chunk):
-            gd_ref[c * chunk : (c + 1) * chunk, :] = acc_d[:, c * chunk : (c + 1) * chunk].T.astype(BF16)
-
-
-def decoder_block(rows, idx, cot, pos, mask, vecs, wqkv, wo, wu, wd):
+        grad_ref[:, : 3 * width] = acc_qkv[...].astype(BF16)
+        grad_ref[:, 3 * width : 4 * width] = acc_o[...].astype(BF16)
+        grad_ref[:, 4 * width : 4 * width + ff] = acc_u[...].astype(BF16)
+        grad_ref[:, 4 * width + ff : 4 * width + 2 * ff] = acc_d[...].astype(BF16)
+        grad_ref[:, 4 * width + 2 * ff :] = columns_of_vectors(gvec_ref[...])
+
+
+def decoder_block(rows, idx, cot, pos, mask, pack, wd):
     n_half, slots, width = rows.shape
     cells = cot.shape[1]
-    ff = wu.shape[1]
+    ff = wd.shape[0]
     halves = 2
     m_rows = halves * cells
-    whole = lambda *shape: pl.BlockSpec(shape, lambda i: (0,) * len(shape), pipeline_mode=pl.Buffered(1))
     vm = pltpu.VMEM
+    flops = 6 * n_half * cells * (4 * width + 2 * ff) * width * 2
+
+    def whole(*shape, at=0):
+        index = (0,) * (len(shape) - 1) + (at,)
+        return pl.BlockSpec(shape, lambda i: index, pipeline_mode=pl.Buffered(1))
+
     return pl.pallas_call(
         decoder_kernel,
         grid=(n_half // halves,),
@@ -260,35 +279,29 @@
             pl.BlockSpec((halves, cells, width), lambda i: (i, 0, 0)),
             whole(cells, width),
             whole(cells, LANES),
-            whole(8, width),
+            whole(width, LANES, at=(4 * width + 2 * ff) // LANES),
             whole(width, 3 * width),
-            whole(width, width),
-            whole(width, ff),
+            whole(width, width, at=3),
+            whole(width, ff, at=1),
             whole(ff, width),
         ],
         out_specs=[
             pl.BlockSpec((halves, cells, width), lambda i: (i, 0, 0)),
             pl.BlockSpec((halves, slots, width), lambda i: (i, 0, 0)),
-            whole(width, 3 * width),
-            whole(width, width),
-            whole(width, ff),
-            whole(ff, width),
-            whole(8, width),
+            whole(width, 4 * width + 2 * ff + LANES),
         ],
         out_shape=[
             jax.ShapeDtypeStruct((n_half, cells, width), BF16),
             jax.ShapeDtypeStruct((n_half, slots, width), BF16),
-            jax.ShapeDtypeStruct((width, 3 * width), BF16),
-            jax.ShapeDtypeStruct((width, width), BF16),
-            jax.ShapeDtypeStruct((width, ff), BF16),
-            jax.ShapeDtypeStruct((ff, width), BF16),
-            jax.ShapeDtypeStruct((8, width), F32),
+            jax.ShapeDtypeStruct((width, 4 * width + 2 * ff + LANES), BF16),
         ],
         scratch_shapes=[
             vm((width, 3 * width), F32),
             vm((width, width), F32),
             vm((width, ff), F32),
             vm((width, ff), F32),
+            vm((8, width), F32),
+            vm((8, width), F32),
             vm((m_rows, width), F32),
             vm((m_rows, 3 * width), BF16),
             vm((m_rows, width), F32),
@@ -301,10 +314,11 @@
             vm((m_rows, 3 * width), BF16),
         ],
         compiler_params=pltpu.CompilerParams(
-            dimension_semantics=("arbitrary",), vmem_limit_bytes=58 * 1024 * 1024
+            dimension_semantics=("arbitrary",), vmem_limit_bytes=VMEM_BYTES
         ),
+        cost_estimate=pl.CostEstimate(flops=flops, bytes_accessed=40 << 20, transcendentals=0),
         name="decoder_block",
-    )(rows, idx.reshape(n_half, 1, slots), cot, pos, mask, vecs, wqkv, wo, wu, wd)
+    )(rows, idx.reshape(n_half, 1, slots), cot, pos, mask, pack, pack, pack, pack, wd)
 
 
 def enc_spread(t, head_masks):
@@ -317,7 +331,10 @@
     return head_dim, [(lane // head_dim == h) for h in range(LANES // head_dim)]
 
 
-def enc_attend_kernel(x_ref, mask_ref, vec_ref, wqkv_ref, wo_ref, qkv_ref, p_ref, o_ref, x2_ref):
+def enc_attend_kernel(
+    x_ref, mask_ref, small_ref, wqkv_ref, wo_ref, qkv_ref, p_ref, o_ref, x2_ref, vec_ref
+):
+    vec_ref[...] = vectors_of(small_ref)
     clips, slots, width = x_ref.shape
     m_rows = clips * slots
     head_dim, head_masks = enc_heads(width)
@@ -372,7 +389,7 @@
 
 def enc_feed_back_kernel(
     dsent_ref, enc_ref, proj_ref, h_ref, gp_ref, x2_ref, vec_ref, wu_ref, wd_ref,
-    gproj_ref, gu_ref, gd_ref, dx2_ref, gvec_ref,
+    gproj_ref, grad_ref, dx2_ref, gvec_ref,
     a2t_s, dz_s, dzt_s, da_s,
 ):
     ff = wu_ref.shape[1]
@@ -393,8 +410,9 @@
         at = pl.ds(pl.multiple_of(c * chunk, chunk), chunk)
         dh = mm_t(dz_s[...], wd_ref[at, :])
         du = (gp_ref[:, at].astype(F32) * dh).astype(BF16)
-        gd_ref[at, :] = mm(dzt_s[...], h_ref[:, at]).T.astype(BF16)
-        gu_ref[:, at] = mm(a2t_s[...], du).astype(BF16)
+        below = pl.ds(pl.multiple_of(ff + c * chunk, chunk), chunk)
+        grad_ref[:, at] = mm(a2t_s[...], du).astype(BF16)
+        grad_ref[:, below] = mm(dzt_s[...], h_ref[:, at]).astype(BF16)
         da_s[...] += mm_t(du, wu_ref[:, at])
         return carry
 
@@ -408,9 +426,9 @@
 
 
 def enc_attend_back_kernel(
-    dx2_ref, o_ref, qkv_ref, p_ref, x_ref, vec_ref, wqkv_ref, wo_ref,
-    gqkv_ref, go_ref, dvis_ref, gvec_ref,
-    do_s, dqkv_s,
+    dx2_ref, o_ref, qkv_ref, p_ref, x_ref, vec_ref, wqkv_ref, wo_ref, gproj_ref, gvec2_ref,
+    grad_ref, dvis_ref,
+    gvec_ref, do_s, dqkv_s,
 ):
     clips, slots, width = x_ref.shape
     m_rows = clips * slots
@@ -419,7 +437,7 @@
     scale = head_dim ** (-0.5)
     gain1, shift1 = vec_ref[0:1, :], vec_ref[1:2, :]
     dy2 = dx2_ref[...].astype(BF16)
-    go_ref[...] = mm(o_ref[...].T, dy2).astype(BF16)
+    grad_ref[:, 3 * width : 4 * width] = mm(o_ref[...].T, dy2).astype(BF16)
     do_s[...] = mm_t(dy2, wo_ref[...]).astype(BF16)
 
     def fold(t):
@@ -452,120 +470,237 @@
     x = x_ref[...].reshape(m_rows, width).astype(F32)
     xhat, rstd = normalise(x)
     a1t = (xhat * gain1 + shift1).astype(BF16).T
-    gqkv_ref[...] = mm(a1t, dqkv_s[...]).astype(BF16)
+    grad_ref[:, : 3 * width] = mm(a1t, dqkv_s[...]).astype(BF16)
     da = mm_t(dqkv_s[...], wqkv_ref[...])
-    gvec_ref[...] = jnp.zeros_like(gvec_ref)
+    gvec_ref[...] = gvec2_ref[...]
     gvec_ref[0:1, :] = jnp.sum(da * xhat, axis=0, keepdims=True)
     gvec_ref[1:2, :] = jnp.sum(da, axis=0, keepdims=True)
     dx = dx2_ref[...] + norm_back(da, xhat, rstd, gain1)
     dvis_ref[...] = dx.reshape(clips, slots, width).astype(BF16)
-
-
-def whole_call(kernel, outs, scratch, name, *args):
+    grad_ref[:, 4 * width : -LANES] = gproj_ref[...]
+    grad_ref[:, -LANES:] = columns_of_vectors(gvec_ref[...])
+
+
+def whole_call(kernel, args, outs, scratch, name, flops):
+    arrays, specs = [], []
+    for arg in args:
+        array, shape, at = arg if isinstance(arg, tuple) else (arg, arg.shape, 0)
+        index = (0,) * (len(shape) - 1) + (at,)
+        arrays.append(array)
+        specs.append(pl.BlockSpec(shape, lambda i, index=index: index, pipeline_mode=pl.Buffered(1)))
+    zero = lambda shape: pl.BlockSpec(shape, lambda i: (0,) * len(shape), pipeline_mode=pl.Buffered(1))
     return pl.pallas_call(
         kernel,
+        grid=(1,),
+        in_specs=specs,
+        out_specs=[zero(s) for s, _ in outs],
         out_shape=[jax.ShapeDtypeStruct(s, d) for s, d in outs],
         scratch_shapes=[pltpu.VMEM(s, d) for s, d in scratch],
-        compiler_params=pltpu.CompilerParams(vmem_limit_bytes=58 * 1024 * 1024),
+        compiler_params=pltpu.CompilerParams(vmem_limit_bytes=VMEM_BYTES),
+        cost_estimate=pl.CostEstimate(flops=flops, bytes_accessed=16 << 20, transcendentals=0),
         name=name,
-    )(*args)
-
-
-def enc_attend(x, mask, vecs, wqkv, wo):
+    )(*arrays)
+
+
+def enc_blocks(pack, width, ff, sent):
+    return (
+        (pack, (width, 3 * width), 0),
+        (pack, (width, width), 3),
+        (pack, (width, ff), 4 * width // ff),
+        (pack, (width, sent), (4 * width + ff) // sent),
+        (pack, (width, LANES), (4 * width + ff + sent) // LANES),
+    )
+
+
+def enc_attend(x, mask, blocks):
     clips, slots, width = x.shape
     m = clips * slots
-    outs = [((m, 3 * width), BF16), ((m, HEADS_ENC * slots), BF16), ((m, width), BF16), ((m, width), F32)]
-    return whole_call(enc_attend_kernel, outs, [], "enc_attend", x, mask, vecs, wqkv, wo)
-
-
-def enc_feed(x2, vecs, wu, wd, proj):
+    outs = [
+        ((m, 3 * width), BF16),
+        ((m, HEADS_ENC * slots), BF16),
+        ((m, width), BF16),
+        ((m, width), F32),
+        ((8, width), F32),
+    ]
+    qkv, out, _, _, small = blocks
+    return whole_call(enc_attend_kernel, (x, mask, small, qkv, out), outs, [], "enc_attend", 10**10)
+
+
+def enc_feed(x2, vecs, blocks, wd):
     m, width = x2.shape
-    ff = wu.shape[1]
-    outs = [((m, proj.shape[1]), BF16), ((m, width), BF16), ((m, ff), BF16), ((m, ff), BF16)]
+    ff = wd.shape[0]
+    _, _, up, proj, _ = blocks
+    outs = [((m, proj[1][1]), BF16), ((m, width), BF16), ((m, ff), BF16), ((m, ff), BF16)]
     scratch = [((m, width), BF16), ((m, width), F32)]
-    return whole_call(enc_feed_kernel, outs, scratch, "enc_feed", x2, vecs, wu, wd, proj)
-
-
-def enc_feed_back(dsent, enc, proj, h, gp, x2, vecs, wu, wd):
+    return whole_call(enc_feed_kernel, (x2, vecs, up, wd, proj), outs, scratch, "enc_feed", 18 * 10**9)
+
+
+def enc_feed_back(dsent, enc, h, gp, x2, vecs, blocks, wd):
     m, width = x2.shape
-    ff = wu.shape[1]
-    outs = [(proj.shape, BF16), (wu.shape, BF16), (wd.shape, BF16), ((m, width), F32), ((8, width), F32)]
+    ff = wd.shape[0]
+    _, _, up, proj, _ = blocks
+    outs = [(proj[1], BF16), ((width, 2 * ff), BF16), ((m, width), F32), ((8, width), F32)]
     scratch = [((width, m), BF16), ((m, width), BF16), ((width, m), BF16), ((m, width), F32)]
-    return whole_call(
-        enc_feed_back_kernel, outs, scratch, "enc_feed_back", dsent, enc, proj, h, gp, x2, vecs, wu, wd
-    )
-
-
-def enc_attend_back(dx2, o, qkv, p, x, vecs, wqkv, wo):
+    args = (dsent, enc, proj, h, gp, x2, vecs, up, wd)
+    return whole_call(enc_feed_back_kernel, args, outs, scratch, "enc_feed_back", 24 * 10**9)
+
+
+def enc_attend_back(dx2, o, qkv, p, x, vecs, blocks, gproj, gvec):
     m, width = dx2.shape
-    outs = [(wqkv.shape, BF16), (wo.shape, BF16), (x.shape, BF16), ((8, width), F32)]
-    scratch = [((m, width), BF16), ((m, 3 * width), BF16)]
-    return whole_call(
-        enc_attend_back_kernel, outs, scratch, "enc_attend_back", dx2, o, qkv, p, x, vecs, wqkv, wo
-    )
+    w_qkv, w_out, _, _, _ = blocks
+    outs = [((width, 4 * width + gproj.shape[1] + LANES), BF16), (x.shape, BF16)]
+    scratch = [((8, width), F32), ((m, width), BF16), ((m, 3 * width), BF16)]
+    args = (dx2, o, qkv, p, x, vecs, w_qkv, w_out, gproj, gvec)
+    return whole_call(enc_attend_back_kernel, args, outs, scratch, "enc_attend_back", 14 * 10**9)
+
+
+def unpack_kernel(spans, tall, sum_ref, *out_refs):
+    for (start, size), ref in zip(spans, out_refs[:-2]):
+        ref[...] = sum_ref[:, start : start + size].astype(F32)
+    start, size = tall
+    chunk = 512
+    for c in range(size // chunk):
+        part = sum_ref[:, start + c * chunk : start + (c + 1) * chunk].astype(F32)
+        out_refs[-2][c * chunk : (c + 1) * chunk, :] = part.T
+    out_refs[-1][...] = sum_ref[:, start + size :].astype(F32).T[0:8, :]
+
+
+def unpack_sums(packed, spans, tall):
+    rows, wide = packed.shape
+    step = LANES
+    size = tall[1]
+    side = lambda n: pl.BlockSpec((step, n), lambda i: (i, 0))
+    down = lambda n: pl.BlockSpec((n, step), lambda i: (0, i))
+    return pl.pallas_call(
+        functools.partial(unpack_kernel, spans, tall),
+        grid=(rows // step,),
+        in_specs=[side(wide)],
+        out_specs=[side(n) for _, n in spans] + [down(size), down(8)],
+        out_shape=[jax.ShapeDtypeStruct((rows, n), F32) for _, n in spans]
+        + [jax.ShapeDtypeStruct((size, rows), F32), jax.ShapeDtypeStruct((8, rows), F32)],
+        compiler_params=pltpu.CompilerParams(vmem_limit_bytes=VMEM_BYTES),
+        cost_estimate=pl.CostEstimate(flops=0, bytes_accessed=6 * rows * wide, transcendentals=0),
+        name="unpack_sums",
+    )(packed)
 
 
 AXES = ("clip", "band")
 
 
-def split_bits(parts):
-    return parts.bit_length() - 1
-
-
-def bit_order(count):
-    first = [b for b in (0, 2, 1) if b < count]
-    rest = [b for b in range(count - 1, -1, -1) if b not in first]
-    return first + rest
-
-
-def swap_order(order):
-    if len(order) < 3:
-        return order
-    return [order[0], order[2], order[1]] + order[3:]
-
-
-def partner_pairs(total, bit):
-    return [(i, i ^ (1 << bit)) for i in range(total)]
-
-
-def scatter_sum(partial, total, order):
-    me = lax.axis_index(AXES)
-    left = list(range(split_bits(total) - 1, -1, -1))
-    rows = partial.shape[0] // total
-    held = partial.reshape((2,) * len(left) + (rows,) + partial.shape[1:])
-    for bit in order:
-        place = left.index(bit)
-        mine = (me >> bit) & 1
-        keep = lax.dynamic_index_in_dim(held, mine, place, keepdims=False)
-        give = lax.dynamic_index_in_dim(held, 1 - mine, place, keepdims=False)
-        got = lax.ppermute(give, AXES, partner_pairs(total, bit))
-        held = (keep.astype(F32) + got.astype(F32)).astype(BF16)
-        left.remove(bit)
-    return held
-
-
-def gather_rows(shard, total, order):
-    me = lax.axis_index(AXES)
-    have = []
-    held = shard
-    for bit in reversed(order):
-        mine = (me >> bit) & 1
-        got = lax.ppermute(held, AXES, partner_pairs(total, bit))
-        low = jnp.where(mine == 0, held, got)
-        high = jnp.where(mine == 0, got, held)
-        have = sorted(have + [bit], reverse=True)
-        held = jnp.stack([low, high], axis=have.index(bit))
-    return held.reshape((total * shard.shape[0],) + shard.shape[1:])
+def partner_pairs(total, mask):
+    return [(i, i ^ mask) for i in range(total)]
+
+
+def add_low(*parts):
+    return sum(part.astype(F32) for part in parts).astype(BF16)
+
+
+class RunningSum:
+    def __init__(self, partial, total, cut):
+        bits = total.bit_length() - 1
+        rows = partial.shape[0] // total
+        self.total = total
+        self.held = [partial.reshape((2,) * bits + (rows, partial.shape[1]))]
+        self.left = [list(range(bits - 1, -1, -1))]
+        self.cut = cut
+        self.plan = [[[0]], [[2], [1]], [[1], [2]]]
+        rest = list(range(3, bits))
+        while rest:
+            self.plan.append([rest[:2]])
+            rest = rest[2:]
+
+    def offers(self):
+        me = lax.axis_index(AXES)
+        groups = self.plan[0]
+        if len(groups) > len(self.held):
+            (held,), (left,) = self.held, self.left
+            self.held = [held[..., : self.cut], held[..., self.cut :]]
+            self.left = [list(left), list(left)]
+        if len(groups) < len(self.held):
+            self.held = [jnp.concatenate(self.held, axis=-1)]
+            self.left = self.left[:1]
+        self.keep, gives, self.masks = [], [], []
+        for held, left, group in zip(self.held, self.left, groups):
+            low, ways = group[0], 1 << len(group)
+            place = left.index(group[-1])
+            mine = (me >> low) & (ways - 1)
+            shape = held.shape
+            held = held.reshape(shape[:place] + (ways,) + shape[place + len(group) :])
+            self.keep.append(lax.dynamic_index_in_dim(held, mine, place, keepdims=False))
+            for k in range(1, ways):
+                gives.append(lax.dynamic_index_in_dim(held, mine ^ k, place, keepdims=False))
+                self.masks.append(k << low)
+            for bit in group:
+                left.remove(bit)
+        return gives
+
+    def deliver(self, gives):
+        got = [
+            lax.ppermute(give, AXES, partner_pairs(self.total, mask))
+            for give, mask in zip(gives, self.masks)
+        ]
+        each = len(got) // len(self.keep)
+        self.held = [
+            add_low(keep, *got[i * each : (i + 1) * each]) for i, keep in enumerate(self.keep)
+        ]
+        self.plan = self.plan[1:]
+
+    def step(self):
+        self.deliver(self.offers())
+
+    def finish(self):
+        while self.plan:
+            self.step()
+        return jnp.concatenate(self.held, axis=-1)
+
+
+def together(*groups):
+    return lax.optimization_barrier(groups)
+
+
+def gather_rows(shard):
+    return lax.all_gather(shard, AXES, axis=0, tiled=True)
 
 
 def columns_of(vectors):
     block = jnp.stack(vectors, axis=1)
-    return jnp.pad(block, ((0, 0), (0, LANES - len(vectors)))).astype(BF16)
-
-
-def rows_of(block, count):
-    vectors = block[:, :count].T.astype(F32)
-    return jnp.pad(vectors, ((0, 8 - count), (0, 0)))
+    return jnp.pad(block, ((0, 0), (0, LANES - len(vectors))))
+
+
+def blocks_beside(tall, rows):
+    return [tall[i : i + rows] for i in range(0, tall.shape[0], rows)]
+
+
+def blocks_below(beside, total, width):
+    rows = beside.shape[0] // total
+    count = beside.shape[1] // width
+    parts = [beside[:, i * width : (i + 1) * width].reshape(total, rows, width) for i in range(count)]
+    return jnp.concatenate(parts, axis=1).reshape(-1, width)
+
+
+def swap_band(array, bit):
+    return lax.ppermute(array, "band", [(i, i ^ bit) for i in range(4)])
+
+
+def owners_to_bands(array):
+    band = lax.axis_index("band")
+    half, side = band // 2, band % 2
+    own = lax.dynamic_index_in_dim(array, half, 0, keepdims=False)
+    got = swap_band(lax.dynamic_index_in_dim(array, 1 - half, 0, keepdims=False), 2)
+    pair = jnp.stack([jnp.where(half == 0, own, got), jnp.where(half == 0, got, own)])
+    other = swap_band(pair, 1)
+    return jnp.stack([jnp.where(side == 0, pair, other), jnp.where(side == 0, other, pair)], axis=1)
+
+
+def bands_to_owners(array):
+    band = lax.axis_index("band")
+    half, side = band // 2, band % 2
+    own = lax.dynamic_index_in_dim(array, side, 1, keepdims=False)
+    got = swap_band(lax.dynamic_index_in_dim(array, 1 - side, 1, keepdims=False), 1)
+    pair = own + got
+    own = lax.dynamic_index_in_dim(pair, half, 0, keepdims=False)
+    got = swap_band(lax.dynamic_index_in_dim(pair, 1 - half, 0, keepdims=False), 2)
+    return jnp.stack([jnp.where(half == 0, own, got), jnp.where(half == 0, got, own)])
 
 
 def position_table(places):
@@ -602,32 +737,22 @@
     cotangent,
 ):
     total = lax.axis_size(AXES)
-    order = bit_order(split_bits(total))
-    order_two = swap_order(order)
-    enc_wide = enc_out.shape[1]
-    dec_wide = dec_out.shape[1]
-    pack_one = jnp.concatenate(
-        [enc_qkv, enc_out, proj, columns_of([enc_gain1, enc_shift1, enc_gain2, enc_shift2])], axis=1
-    )
-    pack_one = gather_rows(pack_one, total, order)
-    whole_up = gather_rows(enc_up, total, order_two)
-    whole_down = gather_rows(enc_down, total, order)
-    enc_vecs = rows_of(pack_one[:, 4 * enc_wide + dec_wide :], 4)
-    whole_qkv = pack_one[:, : 3 * enc_wide]
-    whole_out = pack_one[:, 3 * enc_wide : 4 * enc_wide]
-    whole_proj = pack_one[:, 4 * enc_wide : 4 * enc_wide + dec_wide]
-    pack_two = jnp.concatenate(
-        [
-            dec_qkv,
-            dec_out,
-            columns_of([dec_gain1, dec_shift1, dec_gain2, dec_shift2, mask_token]),
-        ],
-        axis=1,
-    )
-    pack_two = gather_rows(pack_two, total, order_two)
-    dec_whole_up = gather_rows(dec_up, total, order)
-    dec_whole_down = gather_rows(dec_down, total, order_two)
-    dec_vecs = rows_of(pack_two[:, 4 * dec_wide :], 5)
+    enc_wide, dec_wide = enc_out.shape[1], dec_out.shape[1]
+    enc_ff, dec_ff = enc_up.shape[1], dec_up.shape[1]
+    enc_small = columns_of([enc_gain1, enc_shift1, enc_gain2, enc_shift2])
+    enc_pack = jnp.concatenate(
+        [enc_qkv, enc_out, enc_up, proj, enc_small] + blocks_beside(enc_down, enc_out.shape[0]), axis=1
+    )
+    enc_pack = gather_rows(enc_pack)
+    enc_end = 4 * enc_wide + enc_ff + dec_wide + LANES
+    whole_down = blocks_below(enc_pack[:, enc_end:], total, enc_wide)
+    dec_small = columns_of([dec_gain1, dec_shift1, dec_gain2, dec_shift2, mask_token])
+    dec_pack = jnp.concatenate(
+        [dec_qkv, dec_out, dec_up] + blocks_beside(dec_down, dec_out.shape[0]) + [dec_small], axis=1
+    )
+    dec_pack = gather_rows(dec_pack)
+    dec_end = 4 * dec_wide + dec_ff
+    dec_whole_down = blocks_below(dec_pack[:, dec_end : dec_end + dec_ff], total, dec_wide)
 
     clip_count, slot_total, _ = visible.shape
     half_clips = clip_count // 2
@@ -635,37 +760,25 @@
     slot_ids = jnp.arange(slot_total)
     valid_rows = slot_ids[None, :] < visible_count[:, None]
     valid_mask = valid_rows.astype(F32)[:, None, :]
-    qkv, probs, mixed, middle = enc_attend(visible, valid_mask, enc_vecs, whole_qkv, whole_out)
-    sent_rows, encoded, hidden, slope = enc_feed(middle, enc_vecs, whole_up, whole_down, whole_proj)
-    sent_rows = sent_rows.reshape(clip_count, slot_total, dec_wide)
-
-    rolled_time = (keep_index // FREQ + TIME - SHIFT) % TIME
-    rolled_freq = (keep_index % FREQ + FREQ - SHIFT) % FREQ
-    target_band = rolled_freq // band_height
-    slot_index = rolled_time * band_height + rolled_freq % band_height
-    band_ids = jnp.arange(2)
-    chosen = valid_rows[:, None, :] & (target_band[:, None, :] == band_ids[None, :, None])
-    chosen = chosen.reshape(2, half_clips, 2, slot_total).transpose(0, 2, 1, 3)
-    outgoing = jnp.where(
-        chosen[..., None],
-        sent_rows.reshape(2, 1, half_clips, slot_total, dec_wide),
-        jnp.zeros((), BF16),
-    )
-    outgoing = outgoing.reshape(4, half_clips, slot_total, dec_wide)
-    slot_out = jnp.where(chosen, slot_index.reshape(2, 1, half_clips, slot_total), -1).astype(BF16)
-    slot_out = slot_out.reshape(4, half_clips, slot_total)
-    arrived = lax.all_to_all(outgoing, "band", split_axis=0, concat_axis=0, tiled=True)
-    arrived_slot = lax.all_to_all(slot_out, "band", split_axis=0, concat_axis=0, tiled=True)
+    cell_number = jnp.where(valid_rows, keep_index, -1).reshape(2, half_clips, slot_total)
+    cell_number = owners_to_bands(cell_number).reshape(-1, slot_total)
+    band_pick = lax.axis_index("band") % 2
+    rolled_time = (cell_number // FREQ + TIME - SHIFT) % TIME
+    rolled_freq = (cell_number % FREQ + FREQ - SHIFT) % FREQ
+    here = (cell_number >= 0) & (rolled_freq // band_height == band_pick)
+    arrived_index = jnp.where(here, rolled_time * band_height + rolled_freq % band_height, -1)
+
+    blocks = enc_blocks(enc_pack, enc_wide, enc_ff, dec_wide)
+    qkv, probs, mixed, middle, vecs = enc_attend(visible, valid_mask, blocks)
+    sent_rows, encoded, hidden, slope = enc_feed(middle, vecs, blocks, whole_down)
+    arrived_rows = owners_to_bands(sent_rows.reshape(2, half_clips, slot_total, dec_wide))
     half_total = 4 * half_clips
-    arrived_rows = arrived.reshape(half_total, slot_total, dec_wide)
-    arrived_index = arrived_slot.reshape(half_total, slot_total).astype(jnp.int32)
 
     cell_count = TIME * band_height
     places = jnp.arange(cell_count)
-    band_pick = lax.axis_index("band") % 2
     cell_freq = band_pick * band_height + places % band_height
     patch_number = (places // band_height + SHIFT) % TIME * FREQ + (cell_freq + SHIFT) % FREQ
-    span = LANES * D_DEC // (HEADS_DEC * LANES)
+    span = D_DEC // HEADS_DEC
     query = places[:, None]
     key = query // span * span + jnp.arange(LANES)[None, :] % span
 
@@ -676,72 +789,81 @@
 
     cells_in = WINDOW * WINDOW
     allowed = (query // cells_in == key // cells_in) & (label(query) == label(key))
-    decoded, returning, g_dqkv, g_dout, g_dup, g_ddown, g_dvec = decoder_block(
-        arrived_rows,
+    decoded, returning, dec_grad = decoder_block(
+        arrived_rows.reshape(half_total, slot_total, dec_wide),
         arrived_index,
         cotangent.reshape(half_total, cell_count, dec_wide),
         position_table(patch_number),
         allowed.astype(F32),
-        dec_vecs,
-        pack_two[:, : 3 * dec_wide],
-        pack_two[:, 3 * dec_wide : 4 * dec_wide],
-        dec_whole_up,
+        dec_pack,
         dec_whole_down,
     )
     decoded_out = decoded.reshape(cotangent.shape)
 
-    returning = returning.reshape(4, half_clips, slot_total, dec_wide)
-    coming = lax.all_to_all(returning, "band", split_axis=0, concat_axis=0, tiled=True)
-    grad_sent = jnp.sum(coming.astype(F32).reshape(2, 2, half_clips, slot_total, dec_wide), axis=1)
-    grad_sent = grad_sent.astype(BF16).reshape(-1, dec_wide)
-
-    dec_pack = jnp.concatenate([g_dqkv, g_dout, columns_of([g_dvec[i] for i in range(5)])], axis=1)
-    dec_pack = scatter_sum(dec_pack, total, order_two)
-    dec_up_sum = scatter_sum(g_dup, total, order)
-    dec_down_sum = scatter_sum(g_ddown, total, order_two)
-    dec_pack = gather_rows(dec_pack, total, order_two).astype(F32)
-    dec_up_sum = gather_rows(dec_up_sum, total, order).astype(F32)
-    dec_down_sum = gather_rows(dec_down_sum, total, order_two).astype(F32)
-    dec_vec_sums = rows_of(dec_pack[:, 4 * dec_wide :], 5)
-
-    g_proj, g_eup, g_edown, grad_middle, g_evec2 = enc_feed_back(
-        grad_sent, encoded, whole_proj, hidden, slope, middle, enc_vecs, whole_up, whole_down
-    )
-    enc_up_sum = scatter_sum(g_eup, total, order_two)
-    enc_down_sum = scatter_sum(g_edown, total, order)
-    g_eqkv, g_eout, grad_visible, g_evec1 = enc_attend_back(
-        grad_middle, mixed, qkv, probs, visible, enc_vecs, whole_qkv, whole_out
-    )
-    g_evec = g_evec1 + g_evec2
-    enc_pack = jnp.concatenate(
-        [g_eqkv, g_eout, g_proj, columns_of([g_evec[i] for i in range(4)])], axis=1
-    )
-    enc_pack = scatter_sum(enc_pack, total, order)
-    enc_up_sum = gather_rows(enc_up_sum, total, order_two).astype(F32)
-    enc_down_sum = gather_rows(enc_down_sum, total, order).astype(F32)
-    enc_pack = gather_rows(enc_pack, total, order).astype(F32)
-    enc_vec_sums = rows_of(enc_pack[:, 4 * enc_wide + dec_wide :], 4)
+    middle_cut = lambda grad: grad.shape[1] // 256 * 128
+    dec_run = RunningSum(dec_grad, total, middle_cut(dec_grad))
+    dec_run.step()
+    grad_sent = bands_to_owners(returning.reshape(2, 2, half_clips, slot_total, dec_wide))
+    grad_sent = grad_sent.reshape(-1, dec_wide)
+    grad_sent, gives = together(grad_sent, dec_run.offers())
+    dec_run.deliver(gives)
+    g_proj, grad_feed, grad_middle, g_vec = enc_feed_back(
+        grad_sent, encoded, hidden, slope, middle, vecs, blocks, whole_down
+    )
+    grad_feed, grad_middle, gives = together(grad_feed, grad_middle, dec_run.offers())
+    dec_run.deliver(gives)
+    feed_run = RunningSum(grad_feed, total, enc_ff)
+    feed_run.step()
+    grad_attend, grad_visible = enc_attend_back(
+        grad_middle, mixed, qkv, probs, visible, vecs, blocks, g_proj, g_vec
+    )
+    grad_attend, gives, feed_gives = together(grad_attend, dec_run.offers(), feed_run.offers())
+    dec_run.deliver(gives)
+    feed_run.deliver(feed_gives)
+    attend_run = RunningSum(grad_attend, total, middle_cut(grad_attend))
+    attend_run.step()
+    dec_shard = dec_run.finish()
+    dec_shard, feed_gives, gives = together(dec_shard, feed_run.offers(), attend_run.offers())
+    dec_sum = gather_rows(dec_shard)
+    feed_run.deliver(feed_gives)
+    feed_gives, gives = together(feed_run.offers(), gives)
+    feed_run.deliver(feed_gives)
+    attend_run.deliver(gives)
+    attend_run.step()
+    feed_sum = feed_run.finish()
+    attend_sum = attend_run.finish()
+    small_at = attend_sum.shape[1] - LANES
+    enc_shard = jnp.concatenate(
+        [attend_sum[:, :small_at], feed_sum, attend_sum[:, small_at:]], axis=1
+    )
+    enc_sum = gather_rows(enc_shard)
+
+    spans = [(0, 3 * dec_wide), (3 * dec_wide, dec_wide), (4 * dec_wide, dec_ff)]
+    d_qkv, d_out, d_up, d_down, dec_vecs = unpack_sums(dec_sum, spans, (dec_end, dec_ff))
+    start = 4 * enc_wide + dec_wide
+    spans = [(0, 3 * enc_wide), (3 * enc_wide, enc_wide), (4 * enc_wide, dec_wide), (start, enc_ff)]
+    e_qkv, e_out, e_proj, e_up, e_down, enc_vecs = unpack_sums(enc_sum, spans, (start + enc_ff, enc_ff))
     return (
         decoded_out,
         grad_visible,
-        enc_vec_sums[0],
-        enc_vec_sums[1],
-        enc_pack[:, : 3 * enc_wide],
-        enc_pack[:, 3 * enc_wide : 4 * enc_wide],
-        enc_vec_sums[2],
-        enc_vec_sums[3],
-        enc_up_sum,
-        enc_down_sum,
-        enc_pack[:, 4 * enc_wide : 4 * enc_wide + dec_wide],
-        dec_vec_sums[4],
-        dec_vec_sums[0],
-        dec_vec_sums[1],
-        dec_pack[:, : 3 * dec_wide],
-        dec_pack[:, 3 * dec_wide : 4 * dec_wide],
-        dec_vec_sums[2],
-        dec_vec_sums[3],
-        dec_up_sum,
-        dec_down_sum,
+        enc_vecs[0],
+        enc_vecs[1],
+        e_qkv,
+        e_out,
+        enc_vecs[2],
+        enc_vecs[3],
+        e_up,
+        e_down,
+        e_proj,
+        dec_vecs[4],
+        dec_vecs[0],
+        dec_vecs[1],
+        d_qkv,
+        d_out,
+        dec_vecs[2],
+        dec_vecs[3],
+        d_up,
+        d_down,
     )
 
 

time: 823 us -> 693 us (0.84)
  waiting for transfers between devices: 404 us -> 331 us
  starting transfers between devices: 100 us -> 33.6 us
  Pallas kernels: 181 us -> 208 us
  other arithmetic: 57.1 us -> 35.1 us
  between operations: 2.8 us -> 14.7 us
    ppermute x90 -> x30, waiting for transfers between devices: 385 us -> 113 us  [the longest x24 94.7 us: deliver(): lax.ppermute(give, AXES, partner_pairs(self.total, mask))]
    all_gather x0 -> x4, waiting for transfers between devices: none -> 217 us  [gather_rows(): return lax.all_gather(shard, AXES, axis=0, tiled=True)]
    ppermute x90 -> x30, starting transfers between devices: 88.3 us -> 33.5 us  [the longest x24 27.1 us: deliver(): lax.ppermute(give, AXES, partner_pairs(self.total, mask))]
    pallas_call x4 -> x6, Pallas kernels: 65.9 us -> 92.3 us  [the longest x4 68.4 us: whole_call(): pl.pallas_call(kernel, grid=(1,), in_specs=specs, out_specs=[zero(s) for...]
    another operation x116 -> x10, other arithmetic: 23.1 us -> 3.09 us  [the longest x2 1.83 us: bands_to_owners(): jnp.stack([jnp.where(half == 0, own, got), jnp.where(half == 0, got, own)])]
    convert_element_type x8 -> x0, local copies, waits for them, and re-layouts: 19.7 us -> none  [the longest x1 5.15 us: shards(): enc_pack = gather_rows(enc_pack, total, order).astype(F32)]
    all_to_all x3 -> x0, waiting for transfers between devices: 19.1 us -> none  [the longest x1 10.9 us: shards(): lax.all_to_all(outgoing, 'band', split_axis=0, concat_axis=0, tiled=True)]
    all_to_all x3 -> x0, starting transfers between devices: 12 us -> none  [the longest x1 4.25 us: shards(): lax.all_to_all(returning, 'band', split_axis=0, concat_axis=0, tiled=True)]
  transfers between devices with their start and end apart: 93 -> 34, of which waited for: 53 -> 15; matrix products, arithmetic and copies ran while one was open for 12% -> 7% of each run, Pallas kernels for 8% -> 11%
where the time goes in v3:
time: 693 us; the launch traced here: 683 us
  waiting for transfers between devices  331 us (48%)
  Pallas kernels  208 us (30%)
  local copies, waits for them, and re-layouts  60.4 us (9%)
  other arithmetic  35.1 us (5%)
  starting transfers between devices  33.6 us (5%)
  between operations  14.7 us (2%)
    all_gather x4, waiting for transfers between devices, gather_rows(): return lax.all_gather(shard, AXES, axis=0, tiled=True)  217 us
    pallas_call x1, Pallas kernels, decoder_block(): pl.pallas_call(decoder_kernel, grid=(n_half // halves,), in_specs=[pl.Blo...  116 us
    ppermute x24, waiting for transfers between devices, deliver(): lax.ppermute(give, AXES, partner_pairs(self.total, mask))  94.7 us
    pallas_call x4, Pallas kernels, whole_call(): pl.pallas_call(kernel, grid=(1,), in_specs=specs, out_specs=[zero(s) for...  68.4 us
    ppermute x24, starting transfers between devices, deliver(): lax.ppermute(give, AXES, partner_pairs(self.total, mask))  27.1 us
    pallas_call x2, Pallas kernels, unpack_sums(): pl.pallas_call(functools.partial(unpack_kernel, spans, tall), grid=(rows...  23.9 us
    convert_element_type x18, other arithmetic, add_low(): return sum((part.astype(F32) for part in parts)).astype(BF16)  20.1 us
    ppermute x6, waiting for transfers between devices, swap_band(): return lax.ppermute(array, 'band', [(i, i ^ bit) for i in range(4)])  18.7 us
  transfers between devices with their start and end apart: 34, of which 15 were waited for; matrix products, arithmetic and copies ran while one was open for 7% of the time, Pallas kernels for 11%

profile of v3, /device:TPU:0, one launch (start us, length us, event | category | flops | bytes accessed | tf_op | source)
XLA Modules:
  0.0 682.7 jit_solution(16066889113532707425)
XLA Ops:
  26.1 3.0 collective-permute-start.2
  32.6 2.0 reshape.623.cot_ref
  34.7 91.0 %all-gather.5.cloned.1.call-done.small_ref.wqkv_ref.wo_ref.wu_ref.proj_ref = bf16[768,9856]{1,0:T(8,128)(2,1)} async-done(((bf16[24,9856]{1,0:T(8,128)(2,1)}), bf16[768,9856]{1,0:T(8,128)(2,1)}) %all-gather.5.cloned.1.call-update) | async-done | bytes 15138832 | tf_op jit(solution)/shard_map/all_gather | solution.py:662
  125.7 2.7 fusion.60
  128.4 2.5 pad_maximum_fusion
  130.8 10.1 %enc_attend.1 = (bf16[512,2304]{1,0:T(8,128)(2,1)}, bf16[512,1536]{1,0:T(8,128)(2,1)}, bf16[512,768]{1,0:T(8,128)(2,1)}, f32[512,768]{1,0:T(8,128)}, f32[8,768]{1,0:T(8,128)}) custom-call(bf16[4,128,768]{2,1,0:T(8,128)(2,1)} %x_ref.3, f32[4,1,128]{2,1,0:T(1,128)} %compare_convert_fusion.mask_ref, ...), custom_call_target="tpu_custom_call" | custom-call | flops 10000000000 | bytes 16777216 | tf_op jit(solution)/shard_map/enc_attend/pallas_call | solution.py:492
  140.9 18.6 %enc_feed.1 = (bf16[512,512]{1,0:T(8,128)(2,1)}, bf16[512,768]{1,0:T(8,128)(2,1)}, bf16[512,3072]{1,0:T(8,128)(2,1)}, bf16[512,3072]{1,0:T(8,128)(2,1)}) custom-call(f32[512,768]{1,0:T(8,128)} %get-tuple-element.72.x2_ref, f32[8,768]{1,0:T(8,128)} %get-tuple-element.73.vec_ref, ...), custom_call_target="tpu_custom_call" | custom-call | flops 17999998976 | bytes 16777216 | tf_op jit(solution)/shard_map/enc_feed/pallas_call | solution.py:492
  162.0 7.0 %collective-permute-done = bf16[2,128,512]{2,1,0:T(8,128)(2,1)S(1)} collective-permute-done((bf16[2,128,512]{2,1,0:T(8,128)(2,1)S(1)}, bf16[2,128,512]{2,1,0:T(8,128)(2,1)S(1)}, u32[]{:S(2)}, u32[]{:S(2)}) %collective-permute-start) | collective-permute-done | bytes 262176 | tf_op jit(solution)/shard_map/ppermute | solution.py:682
  170.8 26.5 %all-gather.7.cloned.1.call-done.small_ref.wqkv_ref.wo_ref.wu_ref = bf16[512,6272]{1,0:T(8,128)(2,1)} async-done(((bf16[16,6272]{1,0:T(8,128)(2,1)}), bf16[512,6272]{1,0:T(8,128)(2,1)}) %all-gather.7.cloned.1.call-update) | async-done | bytes 6422544 | tf_op jit(solution)/shard_map/all_gather | solution.py:662
  197.4 1.7 fusion.61
  201.8 115.8 %decoder_block.1 = (bf16[8,256,512]{2,1,0:T(8,128)(2,1)}, bf16[8,128,512]{2,1,0:T(8,128)(2,1)}, bf16[512,6272]{1,0:T(8,128)(2,1)}) custom-call(bf16[8,128,512]{2,1,0:T(8,128)(2,1)} %bitcast.223, s32[8,1,128]{2,1,0:T(1,128)} %and_select_fusion.3.idx_ref, bf16[8,256,512]{2,1,0:T(8,128)(2,1)} %reshape.623.cot_ref, f32[256,512]{1,0:T(8,128)} %pad_maximum_fusion.7.pos_ref, ...), custom_call_target="tpu_custom_call" | custom-call | flops 77309411328 | bytes 41943040 | tf_op jit(solution)/shard_map/decoder_block/pallas_call | solution.py:273
  317.6 3.3 constant_dynamic-slice_fusion.5
  321.0 1.9 copy.89
  323.1 1.9 dynamic-slice_bitcast_fusion.8
  325.2 4.5 collective-permute-done.4
  334.0 7.2 %collective-permute-done.5 = bf16[2,128,512]{2,1,0:T(8,128)(2,1)S(1)} collective-permute-done((bf16[2,128,512]{2,1,0:T(8,128)(2,1)}, bf16[2,128,512]{2,1,0:T(8,128)(2,1)S(1)}, u32[]{:S(2)}, u32[]{:S(2)}) %collective-permute-start.5) | collective-permute-done | bytes 262176 | tf_op jit(solution)/shard_map/ppermute | solution.py:682
  343.0 2.6 fusion.1
  346.1 1.6 collective-permute-start.8
  348.2 23.4 %enc_feed_back.1 = (bf16[768,512]{1,0:T(8,128)(2,1)}, bf16[768,6144]{1,0:T(8,128)(2,1)}, f32[512,768]{1,0:T(8,128)}, f32[8,768]{1,0:T(8,128)}) custom-call(bf16[512,512]{1,0:T(8,128)(2,1)} %bitcast.228, bf16[512,768]{1,0:T(8,128)(2,1)} %get-tuple-element.79.enc_ref, bf16[768,9856]{1,0:T(8,128)(2,1)} %all-gather.5.cloned.1.call-done.small_ref.wqkv_ref.wo_ref.wu_ref.proj_ref, ...), custom_call_target="tpu_custom_call" | custom-call | flops 24000000000 | bytes 16777216 | tf_op jit(solution)/shard_map/enc_feed_back/pallas_call | solution.py:492
  374.9 7.1 %constant_dynamic-slice_fusion.3 = (bf16[2,2,2,2,1,24,6144]{6,5,4,3,2,1,0:T(8,128)(2,1)}, bf16[2,2,2,2,1,24,6144]{6,5,4,3,2,1,0:T(8,128)(2,1)S(1)}) fusion(bf16[2,2,2,2,2,24,6144]{6,5,4,3,2,1,0:T(8,128)(2,1)} %bitcast.201, s32[]{:T(128)S(6)} %select_n.395, s32[]{:T(128)S(6)} %select_n.396), kind=kLoop, calls=%fused_computation.151 | loop fusion | bytes 18874376 | tf_op jit(solution)/shard_map/jit(dynamic_index_in_dim)/dynamic_slice | solution.py:629
  382.0 2.7 copy.88
  386.7 16.4 %enc_attend_back.1 = (bf16[768,3712]{1,0:T(8,128)(2,1)}, bf16[4,128,768]{2,1,0:T(8,128)(2,1)}) custom-call(f32[512,768]{1,0:T(8,128)} %get-tuple-element.86.dx2_ref, bf16[512,768]{1,0:T(8,128)(2,1)} %get-tuple-element.87.o_ref, bf16[512,2304]{1,0:T(8,128)(2,1)} %get-tuple-element.88.qkv_ref, bf16[512,1536]{1,0:T(8,128)(2,1)} %get-tuple-element.89.p_ref, ...), custom_call_target="tpu_custom_call" | custom-call | flops 14000000000 | bytes 16777216 | tf_op jit(solution)/shard_map/enc_attend_back/pallas_call | solution.py:492
  404.6 4.5 fusion
  410.9 1.7 dynamic-slice_bitcast_fusion.1
  415.0 2.0 collective-permute-start.16
  417.4 1.8 copy.90
  420.6 2.0 collective-permute-done.14
  424.1 7.4 %collective-permute-done.15 = bf16[16,6272]{1,0:T(8,128)(2,1)S(1)} collective-permute-done((bf16[16,6272]{1,0:T(8,128)(2,1)S(1)}, bf16[16,6272]{1,0:T(8,128)(2,1)S(1)}, u32[]{:S(2)}, u32[]{:S(2)}) %collective-permute-start.15) | collective-permute-done | bytes 200736 | tf_op jit(solution)/shard_map/ppermute | solution.py:639
  432.3 15.6 %collective-permute-done.17 = bf16[2,2,2,24,3072]{4,3,1,0,2:T(8,128)(2,1)} collective-permute-done((bf16[2,2,2,24,3072]{4,3,1,0,2:T(8,128)(2,1)}, bf16[2,2,2,24,3072]{4,3,1,0,2:T(8,128)(2,1)}, u32[]{:S(2)}, u32[]{:S(2)}) %collective-permute-start.17) | collective-permute-done | bytes 1179680 | tf_op jit(solution)/shard_map/ppermute | solution.py:639
  447.8 2.0 fusion.3
  450.8 1.7 fusion.4
  453.7 2.5 fusion.2
  457.4 1.6 collective-permute-start.18
  459.5 14.6 %collective-permute-done.18 = bf16[2,2,24,3072]{3,2,1,0:T(8,128)(2,1)S(1)} collective-permute-done((bf16[2,2,24,3072]{3,2,1,0:T(8,128)(2,1)}, bf16[2,2,24,3072]{3,2,1,0:T(8,128)(2,1)S(1)}, u32[]{:S(2)}, u32[]{:S(2)}) %collective-permute-start.18) | collective-permute-done | bytes 589856 | tf_op jit(solution)/shard_map/ppermute | solution.py:639
  479.7 1.8 collective-permute-start.28
  481.5 2.0 collective-permute-start.29
  483.5 15.2 %collective-permute-done.20 = bf16[2,2,2,24,1792]{4,3,1,0,2:T(8,128)(2,1)S(1)} collective-permute-done((bf16[2,2,2,24,1792]{4,3,1,0,2:T(8,128)(2,1)S(1)}, bf16[2,2,2,24,1792]{4,3,1,0,2:T(8,128)(2,1)S(1)}, u32[]{:S(2)}, u32[]{:S(2)}) %collective-permute-start.20) | collective-permute-done | bytes 688160 | tf_op jit(solution)/shard_map/ppermute | solution.py:639
  499.0 1.6 collective-permute-start.21
  501.3 5.8 collective-permute-done.21
  507.1 2.0 collective-permute-done.23
  509.4 1.6 collective-permute-start.25
  511.0 2.8 collective-permute-start.26
  514.0 2.7 collective-permute-done.24
  516.7 29.4 %collective-permute-done.25 = bf16[24,3712]{1,0:T(8,128)(2,1)S(1)} collective-permute-done((bf16[24,3712]{1,0:T(8,128)(2,1)S(1)}, bf16[24,3712]{1,0:T(8,128)(2,1)S(1)}, u32[]{:S(2)}, u32[]{:S(2)}) %collective-permute-start.25) | collective-permute-done | bytes 178208 | tf_op jit(solution)/shard_map/ppermute | solution.py:639
  547.1 2.0 reshape.629
  549.1 7.9 %unpack_sums.3 = (f32[512,1536]{1,0:T(8,128)}, f32[512,512]{1,0:T(8,128)}, f32[512,2048]{1,0:T(8,128)}, f32[2048,512]{1,0:T(8,128)}, f32[8,512]{1,0:T(8,128)}) custom-call(bf16[512,6272]{1,0:T(8,128)(2,1)} %all-gather.11.cloned.1.call-done.sum_ref), custom_call_target="tpu_custom_call" | custom-call | bytes 19267584 | tf_op jit(solution)/shard_map/unpack_sums/pallas_call | solution.py:574
  558.5 99.8 %all-gather.9.cloned.1.call-done.sum_ref = bf16[768,9856]{1,0:T(8,128)(2,1)} async-done(((bf16[24,9856]{1,0:T(8,128)(2,1)}), bf16[768,9856]{1,0:T(8,128)(2,1)}) %all-gather.9.cloned.1.call-update) | async-done | bytes 15138832 | tf_op jit(solution)/shard_map/all_gather | solution.py:662
  658.2 16.0 %unpack_sums.2 = (f32[768,2304]{1,0:T(8,128)}, f32[768,768]{1,0:T(8,128)}, f32[768,512]{1,0:T(8,128)}, f32[768,3072]{1,0:T(8,128)}, f32[3072,768]{1,0:T(8,128)}, /*index=5*/f32[8,768]{1,0:T(8,128)}) custom-call(bf16[768,9856]{1,0:T(8,128)(2,1)} %all-gather.9.cloned.1.call-done.sum_ref), custom_call_target="tpu_custom_call" | custom-call | bytes 45416448 | tf_op jit(solution)/shard_map/unpack_sums/pallas_call | solution.py:574
  (177 shorter events, 67.0 us)
Async XLA Ops:
  7.2 23.8 %copy-start.12 = (s32[4]{0:T(128)S(1)}, s32[4]{0:T(128)}, u32[]{:S(2)}) copy-start(s32[4]{0:T(128)} %param.24) | copy-start | bytes 52
  7.2 25.4 %copy-start.7 = (bf16[1,8,64,4,512]{4,3,2,1,0:T(4,128)(2,1)S(1)}, bf16[1,8,64,4,512]{4,3,2,1,0:T(4,128)(2,1)}, u32[]{:S(2)}) copy-start(bf16[1,8,64,4,512]{4,3,2,1,0:T(4,128)(2,1)} %param.43) | copy-start | bytes 6291460
  7.2 118.5 %all-gather.5.cloned.1.call-start = ((), (), s32[]{:S(2)}) async-start(), calls=%async_computation | async-start | bytes 15611904 | tf_op jit(solution)/shard_map/all_gather | solution.py:662
  15.5 181.9 %all-gather.7.cloned.1.call-start = ((), (), s32[]{:S(2)}) async-start(), calls=%async_computation.1 | async-start | bytes 6623232 | tf_op jit(solution)/shard_map/all_gather | solution.py:662
  25.3 523.8 %all-gather.11.cloned.1.call-start = ((), (), s32[]{:S(2)}) async-start(), calls=%async_computation.3 | async-start | bytes 6623232 | tf_op jit(solution)/shard_map/all_gather | solution.py:662
  26.1 8.5 %collective-permute-start.2 = (s32[2,128]{1,0:T(2,128)S(1)}, s32[2,128]{1,0:T(2,128)S(1)}, u32[]{:S(2)}, u32[]{:S(2)}) collective-permute-start(s32[2,128]{1,0:T(2,128)S(1)} %fusion.58), channel_id=1, source_target_pairs={{0,2},{1,3},{2,0},{3,1},{4,6},{5,7},{6,4},{7,5},{8,10},{9,11},{10,... | collective-permute-start | bytes 3080 | tf_op jit(solution)/shard_map/ppermute | solution.py:682
  34.6 127.3 %collective-permute-start.3 = (s32[2,2,128]{2,1,0:T(2,128)S(1)}, s32[2,2,128]{2,1,0:T(2,128)S(1)}, u32[]{:S(2)}, u32[]{:S(2)}) collective-permute-start(s32[2,2,128]{2,1,0:T(2,128)S(1)} %pad_add_fusion.1), channel_id=1, source_target_pairs={{0,1},{1,0},{2,3},{3,2},{4,5},{5,4},{6,7},{7,6},{8,9},{9,8},{10,11... | collective-permute-start | bytes 6152 | tf_op jit(solution)/shard_map/ppermute | solution.py:682
  160.5 8.5 %collective-permute-start = (bf16[2,128,512]{2,1,0:T(8,128)(2,1)S(1)}, bf16[2,128,512]{2,1,0:T(8,128)(2,1)S(1)}, u32[]{:S(2)}, u32[]{:S(2)}) collective-permute-start(bf16[2,128,512]{2,1,0:T(8,128)(2,1)S(1)} %dynamic-slice_bitcast_fusion.17), channel_id=1, source_target_pairs={{0,2},{1,3},{2,0},{3,1},{4,6},{5,7},{6,4},{7,5},{8,10},{9,11},{10,... | collective-permute-start | bytes 786440 | tf_op jit(solution)/shard_map/ppermute | solution.py:682
  170.1 30.5 %collective-permute-start.1 = (bf16[2,2,128,512]{3,2,1,0:T(8,128)(2,1)S(1)}, bf16[2,2,128,512]{3,2,1,0:T(8,128)(2,1)S(1)}, u32[]{:S(2)}, u32[]{:S(2)}) collective-permute-start(bf16[2,2,128,512]{3,2,1,0:T(8,128)(2,1)S(1)} %pad_maximum_fusion.6), channel_id=1, source_target_pairs={{0,1},{1,0},{2,3},{3,2},{4,5},{5,4},{6,7},{7,6},{8,9},{9,8},{10,11... | collective-permute-start | bytes 1572872 | tf_op jit(solution)/shard_map/ppermute | solution.py:682
  322.9 20.1 %collective-permute-start.6 = (bf16[2,2,2,2,16,6272]{5,4,1,0,2,3:T(8,128)(2,1)}, bf16[2,2,2,2,16,6272]{5,4,1,0,2,3:T(8,128)(2,1)}, u32[]{:S(2)}, u32[]{:S(2)}) collective-permute-start(bf16[2,2,2,2,16,6272]{5,4,1,0,2,3:T(8,128)(2,1)} %bitcast.197), channel_id=1, source_target_pairs={{0,1},{1,0},{2,3},{3,2},{4,5},{5,4},{6,7},{7,6},{8,9},{9,8},{10,11... | collective-permute-start | bytes 9633800 | tf_op jit(solution)/shard_map/ppermute | solution.py:639
  325.0 4.7 collective-permute-start.4
  332.5 8.7 %collective-permute-start.5 = (bf16[2,128,512]{2,1,0:T(8,128)(2,1)}, bf16[2,128,512]{2,1,0:T(8,128)(2,1)S(1)}, u32[]{:S(2)}, u32[]{:S(2)}) collective-permute-start(bf16[2,128,512]{2,1,0:T(8,128)(2,1)} %dynamic-slice_bitcast_fusion.16), channel_id=1, source_target_pairs={{0,2},{1,3},{2,0},{3,1},{4,6},{5,7},{6,4},{7,5},{8,10},{9,11},{10,... | collective-permute-start | bytes 786440 | tf_op jit(solution)/shard_map/ppermute | solution.py:682
  346.1 26.7 %collective-permute-start.8 = (bf16[2,2,2,16,3200]{4,3,1,0,2:T(8,128)(2,1)S(1)}, bf16[2,2,2,16,3200]{4,3,1,0,2:T(8,128)(2,1)}, u32[]{:S(2)}, u32[]{:S(2)}) collective-permute-start(bf16[2,2,2,16,3200]{4,3,1,0,2:T(8,128)(2,1)S(1)} %dynamic-slice_bitcast_fusion.2), channel_id=1, source_target_pairs={{0,2},{1,3},{2,0},{3,1},{4,6},{5,7},{6,4},{7,5},{8,10},{9,11},{10,... | collective-permute-start | bytes 2457608 | tf_op jit(solution)/shard_map/ppermute | solution.py:639
  347.7 23.9 %collective-permute-start.7 = (bf16[2,2,2,16,3072]{4,3,1,0,2:T(8,128)(2,1)S(1)}, bf16[2,2,2,16,3072]{4,3,1,0,2:T(8,128)(2,1)S(1)}, u32[]{:S(2)}, u32[]{:S(2)}) collective-permute-start(bf16[2,2,2,16,3072]{4,3,1,0,2:T(8,128)(2,1)S(1)} %dynamic-slice_bitcast_fusion.3), channel_id=1, source_target_pairs={{0,4},{1,5},{2,6},{3,7},{4,0},{5,1},{6,2},{7,3},{8,12},{9,13},{10,... | collective-permute-start | bytes 2359304 | tf_op jit(solution)/shard_map/ppermute | solution.py:639
  371.8 1.0 copy-start.5
  384.7 19.9 %collective-permute-start.11 = (bf16[2,2,2,2,24,6144]{5,4,1,0,2,3:T(8,128)(2,1)}, bf16[2,2,2,2,24,6144]{5,4,1,0,2,3:T(8,128)(2,1)}, u32[]{:S(2)}, u32[]{:S(2)}) collective-permute-start(bf16[2,2,2,2,24,6144]{5,4,1,0,2,3:T(8,128)(2,1)} %bitcast.196), channel_id=1, source_target_pairs={{0,1},{1,0},{2,3},{3,2},{4,5},{5,4},{6,7},{7,6},{8,9},{9,8},{10,11... | collective-permute-start | bytes 14155784 | tf_op jit(solution)/shard_map/ppermute | solution.py:639
  384.7 18.4 %collective-permute-start.9 = (bf16[2,2,16,3072]{3,2,1,0:T(8,128)(2,1)}, bf16[2,2,16,3072]{3,2,1,0:T(8,128)(2,1)}, u32[]{:S(2)}, u32[]{:S(2)}) collective-permute-start(bf16[2,2,16,3072]{3,2,1,0:T(8,128)(2,1)} %dynamic-slice_bitcast_fusion.10), channel_id=1, source_target_pairs={{0,2},{1,3},{2,0},{3,1},{4,6},{5,7},{6,4},{7,5},{8,10},{9,11},{10,... | collective-permute-start | bytes 1179656 | tf_op jit(solution)/shard_map/ppermute | solution.py:639
  386.1 18.2 %collective-permute-start.10 = (bf16[2,2,16,3200]{3,2,1,0:T(8,128)(2,1)}, bf16[2,2,16,3200]{3,2,1,0:T(8,128)(2,1)S(1)}, u32[]{:S(2)}, u32[]{:S(2)}) collective-permute-start(bf16[2,2,16,3200]{3,2,1,0:T(8,128)(2,1)} %dynamic-slice_bitcast_fusion.9), channel_id=1, source_target_pairs={{0,4},{1,5},{2,6},{3,7},{4,0},{5,1},{6,2},{7,3},{8,12},{9,13},{10,... | collective-permute-start | bytes 1228808 | tf_op jit(solution)/shard_map/ppermute | solution.py:639
  386.7 17.9 %slice-start = ((s8[4718592]{0:T(1024)(128)(4,1)}), s8[4194304]{0:T(1024)(128)(4,1)S(1)}, s32[]{:S(2)}) async-start(s8[4718592]{0:T(1024)(128)(4,1)} %bitcast.199), calls=%async_computation.4 | async-start | bytes 8388608
  386.7 17.9 %slice-start.1 = ((s8[4718592]{0:T(1024)(128)(4,1)}), s8[524288]{0:T(1024)(128)(4,1)S(1)}, s32[]{:S(2)}) async-start(s8[4718592]{0:T(1024)(128)(4,1)} %bitcast.199), calls=%async_computation.5 | async-start | bytes 1048576
  404.6 12.3 %slice-start.2 = ((s8[5701632]{0:T(1024)(128)(4,1)}), s8[4194304]{0:T(1024)(128)(4,1)S(1)}, s32[]{:S(2)}) async-start(s8[5701632]{0:T(1024)(128)(4,1)} %bitcast.203), calls=%async_computation.6 | async-start | bytes 8388608
  409.1 7.8 %slice-start.3 = ((s8[5701632]{0:T(1024)(128)(4,1)}), s8[1507328]{0:T(1024)(128)(4,1)S(1)}, s32[]{:S(2)}) async-start(s8[5701632]{0:T(1024)(128)(4,1)} %bitcast.203), calls=%async_computation.7 | async-start | bytes 3014656
  409.6 3.0 copy-start
  409.6 3.0 copy-start.2
  412.6 10.1 %collective-permute-start.14 = (bf16[16,6272]{1,0:T(8,128)(2,1)S(1)}, bf16[16,6272]{1,0:T(8,128)(2,1)S(1)}, u32[]{:S(2)}, u32[]{:S(2)}) collective-permute-start(bf16[16,6272]{1,0:T(8,128)(2,1)S(1)} %get-tuple-element.99), channel_id=1, source_target_pairs={{0,8},{1,9},{2,10},{3,11},{4,12},{5,13},{6,14},{7,15},{8,0},{9,1},... | collective-permute-start | bytes 602120 | tf_op jit(solution)/shard_map/ppermute | solution.py:639
  414.1 17.4 %collective-permute-start.15 = (bf16[16,6272]{1,0:T(8,128)(2,1)S(1)}, bf16[16,6272]{1,0:T(8,128)(2,1)S(1)}, u32[]{:S(2)}, u32[]{:S(2)}) collective-permute-start(bf16[16,6272]{1,0:T(8,128)(2,1)S(1)} %get-tuple-element.100), channel_id=1, source_target_pairs={{0,16},{1,17},{2,18},{3,19},{4,20},{5,21},{6,22},{7,23},{8,24},{9,... | collective-permute-start | bytes 602120 | tf_op jit(solution)/shard_map/ppermute | solution.py:639
  415.0 16.5 %collective-permute-start.16 = (bf16[16,6272]{1,0:T(8,128)(2,1)S(1)}, bf16[16,6272]{1,0:T(8,128)(2,1)S(1)}, u32[]{:S(2)}, u32[]{:S(2)}) collective-permute-start(bf16[16,6272]{1,0:T(8,128)(2,1)S(1)} %get-tuple-element.101), channel_id=1, source_target_pairs={{0,24},{1,25},{2,26},{3,27},{4,28},{5,29},{6,30},{7,31},{8,16},{9,... | collective-permute-start | bytes 602120 | tf_op jit(solution)/shard_map/ppermute | solution.py:639
  419.1 34.3 %collective-permute-start.12 = (bf16[2,2,2,2,24,3712]{5,4,1,0,2,3:T(8,128)(2,1)}, bf16[2,2,2,2,24,3712]{5,4,1,0,2,3:T(8,128)(2,1)}, u32[]{:S(2)}, u32[]{:S(2)}) collective-permute-start(bf16[2,2,2,2,24,3712]{5,4,1,0,2,3:T(8,128)(2,1)} %bitcast.198), channel_id=1, source_target_pairs={{0,1},{1,0},{2,3},{3,2},{4,5},{5,4},{6,7},{7,6},{8,9},{9,8},{10,11... | collective-permute-start | bytes 8552456 | tf_op jit(solution)/shard_map/ppermute | solution.py:639
  419.1 28.7 %collective-permute-start.17 = (bf16[2,2,2,24,3072]{4,3,1,0,2:T(8,128)(2,1)}, bf16[2,2,2,24,3072]{4,3,1,0,2:T(8,128)(2,1)}, u32[]{:S(2)}, u32[]{:S(2)}) collective-permute-start(bf16[2,2,2,24,3072]{4,3,1,0,2:T(8,128)(2,1)} %dynamic-slice_bitcast_fusion), channel_id=1, source_target_pairs={{0,2},{1,3},{2,0},{3,1},{4,6},{5,7},{6,4},{7,5},{8,10},{9,11},{10,... | collective-permute-start | bytes 3538952 | tf_op jit(solution)/shard_map/ppermute | solution.py:639
  422.7 28.2 %collective-permute-start.13 = (bf16[2,2,2,24,3072]{4,3,1,0,2:T(8,128)(2,1)}, bf16[2,2,2,24,3072]{4,3,1,0,2:T(8,128)(2,1)}, u32[]{:S(2)}, u32[]{:S(2)}) collective-permute-start(bf16[2,2,2,24,3072]{4,3,1,0,2:T(8,128)(2,1)} %dynamic-slice_bitcast_fusion.1), channel_id=1, source_target_pairs={{0,4},{1,5},{2,6},{3,7},{4,0},{5,1},{6,2},{7,3},{8,12},{9,13},{10,... | collective-permute-start | bytes 3538952 | tf_op jit(solution)/shard_map/ppermute | solution.py:639
  432.3 18.6 %copy-start.1 = (bf16[2,2,2,2,24,3072]{5,4,1,0,2,3:T(8,128)(2,1)S(1)}, bf16[2,2,2,2,24,3072]{5,4,1,0,2,3:T(8,128)(2,1)}, u32[]{:S(2)}) copy-start(bf16[2,2,2,2,24,3072]{5,4,1,0,2,3:T(8,128)(2,1)} %copy-done) | copy-start | bytes 7077892
  449.9 2.6 copy-start.3
  452.5 1.2 copy-start.4
  457.4 200.9 %all-gather.9.cloned.1.call-start = ((), (), s32[]{:S(2)}) async-start(), calls=%async_computation.2 | async-start | bytes 15611904 | tf_op jit(solution)/shard_map/all_gather | solution.py:662
  457.4 16.7 %collective-permute-start.18 = (bf16[2,2,24,3072]{3,2,1,0:T(8,128)(2,1)}, bf16[2,2,24,3072]{3,2,1,0:T(8,128)(2,1)S(1)}, u32[]{:S(2)}, u32[]{:S(2)}) collective-permute-start(bf16[2,2,24,3072]{3,2,1,0:T(8,128)(2,1)} %dynamic-slice_bitcast_fusion.7), channel_id=1, source_target_pairs={{0,2},{1,3},{2,0},{3,1},{4,6},{5,7},{6,4},{7,5},{8,10},{9,11},{10,... | collective-permute-start | bytes 1769480 | tf_op jit(solution)/shard_map/ppermute | solution.py:639
  459.0 16.3 %collective-permute-start.19 = (bf16[2,2,24,3072]{3,2,1,0:T(8,128)(2,1)}, bf16[2,2,24,3072]{3,2,1,0:T(8,128)(2,1)S(1)}, u32[]{:S(2)}, u32[]{:S(2)}) collective-permute-start(bf16[2,2,24,3072]{3,2,1,0:T(8,128)(2,1)} %dynamic-slice_bitcast_fusion.6), channel_id=1, source_target_pairs={{0,4},{1,5},{2,6},{3,7},{4,0},{5,1},{6,2},{7,3},{8,12},{9,13},{10,... | collective-permute-start | bytes 1769480 | tf_op jit(solution)/shard_map/ppermute | solution.py:639
  476.5 1.7 copy-start.9
  476.7 22.0 %collective-permute-start.20 = (bf16[2,2,2,24,1792]{4,3,1,0,2:T(8,128)(2,1)S(1)}, bf16[2,2,2,24,1792]{4,3,1,0,2:T(8,128)(2,1)S(1)}, u32[]{:S(2)}, u32[]{:S(2)}) collective-permute-start(bf16[2,2,2,24,1792]{4,3,1,0,2:T(8,128)(2,1)S(1)} %dynamic-slice_bitcast_fusion.5), channel_id=1, source_target_pairs={{0,4},{1,5},{2,6},{3,7},{4,0},{5,1},{6,2},{7,3},{8,12},{9,13},{10,... | collective-permute-start | bytes 2064392 | tf_op jit(solution)/shard_map/ppermute | solution.py:639
  478.2 22.3 %collective-permute-start.22 = (bf16[2,2,2,24,1920]{4,3,1,0,2:T(8,128)(2,1)S(1)}, bf16[2,2,2,24,1920]{4,3,1,0,2:T(8,128)(2,1)S(1)}, u32[]{:S(2)}, u32[]{:S(2)}) collective-permute-start(bf16[2,2,2,24,1920]{4,3,1,0,2:T(8,128)(2,1)S(1)} %copy-done.9), channel_id=1, source_target_pairs={{0,2},{1,3},{2,0},{3,1},{4,6},{5,7},{6,4},{7,5},{8,10},{9,11},{10,... | collective-permute-start | bytes 2211848 | tf_op jit(solution)/shard_map/ppermute | solution.py:639
  479.1 31.9 %collective-permute-start.27 = (bf16[24,6144]{1,0:T(8,128)(2,1)S(1)}, bf16[24,6144]{1,0:T(8,128)(2,1)S(1)}, u32[]{:S(2)}, u32[]{:S(2)}) collective-permute-start(bf16[24,6144]{1,0:T(8,128)(2,1)S(1)} %get-tuple-element.109), channel_id=1, source_target_pairs={{0,8},{1,9},{2,10},{3,11},{4,12},{5,13},{6,14},{7,15},{8,0},{9,1},... | collective-permute-start | bytes 884744 | tf_op jit(solution)/shard_map/ppermute | solution.py:639
  479.7 34.1 %collective-permute-start.28 = (bf16[24,6144]{1,0:T(8,128)(2,1)S(1)}, bf16[24,6144]{1,0:T(8,128)(2,1)S(1)}, u32[]{:S(2)}, u32[]{:S(2)}) collective-permute-start(bf16[24,6144]{1,0:T(8,128)(2,1)S(1)} %get-tuple-element.110), channel_id=1, source_target_pairs={{0,16},{1,17},{2,18},{3,19},{4,20},{5,21},{6,22},{7,23},{8,24},{9,... | collective-permute-start | bytes 884744 | tf_op jit(solution)/shard_map/ppermute | solution.py:639
  481.5 32.3 %collective-permute-start.29 = (bf16[24,6144]{1,0:T(8,128)(2,1)S(1)}, bf16[24,6144]{1,0:T(8,128)(2,1)S(1)}, u32[]{:S(2)}, u32[]{:S(2)}) collective-permute-start(bf16[24,6144]{1,0:T(8,128)(2,1)S(1)} %get-tuple-element.111), channel_id=1, source_target_pairs={{0,24},{1,25},{2,26},{3,27},{4,28},{5,29},{6,30},{7,31},{8,16},{9,... | collective-permute-start | bytes 884744 | tf_op jit(solution)/shard_map/ppermute | solution.py:639
  499.0 8.1 %collective-permute-start.21 = (bf16[2,2,24,1792]{3,2,1,0:T(8,128)(2,1)S(1)}, bf16[2,2,24,1792]{3,2,1,0:T(8,128)(2,1)S(1)}, u32[]{:S(2)}, u32[]{:S(2)}) collective-permute-start(bf16[2,2,24,1792]{3,2,1,0:T(8,128)(2,1)S(1)} %dynamic-slice_bitcast_fusion.12), channel_id=1, source_target_pairs={{0,2},{1,3},{2,0},{3,1},{4,6},{5,7},{6,4},{7,5},{8,10},{9,11},{10,... | collective-permute-start | bytes 1032200 | tf_op jit(solution)/shard_map/ppermute | solution.py:639
  500.8 8.4 %collective-permute-start.23 = (bf16[2,2,24,1920]{3,2,1,0:T(8,128)(2,1)S(1)}, bf16[2,2,24,1920]{3,2,1,0:T(8,128)(2,1)S(1)}, u32[]{:S(2)}, u32[]{:S(2)}) collective-permute-start(bf16[2,2,24,1920]{3,2,1,0:T(8,128)(2,1)S(1)} %dynamic-slice_bitcast_fusion.11), channel_id=1, source_target_pairs={{0,4},{1,5},{2,6},{3,7},{4,0},{5,1},{6,2},{7,3},{8,12},{9,13},{10,... | collective-permute-start | bytes 1105928 | tf_op jit(solution)/shard_map/ppermute | solution.py:639
  509.3 37.8 %copy-start.8 = (bf16[8,256,512]{2,1,0:T(8,128)(2,1)S(1)}, bf16[8,256,512]{2,1,0:T(8,128)(2,1)}, u32[]{:S(2)}) copy-start(bf16[8,256,512]{2,1,0:T(8,128)(2,1)} %get-tuple-element.75) | copy-start | bytes 6291460
  509.4 7.4 %collective-permute-start.24 = (bf16[24,3712]{1,0:T(8,128)(2,1)S(1)}, bf16[24,3712]{1,0:T(8,128)(2,1)S(1)}, u32[]{:S(2)}, u32[]{:S(2)}) collective-permute-start(bf16[24,3712]{1,0:T(8,128)(2,1)S(1)} %get-tuple-element.156), channel_id=1, source_target_pairs={{0,8},{1,9},{2,10},{3,11},{4,12},{5,13},{6,14},{7,15},{8,0},{9,1},... | collective-permute-start | bytes 534536 | tf_op jit(solution)/shard_map/ppermute | solution.py:639
  509.4 36.7 %collective-permute-start.25 = (bf16[24,3712]{1,0:T(8,128)(2,1)S(1)}, bf16[24,3712]{1,0:T(8,128)(2,1)S(1)}, u32[]{:S(2)}, u32[]{:S(2)}) collective-permute-start(bf16[24,3712]{1,0:T(8,128)(2,1)S(1)} %get-tuple-element.158), channel_id=1, source_target_pairs={{0,16},{1,17},{2,18},{3,19},{4,20},{5,21},{6,22},{7,23},{8,24},{9,... | collective-permute-start | bytes 534536 | tf_op jit(solution)/shard_map/ppermute | solution.py:639
  511.0 35.1 %collective-permute-start.26 = (bf16[24,3712]{1,0:T(8,128)(2,1)S(1)}, bf16[24,3712]{1,0:T(8,128)(2,1)S(1)}, u32[]{:S(2)}, u32[]{:S(2)}) collective-permute-start(bf16[24,3712]{1,0:T(8,128)(2,1)S(1)} %get-tuple-element.157), channel_id=1, source_target_pairs={{0,24},{1,25},{2,26},{3,27},{4,28},{5,29},{6,30},{7,31},{8,16},{9,... | collective-permute-start | bytes 534536 | tf_op jit(solution)/shard_map/ppermute | solution.py:639
  (3 other events, 2.2 us)
Sparse Core Ops, SparseCore 0:
  15.6 110.0 all-gather.4
  129.1 68.2 all-gather.6
  457.5 90.6 all-gather.10
  551.5 106.7 all-gather.8

commit v4 on v3

--- a/solution.py
+++ b/solution.py
@@ -83,6 +83,16 @@
     return block.T.astype(BF16)
 
 
+def by_core(core_ref, fill, keep_ref, give_ref):
+    @pl.when(core_ref[0] == 0)
+    def _():
+        fill(keep_ref, give_ref)
+
+    @pl.when(core_ref[0] != 0)
+    def _():
+        fill(give_ref, keep_ref)
+
+
 def segment_sum(x, ones):
     high = x.astype(BF16)
     low = (x - high.astype(F32)).astype(BF16)
@@ -99,8 +109,8 @@
 
 
 def decoder_kernel(
-    rows_ref, idx_ref, cot_ref, pos_ref, mask_ref, small_ref, wqkv_ref, wo_ref, wu_ref, wd_ref,
-    out_ref, ret_ref, grad_ref,
+    core_ref, rows_ref, idx_ref, cot_ref, pos_ref, mask_ref, small_ref, wqkv_ref, wo_ref, wu_ref, wd_ref,
+    out_ref, ret_ref, keep_ref, give_ref,
     acc_qkv, acc_o, acc_u, acc_d, gvec_ref, vec_ref,
     x_s, qkv_s, p_s, o_s, a2_s, a2t_s, dzt_s, da_s, y_s, dqkv_s,
 ):
@@ -250,19 +260,27 @@
 
     @pl.when(step == last)
     def _():
-        grad_ref[:, : 3 * width] = acc_qkv[...].astype(BF16)
-        grad_ref[:, 3 * width : 4 * width] = acc_o[...].astype(BF16)
-        grad_ref[:, 4 * width : 4 * width + ff] = acc_u[...].astype(BF16)
-        grad_ref[:, 4 * width + ff : 4 * width + 2 * ff] = acc_d[...].astype(BF16)
-        grad_ref[:, 4 * width + 2 * ff :] = columns_of_vectors(gvec_ref[...])
-
-
-def decoder_block(rows, idx, cot, pos, mask, pack, wd):
+        half = ff // 2
+
+        def fill(first, second):
+            first[:, : 3 * width] = acc_qkv[...].astype(BF16)
+            first[:, 3 * width : 4 * width] = acc_o[...].astype(BF16)
+            first[:, 4 * width : 4 * width + half] = acc_u[:, :half].astype(BF16)
+            first[:, 4 * width + half :] = columns_of_vectors(gvec_ref[...])
+            second[:, :half] = acc_u[:, half:].astype(BF16)
+            second[:, half : half + ff] = acc_d[...].astype(BF16)
+            second[:, half + ff :] = jnp.zeros((width, second.shape[1] - half - ff), BF16)
+
+        by_core(core_ref, fill, keep_ref, give_ref)
+
+
+def decoder_block(core, rows, idx, cot, pos, mask, pack_one, pack_two, wd):
     n_half, slots, width = rows.shape
     cells = cot.shape[1]
     ff = wd.shape[0]
     halves = 2
     m_rows = halves * cells
+    half_wide = 4 * width + ff // 2 + LANES
     vm = pltpu.VMEM
     flops = 6 * n_half * cells * (4 * width + 2 * ff) * width * 2
 
@@ -274,26 +292,29 @@
         decoder_kernel,
         grid=(n_half // halves,),
         in_specs=[
+            pl.BlockSpec(memory_space=pltpu.SMEM),
             pl.BlockSpec((halves, slots, width), lambda i: (i, 0, 0)),
             pl.BlockSpec((halves, 1, slots), lambda i: (i, 0, 0)),
             pl.BlockSpec((halves, cells, width), lambda i: (i, 0, 0)),
             whole(cells, width),
             whole(cells, LANES),
-            whole(width, LANES, at=(4 * width + 2 * ff) // LANES),
+            whole(width, LANES, at=(4 * width + ff // 2) // LANES),
             whole(width, 3 * width),
             whole(width, width, at=3),
-            whole(width, ff, at=1),
+            whole(width, ff),
             whole(ff, width),
         ],
         out_specs=[
             pl.BlockSpec((halves, cells, width), lambda i: (i, 0, 0)),
             pl.BlockSpec((halves, slots, width), lambda i: (i, 0, 0)),
-            whole(width, 4 * width + 2 * ff + LANES),
+            whole(width, half_wide),
+            whole(width, half_wide),
         ],
         out_shape=[
             jax.ShapeDtypeStruct((n_half, cells, width), BF16),
             jax.ShapeDtypeStruct((n_half, slots, width), BF16),
-            jax.ShapeDtypeStruct((width, 4 * width + 2 * ff + LANES), BF16),
+            jax.ShapeDtypeStruct((width, half_wide), BF16),
+            jax.ShapeDtypeStruct((width, half_wide), BF16),
         ],
         scratch_shapes=[
             vm((width, 3 * width), F32),
@@ -318,7 +339,10 @@
         ),
         cost_estimate=pl.CostEstimate(flops=flops, bytes_accessed=40 << 20, transcendentals=0),
         name="decoder_block",
-    )(rows, idx.reshape(n_half, 1, slots), cot, pos, mask, pack, pack, pack, pack, wd)
+    )(
+        core, rows, idx.reshape(n_half, 1, slots), cot, pos, mask,
+        pack_one, pack_one, pack_one, pack_two, wd,
+    )
 
 
 def enc_spread(t, head_masks):
@@ -388,8 +412,8 @@
 
 
 def enc_feed_back_kernel(
-    dsent_ref, enc_ref, proj_ref, h_ref, gp_ref, x2_ref, vec_ref, wu_ref, wd_ref,
-    gproj_ref, grad_ref, dx2_ref, gvec_ref,
+    core_ref, dsent_ref, enc_ref, proj_ref, h_ref, gp_ref, x2_ref, vec_ref, wu_ref, wd_ref,
+    gproj_ref, keep_ref, give_ref, dx2_ref, gvec_ref,
     a2t_s, dz_s, dzt_s, da_s,
 ):
     ff = wu_ref.shape[1]
@@ -410,9 +434,11 @@
         at = pl.ds(pl.multiple_of(c * chunk, chunk), chunk)
         dh = mm_t(dz_s[...], wd_ref[at, :])
         du = (gp_ref[:, at].astype(F32) * dh).astype(BF16)
-        below = pl.ds(pl.multiple_of(ff + c * chunk, chunk), chunk)
-        grad_ref[:, at] = mm(a2t_s[...], du).astype(BF16)
-        grad_ref[:, below] = mm(dzt_s[...], h_ref[:, at]).astype(BF16)
+        up_grad = mm(a2t_s[...], du).astype(BF16)
+        down_grad = mm(dzt_s[...], h_ref[:, at]).astype(BF16)
+        first = core_ref[0] == 0
+        keep_ref[:, at] = jnp.where(first, up_grad, down_grad)
+        give_ref[:, at] = jnp.where(first, down_grad, up_grad)
         da_s[...] += mm_t(du, wu_ref[:, at])
         return carry
 
@@ -426,9 +452,9 @@
 
 
 def enc_attend_back_kernel(
-    dx2_ref, o_ref, qkv_ref, p_ref, x_ref, vec_ref, wqkv_ref, wo_ref, gproj_ref, gvec2_ref,
-    grad_ref, dvis_ref,
-    gvec_ref, do_s, dqkv_s,
+    core_ref, dx2_ref, o_ref, qkv_ref, p_ref, x_ref, vec_ref, wqkv_ref, wo_ref, gproj_ref, gvec2_ref,
+    keep_ref, give_ref, dvis_ref,
+    gvec_ref, do_s, dqkv_s, gqkv_s, go_s,
 ):
     clips, slots, width = x_ref.shape
     m_rows = clips * slots
@@ -437,7 +463,7 @@
     scale = head_dim ** (-0.5)
     gain1, shift1 = vec_ref[0:1, :], vec_ref[1:2, :]
     dy2 = dx2_ref[...].astype(BF16)
-    grad_ref[:, 3 * width : 4 * width] = mm(o_ref[...].T, dy2).astype(BF16)
+    go_s[...] = mm(o_ref[...].T, dy2).astype(BF16)
     do_s[...] = mm_t(dy2, wo_ref[...]).astype(BF16)
 
     def fold(t):
@@ -470,21 +496,37 @@
     x = x_ref[...].reshape(m_rows, width).astype(F32)
     xhat, rstd = normalise(x)
     a1t = (xhat * gain1 + shift1).astype(BF16).T
-    grad_ref[:, : 3 * width] = mm(a1t, dqkv_s[...]).astype(BF16)
+    gqkv_s[...] = mm(a1t, dqkv_s[...]).astype(BF16)
     da = mm_t(dqkv_s[...], wqkv_ref[...])
     gvec_ref[...] = gvec2_ref[...]
     gvec_ref[0:1, :] = jnp.sum(da * xhat, axis=0, keepdims=True)
     gvec_ref[1:2, :] = jnp.sum(da, axis=0, keepdims=True)
     dx = dx2_ref[...] + norm_back(da, xhat, rstd, gain1)
     dvis_ref[...] = dx.reshape(clips, slots, width).astype(BF16)
-    grad_ref[:, 4 * width : -LANES] = gproj_ref[...]
-    grad_ref[:, -LANES:] = columns_of_vectors(gvec_ref[...])
+    half = keep_ref.shape[1]
+    tail = 3 * width - half
+    sent = gproj_ref.shape[1]
+
+    def fill(first, second):
+        first[...] = gqkv_s[:, :half]
+        second[:, :tail] = gqkv_s[:, half:]
+        second[:, tail : tail + width] = go_s[...]
+        second[:, tail + width : tail + width + sent] = gproj_ref[...]
+        end = tail + width + sent
+        second[:, end : end + LANES] = columns_of_vectors(gvec_ref[...])
+        second[:, end + LANES :] = jnp.zeros((width, half - end - LANES), BF16)
+
+    by_core(core_ref, fill, keep_ref, give_ref)
 
 
 def whole_call(kernel, args, outs, scratch, name, flops):
     arrays, specs = [], []
     for arg in args:
         array, shape, at = arg if isinstance(arg, tuple) else (arg, arg.shape, 0)
+        if len(shape) == 1:
+            arrays.append(array)
+            specs.append(pl.BlockSpec(memory_space=pltpu.SMEM))
+            continue
         index = (0,) * (len(shape) - 1) + (at,)
         arrays.append(array)
         specs.append(pl.BlockSpec(shape, lambda i, index=index: index, pipeline_mode=pl.Buffered(1)))
@@ -535,51 +577,73 @@
     return whole_call(enc_feed_kernel, (x2, vecs, up, wd, proj), outs, scratch, "enc_feed", 18 * 10**9)
 
 
-def enc_feed_back(dsent, enc, h, gp, x2, vecs, blocks, wd):
+def enc_feed_back(core, dsent, enc, h, gp, x2, vecs, blocks, wd):
     m, width = x2.shape
     ff = wd.shape[0]
     _, _, up, proj, _ = blocks
-    outs = [(proj[1], BF16), ((width, 2 * ff), BF16), ((m, width), F32), ((8, width), F32)]
+    half = (width, ff)
+    outs = [(proj[1], BF16), (half, BF16), (half, BF16), ((m, width), F32), ((8, width), F32)]
     scratch = [((width, m), BF16), ((m, width), BF16), ((width, m), BF16), ((m, width), F32)]
-    args = (dsent, enc, proj, h, gp, x2, vecs, up, wd)
+    args = (core, dsent, enc, proj, h, gp, x2, vecs, up, wd)
     return whole_call(enc_feed_back_kernel, args, outs, scratch, "enc_feed_back", 24 * 10**9)
 
 
-def enc_attend_back(dx2, o, qkv, p, x, vecs, blocks, gproj, gvec):
+def attend_half(width, sent):
+    blocks = (4 * width + sent + LANES) // LANES
+    return (blocks + 1) // 2 * LANES
+
+
+def enc_attend_back(core, dx2, o, qkv, p, x, vecs, blocks, gproj, gvec):
     m, width = dx2.shape
     w_qkv, w_out, _, _, _ = blocks
-    outs = [((width, 4 * width + gproj.shape[1] + LANES), BF16), (x.shape, BF16)]
-    scratch = [((8, width), F32), ((m, width), BF16), ((m, 3 * width), BF16)]
-    args = (dx2, o, qkv, p, x, vecs, w_qkv, w_out, gproj, gvec)
+    half = (width, attend_half(width, gproj.shape[1]))
+    outs = [(half, BF16), (half, BF16), (x.shape, BF16)]
+    scratch = [
+        ((8, width), F32),
+        ((m, width), BF16),
+        ((m, 3 * width), BF16),
+        ((width, 3 * width), BF16),
+        ((width, width), BF16),
+    ]
+    args = (core, dx2, o, qkv, p, x, vecs, w_qkv, w_out, gproj, gvec)
     return whole_call(enc_attend_back_kernel, args, outs, scratch, "enc_attend_back", 14 * 10**9)
 
 
-def unpack_kernel(spans, tall, sum_ref, *out_refs):
-    for (start, size), ref in zip(spans, out_refs[:-2]):
-        ref[...] = sum_ref[:, start : start + size].astype(F32)
-    start, size = tall
+def unpack_kernel(pieces, tall, small, packed_ref, *out_refs):
+    chips, _, rows, _ = packed_ref.shape
+
+    def read(part, start, size):
+        return packed_ref[:, part, :, start : start + size].reshape(chips * rows, size).astype(F32)
+
+    for out, to, part, start, size in pieces:
+        out_refs[out][:, to : to + size] = read(part, start, size)
+    part, start, size = tall
     chunk = 512
     for c in range(size // chunk):
-        part = sum_ref[:, start + c * chunk : start + (c + 1) * chunk].astype(F32)
-        out_refs[-2][c * chunk : (c + 1) * chunk, :] = part.T
-    out_refs[-1][...] = sum_ref[:, start + size :].astype(F32).T[0:8, :]
-
-
-def unpack_sums(packed, spans, tall):
-    rows, wide = packed.shape
-    step = LANES
-    size = tall[1]
+        out_refs[-2][c * chunk : (c + 1) * chunk, :] = read(part, start + c * chunk, chunk).T
+    out_refs[-1][...] = read(*small, LANES).T[0:8, :]
+
+
+def unpack_sums(packed, widths, pieces, tall, small):
+    chips, _, rows, wide = packed.shape
+    height = chips * rows
+    if rows % 16:
+        packed = packed.transpose(1, 0, 2, 3).reshape(2, 16, height // 16, wide).transpose(1, 0, 2, 3)
+        chips, _, rows, wide = packed.shape
+    group = LANES // math.gcd(rows, LANES)
+    step = group * rows
+    size = tall[2]
     side = lambda n: pl.BlockSpec((step, n), lambda i: (i, 0))
     down = lambda n: pl.BlockSpec((n, step), lambda i: (0, i))
     return pl.pallas_call(
-        functools.partial(unpack_kernel, spans, tall),
-        grid=(rows // step,),
-        in_specs=[side(wide)],
-        out_specs=[side(n) for _, n in spans] + [down(size), down(8)],
-        out_shape=[jax.ShapeDtypeStruct((rows, n), F32) for _, n in spans]
-        + [jax.ShapeDtypeStruct((size, rows), F32), jax.ShapeDtypeStruct((8, rows), F32)],
+        functools.partial(unpack_kernel, pieces, tall, small),
+        grid=(chips // group,),
+        in_specs=[pl.BlockSpec((group, 2, rows, wide), lambda i: (i, 0, 0, 0))],
+        out_specs=[side(n) for n in widths] + [down(size), down(8)],
+        out_shape=[jax.ShapeDtypeStruct((height, n), F32) for n in widths]
+        + [jax.ShapeDtypeStruct((size, height), F32), jax.ShapeDtypeStruct((8, height), F32)],
         compiler_params=pltpu.CompilerParams(vmem_limit_bytes=VMEM_BYTES),
-        cost_estimate=pl.CostEstimate(flops=0, bytes_accessed=6 * rows * wide, transcendentals=0),
+        cost_estimate=pl.CostEstimate(flops=0, bytes_accessed=6 * height * wide, transcendentals=0),
         name="unpack_sums",
     )(packed)
 
@@ -596,14 +660,15 @@
 
 
 class RunningSum:
-    def __init__(self, partial, total, cut):
+    def __init__(self, keep, give, total):
         bits = total.bit_length() - 1
-        rows = partial.shape[0] // total
         self.total = total
-        self.held = [partial.reshape((2,) * bits + (rows, partial.shape[1]))]
-        self.left = [list(range(bits - 1, -1, -1))]
-        self.cut = cut
-        self.plan = [[[0]], [[2], [1]], [[1], [2]]]
+        self.cut = keep.shape[1] // 256 * 128
+        got = lax.ppermute(give, AXES, partner_pairs(total, 1))
+        rows = keep.shape[0] // (total // 2)
+        self.held = [add_low(keep, got).reshape((2,) * (bits - 1) + (rows, keep.shape[1]))]
+        self.left = [list(range(bits - 1, 0, -1))]
+        self.plan = [[[2], [1]], [[1], [2]]]
         rest = list(range(3, bits))
         while rest:
             self.plan.append([rest[:2]])
@@ -645,13 +710,58 @@
         ]
         self.plan = self.plan[1:]
 
-    def step(self):
-        self.deliver(self.offers())
-
     def finish(self):
         while self.plan:
-            self.step()
+            self.deliver(self.offers())
         return jnp.concatenate(self.held, axis=-1)
+
+
+class RunningGather:
+    def __init__(self, shard, total, cut, axis):
+        bits = total.bit_length() - 1
+        self.total, self.cut, self.axis = total, cut, axis
+        self.shape = shard.shape
+        rest, self.plan = list(range(3, bits)), []
+        while rest:
+            self.plan.append([rest[:2]])
+            rest = rest[2:]
+        self.plan += [[[1], [2]], [[2], [1]], [[0], [0]]]
+        self.held, self.have = [shard], [[]]
+
+    def offers(self):
+        groups = self.plan[0]
+        if len(groups) > len(self.held):
+            held, at = self.held[0], self.held[0].ndim - 2 + self.axis
+            first = lax.slice_in_dim(held, 0, self.cut, axis=at)
+            self.held = [first, lax.slice_in_dim(held, self.cut, held.shape[at], axis=at)]
+            self.have = [list(self.have[0]), list(self.have[0])]
+        gives, self.masks = [], []
+        for held, group in zip(self.held, groups):
+            for k in range(1, 1 << len(group)):
+                gives.append(held)
+                self.masks.append(k << group[0])
+        return gives
+
+    def deliver(self, gives):
+        me = lax.axis_index(AXES)
+        got = [
+            lax.ppermute(give, AXES, partner_pairs(self.total, mask))
+            for give, mask in zip(gives, self.masks)
+        ]
+        each = len(got) // len(self.held)
+        for i, group in enumerate(self.plan[0]):
+            parts = [self.held[i]] + got[i * each : (i + 1) * each]
+            for b, bit in enumerate(group):
+                flip = ((me >> bit) & 1) == 1
+                parts = [jnp.where(flip, parts[k ^ (1 << b)], part) for k, part in enumerate(parts)]
+            self.have[i] = sorted(self.have[i] + group, reverse=True)
+            at = self.have[i].index(group[-1])
+            held = jnp.stack(parts, axis=at)
+            self.held[i] = held.reshape(held.shape[:at] + (2,) * len(group) + held.shape[at + 1 :])
+        self.plan = self.plan[1:]
+
+    def result(self):
+        return [held.reshape((self.total,) + held.shape[-2:]) for held in self.held]
 
 
 def together(*groups):
@@ -675,7 +785,7 @@
     rows = beside.shape[0] // total
     count = beside.shape[1] // width
     parts = [beside[:, i * width : (i + 1) * width].reshape(total, rows, width) for i in range(count)]
-    return jnp.concatenate(parts, axis=1).reshape(-1, width)
+    return jnp.concatenate(parts, axis=1)
 
 
 def swap_band(array, bit):
@@ -739,20 +849,30 @@
     total = lax.axis_size(AXES)
     enc_wide, dec_wide = enc_out.shape[1], dec_out.shape[1]
     enc_ff, dec_ff = enc_up.shape[1], dec_up.shape[1]
+    core = (lax.axis_index(AXES) % 2).reshape(1)
     enc_small = columns_of([enc_gain1, enc_shift1, enc_gain2, enc_shift2])
-    enc_pack = jnp.concatenate(
-        [enc_qkv, enc_out, enc_up, proj, enc_small] + blocks_beside(enc_down, enc_out.shape[0]), axis=1
-    )
-    enc_pack = gather_rows(enc_pack)
-    enc_end = 4 * enc_wide + enc_ff + dec_wide + LANES
-    whole_down = blocks_below(enc_pack[:, enc_end:], total, enc_wide)
+    enc_pack = gather_rows(jnp.concatenate([enc_qkv, enc_out, enc_up, proj, enc_small], axis=1))
     dec_small = columns_of([dec_gain1, dec_shift1, dec_gain2, dec_shift2, mask_token])
-    dec_pack = jnp.concatenate(
-        [dec_qkv, dec_out, dec_up] + blocks_beside(dec_down, dec_out.shape[0]) + [dec_small], axis=1
-    )
-    dec_pack = gather_rows(dec_pack)
-    dec_end = 4 * dec_wide + dec_ff
-    dec_whole_down = blocks_below(dec_pack[:, dec_end : dec_end + dec_ff], total, dec_wide)
+    dec_tall = blocks_beside(dec_down, dec_out.shape[0])
+    near, far = dec_tall[: len(dec_tall) // 2], dec_tall[len(dec_tall) // 2 :]
+    dec_first = jnp.concatenate([dec_qkv, dec_out] + near + [dec_small], axis=1)
+    dec_pack = jnp.concatenate([dec_first, dec_up] + far, axis=1)
+    down_run = RunningGather(enc_down, total, enc_down.shape[0] // 2, 0)
+    dec_run = RunningGather(dec_pack, total, dec_first.shape[1], 1)
+    while len(down_run.plan) > 3:
+        down_run.deliver(down_run.offers())
+    gives, dec_gives = together(down_run.offers(), dec_run.offers())
+    down_run.deliver(gives)
+    dec_run.deliver(dec_gives)
+    while len(dec_run.plan) > 3:
+        dec_run.deliver(dec_run.offers())
+    down_run.deliver(down_run.offers())
+    gives, dec_gives = together(down_run.offers(), dec_run.offers())
+    down_run.deliver(gives)
+    dec_run.deliver(dec_gives)
+    whole_down = jnp.concatenate(down_run.result(), axis=1).reshape(-1, enc_wide)
+    enc_pack, whole_down, gives = together(enc_pack, whole_down, dec_run.offers())
+    dec_run.deliver(gives)
 
     clip_count, slot_total, _ = visible.shape
     half_clips = clip_count // 2
@@ -771,6 +891,12 @@
     blocks = enc_blocks(enc_pack, enc_wide, enc_ff, dec_wide)
     qkv, probs, mixed, middle, vecs = enc_attend(visible, valid_mask, blocks)
     sent_rows, encoded, hidden, slope = enc_feed(middle, vecs, blocks, whole_down)
+    sent_rows, gives = together(sent_rows, dec_run.offers())
+    dec_run.deliver(gives)
+    pack_one, pack_two = [part.reshape(-1, part.shape[2]) for part in dec_run.result()]
+    tall_one = blocks_below(pack_one[:, 4 * dec_wide : 4 * dec_wide + dec_ff // 2], total, dec_wide)
+    tall_two = blocks_below(pack_two[:, dec_ff:], total, dec_wide)
+    dec_whole_down = jnp.concatenate([tall_one, tall_two], axis=1).reshape(-1, dec_wide)
     arrived_rows = owners_to_bands(sent_rows.reshape(2, half_clips, slot_total, dec_wide))
     half_total = 4 * half_clips
 
@@ -789,39 +915,37 @@
 
     cells_in = WINDOW * WINDOW
     allowed = (query // cells_in == key // cells_in) & (label(query) == label(key))
-    decoded, returning, dec_grad = decoder_block(
+    decoded, returning, keep, give = decoder_block(
+        core,
         arrived_rows.reshape(half_total, slot_total, dec_wide),
         arrived_index,
         cotangent.reshape(half_total, cell_count, dec_wide),
         position_table(patch_number),
         allowed.astype(F32),
-        dec_pack,
+        pack_one,
+        pack_two,
         dec_whole_down,
     )
     decoded_out = decoded.reshape(cotangent.shape)
 
-    middle_cut = lambda grad: grad.shape[1] // 256 * 128
-    dec_run = RunningSum(dec_grad, total, middle_cut(dec_grad))
-    dec_run.step()
+    dec_run = RunningSum(keep, give, total)
     grad_sent = bands_to_owners(returning.reshape(2, 2, half_clips, slot_total, dec_wide))
     grad_sent = grad_sent.reshape(-1, dec_wide)
     grad_sent, gives = together(grad_sent, dec_run.offers())
     dec_run.deliver(gives)
-    g_proj, grad_feed, grad_middle, g_vec = enc_feed_back(
-        grad_sent, encoded, hidden, slope, middle, vecs, blocks, whole_down
+    g_proj, keep, give, grad_middle, g_vec = enc_feed_back(
+        core, grad_sent, encoded, hidden, slope, middle, vecs, blocks, whole_down
     )
-    grad_feed, grad_middle, gives = together(grad_feed, grad_middle, dec_run.offers())
+    keep, give, grad_middle, gives = together(keep, give, grad_middle, dec_run.offers())
     dec_run.deliver(gives)
-    feed_run = RunningSum(grad_feed, total, enc_ff)
-    feed_run.step()
-    grad_attend, grad_visible = enc_attend_back(
-        grad_middle, mixed, qkv, probs, visible, vecs, blocks, g_proj, g_vec
+    feed_run = RunningSum(keep, give, total)
+    keep, give, grad_visible = enc_attend_back(
+        core, grad_middle, mixed, qkv, probs, visible, vecs, blocks, g_proj, g_vec
     )
-    grad_attend, gives, feed_gives = together(grad_attend, dec_run.offers(), feed_run.offers())
+    keep, give, gives, feed_gives = together(keep, give, dec_run.offers(), feed_run.offers())
     dec_run.deliver(gives)
     feed_run.deliver(feed_gives)
-    attend_run = RunningSum(grad_attend, total, middle_cut(grad_attend))
-    attend_run.step()
+    attend_run = RunningSum(keep, give, total)
     dec_shard = dec_run.finish()
     dec_shard, feed_gives, gives = together(dec_shard, feed_run.offers(), attend_run.offers())
     dec_sum = gather_rows(dec_shard)
@@ -829,20 +953,40 @@
     feed_gives, gives = together(feed_run.offers(), gives)
     feed_run.deliver(feed_gives)
     attend_run.deliver(gives)
-    attend_run.step()
+    attend_run.deliver(attend_run.offers())
     feed_sum = feed_run.finish()
     attend_sum = attend_run.finish()
-    small_at = attend_sum.shape[1] - LANES
-    enc_shard = jnp.concatenate(
-        [attend_sum[:, :small_at], feed_sum, attend_sum[:, small_at:]], axis=1
+    enc_sum = gather_rows(jnp.concatenate([attend_sum, feed_sum], axis=1))
+
+    by_chip = lambda packed, shard: packed.reshape(total // 2, 2, shard.shape[0], packed.shape[1])
+    half = dec_ff // 2
+    d_qkv, d_out, d_up, d_down, dec_vecs = unpack_sums(
+        by_chip(dec_sum, dec_shard),
+        (3 * dec_wide, dec_wide, dec_ff),
+        (
+            (0, 0, 0, 0, 3 * dec_wide),
+            (1, 0, 0, 3 * dec_wide, dec_wide),
+            (2, 0, 0, 4 * dec_wide, half),
+            (2, half, 1, 0, half),
+        ),
+        (1, half, dec_ff),
+        (0, 4 * dec_wide + half),
     )
-    enc_sum = gather_rows(enc_shard)
-
-    spans = [(0, 3 * dec_wide), (3 * dec_wide, dec_wide), (4 * dec_wide, dec_ff)]
-    d_qkv, d_out, d_up, d_down, dec_vecs = unpack_sums(dec_sum, spans, (dec_end, dec_ff))
-    start = 4 * enc_wide + dec_wide
-    spans = [(0, 3 * enc_wide), (3 * enc_wide, enc_wide), (4 * enc_wide, dec_wide), (start, enc_ff)]
-    e_qkv, e_out, e_proj, e_up, e_down, enc_vecs = unpack_sums(enc_sum, spans, (start + enc_ff, enc_ff))
+    half = attend_sum.shape[1]
+    tail = 3 * enc_wide - half
+    e_qkv, e_out, e_proj, e_up, e_down, enc_vecs = unpack_sums(
+        by_chip(enc_sum, attend_sum),
+        (3 * enc_wide, enc_wide, dec_wide, enc_ff),
+        (
+            (0, 0, 0, 0, half),
+            (0, half, 1, 0, tail),
+            (1, 0, 1, tail, enc_wide),
+            (2, 0, 1, tail + enc_wide, dec_wide),
+            (3, 0, 0, half, enc_ff),
+        ),
+        (1, half, enc_ff),
+        (1, tail + enc_wide + dec_wide),
+    )
     return (
         decoded_out,
         grad_visible,

time: 693 us -> 646 us (0.932)
  waiting for transfers between devices: 331 us -> 257 us
  starting transfers between devices: 33.6 us -> 83.4 us
  local copies, waits for them, and re-layouts: 60.4 us -> 41.2 us
  Pallas kernels: 208 us -> 195 us
  other arithmetic: 35.1 us -> 44.8 us
    all_gather x4 -> x3, waiting for transfers between devices: 217 us -> 107 us  [gather_rows(): return lax.all_gather(shard, AXES, axis=0, tiled=True)]
    ppermute x24 -> x39, starting transfers between devices: 27.1 us -> 77.4 us  [deliver(): lax.ppermute(give, AXES, partner_pairs(self.total, mask))]
    ppermute x24 -> x39, waiting for transfers between devices: 94.7 us -> 131 us  [deliver(): lax.ppermute(give, AXES, partner_pairs(self.total, mask))]
    pallas_call x1, Pallas kernels: 116 us -> 104 us  [decoder_block(): pl.pallas_call(decoder_kernel, grid=(n_half // halves,), in_specs=[pl.Blo...]
    dynamic_slice x3, local copies, waits for them, and re-layouts: 10.8 us -> 0.45 us  [offers(): lax.dynamic_index_in_dim(held, mine, place, keepdims=False)]
    another operation x0 -> x26, other arithmetic: none -> 8.11 us  [deliver(): held = jnp.stack(parts, axis=at)]
    unnamed x49 -> x73, local copies, waits for them, and re-layouts: 13.7 us -> 17 us
  transfers between devices with their start and end apart: 34 -> 51, of which waited for: 15 -> 21; matrix products, arithmetic and copies ran while one was open for 7% -> 9% of each run, Pallas kernels for 11% -> 12%
where the time goes in v4:
time: 646 us; the launch traced here: 636 us
  waiting for transfers between devices  257 us (40%)
  Pallas kernels  195 us (30%)
  starting transfers between devices  83.4 us (13%)
  other arithmetic  44.8 us (7%)
  local copies, waits for them, and re-layouts  41.2 us (6%)
  between operations  15 us (2%)
    ppermute x39, waiting for transfers between devices, deliver(): lax.ppermute(give, AXES, partner_pairs(self.total, mask))  131 us
    all_gather x3, waiting for transfers between devices, gather_rows(): return lax.all_gather(shard, AXES, axis=0, tiled=True)  107 us
    pallas_call x1, Pallas kernels, decoder_block(): pl.pallas_call(decoder_kernel, grid=(n_half // halves,), in_specs=[pl.Blo...  104 us
    ppermute x39, starting transfers between devices, deliver(): lax.ppermute(give, AXES, partner_pairs(self.total, mask))  77.4 us
    pallas_call x4, Pallas kernels, whole_call(): pl.pallas_call(kernel, grid=(1,), in_specs=specs, out_specs=[zero(s) for...  69.2 us
    pallas_call x2, Pallas kernels, unpack_sums(): pl.pallas_call(functools.partial(unpack_kernel, pieces, tall, small), gri...  21.7 us
    convert_element_type x18, other arithmetic, add_low(): return sum((part.astype(F32) for part in parts)).astype(BF16)  19.7 us
    ppermute x6, waiting for transfers between devices, swap_band(): return lax.ppermute(array, 'band', [(i, i ^ bit) for i in range(4)])  18.1 us
  transfers between devices with their start and end apart: 51, of which 21 were waited for; matrix products, arithmetic and copies ran while one was open for 9% of the time, Pallas kernels for 12%

profile of v4, /device:TPU:0, one launch (start us, length us, event | category | flops | bytes accessed | tf_op | source)
XLA Modules:
  0.0 636.5 jit_solution(15672301217580657577)
XLA Ops:
  12.2 5.1 collective-permute-start
  19.3 1.7 collective-permute-start.18
  26.4 1.7 multiply_sine_fusion
  28.9 7.7 %collective-permute-done.1 = bf16[96,768]{1,0:T(8,128)(2,1)S(1)} collective-permute-done((bf16[96,768]{1,0:T(8,128)(2,1)}, bf16[96,768]{1,0:T(8,128)(2,1)S(1)}, u32[]{:S(2)}, u32[]{:S(2)}) %collective-permute-start.1) | collective-permute-done | bytes 147488 | tf_op jit(solution)/shard_map/ppermute | solution.py:748
  36.8 8.5 %collective-permute-start.7 = (bf16[16,6272]{1,0:T(8,128)(2,1)S(1)}, bf16[16,6272]{1,0:T(8,128)(2,1)S(1)}, u32[]{:S(2)}, u32[]{:S(2)}) collective-permute-start(bf16[16,6272]{1,0:T(8,128)(2,1)S(1)} %constant_dynamic-update-slice_fusion.5), channel_id=1, source_target_pairs={{0,24},{1,25},{2,26},{3,27},{4,28},{5,29},{6,30},{7,31},{8,16},{9,... | collective-permute-start | bytes 602120 | tf_op jit(solution)/shard_map/ppermute | solution.py:748
  48.1 2.9 collective-permute-done.7
  51.9 9.7 %collective-permute-done.8 = bf16[16,6272]{1,0:T(8,128)(2,1)S(1)} collective-permute-done((bf16[16,6272]{1,0:T(8,128)(2,1)S(1)}, bf16[16,6272]{1,0:T(8,128)(2,1)S(1)}, u32[]{:S(2)}, u32[]{:S(2)}) %collective-permute-start.8) | collective-permute-done | bytes 200736 | tf_op jit(solution)/shard_map/ppermute | solution.py:748
  61.9 2.4 collective-permute-start.4
  64.3 1.6 collective-permute-start.6
  67.6 7.0 %collective-permute-done.4 = bf16[2,2,2,48,768]{4,3,1,0,2:T(8,128)(2,1)S(1)} collective-permute-done((bf16[2,2,2,48,768]{4,3,1,0,2:T(8,128)(2,1)S(1)}, bf16[2,2,2,48,768]{4,3,1,0,2:T(8,128)(2,1)S(1)}, u32[]{:S(2)}, u32[]{:S(2)}) %collective-permute-start.4) | collective-permute-done | bytes 589856 | tf_op jit(solution)/shard_map/ppermute | solution.py:748
  76.8 4.0 reshape.627.cot_ref
  80.8 1.8 pad_maximum_fusion.21.pos_ref
  84.1 1.7 collective-permute-start.12
  85.8 7.0 %collective-permute-done.13 = bf16[2,2,16,3072]{3,2,1,0:T(8,128)(2,1)} collective-permute-done((bf16[2,2,16,3072]{3,2,1,0:T(8,128)(2,1)}, bf16[2,2,16,3072]{3,2,1,0:T(8,128)(2,1)}, u32[]{:S(2)}, u32[]{:S(2)}) %collective-permute-start.13) | collective-permute-done | bytes 393248 | tf_op jit(solution)/shard_map/ppermute | solution.py:748
  94.8 10.2 %collective-permute-done.12 = bf16[2,2,16,3200]{3,2,1,0:T(8,128)(2,1)S(1)} collective-permute-done((bf16[2,2,16,3200]{3,2,1,0:T(8,128)(2,1)}, bf16[2,2,16,3200]{3,2,1,0:T(8,128)(2,1)S(1)}, u32[]{:S(2)}, u32[]{:S(2)}) %collective-permute-start.12) | collective-permute-done | bytes 409632 | tf_op jit(solution)/shard_map/ppermute | solution.py:748
  107.6 2.7 pad_maximum_fusion
  110.3 11.6 %all-gather.4.cloned.1.call-done.small_ref.wqkv_ref.wo_ref.wu_ref.proj_ref = bf16[768,6784]{1,0:T(8,128)(2,1)} async-done(((bf16[24,6784]{1,0:T(8,128)(2,1)}), bf16[768,6784]{1,0:T(8,128)(2,1)}) %all-gather.4.cloned.1.call-update) | async-done | bytes 10420240 | tf_op jit(solution)/shard_map/all_gather | solution.py:772
  124.0 10.0 %enc_attend.1 = (bf16[512,2304]{1,0:T(8,128)(2,1)}, bf16[512,1536]{1,0:T(8,128)(2,1)}, bf16[512,768]{1,0:T(8,128)(2,1)}, f32[512,768]{1,0:T(8,128)}, f32[8,768]{1,0:T(8,128)}) custom-call(bf16[4,128,768]{2,1,0:T(8,128)(2,1)} %x_ref.3, f32[4,1,128]{2,1,0:T(1,128)} %compare_convert_fusion.mask_ref, ...), custom_call_target="tpu_custom_call" | custom-call | flops 10000000000 | bytes 16777216 | tf_op jit(solution)/shard_map/enc_attend/pallas_call | solution.py:534
  134.0 18.7 %enc_feed.1 = (bf16[512,512]{1,0:T(8,128)(2,1)}, bf16[512,768]{1,0:T(8,128)(2,1)}, bf16[512,3072]{1,0:T(8,128)(2,1)}, bf16[512,3072]{1,0:T(8,128)(2,1)}) custom-call(f32[512,768]{1,0:T(8,128)} %get-tuple-element.103.x2_ref, f32[8,768]{1,0:T(8,128)} %get-tuple-element.104.vec_ref, ...), custom_call_target="tpu_custom_call" | custom-call | flops 17999998976 | bytes 16777216 | tf_op jit(solution)/shard_map/enc_feed/pallas_call | solution.py:534
  157.9 5.3 collective-permute-done.16
  169.7 1.8 pad_maximum_fusion.5
  172.0 104.2 %decoder_block.1 = (bf16[8,256,512]{2,1,0:T(8,128)(2,1)}, bf16[8,128,512]{2,1,0:T(8,128)(2,1)}, bf16[512,3200]{1,0:T(8,128)(2,1)}, bf16[512,3200]{1,0:T(8,128)(2,1)}) custom-call(s32[1]{0:T(128)} %bitcast.core_ref, bf16[8,128,512]{2,1,0:T(8,128)(2,1)} %bitcast.297, s32[8,1,128]{2,1,0:T(1,128)} %and_select_fusion.3.idx_ref, ...), custom_call_target="tpu_custom_call" | custom-call | flops 77309411328 | bytes 41943040 | tf_op jit(solution)/shard_map/decoder_block/pallas_call | solution.py:291
  277.9 5.1 collective-permute-done.22
  287.4 7.1 %collective-permute-done.23 = bf16[2,128,512]{2,1,0:T(8,128)(2,1)S(1)} collective-permute-done((bf16[2,128,512]{2,1,0:T(8,128)(2,1)}, bf16[2,128,512]{2,1,0:T(8,128)(2,1)S(1)}, u32[]{:S(2)}, u32[]{:S(2)}) %collective-permute-start.23) | collective-permute-done | bytes 262176 | tf_op jit(solution)/shard_map/ppermute | solution.py:792
  296.3 2.7 add_convert_fusion.1
  301.7 23.4 %enc_feed_back.1 = (bf16[768,512]{1,0:T(8,128)(2,1)}, bf16[768,3072]{1,0:T(8,128)(2,1)}, bf16[768,3072]{1,0:T(8,128)(2,1)}, f32[512,768]{1,0:T(8,128)}, f32[8,768]{1,0:T(8,128)}) custom-call(s32[1]{0:T(128)} %bitcast.core_ref, bf16[512,512]{1,0:T(8,128)(2,1)} %bitcast.304, bf16[512,768]{1,0:T(8,128)(2,1)} %get-tuple-element.117.enc_ref, ...), custom_call_target="tpu_custom_call" | custom-call | flops 24000000000 | bytes 16777216 | tf_op jit(solution)/shard_map/enc_feed_back/pallas_call | solution.py:534
  328.9 17.1 %enc_attend_back.1 = (bf16[768,1920]{1,0:T(8,128)(2,1)}, bf16[768,1920]{1,0:T(8,128)(2,1)}, bf16[4,128,768]{2,1,0:T(8,128)(2,1)}) custom-call(s32[1]{0:T(128)} %bitcast.core_ref, f32[512,768]{1,0:T(8,128)} %get-tuple-element.125.dx2_ref, bf16[512,768]{1,0:T(8,128)(2,1)} %get-tuple-element.126.o_ref, bf16[512,2304]{1,0:T(8,128)(2,1)} %get-tuple-element.127.qkv_ref, ...), custom_call_target="tpu_custom_call" | custom-call | flops 14000000000 | bytes 16777216 | tf_op jit(solution)/shard_map/enc_attend_back/pallas_call | solution.py:534
  349.5 4.3 add_convert_fusion
  357.2 1.9 collective-permute-start.34
  361.6 5.8 collective-permute-done.34
  368.9 9.8 %collective-permute-done.33 = bf16[32,3200]{1,0:T(8,128)(2,1)} collective-permute-done((bf16[32,3200]{1,0:T(8,128)(2,1)}, bf16[32,3200]{1,0:T(8,128)(2,1)}, u32[]{:S(2)}, u32[]{:S(2)}) %collective-permute-start.33) | collective-permute-done | bytes 204832 | tf_op jit(solution)/shard_map/ppermute | solution.py:704
  378.7 2.0 fusion.17
  380.7 4.6 collective-permute-done.31
  387.9 6.4 %collective-permute-done.35 = bf16[2,2,2,48,1536]{4,3,2,1,0:T(8,128)(2,1)} collective-permute-done((bf16[2,2,2,48,1536]{4,3,2,1,0:T(8,128)(2,1)}, bf16[2,2,2,48,1536]{4,3,2,1,0:T(8,128)(2,1)}, u32[]{:S(2)}, u32[]{:S(2)}) %collective-permute-start.35) | collective-permute-done | bytes 1179680 | tf_op jit(solution)/shard_map/ppermute | solution.py:704
  397.1 2.6 add_convert_fusion.2
  405.0 10.3 %collective-permute-done.37 = bf16[2,2,48,1536]{3,2,1,0:T(8,128)(2,1)S(1)} collective-permute-done((bf16[2,2,48,1536]{3,2,1,0:T(8,128)(2,1)}, bf16[2,2,48,1536]{3,2,1,0:T(8,128)(2,1)S(1)}, u32[]{:S(2)}, u32[]{:S(2)}) %collective-permute-start.37) | collective-permute-done | bytes 589856 | tf_op jit(solution)/shard_map/ppermute | solution.py:704
  420.7 12.7 %collective-permute-done.38 = bf16[2,2,2,48,896]{4,3,1,0,2:T(8,128)(2,1)S(1)} collective-permute-done((bf16[2,2,2,48,896]{4,3,1,0,2:T(8,128)(2,1)S(1)}, bf16[2,2,2,48,896]{4,3,1,0,2:T(8,128)(2,1)S(1)}, u32[]{:S(2)}, u32[]{:S(2)}) %collective-permute-start.38) | collective-permute-done | bytes 688160 | tf_op jit(solution)/shard_map/ppermute | solution.py:704
  435.1 6.8 %collective-permute-done.40 = bf16[2,2,2,48,1024]{4,3,2,1,0:T(8,128)(2,1)S(1)} collective-permute-done((bf16[2,2,2,48,1024]{4,3,2,1,0:T(8,128)(2,1)S(1)}, bf16[2,2,2,48,1024]{4,3,2,1,0:T(8,128)(2,1)S(1)}, u32[]{:S(2)}, u32[]{:S(2)}) %collective-permute-start.40) | collective-permute-done | bytes 786464 | tf_op jit(solution)/shard_map/ppermute | solution.py:704
  443.1 9.7 %collective-permute-start.46 = (bf16[48,3072]{1,0:T(8,128)(2,1)S(1)}, bf16[48,3072]{1,0:T(8,128)(2,1)S(1)}, u32[]{:S(2)}, u32[]{:S(2)}) collective-permute-start(bf16[48,3072]{1,0:T(8,128)(2,1)S(1)} %get-tuple-element.152), channel_id=1, source_target_pairs={{0,16},{1,17},{2,18},{3,19},{4,20},{5,21},{6,22},{7,23},{8,24},{9,... | collective-permute-start | bytes 884744 | tf_op jit(solution)/shard_map/ppermute | solution.py:704
  453.3 1.8 collective-permute-start.44
  455.0 5.1 collective-permute-start.43
  460.2 15.4 %collective-permute-start.42 = (bf16[48,1920]{1,0:T(8,128)(2,1)S(1)}, bf16[48,1920]{1,0:T(8,128)(2,1)S(1)}, u32[]{:S(2)}, u32[]{:S(2)}) collective-permute-start(bf16[48,1920]{1,0:T(8,128)(2,1)S(1)} %get-tuple-element.222), channel_id=1, source_target_pairs={{0,8},{1,9},{2,10},{3,11},{4,12},{5,13},{6,14},{7,15},{8,0},{9,1},... | collective-permute-start | bytes 552968 | tf_op jit(solution)/shard_map/ppermute | solution.py:704
  475.5 22.3 %collective-permute-done.46 = bf16[48,3072]{1,0:T(8,128)(2,1)S(1)} collective-permute-done((bf16[48,3072]{1,0:T(8,128)(2,1)S(1)}, bf16[48,3072]{1,0:T(8,128)(2,1)S(1)}, u32[]{:S(2)}, u32[]{:S(2)}) %collective-permute-start.46) | collective-permute-done | bytes 294944 | tf_op jit(solution)/shard_map/ppermute | solution.py:704
  498.0 8.0 %collective-permute-done.43 = bf16[48,1920]{1,0:T(8,128)(2,1)S(1)} collective-permute-done((bf16[48,1920]{1,0:T(8,128)(2,1)S(1)}, bf16[48,1920]{1,0:T(8,128)(2,1)S(1)}, u32[]{:S(2)}, u32[]{:S(2)}) %collective-permute-start.43) | collective-permute-done | bytes 184352 | tf_op jit(solution)/shard_map/ppermute | solution.py:704
  506.9 2.0 reshape.633
  508.9 8.0 %unpack_sums.3 = (f32[512,1536]{1,0:T(8,128)}, f32[512,512]{1,0:T(8,128)}, f32[512,2048]{1,0:T(8,128)}, f32[2048,512]{1,0:T(8,128)}, f32[8,512]{1,0:T(8,128)}) custom-call(bf16[16,2,32,3200]{3,2,1,0:T(8,128)(2,1)} %bitcast.273), custom_call_target="tpu_custom_call" | custom-call | bytes 9830400 | tf_op jit(solution)/shard_map/unpack_sums/pallas_call | solution.py:638
  518.5 95.8 %all-gather.6.cloned.1.call-done = bf16[1536,4992]{1,0:T(8,128)(2,1)} async-done(((bf16[48,4992]{1,0:T(8,128)(2,1)}), bf16[1536,4992]{1,0:T(8,128)(2,1)}) %all-gather.6.cloned.1.call-update) | async-done | bytes 15335440 | tf_op jit(solution)/shard_map/all_gather | solution.py:772
  614.3 13.7 %unpack_sums.2 = (f32[768,2304]{1,0:T(8,128)}, f32[768,768]{1,0:T(8,128)}, f32[768,512]{1,0:T(8,128)}, f32[768,3072]{1,0:T(8,128)}, f32[3072,768]{1,0:T(8,128)}, /*index=5*/f32[8,768]{1,0:T(8,128)}) custom-call(bf16[16,2,48,4992]{3,2,1,0:T(8,128)(2,1)} %bitcast.262), custom_call_target="tpu_custom_call" | custom-call | bytes 23003136 | tf_op jit(solution)/shard_map/unpack_sums/pallas_call | solution.py:638
  (251 shorter events, 89.8 us)
Async XLA Ops:
  7.2 114.8 %all-gather.4.cloned.1.call-start = ((), (), s32[]{:S(2)}) async-start(), calls=%async_computation | async-start | bytes 10745856 | tf_op jit(solution)/shard_map/all_gather | solution.py:772
  12.2 496.7 %all-gather.8.cloned.1.call-start = ((), (), s32[]{:S(2)}) async-start(), calls=%async_computation.2 | async-start | bytes 6758400 | tf_op jit(solution)/shard_map/all_gather | solution.py:772
  12.2 16.6 %collective-permute-start = (bf16[96,768]{1,0:T(8,128)(2,1)}, bf16[96,768]{1,0:T(8,128)(2,1)S(1)}, u32[]{:S(2)}, u32[]{:S(2)}) collective-permute-start(bf16[96,768]{1,0:T(8,128)(2,1)} %param.32), channel_id=1, source_target_pairs={{0,24},{1,25},{2,26},{3,27},{4,28},{5,29},{6,30},{7,31},{8,16},{9,... | collective-permute-start | bytes 442376 | tf_op jit(solution)/shard_map/ppermute | solution.py:748
  17.4 19.2 %collective-permute-start.1 = (bf16[96,768]{1,0:T(8,128)(2,1)}, bf16[96,768]{1,0:T(8,128)(2,1)S(1)}, u32[]{:S(2)}, u32[]{:S(2)}) collective-permute-start(bf16[96,768]{1,0:T(8,128)(2,1)} %param.32), channel_id=1, source_target_pairs={{0,16},{1,17},{2,18},{3,19},{4,20},{5,21},{6,22},{7,23},{8,24},{9,... | collective-permute-start | bytes 442376 | tf_op jit(solution)/shard_map/ppermute | solution.py:748
  17.4 19.2 %collective-permute-start.2 = (bf16[96,768]{1,0:T(8,128)(2,1)}, bf16[96,768]{1,0:T(8,128)(2,1)S(1)}, u32[]{:S(2)}, u32[]{:S(2)}) collective-permute-start(bf16[96,768]{1,0:T(8,128)(2,1)} %param.32), channel_id=1, source_target_pairs={{0,8},{1,9},{2,10},{3,11},{4,12},{5,13},{6,14},{7,15},{8,0},{9,1},... | collective-permute-start | bytes 442376 | tf_op jit(solution)/shard_map/ppermute | solution.py:748
  19.3 137.4 %collective-permute-start.18 = (s32[2,128]{1,0:T(2,128)}, s32[2,128]{1,0:T(2,128)}, u32[]{:S(2)}, u32[]{:S(2)}) collective-permute-start(s32[2,128]{1,0:T(2,128)} %fusion.55), channel_id=1, source_target_pairs={{0,2},{1,3},{2,0},{3,1},{4,6},{5,7},{6,4},{7,5},{8,10},{9,11},{10,... | collective-permute-start | bytes 3080 | tf_op jit(solution)/shard_map/ppermute | solution.py:792
  36.8 14.2 %collective-permute-start.7 = (bf16[16,6272]{1,0:T(8,128)(2,1)S(1)}, bf16[16,6272]{1,0:T(8,128)(2,1)S(1)}, u32[]{:S(2)}, u32[]{:S(2)}) collective-permute-start(bf16[16,6272]{1,0:T(8,128)(2,1)S(1)} %constant_dynamic-update-slice_fusion.5), channel_id=1, source_target_pairs={{0,24},{1,25},{2,26},{3,27},{4,28},{5,29},{6,30},{7,31},{8,16},{9,... | collective-permute-start | bytes 602120 | tf_op jit(solution)/shard_map/ppermute | solution.py:748
  45.3 16.3 %collective-permute-start.8 = (bf16[16,6272]{1,0:T(8,128)(2,1)S(1)}, bf16[16,6272]{1,0:T(8,128)(2,1)S(1)}, u32[]{:S(2)}, u32[]{:S(2)}) collective-permute-start(bf16[16,6272]{1,0:T(8,128)(2,1)S(1)} %constant_dynamic-update-slice_fusion.5), channel_id=1, source_target_pairs={{0,16},{1,17},{2,18},{3,19},{4,20},{5,21},{6,22},{7,23},{8,24},{9,... | collective-permute-start | bytes 602120 | tf_op jit(solution)/shard_map/ppermute | solution.py:748
  45.3 16.3 %collective-permute-start.9 = (bf16[16,6272]{1,0:T(8,128)(2,1)S(1)}, bf16[16,6272]{1,0:T(8,128)(2,1)S(1)}, u32[]{:S(2)}, u32[]{:S(2)}) collective-permute-start(bf16[16,6272]{1,0:T(8,128)(2,1)S(1)} %constant_dynamic-update-slice_fusion.5), channel_id=1, source_target_pairs={{0,8},{1,9},{2,10},{3,11},{4,12},{5,13},{6,14},{7,15},{8,0},{9,1},... | collective-permute-start | bytes 602120 | tf_op jit(solution)/shard_map/ppermute | solution.py:748
  46.6 15.1 %collective-permute-start.5 = (bf16[2,2,48,768]{3,2,1,0:T(8,128)(2,1)S(1)}, bf16[2,2,48,768]{3,2,1,0:T(8,128)(2,1)S(1)}, u32[]{:S(2)}, u32[]{:S(2)}) collective-permute-start(bf16[2,2,48,768]{3,2,1,0:T(8,128)(2,1)S(1)} %get-tuple-element.94), channel_id=1, source_target_pairs={{0,4},{1,5},{2,6},{3,7},{4,0},{5,1},{6,2},{7,3},{8,12},{9,13},{10,... | collective-permute-start | bytes 884744 | tf_op jit(solution)/shard_map/ppermute | solution.py:748
  50.9 10.8 %collective-permute-start.3 = (bf16[2,2,48,768]{3,2,1,0:T(8,128)(2,1)S(1)}, bf16[2,2,48,768]{3,2,1,0:T(8,128)(2,1)S(1)}, u32[]{:S(2)}, u32[]{:S(2)}) collective-permute-start(bf16[2,2,48,768]{3,2,1,0:T(8,128)(2,1)S(1)} %get-tuple-element.93), channel_id=1, source_target_pairs={{0,2},{1,3},{2,0},{3,1},{4,6},{5,7},{6,4},{7,5},{8,10},{9,11},{10,... | collective-permute-start | bytes 884744 | tf_op jit(solution)/shard_map/ppermute | solution.py:748
  61.9 12.8 %collective-permute-start.4 = (bf16[2,2,2,48,768]{4,3,1,0,2:T(8,128)(2,1)S(1)}, bf16[2,2,2,48,768]{4,3,1,0,2:T(8,128)(2,1)S(1)}, u32[]{:S(2)}, u32[]{:S(2)}) collective-permute-start(bf16[2,2,2,48,768]{4,3,1,0,2:T(8,128)(2,1)S(1)} %pad_maximum_fusion.18), channel_id=1, source_target_pairs={{0,4},{1,5},{2,6},{3,7},{4,0},{5,1},{6,2},{7,3},{8,12},{9,13},{10,... | collective-permute-start | bytes 1769480 | tf_op jit(solution)/shard_map/ppermute | solution.py:748
  64.3 10.4 %collective-permute-start.6 = (bf16[2,2,2,48,768]{4,3,1,0,2:T(8,128)(2,1)S(1)}, bf16[2,2,2,48,768]{4,3,1,0,2:T(8,128)(2,1)S(1)}, u32[]{:S(2)}, u32[]{:S(2)}) collective-permute-start(bf16[2,2,2,48,768]{4,3,1,0,2:T(8,128)(2,1)S(1)} %pad_maximum_fusion.19), channel_id=1, source_target_pairs={{0,2},{1,3},{2,0},{3,1},{4,6},{5,7},{6,4},{7,5},{8,10},{9,11},{10,... | collective-permute-start | bytes 1769480 | tf_op jit(solution)/shard_map/ppermute | solution.py:748
  76.5 16.3 %collective-permute-start.13 = (bf16[2,2,16,3072]{3,2,1,0:T(8,128)(2,1)}, bf16[2,2,16,3072]{3,2,1,0:T(8,128)(2,1)}, u32[]{:S(2)}, u32[]{:S(2)}) collective-permute-start(bf16[2,2,16,3072]{3,2,1,0:T(8,128)(2,1)} %slice.117), channel_id=1, source_target_pairs={{0,4},{1,5},{2,6},{3,7},{4,0},{5,1},{6,2},{7,3},{8,12},{9,13},{10,... | collective-permute-start | bytes 1179656 | tf_op jit(solution)/shard_map/ppermute | solution.py:748
  83.5 22.7 %collective-permute-start.11 = (bf16[2,2,2,2,48,768]{5,4,1,0,2,3:T(8,128)(2,1)}, bf16[2,2,2,2,48,768]{5,4,1,0,2,3:T(8,128)(2,1)S(1)}, u32[]{:S(2)}, u32[]{:S(2)}) collective-permute-start(bf16[2,2,2,2,48,768]{5,4,1,0,2,3:T(8,128)(2,1)} %get-tuple-element.99), channel_id=1, source_target_pairs={{0,1},{1,0},{2,3},{3,2},{4,5},{5,4},{6,7},{7,6},{8,9},{9,8},{10,11... | collective-permute-start | bytes 3538952 | tf_op jit(solution)/shard_map/ppermute | solution.py:748
  83.5 23.4 %collective-permute-start.10 = (bf16[2,2,2,2,48,768]{5,4,1,0,2,3:T(8,128)(2,1)}, bf16[2,2,2,2,48,768]{5,4,1,0,2,3:T(8,128)(2,1)S(1)}, u32[]{:S(2)}, u32[]{:S(2)}) collective-permute-start(bf16[2,2,2,2,48,768]{5,4,1,0,2,3:T(8,128)(2,1)} %get-tuple-element.98), channel_id=1, source_target_pairs={{0,1},{1,0},{2,3},{3,2},{4,5},{5,4},{6,7},{7,6},{8,9},{9,8},{10,11... | collective-permute-start | bytes 3538952 | tf_op jit(solution)/shard_map/ppermute | solution.py:748
  84.1 21.0 %collective-permute-start.12 = (bf16[2,2,16,3200]{3,2,1,0:T(8,128)(2,1)}, bf16[2,2,16,3200]{3,2,1,0:T(8,128)(2,1)S(1)}, u32[]{:S(2)}, u32[]{:S(2)}) collective-permute-start(bf16[2,2,16,3200]{3,2,1,0:T(8,128)(2,1)} %slice.116), channel_id=1, source_target_pairs={{0,2},{1,3},{2,0},{3,1},{4,6},{5,7},{6,4},{7,5},{8,10},{9,11},{10,... | collective-permute-start | bytes 1228808 | tf_op jit(solution)/shard_map/ppermute | solution.py:748
  122.0 31.0 %collective-permute-start.14 = (bf16[2,2,2,16,3200]{4,3,1,0,2:T(8,128)(2,1)S(1)}, bf16[2,2,2,16,3200]{4,3,1,0,2:T(8,128)(2,1)S(1)}, u32[]{:S(2)}, u32[]{:S(2)}) collective-permute-start(bf16[2,2,2,16,3200]{4,3,1,0,2:T(8,128)(2,1)S(1)} %copy-done.17), channel_id=1, source_target_pairs={{0,4},{1,5},{2,6},{3,7},{4,0},{5,1},{6,2},{7,3},{8,12},{9,13},{10,... | collective-permute-start | bytes 2457608 | tf_op jit(solution)/shard_map/ppermute | solution.py:748
  123.4 29.2 %collective-permute-start.15 = (bf16[2,2,2,16,3072]{4,3,2,1,0:T(8,128)(2,1)S(1)}, bf16[2,2,2,16,3072]{4,3,2,1,0:T(8,128)(2,1)S(1)}, u32[]{:S(2)}, u32[]{:S(2)}) collective-permute-start(bf16[2,2,2,16,3072]{4,3,2,1,0:T(8,128)(2,1)S(1)} %copy-done.18), channel_id=1, source_target_pairs={{0,2},{1,3},{2,0},{3,1},{4,6},{5,7},{6,4},{7,5},{8,10},{9,11},{10,... | collective-permute-start | bytes 2359304 | tf_op jit(solution)/shard_map/ppermute | solution.py:748
  155.2 8.0 %collective-permute-start.16 = (bf16[2,128,512]{2,1,0:T(8,128)(2,1)S(1)}, bf16[2,128,512]{2,1,0:T(8,128)(2,1)S(1)}, u32[]{:S(2)}, u32[]{:S(2)}) collective-permute-start(bf16[2,128,512]{2,1,0:T(8,128)(2,1)S(1)} %dynamic-slice_bitcast_fusion.14), channel_id=1, source_target_pairs={{0,2},{1,3},{2,0},{3,1},{4,6},{5,7},{6,4},{7,5},{8,10},{9,11},{10,... | collective-permute-start | bytes 786440 | tf_op jit(solution)/shard_map/ppermute | solution.py:792
  156.7 9.7 %collective-permute-start.21 = (bf16[2,2,2,2,16,3072]{5,4,3,2,1,0:T(8,128)(2,1)S(1)}, bf16[2,2,2,2,16,3072]{5,4,3,2,1,0:T(8,128)(2,1)S(1)}, u32[]{:S(2)}, u32[]{:S(2)}) collective-permute-start(bf16[2,2,2,2,16,3072]{5,4,3,2,1,0:T(8,128)(2,1)S(1)} %pad_maximum_fusion.7), channel_id=1, source_target_pairs={{0,1},{1,0},{2,3},{3,2},{4,5},{5,4},{6,7},{7,6},{8,9},{9,8},{10,11... | collective-permute-start | bytes 4718600 | tf_op jit(solution)/shard_map/ppermute | solution.py:748
  157.4 6.0 collective-permute-start.19
  276.2 20.1 %collective-permute-start.24 = (bf16[512,3200]{1,0:T(8,128)(2,1)}, bf16[512,3200]{1,0:T(8,128)(2,1)}, u32[]{:S(2)}, u32[]{:S(2)}) collective-permute-start(bf16[512,3200]{1,0:T(8,128)(2,1)} %get-tuple-element.115), channel_id=1, source_target_pairs={{0,1},{1,0},{2,3},{3,2},{4,5},{5,4},{6,7},{7,6},{8,9},{9,8},{10,11... | collective-permute-start | bytes 9830408 | tf_op jit(solution)/shard_map/ppermute | solution.py:667
  285.9 8.6 %collective-permute-start.23 = (bf16[2,128,512]{2,1,0:T(8,128)(2,1)}, bf16[2,128,512]{2,1,0:T(8,128)(2,1)S(1)}, u32[]{:S(2)}, u32[]{:S(2)}) collective-permute-start(bf16[2,128,512]{2,1,0:T(8,128)(2,1)} %dynamic-slice_bitcast_fusion.13), channel_id=1, source_target_pairs={{0,2},{1,3},{2,0},{3,1},{4,6},{5,7},{6,4},{7,5},{8,10},{9,11},{10,... | collective-permute-start | bytes 786440 | tf_op jit(solution)/shard_map/ppermute | solution.py:792
  299.6 25.5 %collective-permute-start.25 = (bf16[2,2,2,32,1536]{4,3,1,0,2:T(8,128)(2,1)S(1)}, bf16[2,2,2,32,1536]{4,3,1,0,2:T(8,128)(2,1)S(1)}, u32[]{:S(2)}, u32[]{:S(2)}) collective-permute-start(bf16[2,2,2,32,1536]{4,3,1,0,2:T(8,128)(2,1)S(1)} %bitcast.300), channel_id=1, source_target_pairs={{0,4},{1,5},{2,6},{3,7},{4,0},{5,1},{6,2},{7,3},{8,12},{9,13},{10,... | collective-permute-start | bytes 2359304 | tf_op jit(solution)/shard_map/ppermute | solution.py:704
  300.2 26.1 %collective-permute-start.26 = (bf16[2,2,2,32,1664]{4,3,2,1,0:T(8,128)(2,1)S(1)}, bf16[2,2,2,32,1664]{4,3,2,1,0:T(8,128)(2,1)S(1)}, u32[]{:S(2)}, u32[]{:S(2)}) collective-permute-start(bf16[2,2,2,32,1664]{4,3,2,1,0:T(8,128)(2,1)S(1)} %dynamic-slice_bitcast_fusion.1), channel_id=1, source_target_pairs={{0,2},{1,3},{2,0},{3,1},{4,6},{5,7},{6,4},{7,5},{8,10},{9,11},{10,... | collective-permute-start | bytes 2555912 | tf_op jit(solution)/shard_map/ppermute | solution.py:704
  326.6 22.8 %collective-permute-start.29 = (bf16[768,3072]{1,0:T(8,128)(2,1)}, bf16[768,3072]{1,0:T(8,128)(2,1)}, u32[]{:S(2)}, u32[]{:S(2)}) collective-permute-start(bf16[768,3072]{1,0:T(8,128)(2,1)} %get-tuple-element.137), channel_id=1, source_target_pairs={{0,1},{1,0},{2,3},{3,2},{4,5},{5,4},{6,7},{7,6},{8,9},{9,8},{10,11... | collective-permute-start | bytes 14155784 | tf_op jit(solution)/shard_map/ppermute | solution.py:667
  326.7 20.4 %collective-permute-start.28 = (bf16[2,2,32,1664]{3,2,1,0:T(8,128)(2,1)S(1)}, bf16[2,2,32,1664]{3,2,1,0:T(8,128)(2,1)}, u32[]{:S(2)}, u32[]{:S(2)}) collective-permute-start(bf16[2,2,32,1664]{3,2,1,0:T(8,128)(2,1)S(1)} %dynamic-slice_bitcast_fusion.6), channel_id=1, source_target_pairs={{0,4},{1,5},{2,6},{3,7},{4,0},{5,1},{6,2},{7,3},{8,12},{9,13},{10,... | collective-permute-start | bytes 1277960 | tf_op jit(solution)/shard_map/ppermute | solution.py:704
  328.3 17.7 %collective-permute-start.27 = (bf16[2,2,32,1536]{3,2,1,0:T(8,128)(2,1)}, bf16[2,2,32,1536]{3,2,1,0:T(8,128)(2,1)}, u32[]{:S(2)}, u32[]{:S(2)}) collective-permute-start(bf16[2,2,32,1536]{3,2,1,0:T(8,128)(2,1)} %dynamic-slice_bitcast_fusion.8), channel_id=1, source_target_pairs={{0,2},{1,3},{2,0},{3,1},{4,6},{5,7},{6,4},{7,5},{8,10},{9,11},{10,... | collective-permute-start | bytes 1179656 | tf_op jit(solution)/shard_map/ppermute | solution.py:704
  356.7 40.4 %collective-permute-start.30 = (bf16[768,1920]{1,0:T(8,128)(2,1)}, bf16[768,1920]{1,0:T(8,128)(2,1)}, u32[]{:S(2)}, u32[]{:S(2)}) collective-permute-start(bf16[768,1920]{1,0:T(8,128)(2,1)} %get-tuple-element.139), channel_id=1, source_target_pairs={{0,1},{1,0},{2,3},{3,2},{4,5},{5,4},{6,7},{7,6},{8,9},{9,8},{10,11... | collective-permute-start | bytes 8847368 | tf_op jit(solution)/shard_map/ppermute | solution.py:667
  356.7 28.7 %collective-permute-start.31 = (bf16[2,2,2,48,1536]{4,3,1,0,2:T(8,128)(2,1)}, bf16[2,2,2,48,1536]{4,3,1,0,2:T(8,128)(2,1)}, u32[]{:S(2)}, u32[]{:S(2)}) collective-permute-start(bf16[2,2,2,48,1536]{4,3,1,0,2:T(8,128)(2,1)} %bitcast.258), channel_id=1, source_target_pairs={{0,4},{1,5},{2,6},{3,7},{4,0},{5,1},{6,2},{7,3},{8,12},{9,13},{10,... | collective-permute-start | bytes 3538952 | tf_op jit(solution)/shard_map/ppermute | solution.py:704
  357.2 10.2 %collective-permute-start.34 = (bf16[32,3200]{1,0:T(8,128)(2,1)}, bf16[32,3200]{1,0:T(8,128)(2,1)}, u32[]{:S(2)}, u32[]{:S(2)}) collective-permute-start(bf16[32,3200]{1,0:T(8,128)(2,1)} %get-tuple-element.143), channel_id=1, source_target_pairs={{0,24},{1,25},{2,26},{3,27},{4,28},{5,29},{6,30},{7,31},{8,16},{9,... | collective-permute-start | bytes 614408 | tf_op jit(solution)/shard_map/ppermute | solution.py:704
  359.1 19.6 %collective-permute-start.33 = (bf16[32,3200]{1,0:T(8,128)(2,1)}, bf16[32,3200]{1,0:T(8,128)(2,1)}, u32[]{:S(2)}, u32[]{:S(2)}) collective-permute-start(bf16[32,3200]{1,0:T(8,128)(2,1)} %get-tuple-element.142), channel_id=1, source_target_pairs={{0,16},{1,17},{2,18},{3,19},{4,20},{5,21},{6,22},{7,23},{8,24},{9,... | collective-permute-start | bytes 614408 | tf_op jit(solution)/shard_map/ppermute | solution.py:704
  360.0 18.7 %collective-permute-start.32 = (bf16[32,3200]{1,0:T(8,128)(2,1)}, bf16[32,3200]{1,0:T(8,128)(2,1)}, u32[]{:S(2)}, u32[]{:S(2)}) collective-permute-start(bf16[32,3200]{1,0:T(8,128)(2,1)} %get-tuple-element.141), channel_id=1, source_target_pairs={{0,8},{1,9},{2,10},{3,11},{4,12},{5,13},{6,14},{7,15},{8,0},{9,1},... | collective-permute-start | bytes 614408 | tf_op jit(solution)/shard_map/ppermute | solution.py:704
  367.4 26.8 %collective-permute-start.35 = (bf16[2,2,2,48,1536]{4,3,2,1,0:T(8,128)(2,1)}, bf16[2,2,2,48,1536]{4,3,2,1,0:T(8,128)(2,1)}, u32[]{:S(2)}, u32[]{:S(2)}) collective-permute-start(bf16[2,2,2,48,1536]{4,3,2,1,0:T(8,128)(2,1)} %dynamic-slice_bitcast_fusion), channel_id=1, source_target_pairs={{0,2},{1,3},{2,0},{3,1},{4,6},{5,7},{6,4},{7,5},{8,10},{9,11},{10,... | collective-permute-start | bytes 3538952 | tf_op jit(solution)/shard_map/ppermute | solution.py:704
  402.0 212.3 %all-gather.6.cloned.1.call-start = ((), (), s32[]{:S(2)}) async-start(), calls=%async_computation.1 | async-start | bytes 15814656 | tf_op jit(solution)/shard_map/all_gather | solution.py:772
  402.0 13.2 %collective-permute-start.37 = (bf16[2,2,48,1536]{3,2,1,0:T(8,128)(2,1)}, bf16[2,2,48,1536]{3,2,1,0:T(8,128)(2,1)S(1)}, u32[]{:S(2)}, u32[]{:S(2)}) collective-permute-start(bf16[2,2,48,1536]{3,2,1,0:T(8,128)(2,1)} %dynamic-slice_bitcast_fusion.3), channel_id=1, source_target_pairs={{0,4},{1,5},{2,6},{3,7},{4,0},{5,1},{6,2},{7,3},{8,12},{9,13},{10,... | collective-permute-start | bytes 1769480 | tf_op jit(solution)/shard_map/ppermute | solution.py:704
  403.5 13.0 %collective-permute-start.36 = (bf16[2,2,48,1536]{3,2,1,0:T(8,128)(2,1)}, bf16[2,2,48,1536]{3,2,1,0:T(8,128)(2,1)S(1)}, u32[]{:S(2)}, u32[]{:S(2)}) collective-permute-start(bf16[2,2,48,1536]{3,2,1,0:T(8,128)(2,1)} %dynamic-slice_bitcast_fusion.4), channel_id=1, source_target_pairs={{0,2},{1,3},{2,0},{3,1},{4,6},{5,7},{6,4},{7,5},{8,10},{9,11},{10,... | collective-permute-start | bytes 1769480 | tf_op jit(solution)/shard_map/ppermute | solution.py:704
  417.8 15.6 %collective-permute-start.38 = (bf16[2,2,2,48,896]{4,3,1,0,2:T(8,128)(2,1)S(1)}, bf16[2,2,2,48,896]{4,3,1,0,2:T(8,128)(2,1)S(1)}, u32[]{:S(2)}, u32[]{:S(2)}) collective-permute-start(bf16[2,2,2,48,896]{4,3,1,0,2:T(8,128)(2,1)S(1)} %bitcast.301), channel_id=1, source_target_pairs={{0,4},{1,5},{2,6},{3,7},{4,0},{5,1},{6,2},{7,3},{8,12},{9,13},{10,... | collective-permute-start | bytes 2064392 | tf_op jit(solution)/shard_map/ppermute | solution.py:704
  419.2 22.7 %collective-permute-start.40 = (bf16[2,2,2,48,1024]{4,3,2,1,0:T(8,128)(2,1)S(1)}, bf16[2,2,2,48,1024]{4,3,2,1,0:T(8,128)(2,1)S(1)}, u32[]{:S(2)}, u32[]{:S(2)}) collective-permute-start(bf16[2,2,2,48,1024]{4,3,2,1,0:T(8,128)(2,1)S(1)} %copy-done.19), channel_id=1, source_target_pairs={{0,2},{1,3},{2,0},{3,1},{4,6},{5,7},{6,4},{7,5},{8,10},{9,11},{10,... | collective-permute-start | bytes 2359304 | tf_op jit(solution)/shard_map/ppermute | solution.py:704
  433.6 19.3 %collective-permute-start.39 = (bf16[2,2,48,896]{3,2,1,0:T(8,128)(2,1)S(1)}, bf16[2,2,48,896]{3,2,1,0:T(8,128)(2,1)S(1)}, u32[]{:S(2)}, u32[]{:S(2)}) collective-permute-start(bf16[2,2,48,896]{3,2,1,0:T(8,128)(2,1)S(1)} %dynamic-slice_bitcast_fusion.9), channel_id=1, source_target_pairs={{0,2},{1,3},{2,0},{3,1},{4,6},{5,7},{6,4},{7,5},{8,10},{9,11},{10,... | collective-permute-start | bytes 1032200 | tf_op jit(solution)/shard_map/ppermute | solution.py:704
  442.3 10.7 %collective-permute-start.41 = (bf16[2,2,48,1024]{3,2,1,0:T(8,128)(2,1)S(1)}, bf16[2,2,48,1024]{3,2,1,0:T(8,128)(2,1)S(1)}, u32[]{:S(2)}, u32[]{:S(2)}) collective-permute-start(bf16[2,2,48,1024]{3,2,1,0:T(8,128)(2,1)S(1)} %dynamic-slice_bitcast_fusion.7), channel_id=1, source_target_pairs={{0,4},{1,5},{2,6},{3,7},{4,0},{5,1},{6,2},{7,3},{8,12},{9,13},{10,... | collective-permute-start | bytes 1179656 | tf_op jit(solution)/shard_map/ppermute | solution.py:704
  442.3 17.8 %collective-permute-start.47 = (bf16[48,3072]{1,0:T(8,128)(2,1)S(1)}, bf16[48,3072]{1,0:T(8,128)(2,1)S(1)}, u32[]{:S(2)}, u32[]{:S(2)}) collective-permute-start(bf16[48,3072]{1,0:T(8,128)(2,1)S(1)} %get-tuple-element.153), channel_id=1, source_target_pairs={{0,24},{1,25},{2,26},{3,27},{4,28},{5,29},{6,30},{7,31},{8,16},{9,... | collective-permute-start | bytes 884744 | tf_op jit(solution)/shard_map/ppermute | solution.py:704
  443.1 54.7 %collective-permute-start.46 = (bf16[48,3072]{1,0:T(8,128)(2,1)S(1)}, bf16[48,3072]{1,0:T(8,128)(2,1)S(1)}, u32[]{:S(2)}, u32[]{:S(2)}) collective-permute-start(bf16[48,3072]{1,0:T(8,128)(2,1)S(1)} %get-tuple-element.152), channel_id=1, source_target_pairs={{0,16},{1,17},{2,18},{3,19},{4,20},{5,21},{6,22},{7,23},{8,24},{9,... | collective-permute-start | bytes 884744 | tf_op jit(solution)/shard_map/ppermute | solution.py:704
  452.9 45.0 %collective-permute-start.45 = (bf16[48,3072]{1,0:T(8,128)(2,1)S(1)}, bf16[48,3072]{1,0:T(8,128)(2,1)S(1)}, u32[]{:S(2)}, u32[]{:S(2)}) collective-permute-start(bf16[48,3072]{1,0:T(8,128)(2,1)S(1)} %get-tuple-element.151), channel_id=1, source_target_pairs={{0,8},{1,9},{2,10},{3,11},{4,12},{5,13},{6,14},{7,15},{8,0},{9,1},... | collective-permute-start | bytes 884744 | tf_op jit(solution)/shard_map/ppermute | solution.py:704
  453.3 44.7 %collective-permute-start.44 = (bf16[48,1920]{1,0:T(8,128)(2,1)S(1)}, bf16[48,1920]{1,0:T(8,128)(2,1)S(1)}, u32[]{:S(2)}, u32[]{:S(2)}) collective-permute-start(bf16[48,1920]{1,0:T(8,128)(2,1)S(1)} %get-tuple-element.223), channel_id=1, source_target_pairs={{0,24},{1,25},{2,26},{3,27},{4,28},{5,29},{6,30},{7,31},{8,16},{9,... | collective-permute-start | bytes 552968 | tf_op jit(solution)/shard_map/ppermute | solution.py:704
  455.0 50.9 %collective-permute-start.43 = (bf16[48,1920]{1,0:T(8,128)(2,1)S(1)}, bf16[48,1920]{1,0:T(8,128)(2,1)S(1)}, u32[]{:S(2)}, u32[]{:S(2)}) collective-permute-start(bf16[48,1920]{1,0:T(8,128)(2,1)S(1)} %get-tuple-element.224), channel_id=1, source_target_pairs={{0,16},{1,17},{2,18},{3,19},{4,20},{5,21},{6,22},{7,23},{8,24},{9,... | collective-permute-start | bytes 552968 | tf_op jit(solution)/shard_map/ppermute | solution.py:704
  460.2 45.8 %collective-permute-start.42 = (bf16[48,1920]{1,0:T(8,128)(2,1)S(1)}, bf16[48,1920]{1,0:T(8,128)(2,1)S(1)}, u32[]{:S(2)}, u32[]{:S(2)}) collective-permute-start(bf16[48,1920]{1,0:T(8,128)(2,1)S(1)} %get-tuple-element.222), channel_id=1, source_target_pairs={{0,8},{1,9},{2,10},{3,11},{4,12},{5,13},{6,14},{7,15},{8,0},{9,1},... | collective-permute-start | bytes 552968 | tf_op jit(solution)/shard_map/ppermute | solution.py:704
  (32 other events, 278.7 us)
Sparse Core Ops, SparseCore 0:
  12.3 109.6 all-gather.3
  402.1 100.2 all-gather.7
  507.0 107.2 all-gather.5

commit v5 on v4

--- a/solution.py
+++ b/solution.py
@@ -94,9 +94,7 @@
 
 
 def segment_sum(x, ones):
-    high = x.astype(BF16)
-    low = (x - high.astype(F32)).astype(BF16)
-    return mm(high, ones) + mm(low, ones)
+    return mm(x.astype(BF16), ones)
 
 
 def window_max(s):
@@ -200,23 +198,17 @@
     y_s[...] = x2
     da_s[...] = jnp.zeros_like(da_s)
 
-    def ff_body(c, carry):
-        at = pl.ds(pl.multiple_of(c * chunk, chunk), chunk)
-        wu = wu_ref[:, at]
-        wd = wd_ref[at, :]
-        dzc = cot_ref[...].reshape(m_rows, width)
-        u = mm(a2_s[...], wu)
-        dh = mm_t(dzc, wd)
+    for c in range(ff // chunk):
+        at = slice(c * chunk, (c + 1) * chunk)
+        u = mm(a2_s[...], wu_ref[:, at])
+        dh = mm_t(cot_ref[...].reshape(m_rows, width), wd_ref[at, :])
         cdf, bump = gelu_parts(u)
         h = (u * cdf).astype(BF16)
         du = ((cdf + bump) * dh).astype(BF16)
-        y_s[...] += mm(h, wd)
+        y_s[...] += mm(h, wd_ref[at, :])
         acc_d[:, at] += mm(dzt_s[...], h)
         acc_u[:, at] += mm(a2t_s[...], du)
-        da_s[...] += mm_t(du, wu)
-        return carry
-
-    lax.fori_loop(0, ff // chunk, ff_body, 0)
+        da_s[...] += mm_t(du, wu_ref[:, at])
 
     out_ref[...] = y_s[...].reshape(halves, cells, width).astype(BF16)
     da2 = da_s[...]
@@ -274,7 +266,7 @@
         by_core(core_ref, fill, keep_ref, give_ref)
 
 
-def decoder_block(core, rows, idx, cot, pos, mask, pack_one, pack_two, wd):
+def decoder_block(core, rows, idx, cot, pos, mask, pack, wd):
     n_half, slots, width = rows.shape
     cells = cot.shape[1]
     ff = wd.shape[0]
@@ -298,10 +290,10 @@
             pl.BlockSpec((halves, cells, width), lambda i: (i, 0, 0)),
             whole(cells, width),
             whole(cells, LANES),
-            whole(width, LANES, at=(4 * width + ff // 2) // LANES),
+            whole(width, LANES, at=(4 * width + 2 * ff) // LANES),
             whole(width, 3 * width),
             whole(width, width, at=3),
-            whole(width, ff),
+            whole(width, ff, at=1),
             whole(ff, width),
         ],
         out_specs=[
@@ -341,7 +333,7 @@
         name="decoder_block",
     )(
         core, rows, idx.reshape(n_half, 1, slots), cot, pos, mask,
-        pack_one, pack_one, pack_one, pack_two, wd,
+        pack, pack, pack, pack, wd,
     )
 
 
@@ -389,26 +381,26 @@
 def enc_feed_kernel(
     x2_ref, vec_ref, wu_ref, wd_ref, proj_ref, sent_ref, enc_ref, h_ref, gp_ref, a2_s, y_s
 ):
-    ff = wu_ref.shape[1]
-    chunk = 512
-    xhat, rstd = normalise(x2_ref[...])
-    a2_s[...] = (xhat * vec_ref[2:3, :] + vec_ref[3:4, :]).astype(BF16)
-    y_s[...] = x2_ref[...]
-
-    def body(c, carry):
-        at = pl.ds(pl.multiple_of(c * chunk, chunk), chunk)
-        u = mm(a2_s[...], wu_ref[:, at])
-        cdf, bump = gelu_parts(u)
-        h = (u * cdf).astype(BF16)
-        h_ref[:, at] = h
-        gp_ref[:, at] = (cdf + bump).astype(BF16)
-        y_s[...] += mm(h, wd_ref[at, :])
-        return carry
-
-    lax.fori_loop(0, ff // chunk, body, 0)
-    encoded = y_s[...].astype(BF16)
-    enc_ref[...] = encoded
-    sent_ref[...] = mm(encoded, proj_ref[...]).astype(BF16)
+    step = pl.program_id(0)
+
+    @pl.when(step == 0)
+    def _():
+        xhat, rstd = normalise(x2_ref[...])
+        a2_s[...] = (xhat * vec_ref[2:3, :] + vec_ref[3:4, :]).astype(BF16)
+        y_s[...] = x2_ref[...]
+
+    u = mm(a2_s[...], wu_ref[...])
+    cdf, bump = gelu_parts(u)
+    h = (u * cdf).astype(BF16)
+    h_ref[...] = h
+    gp_ref[...] = (cdf + bump).astype(BF16)
+    y_s[...] += mm(h, wd_ref[...])
+
+    @pl.when(step == pl.num_programs(0) - 1)
+    def _():
+        encoded = y_s[...].astype(BF16)
+        enc_ref[...] = encoded
+        sent_ref[...] = mm(encoded, proj_ref[...]).astype(BF16)
 
 
 def enc_feed_back_kernel(
@@ -416,39 +408,39 @@
     gproj_ref, keep_ref, give_ref, dx2_ref, gvec_ref,
     a2t_s, dz_s, dzt_s, da_s,
 ):
-    ff = wu_ref.shape[1]
-    chunk = 512
+    step = pl.program_id(0)
     gain2 = vec_ref[2:3, :]
-    dsent = dsent_ref[...]
-    gproj_ref[...] = mm(enc_ref[...].T, dsent).astype(BF16)
-    dy = mm_t(dsent, proj_ref[...])
-    dx2_ref[...] = dy
-    dz = dy.astype(BF16)
-    dz_s[...] = dz
-    dzt_s[...] = dz.T
-    xhat, rstd = normalise(x2_ref[...])
-    a2t_s[...] = (xhat * gain2 + vec_ref[3:4, :]).astype(BF16).T
-    da_s[...] = jnp.zeros_like(da_s)
-
-    def body(c, carry):
-        at = pl.ds(pl.multiple_of(c * chunk, chunk), chunk)
-        dh = mm_t(dz_s[...], wd_ref[at, :])
-        du = (gp_ref[:, at].astype(F32) * dh).astype(BF16)
-        up_grad = mm(a2t_s[...], du).astype(BF16)
-        down_grad = mm(dzt_s[...], h_ref[:, at]).astype(BF16)
-        first = core_ref[0] == 0
-        keep_ref[:, at] = jnp.where(first, up_grad, down_grad)
-        give_ref[:, at] = jnp.where(first, down_grad, up_grad)
-        da_s[...] += mm_t(du, wu_ref[:, at])
-        return carry
-
-    lax.fori_loop(0, ff // chunk, body, 0)
-    da = da_s[...]
-    xhat, rstd = normalise(x2_ref[...])
-    gvec_ref[...] = jnp.zeros_like(gvec_ref)
-    gvec_ref[2:3, :] = jnp.sum(da * xhat, axis=0, keepdims=True)
-    gvec_ref[3:4, :] = jnp.sum(da, axis=0, keepdims=True)
-    dx2_ref[...] += norm_back(da, xhat, rstd, gain2)
+
+    @pl.when(step == 0)
+    def _():
+        dsent = dsent_ref[...]
+        gproj_ref[...] = mm(enc_ref[...].T, dsent).astype(BF16)
+        dy = mm_t(dsent, proj_ref[...])
+        dx2_ref[...] = dy
+        dz = dy.astype(BF16)
+        dz_s[...] = dz
+        dzt_s[...] = dz.T
+        xhat, rstd = normalise(x2_ref[...])
+        a2t_s[...] = (xhat * gain2 + vec_ref[3:4, :]).astype(BF16).T
+        da_s[...] = jnp.zeros_like(da_s)
+
+    dh = mm_t(dz_s[...], wd_ref[...])
+    du = (gp_ref[...].astype(F32) * dh).astype(BF16)
+    down_grad = mm(dzt_s[...], h_ref[...]).astype(BF16)
+    up_grad = mm(a2t_s[...], du).astype(BF16)
+    da_s[...] += mm_t(du, wu_ref[...])
+    first = core_ref[0] == 0
+    keep_ref[...] = jnp.where(first, up_grad, down_grad)
+    give_ref[...] = jnp.where(first, down_grad, up_grad)
+
+    @pl.when(step == pl.num_programs(0) - 1)
+    def _():
+        da = da_s[...]
+        xhat, rstd = normalise(x2_ref[...])
+        gvec_ref[...] = jnp.zeros_like(gvec_ref)
+        gvec_ref[2:3, :] = jnp.sum(da * xhat, axis=0, keepdims=True)
+        gvec_ref[3:4, :] = jnp.sum(da, axis=0, keepdims=True)
+        dx2_ref[...] += norm_back(da, xhat, rstd, gain2)
 
 
 def enc_attend_back_kernel(
@@ -519,26 +511,37 @@
     by_core(core_ref, fill, keep_ref, give_ref)
 
 
-def whole_call(kernel, args, outs, scratch, name, flops):
+FEED_CHUNK = 512
+
+
+def whole_call(kernel, args, outs, scratch, name, flops, steps=1):
     arrays, specs = [], []
+
+    def block(shape, at):
+        if callable(at):
+            return pl.BlockSpec(shape, at)
+        index = (0,) * (len(shape) - 1) + (at,)
+        return pl.BlockSpec(shape, lambda i: index, pipeline_mode=pl.Buffered(1))
+
     for arg in args:
         array, shape, at = arg if isinstance(arg, tuple) else (arg, arg.shape, 0)
-        if len(shape) == 1:
-            arrays.append(array)
-            specs.append(pl.BlockSpec(memory_space=pltpu.SMEM))
-            continue
-        index = (0,) * (len(shape) - 1) + (at,)
         arrays.append(array)
-        specs.append(pl.BlockSpec(shape, lambda i, index=index: index, pipeline_mode=pl.Buffered(1)))
-    zero = lambda shape: pl.BlockSpec(shape, lambda i: (0,) * len(shape), pipeline_mode=pl.Buffered(1))
+        specs.append(pl.BlockSpec(memory_space=pltpu.SMEM) if len(shape) == 1 else block(shape, at))
+    out_specs, shapes = [], []
+    for out in outs:
+        shape, dtype, part, at = out if len(out) == 4 else out + (out[0], 0)
+        out_specs.append(block(part, at))
+        shapes.append(jax.ShapeDtypeStruct(shape, dtype))
     return pl.pallas_call(
         kernel,
-        grid=(1,),
+        grid=(steps,),
         in_specs=specs,
-        out_specs=[zero(s) for s, _ in outs],
-        out_shape=[jax.ShapeDtypeStruct(s, d) for s, d in outs],
+        out_specs=out_specs,
+        out_shape=shapes,
         scratch_shapes=[pltpu.VMEM(s, d) for s, d in scratch],
-        compiler_params=pltpu.CompilerParams(vmem_limit_bytes=VMEM_BYTES),
+        compiler_params=pltpu.CompilerParams(
+            dimension_semantics=("arbitrary",), vmem_limit_bytes=VMEM_BYTES
+        ),
         cost_estimate=pl.CostEstimate(flops=flops, bytes_accessed=16 << 20, transcendentals=0),
         name=name,
     )(*arrays)
@@ -570,22 +573,31 @@
 
 def enc_feed(x2, vecs, blocks, wd):
     m, width = x2.shape
-    ff = wd.shape[0]
+    ff, chunk = wd.shape[0], FEED_CHUNK
     _, _, up, proj, _ = blocks
-    outs = [((m, proj[1][1]), BF16), ((m, width), BF16), ((m, ff), BF16), ((m, ff), BF16)]
+    across, down = lambda i: (0, i), lambda i: (i, 0)
+    up = (up[0], (width, chunk), lambda i: (0, 4 * width // chunk + i))
+    kept = ((m, ff), BF16, (m, chunk), across)
+    outs = [((m, proj[1][1]), BF16), ((m, width), BF16), kept, kept]
     scratch = [((m, width), BF16), ((m, width), F32)]
-    return whole_call(enc_feed_kernel, (x2, vecs, up, wd, proj), outs, scratch, "enc_feed", 18 * 10**9)
+    args = (x2, vecs, up, (wd, (chunk, width), down), proj)
+    return whole_call(enc_feed_kernel, args, outs, scratch, "enc_feed", 14 * 10**9, ff // chunk)
 
 
 def enc_feed_back(core, dsent, enc, h, gp, x2, vecs, blocks, wd):
     m, width = x2.shape
-    ff = wd.shape[0]
+    ff, chunk = wd.shape[0], FEED_CHUNK
     _, _, up, proj, _ = blocks
-    half = (width, ff)
-    outs = [(proj[1], BF16), (half, BF16), (half, BF16), ((m, width), F32), ((8, width), F32)]
+    across, down = lambda i: (0, i), lambda i: (i, 0)
+    up = (up[0], (width, chunk), lambda i: (0, 4 * width // chunk + i))
+    half = ((width, ff), BF16, (width, chunk), across)
+    outs = [(proj[1], BF16), half, half, ((m, width), F32), ((8, width), F32)]
     scratch = [((width, m), BF16), ((m, width), BF16), ((width, m), BF16), ((m, width), F32)]
-    args = (core, dsent, enc, proj, h, gp, x2, vecs, up, wd)
-    return whole_call(enc_feed_back_kernel, args, outs, scratch, "enc_feed_back", 24 * 10**9)
+    args = (core, dsent, enc, proj, (h, (m, chunk), across), (gp, (m, chunk), across), x2, vecs, up)
+    args += ((wd, (chunk, width), down),)
+    return whole_call(
+        enc_feed_back_kernel, args, outs, scratch, "enc_feed_back", 18 * 10**9, ff // chunk
+    )
 
 
 def attend_half(width, sent):
@@ -609,41 +621,65 @@
     return whole_call(enc_attend_back_kernel, args, outs, scratch, "enc_attend_back", 14 * 10**9)
 
 
-def unpack_kernel(pieces, tall, small, packed_ref, *out_refs):
-    chips, _, rows, _ = packed_ref.shape
-
-    def read(part, start, size):
-        return packed_ref[:, part, :, start : start + size].reshape(chips * rows, size).astype(F32)
-
-    for out, to, part, start, size in pieces:
-        out_refs[out][:, to : to + size] = read(part, start, size)
-    part, start, size = tall
+def unpack_kernel(sections, pieces, talls, smalls, packed_ref, *out_refs):
+    chips, _, unit, _ = packed_ref.shape
+
+    def read(place, start, size):
+        at, part = place
+        first, width, count = sections[at]
+        blocks = [
+            packed_ref[:, part, :, first + k * width + start : first + k * width + start + size]
+            for k in range(count)
+        ]
+        block = blocks[0] if count == 1 else jnp.concatenate(blocks, axis=1)
+        return block.reshape(chips * unit * count, size).astype(F32)
+
+    for out, to, place, start, size in pieces:
+        out_refs[out][:, to : to + size] = read(place, start, size)
     chunk = 512
-    for c in range(size // chunk):
-        out_refs[-2][c * chunk : (c + 1) * chunk, :] = read(part, start + c * chunk, chunk).T
-    out_refs[-1][...] = read(*small, LANES).T[0:8, :]
-
-
-def unpack_sums(packed, widths, pieces, tall, small):
-    chips, _, rows, wide = packed.shape
-    height = chips * rows
-    if rows % 16:
-        packed = packed.transpose(1, 0, 2, 3).reshape(2, 16, height // 16, wide).transpose(1, 0, 2, 3)
-        chips, _, rows, wide = packed.shape
-    group = LANES // math.gcd(rows, LANES)
-    step = group * rows
-    size = tall[2]
-    side = lambda n: pl.BlockSpec((step, n), lambda i: (i, 0))
-    down = lambda n: pl.BlockSpec((n, step), lambda i: (0, i))
+    for out, place, start, size in talls:
+        for c in range(size // chunk):
+            rows = slice(c * chunk, (c + 1) * chunk)
+            out_refs[out][rows, :] = read(place, start + c * chunk, chunk).T
+    for out, place, start in smalls:
+        out_refs[out][...] = read(place, start, LANES).T[0:8, :]
+
+
+def even_units(packed, sections):
+    parts = []
+    for first, width, count in sections:
+        chips, two, unit, _ = packed.shape
+        part = packed[..., first : first + width * count].reshape(chips, two, unit, count, width)
+        part = part.transpose(1, 0, 3, 2, 4).reshape(two, 16, count, chips * unit // 16, width)
+        parts.append(part.transpose(1, 0, 3, 2, 4).reshape(16, two, chips * unit // 16, count * width))
+    return jnp.concatenate(parts, axis=-1)
+
+
+def unpack_sums(packed, sections, outs, pieces, talls, smalls):
+    if packed.shape[2] % 16:
+        packed = even_units(packed, sections)
+    chips, _, unit, wide = packed.shape
+    group = 8
+    specs, shapes = [], []
+    for at, width, turned in outs:
+        step = group * unit * sections[at][2]
+        height = chips * unit * sections[at][2]
+        if turned:
+            specs.append(pl.BlockSpec((turned, step), lambda i: (0, i)))
+            shapes.append(jax.ShapeDtypeStruct((turned, height), F32))
+        else:
+            specs.append(pl.BlockSpec((step, width), lambda i: (i, 0)))
+            shapes.append(jax.ShapeDtypeStruct((height, width), F32))
     return pl.pallas_call(
-        functools.partial(unpack_kernel, pieces, tall, small),
+        functools.partial(unpack_kernel, sections, pieces, talls, smalls),
         grid=(chips // group,),
-        in_specs=[pl.BlockSpec((group, 2, rows, wide), lambda i: (i, 0, 0, 0))],
-        out_specs=[side(n) for n in widths] + [down(size), down(8)],
-        out_shape=[jax.ShapeDtypeStruct((height, n), F32) for n in widths]
-        + [jax.ShapeDtypeStruct((size, height), F32), jax.ShapeDtypeStruct((8, height), F32)],
+        in_specs=[pl.BlockSpec((group, 2, unit, wide), lambda i: (i, 0, 0, 0))],
+        out_specs=specs,
+        out_shape=shapes,
         compiler_params=pltpu.CompilerParams(vmem_limit_bytes=VMEM_BYTES),
-        cost_estimate=pl.CostEstimate(flops=0, bytes_accessed=6 * height * wide, transcendentals=0),
+        cost_estimate=pl.CostEstimate(
+            flops=0, bytes_accessed=12 * chips * unit * wide, transcendentals=0
+        ),
         name="unpack_sums",
     )(packed)
 
@@ -717,24 +753,27 @@
 
 
 class RunningGather:
-    def __init__(self, shard, total, cut, axis):
+    def __init__(self, shard, total):
         bits = total.bit_length() - 1
-        self.total, self.cut, self.axis = total, cut, axis
+        self.total = total
+        self.cut = (shard.shape[1] + LANES) // 256 * 128
         self.shape = shard.shape
         rest, self.plan = list(range(3, bits)), []
         while rest:
             self.plan.append([rest[:2]])
             rest = rest[2:]
-        self.plan += [[[1], [2]], [[2], [1]], [[0], [0]]]
+        self.plan += [[[1], [2]], [[2], [1]], [[0]]]
         self.held, self.have = [shard], [[]]
 
     def offers(self):
         groups = self.plan[0]
         if len(groups) > len(self.held):
-            held, at = self.held[0], self.held[0].ndim - 2 + self.axis
-            first = lax.slice_in_dim(held, 0, self.cut, axis=at)
-            self.held = [first, lax.slice_in_dim(held, self.cut, held.shape[at], axis=at)]
-            self.have = [list(self.have[0]), list(self.have[0])]
+            (held,), (have,) = self.held, self.have
+            self.held = [held[..., : self.cut], held[..., self.cut :]]
+            self.have = [list(have), list(have)]
+        if len(groups) < len(self.held):
+            self.held = [jnp.concatenate(self.held, axis=-1)]
+            self.have = self.have[:1]
         gives, self.masks = [], []
         for held, group in zip(self.held, groups):
             for k in range(1, 1 << len(group)):
@@ -760,8 +799,10 @@
             self.held[i] = held.reshape(held.shape[:at] + (2,) * len(group) + held.shape[at + 1 :])
         self.plan = self.plan[1:]
 
-    def result(self):
-        return [held.reshape((self.total,) + held.shape[-2:]) for held in self.held]
+    def finish(self):
+        while self.plan:
+            self.deliver(self.offers())
+        return self.held[0].reshape((self.total,) + self.shape)
 
 
 def together(*groups):
@@ -802,12 +843,14 @@
     return jnp.stack([jnp.where(side == 0, pair, other), jnp.where(side == 0, other, pair)], axis=1)
 
 
-def bands_to_owners(array):
-    band = lax.axis_index("band")
-    half, side = band // 2, band % 2
+def join_bands(array):
+    side = lax.axis_index("band") % 2
     own = lax.dynamic_index_in_dim(array, side, 1, keepdims=False)
-    got = swap_band(lax.dynamic_index_in_dim(array, 1 - side, 1, keepdims=False), 1)
-    pair = own + got
+    return own + swap_band(lax.dynamic_index_in_dim(array, 1 - side, 1, keepdims=False), 1)
+
+
+def bands_to_owners(pair):
+    half = lax.axis_index("band") // 2
     own = lax.dynamic_index_in_dim(pair, half, 0, keepdims=False)
     got = swap_band(lax.dynamic_index_in_dim(pair, 1 - half, 0, keepdims=False), 2)
     return jnp.stack([jnp.where(half == 0, own, got), jnp.where(half == 0, got, own)])
@@ -852,16 +895,24 @@
     core = (lax.axis_index(AXES) % 2).reshape(1)
     enc_small = columns_of([enc_gain1, enc_shift1, enc_gain2, enc_shift2])
     enc_pack = gather_rows(jnp.concatenate([enc_qkv, enc_out, enc_up, proj, enc_small], axis=1))
+    down_run = RunningGather(enc_down, total)
+    while len(down_run.plan) > 3:
+        down_run.deliver(down_run.offers())
+
+    clip_count, slot_total, _ = visible.shape
+    half_clips = clip_count // 2
+    band_height = FREQ // 2
+    slot_ids = jnp.arange(slot_total)
+    valid_rows = slot_ids[None, :] < visible_count[:, None]
+    valid_mask = valid_rows.astype(F32)[:, None, :]
+    cell_number = jnp.where(valid_rows, keep_index, -1).reshape(2, half_clips, slot_total)
+    cell_number = owners_to_bands(cell_number).reshape(-1, slot_total)
+
     dec_small = columns_of([dec_gain1, dec_shift1, dec_gain2, dec_shift2, mask_token])
     dec_tall = blocks_beside(dec_down, dec_out.shape[0])
-    near, far = dec_tall[: len(dec_tall) // 2], dec_tall[len(dec_tall) // 2 :]
-    dec_first = jnp.concatenate([dec_qkv, dec_out] + near + [dec_small], axis=1)
-    dec_pack = jnp.concatenate([dec_first, dec_up] + far, axis=1)
-    down_run = RunningGather(enc_down, total, enc_down.shape[0] // 2, 0)
-    dec_run = RunningGather(dec_pack, total, dec_first.shape[1], 1)
-    while len(down_run.plan) > 3:
-        down_run.deliver(down_run.offers())
-    gives, dec_gives = together(down_run.offers(), dec_run.offers())
+    dec_pack = jnp.concatenate([dec_qkv, dec_out, dec_up] + dec_tall + [dec_small], axis=1)
+    dec_run = RunningGather(dec_pack, total)
+    cell_number, gives, dec_gives = together(cell_number, down_run.offers(), dec_run.offers())
     down_run.deliver(gives)
     dec_run.deliver(dec_gives)
     while len(dec_run.plan) > 3:
@@ -870,18 +921,10 @@
     gives, dec_gives = together(down_run.offers(), dec_run.offers())
     down_run.deliver(gives)
     dec_run.deliver(dec_gives)
-    whole_down = jnp.concatenate(down_run.result(), axis=1).reshape(-1, enc_wide)
+    whole_down = down_run.finish().reshape(-1, enc_wide)
     enc_pack, whole_down, gives = together(enc_pack, whole_down, dec_run.offers())
     dec_run.deliver(gives)
 
-    clip_count, slot_total, _ = visible.shape
-    half_clips = clip_count // 2
-    band_height = FREQ // 2
-    slot_ids = jnp.arange(slot_total)
-    valid_rows = slot_ids[None, :] < visible_count[:, None]
-    valid_mask = valid_rows.astype(F32)[:, None, :]
-    cell_number = jnp.where(valid_rows, keep_index, -1).reshape(2, half_clips, slot_total)
-    cell_number = owners_to_bands(cell_number).reshape(-1, slot_total)
     band_pick = lax.axis_index("band") % 2
     rolled_time = (cell_number // FREQ + TIME - SHIFT) % TIME
     rolled_freq = (cell_number % FREQ + FREQ - SHIFT) % FREQ
@@ -893,10 +936,10 @@
     sent_rows, encoded, hidden, slope = enc_feed(middle, vecs, blocks, whole_down)
     sent_rows, gives = together(sent_rows, dec_run.offers())
     dec_run.deliver(gives)
-    pack_one, pack_two = [part.reshape(-1, part.shape[2]) for part in dec_run.result()]
-    tall_one = blocks_below(pack_one[:, 4 * dec_wide : 4 * dec_wide + dec_ff // 2], total, dec_wide)
-    tall_two = blocks_below(pack_two[:, dec_ff:], total, dec_wide)
-    dec_whole_down = jnp.concatenate([tall_one, tall_two], axis=1).reshape(-1, dec_wide)
+    dec_pack = dec_run.finish().reshape(-1, dec_pack.shape[1])
+    dec_end = 4 * dec_wide + dec_ff
+    dec_whole_down = blocks_below(dec_pack[:, dec_end : dec_end + dec_ff], total, dec_wide)
+    dec_whole_down = dec_whole_down.reshape(-1, dec_wide)
     arrived_rows = owners_to_bands(sent_rows.reshape(2, half_clips, slot_total, dec_wide))
     half_total = 4 * half_clips
 
@@ -922,15 +965,15 @@
         cotangent.reshape(half_total, cell_count, dec_wide),
         position_table(patch_number),
         allowed.astype(F32),
-        pack_one,
-        pack_two,
+        dec_pack,
         dec_whole_down,
     )
     decoded_out = decoded.reshape(cotangent.shape)
 
+    returning = join_bands(returning.reshape(2, 2, half_clips, slot_total, dec_wide))
+    returning, keep, give = together(returning, keep, give)
     dec_run = RunningSum(keep, give, total)
-    grad_sent = bands_to_owners(returning.reshape(2, 2, half_clips, slot_total, dec_wide))
-    grad_sent = grad_sent.reshape(-1, dec_wide)
+    grad_sent = bands_to_owners(returning).reshape(-1, dec_wide)
     grad_sent, gives = together(grad_sent, dec_run.offers())
     dec_run.deliver(gives)
     g_proj, keep, give, grad_middle, g_vec = enc_feed_back(
@@ -945,47 +988,60 @@
     keep, give, gives, feed_gives = together(keep, give, dec_run.offers(), feed_run.offers())
     dec_run.deliver(gives)
     feed_run.deliver(feed_gives)
+    keep, give, dec_shard, feed_gives = together(keep, give, dec_run.finish(), feed_run.offers())
+    feed_run.deliver(feed_gives)
     attend_run = RunningSum(keep, give, total)
-    dec_shard = dec_run.finish()
-    dec_shard, feed_gives, gives = together(dec_shard, feed_run.offers(), attend_run.offers())
-    dec_sum = gather_rows(dec_shard)
-    feed_run.deliver(feed_gives)
-    feed_gives, gives = together(feed_run.offers(), gives)
+    feed_gives, gives = together(feed_run.offers(), attend_run.offers())
     feed_run.deliver(feed_gives)
     attend_run.deliver(gives)
-    attend_run.deliver(attend_run.offers())
-    feed_sum = feed_run.finish()
-    attend_sum = attend_run.finish()
-    enc_sum = gather_rows(jnp.concatenate([attend_sum, feed_sum], axis=1))
-
-    by_chip = lambda packed, shard: packed.reshape(total // 2, 2, shard.shape[0], packed.shape[1])
+    feed_shard = feed_run.finish()
+    feed_shard, gives = together(feed_shard, attend_run.offers())
+    unit = dec_shard.shape[0] // 2
+    dec_units = [dec_shard[k * unit : (k + 1) * unit] for k in range(2)]
+    feed_units = [feed_shard[k * unit : (k + 1) * unit] for k in range(3)]
+    most_sum = gather_rows(jnp.concatenate(dec_units + feed_units, axis=1))
+    attend_run.deliver(gives)
+    attend_shard = attend_run.finish()
+    attend_sum = RunningGather(attend_shard, total).finish()
+
+    half = attend_shard.shape[1]
+    tail = 3 * enc_wide - half
+    e_qkv, e_out, e_proj, enc_vecs = unpack_sums(
+        attend_sum.reshape((total // 2, 2) + attend_shard.shape),
+        ((0, half, 1),),
+        ((0, 3 * enc_wide, 0), (0, enc_wide, 0), (0, dec_wide, 0), (0, 0, 8)),
+        (
+            (0, 0, (0, 0), 0, half),
+            (0, half, (0, 1), 0, tail),
+            (1, 0, (0, 1), tail, enc_wide),
+            (2, 0, (0, 1), tail + enc_wide, dec_wide),
+        ),
+        (),
+        ((3, (0, 1), tail + enc_wide + dec_wide),),
+    )
     half = dec_ff // 2
-    d_qkv, d_out, d_up, d_down, dec_vecs = unpack_sums(
-        by_chip(dec_sum, dec_shard),
-        (3 * dec_wide, dec_wide, dec_ff),
+    dec_half = dec_shard.shape[1]
+    d_qkv, d_out, d_up, d_down, dec_vecs, e_up, e_down = unpack_sums(
+        most_sum.reshape(total // 2, 2, unit, most_sum.shape[1]),
+        ((0, dec_half, 2), (2 * dec_half, enc_ff, 3)),
         (
-            (0, 0, 0, 0, 3 * dec_wide),
-            (1, 0, 0, 3 * dec_wide, dec_wide),
-            (2, 0, 0, 4 * dec_wide, half),
-            (2, half, 1, 0, half),
+            (0, 3 * dec_wide, 0),
+            (0, dec_wide, 0),
+            (0, dec_ff, 0),
+            (0, 0, dec_ff),
+            (0, 0, 8),
+            (1, enc_ff, 0),
+            (1, 0, enc_ff),
         ),
-        (1, half, dec_ff),
-        (0, 4 * dec_wide + half),
-    )
-    half = attend_sum.shape[1]
-    tail = 3 * enc_wide - half
-    e_qkv, e_out, e_proj, e_up, e_down, enc_vecs = unpack_sums(
-        by_chip(enc_sum, attend_sum),
-        (3 * enc_wide, enc_wide, dec_wide, enc_ff),
         (
-            (0, 0, 0, 0, half),
-            (0, half, 1, 0, tail),
-            (1, 0, 1, tail, enc_wide),
-            (2, 0, 1, tail + enc_wide, dec_wide),
-            (3, 0, 0, half, enc_ff),
+            (0, 0, (0, 0), 0, 3 * dec_wide),
+            (1, 0, (0, 0), 3 * dec_wide, dec_wide),
+            (2, 0, (0, 0), 4 * dec_wide, half),
+            (2, half, (0, 1), 0, half),
+            (5, 0, (1, 0), 0, enc_ff),
         ),
-        (1, half, enc_ff),
-        (1, tail + enc_wide + dec_wide),
+        ((3, (0, 1), half, dec_ff), (6, (1, 1), 0, enc_ff)),
+        ((4, (0, 0), 4 * dec_wide + half),),
     )
     return (
         decoded_out,

time: 646 us -> 603 us (0.933)
  waiting for transfers between devices: 257 us -> 234 us
  Pallas kernels: 195 us -> 178 us
  other arithmetic: 44.8 us -> 55 us
  starting transfers between devices: 83.4 us -> 74.9 us
    all_gather x3 -> x2, waiting for transfers between devices: 107 us -> 23.1 us  [gather_rows(): return lax.all_gather(shard, AXES, axis=0, tiled=True)]
    ppermute x39 -> x45, waiting for transfers between devices: 131 us -> 198 us  [deliver(): lax.ppermute(give, AXES, partner_pairs(self.total, mask))]
    pallas_call x1, Pallas kernels: 104 us -> 95.5 us  [decoder_block(): pl.pallas_call(decoder_kernel, grid=(n_half // halves,), in_specs=[pl.Blo...]
    pallas_call x6, Pallas kernels: 90.9 us -> 82.6 us  [the longest x4 62.1 us: whole_call(): pl.pallas_call(kernel, grid=(steps,), in_specs=specs, out_specs=out_specs...]
    another operation x26 -> x28, other arithmetic: 8.11 us -> 16.3 us  [deliver(): held = jnp.stack(parts, axis=at)]
    ppermute x39 -> x45, starting transfers between devices: 77.4 us -> 71.1 us  [deliver(): lax.ppermute(give, AXES, partner_pairs(self.total, mask))]
    unnamed x73 -> x61, local copies, waits for them, and re-layouts: 17 us -> 17.2 us
  transfers between devices with their start and end apart: 51 -> 56, of which waited for: 21 -> 31; matrix products, arithmetic and copies ran while one was open for 9% -> 10% of each run, Pallas kernels for 12% -> 11%
where the time goes in v5:
time: 603 us; the launch traced here: 598 us
  waiting for transfers between devices  234 us (39%)
  Pallas kernels  178 us (30%)
  starting transfers between devices  74.9 us (12%)
  other arithmetic  55 us (9%)
  local copies, waits for them, and re-layouts  41.4 us (7%)
  between operations  15.3 us (3%)
    ppermute x45, waiting for transfers between devices, deliver(): lax.ppermute(give, AXES, partner_pairs(self.total, mask))  198 us
    pallas_call x1, Pallas kernels, decoder_block(): pl.pallas_call(decoder_kernel, grid=(n_half // halves,), in_specs=[pl.Blo...  95.5 us
    ppermute x45, starting transfers between devices, deliver(): lax.ppermute(give, AXES, partner_pairs(self.total, mask))  71.1 us
    pallas_call x4, Pallas kernels, whole_call(): pl.pallas_call(kernel, grid=(steps,), in_specs=specs, out_specs=out_specs...  62.1 us
    all_gather x2, waiting for transfers between devices, gather_rows(): return lax.all_gather(shard, AXES, axis=0, tiled=True)  23.1 us
    pallas_call x2, Pallas kernels, unpack_sums(): pl.pallas_call(functools.partial(unpack_kernel, sections, pieces, talls,...  20.5 us
    unnamed x61, local copies, waits for them, and re-layouts  17.2 us
    another operation x28, other arithmetic, deliver(): held = jnp.stack(parts, axis=at)  16.3 us
  transfers between devices with their start and end apart: 56, of which 31 were waited for; matrix products, arithmetic and copies ran while one was open for 10% of the time, Pallas kernels for 11%

profile of v5, /device:TPU:0, one launch (start us, length us, event | category | flops | bytes accessed | tf_op | source)
XLA Modules:
  0.0 598.3 jit_solution(16389233674946131156)
XLA Ops:
  12.2 5.1 collective-permute-start.2
  28.3 7.2 %collective-permute-done.3 = bf16[96,768]{1,0:T(8,128)(2,1)S(1)} collective-permute-done((bf16[96,768]{1,0:T(8,128)(2,1)}, bf16[96,768]{1,0:T(8,128)(2,1)S(1)}, u32[]{:S(2)}, u32[]{:S(2)}) %collective-permute-start.3) | collective-permute-done | bytes 147488 | tf_op jit(solution)/shard_map/ppermute | solution.py:787
  36.8 4.3 collective-permute-start.11
  44.6 13.2 %collective-permute-done.10 = bf16[16,6272]{1,0:T(8,128)(2,1)S(1)} collective-permute-done((bf16[16,6272]{1,0:T(8,128)(2,1)S(1)}, bf16[16,6272]{1,0:T(8,128)(2,1)S(1)}, u32[]{:S(2)}, u32[]{:S(2)}) %collective-permute-start.10) | collective-permute-done | bytes 200736 | tf_op jit(solution)/shard_map/ppermute | solution.py:787
  59.8 2.8 collective-permute-start.8
  63.4 8.0 %collective-permute-done.6 = bf16[2,2,2,96,384]{4,3,1,0,2:T(8,128)(2,1)S(1)} collective-permute-done((bf16[2,2,2,96,384]{4,3,1,0,2:T(8,128)(2,1)S(1)}, bf16[2,2,2,96,384]{4,3,1,0,2:T(8,128)(2,1)S(1)}, u32[]{:S(2)}, u32[]{:S(2)}) %collective-permute-start.6) | collective-permute-done | bytes 589856 | tf_op jit(solution)/shard_map/ppermute | solution.py:787
  77.1 12.7 %collective-permute-done.14 = bf16[2,2,16,3072]{3,2,1,0:T(8,128)(2,1)} collective-permute-done((bf16[2,2,16,3072]{3,2,1,0:T(8,128)(2,1)S(1)}, bf16[2,2,16,3072]{3,2,1,0:T(8,128)(2,1)}, u32[]{:S(2)}, u32[]{:S(2)}) %collective-permute-start.14) | collective-permute-done | bytes 393248 | tf_op jit(solution)/shard_map/ppermute | solution.py:787
  95.8 2.6 pad_maximum_fusion.2
  98.4 20.8 %all-gather.3.cloned.1.call-done.small_ref.wqkv_ref.wo_ref.wu_ref.proj_ref = bf16[768,6784]{1,0:T(8,128)(2,1)} async-done(((bf16[24,6784]{1,0:T(8,128)(2,1)}), bf16[768,6784]{1,0:T(8,128)(2,1)}) %all-gather.3.cloned.1.call-update) | async-done | bytes 10420240 | tf_op jit(solution)/shard_map/all_gather | solution.py:813
  121.3 10.0 %enc_attend.1 = (bf16[512,2304]{1,0:T(8,128)(2,1)}, bf16[512,1536]{1,0:T(8,128)(2,1)}, bf16[512,768]{1,0:T(8,128)(2,1)}, f32[512,768]{1,0:T(8,128)}, f32[8,768]{1,0:T(8,128)}) custom-call(bf16[4,128,768]{2,1,0:T(8,128)(2,1)} %x_ref.3, f32[4,1,128]{2,1,0:T(1,128)} %compare_convert_fusion.mask_ref, ...), custom_call_target="tpu_custom_call" | custom-call | flops 10000000000 | bytes 16777216 | tf_op jit(solution)/shard_map/enc_attend/pallas_call | solution.py:535
  131.3 15.4 %enc_feed.1 = (bf16[512,512]{1,0:T(8,128)(2,1)}, bf16[512,768]{1,0:T(8,128)(2,1)}, bf16[512,3072]{1,0:T(8,128)(2,1)}, bf16[512,3072]{1,0:T(8,128)(2,1)}) custom-call(f32[512,768]{1,0:T(8,128)} %get-tuple-element.107.x2_ref, f32[8,768]{1,0:T(8,128)} %get-tuple-element.108.vec_ref, ...), custom_call_target="tpu_custom_call" | custom-call | flops 14000000000 | bytes 16777216 | tf_op jit(solution)/shard_map/enc_feed/pallas_call | solution.py:535
  154.0 4.0 reshape.367.cot_ref
  165.0 2.5 select_bitcast_fusion.1
  171.5 95.5 %decoder_block.1 = (bf16[8,256,512]{2,1,0:T(8,128)(2,1)}, bf16[8,128,512]{2,1,0:T(8,128)(2,1)}, bf16[512,3200]{1,0:T(8,128)(2,1)}, bf16[512,3200]{1,0:T(8,128)(2,1)}) custom-call(s32[1]{0:T(128)} %bitcast.core_ref, bf16[8,128,512]{2,1,0:T(8,128)(2,1)} %bitcast.324, s32[8,1,128]{2,1,0:T(1,128)} %bitcast.335, bf16[8,256,512]{2,1,0:T(8,128)(2,1)} %reshape.367.cot_ref, ...), custom_call_target="tpu_custom_call" | custom-call | flops 77309411328 | bytes 41943040 | tf_op jit(solution)/shard_map/decoder_block/pallas_call | solution.py:283
  269.0 2.1 collective-permute-done.20
  275.8 8.0 %collective-permute-done.21 = bf16[2,128,512]{2,1,0:T(8,128)(2,1)S(1)} collective-permute-done((bf16[2,128,512]{2,1,0:T(8,128)(2,1)}, bf16[2,128,512]{2,1,0:T(8,128)(2,1)S(1)}, u32[]{:S(2)}, u32[]{:S(2)}) %collective-permute-start.21) | collective-permute-done | bytes 262176 | tf_op jit(solution)/shard_map/ppermute | solution.py:833
  285.6 2.7 add_convert_fusion.1
  291.3 19.6 %enc_feed_back.1 = (bf16[768,512]{1,0:T(8,128)(2,1)}, bf16[768,3072]{1,0:T(8,128)(2,1)}, bf16[768,3072]{1,0:T(8,128)(2,1)}, f32[512,768]{1,0:T(8,128)}, f32[8,768]{1,0:T(8,128)}) custom-call(s32[1]{0:T(128)} %bitcast.core_ref, bf16[512,512]{1,0:T(8,128)(2,1)} %bitcast.331, bf16[512,768]{1,0:T(8,128)(2,1)} %get-tuple-element.124.enc_ref, ...), custom_call_target="tpu_custom_call" | custom-call | flops 17999998976 | bytes 16777216 | tf_op jit(solution)/shard_map/enc_feed_back/pallas_call | solution.py:535
  314.4 17.1 %enc_attend_back.1 = (bf16[768,1920]{1,0:T(8,128)(2,1)}, bf16[768,1920]{1,0:T(8,128)(2,1)}, bf16[4,128,768]{2,1,0:T(8,128)(2,1)}) custom-call(s32[1]{0:T(128)} %bitcast.core_ref, f32[512,768]{1,0:T(8,128)} %get-tuple-element.132.dx2_ref, bf16[512,768]{1,0:T(8,128)(2,1)} %get-tuple-element.133.o_ref, bf16[512,2304]{1,0:T(8,128)(2,1)} %get-tuple-element.134.qkv_ref, ...), custom_call_target="tpu_custom_call" | custom-call | flops 14000000000 | bytes 16777216 | tf_op jit(solution)/shard_map/enc_attend_back/pallas_call | solution.py:535
  335.0 4.3 add_convert_fusion
  342.9 2.8 collective-permute-start.29
  348.9 4.4 collective-permute-done.28
  353.3 7.6 %collective-permute-done.29 = bf16[32,3200]{1,0:T(8,128)(2,1)} collective-permute-done((bf16[32,3200]{1,0:T(8,128)(2,1)}, bf16[32,3200]{1,0:T(8,128)(2,1)}, u32[]{:S(2)}, u32[]{:S(2)}) %collective-permute-start.29) | collective-permute-done | bytes 204832 | tf_op jit(solution)/shard_map/ppermute | solution.py:740
  362.3 8.1 %collective-permute-done.32 = bf16[2,2,2,48,1536]{4,3,2,1,0:T(8,128)(2,1)} collective-permute-done((bf16[2,2,2,48,1536]{4,3,2,1,0:T(8,128)(2,1)}, bf16[2,2,2,48,1536]{4,3,2,1,0:T(8,128)(2,1)}, u32[]{:S(2)}, u32[]{:S(2)}) %collective-permute-start.32) | collective-permute-done | bytes 1179680 | tf_op jit(solution)/shard_map/ppermute | solution.py:740
  371.9 2.2 collective-permute-done.31
  379.1 12.6 %collective-permute-done.34 = bf16[2,2,48,1536]{3,2,1,0:T(8,128)(2,1)S(1)} collective-permute-done((bf16[2,2,48,1536]{3,2,1,0:T(8,128)(2,1)S(1)}, bf16[2,2,48,1536]{3,2,1,0:T(8,128)(2,1)S(1)}, u32[]{:S(2)}, u32[]{:S(2)}) %collective-permute-start.34) | collective-permute-done | bytes 589856 | tf_op jit(solution)/shard_map/ppermute | solution.py:740
  396.3 2.9 collective-permute-start.38
  402.9 7.0 %collective-permute-done.37 = bf16[48,3072]{1,0:T(8,128)(2,1)S(1)} collective-permute-done((bf16[48,3072]{1,0:T(8,128)(2,1)S(1)}, bf16[48,3072]{1,0:T(8,128)(2,1)S(1)}, u32[]{:S(2)}, u32[]{:S(2)}) %collective-permute-start.37) | collective-permute-done | bytes 294944 | tf_op jit(solution)/shard_map/ppermute | solution.py:740
  409.9 9.9 %collective-permute-done.38 = bf16[48,3072]{1,0:T(8,128)(2,1)S(1)} collective-permute-done((bf16[48,3072]{1,0:T(8,128)(2,1)S(1)}, bf16[48,3072]{1,0:T(8,128)(2,1)S(1)}, u32[]{:S(2)}, u32[]{:S(2)}) %collective-permute-start.38) | collective-permute-done | bytes 294944 | tf_op jit(solution)/shard_map/ppermute | solution.py:740
  423.7 5.0 collective-permute-done.41
  430.5 7.5 %collective-permute-start.43 = (bf16[48,1920]{1,0:T(8,128)(2,1)S(1)}, bf16[48,1920]{1,0:T(8,128)(2,1)S(1)}, u32[]{:S(2)}, u32[]{:S(2)}) collective-permute-start(bf16[48,1920]{1,0:T(8,128)(2,1)S(1)} %get-tuple-element.242), channel_id=1, source_target_pairs={{0,8},{1,9},{2,10},{3,11},{4,12},{5,13},{6,14},{7,15},{8,0},{9,1},... | collective-permute-start | bytes 552968 | tf_op jit(solution)/shard_map/ppermute | solution.py:740
  440.3 12.0 %collective-permute-done.43 = bf16[48,1920]{1,0:T(8,128)(2,1)S(1)} collective-permute-done((bf16[48,1920]{1,0:T(8,128)(2,1)S(1)}, bf16[48,1920]{1,0:T(8,128)(2,1)S(1)}, u32[]{:S(2)}, u32[]{:S(2)}) %collective-permute-start.43) | collective-permute-done | bytes 184352 | tf_op jit(solution)/shard_map/ppermute | solution.py:740
  452.4 8.9 %collective-permute-done.44 = bf16[48,1920]{1,0:T(8,128)(2,1)S(1)} collective-permute-done((bf16[48,1920]{1,0:T(8,128)(2,1)S(1)}, bf16[48,1920]{1,0:T(8,128)(2,1)S(1)}, u32[]{:S(2)}, u32[]{:S(2)}) %collective-permute-start.44) | collective-permute-done | bytes 184352 | tf_op jit(solution)/shard_map/ppermute | solution.py:740
  462.9 5.3 collective-permute-start.47
  468.2 3.2 collective-permute-done.46
  471.4 26.5 %collective-permute-done.47 = bf16[48,1920]{1,0:T(8,128)(2,1)S(1)} collective-permute-done((bf16[48,1920]{1,0:T(8,128)(2,1)S(1)}, bf16[48,1920]{1,0:T(8,128)(2,1)S(1)}, u32[]{:S(2)}, u32[]{:S(2)}) %collective-permute-start.47) | collective-permute-done | bytes 184352 | tf_op jit(solution)/shard_map/ppermute | solution.py:787
  499.6 3.0 collective-permute-start.49
  502.6 3.5 collective-permute-done.51
  506.3 4.4 collective-permute-start.52
  510.7 6.7 %collective-permute-done.49 = bf16[2,2,48,1024]{3,2,1,0:T(8,128)(2,1)S(1)} collective-permute-done((bf16[2,2,48,1024]{3,2,1,0:T(8,128)(2,1)S(1)}, bf16[2,2,48,1024]{3,2,1,0:T(8,128)(2,1)S(1)}, u32[]{:S(2)}, u32[]{:S(2)}) %collective-permute-start.49) | collective-permute-done | bytes 393248 | tf_op jit(solution)/shard_map/ppermute | solution.py:787
  517.6 27.2 %collective-permute-done.52 = bf16[2,2,2,48,896]{4,3,2,1,0:T(8,128)(2,1)S(1)} collective-permute-done((bf16[2,2,2,48,896]{4,3,2,1,0:T(8,128)(2,1)S(1)}, bf16[2,2,2,48,896]{4,3,2,1,0:T(8,128)(2,1)S(1)}, u32[]{:S(2)}, u32[]{:S(2)}) %collective-permute-start.52) | collective-permute-done | bytes 688160 | tf_op jit(solution)/shard_map/ppermute | solution.py:787
  545.0 6.8 %collective-permute-done.50 = bf16[2,2,2,48,1024]{4,3,1,0,2:T(8,128)(2,1)S(1)} collective-permute-done((bf16[2,2,2,48,1024]{4,3,1,0,2:T(8,128)(2,1)S(1)}, bf16[2,2,2,48,1024]{4,3,1,0,2:T(8,128)(2,1)S(1)}, u32[]{:S(2)}, u32[]{:S(2)}) %collective-permute-start.50) | collective-permute-done | bytes 786464 | tf_op jit(solution)/shard_map/ppermute | solution.py:787
  553.9 4.0 reshape.373
  559.7 2.5 broadcast_select_fusion.1
  562.1 3.1 pad_maximum_fusion.1.packed_ref
  565.3 6.0 %unpack_sums.2 = (f32[768,2304]{1,0:T(8,128)}, f32[768,768]{1,0:T(8,128)}, f32[768,512]{1,0:T(8,128)}, f32[8,768]{1,0:T(8,128)}) custom-call(bf16[16,2,48,1920]{3,2,1,0:T(8,128)(2,1)} %pad_maximum_fusion.1.packed_ref), custom_call_target="tpu_custom_call" | custom-call | bytes 17694720 | tf_op jit(solution)/shard_map/unpack_sums/pallas_call | solution.py:673
  572.8 2.4 all-gather.5.cloned.1.call-done
  575.2 14.4 %unpack_sums.3 = (f32[512,1536]{1,0:T(8,128)}, f32[512,512]{1,0:T(8,128)}, f32[512,2048]{1,0:T(8,128)}, f32[2048,512]{1,0:T(8,128)}, f32[8,512]{1,0:T(8,128)}, /*index=5*/f32[768,3072]{1,0:T(8,128)}, f32[3072,768]{1,0:T(8,128)}) custom-call(bf16[16,2,16,15616]{3,2,1,0:T(8,128)(2,1)} %bitcast.286), custom_call_target="tpu_custom_call" | custom-call | bytes 47972352 | tf_op jit(solution)/shard_map/unpack_sums/pallas_call | solution.py:673
  (251 shorter events, 115.2 us)
Async XLA Ops:
  7.2 112.0 %all-gather.3.cloned.1.call-start = ((), (), s32[]{:S(2)}) async-start(), calls=%async_computation | async-start | bytes 10745856 | tf_op jit(solution)/shard_map/all_gather | solution.py:813
  12.2 563.0 %all-gather.5.cloned.1.call-start = ((), (), s32[]{:S(2)}) async-start(), calls=%async_computation.1 | async-start | bytes 16490496 | tf_op jit(solution)/shard_map/all_gather | solution.py:813
  12.2 16.1 %collective-permute-start.2 = (bf16[96,768]{1,0:T(8,128)(2,1)}, bf16[96,768]{1,0:T(8,128)(2,1)S(1)}, u32[]{:S(2)}, u32[]{:S(2)}) collective-permute-start(bf16[96,768]{1,0:T(8,128)(2,1)} %param.32), channel_id=1, source_target_pairs={{0,24},{1,25},{2,26},{3,27},{4,28},{5,29},{6,30},{7,31},{8,16},{9,... | collective-permute-start | bytes 442376 | tf_op jit(solution)/shard_map/ppermute | solution.py:787
  17.3 18.2 %collective-permute-start.3 = (bf16[96,768]{1,0:T(8,128)(2,1)}, bf16[96,768]{1,0:T(8,128)(2,1)S(1)}, u32[]{:S(2)}, u32[]{:S(2)}) collective-permute-start(bf16[96,768]{1,0:T(8,128)(2,1)} %param.32), channel_id=1, source_target_pairs={{0,16},{1,17},{2,18},{3,19},{4,20},{5,21},{6,22},{7,23},{8,24},{9,... | collective-permute-start | bytes 442376 | tf_op jit(solution)/shard_map/ppermute | solution.py:787
  17.3 18.2 %collective-permute-start.4 = (bf16[96,768]{1,0:T(8,128)(2,1)}, bf16[96,768]{1,0:T(8,128)(2,1)S(1)}, u32[]{:S(2)}, u32[]{:S(2)}) collective-permute-start(bf16[96,768]{1,0:T(8,128)(2,1)} %param.32), channel_id=1, source_target_pairs={{0,8},{1,9},{2,10},{3,11},{4,12},{5,13},{6,14},{7,15},{8,0},{9,1},... | collective-permute-start | bytes 442376 | tf_op jit(solution)/shard_map/ppermute | solution.py:787
  36.7 21.1 %collective-permute-start.10 = (bf16[16,6272]{1,0:T(8,128)(2,1)S(1)}, bf16[16,6272]{1,0:T(8,128)(2,1)S(1)}, u32[]{:S(2)}, u32[]{:S(2)}) collective-permute-start(bf16[16,6272]{1,0:T(8,128)(2,1)S(1)} %constant_dynamic-update-slice_fusion.5), channel_id=1, source_target_pairs={{0,16},{1,17},{2,18},{3,19},{4,20},{5,21},{6,22},{7,23},{8,24},{9,... | collective-permute-start | bytes 602120 | tf_op jit(solution)/shard_map/ppermute | solution.py:787
  36.8 21.0 %collective-permute-start.11 = (bf16[16,6272]{1,0:T(8,128)(2,1)S(1)}, bf16[16,6272]{1,0:T(8,128)(2,1)S(1)}, u32[]{:S(2)}, u32[]{:S(2)}) collective-permute-start(bf16[16,6272]{1,0:T(8,128)(2,1)S(1)} %constant_dynamic-update-slice_fusion.5), channel_id=1, source_target_pairs={{0,8},{1,9},{2,10},{3,11},{4,12},{5,13},{6,14},{7,15},{8,0},{9,1},... | collective-permute-start | bytes 602120 | tf_op jit(solution)/shard_map/ppermute | solution.py:787
  41.0 16.8 %collective-permute-start.9 = (bf16[16,6272]{1,0:T(8,128)(2,1)S(1)}, bf16[16,6272]{1,0:T(8,128)(2,1)S(1)}, u32[]{:S(2)}, u32[]{:S(2)}) collective-permute-start(bf16[16,6272]{1,0:T(8,128)(2,1)S(1)} %constant_dynamic-update-slice_fusion.5), channel_id=1, source_target_pairs={{0,24},{1,25},{2,26},{3,27},{4,28},{5,29},{6,30},{7,31},{8,16},{9,... | collective-permute-start | bytes 602120 | tf_op jit(solution)/shard_map/ppermute | solution.py:787
  41.1 16.8 %collective-permute-start.5 = (bf16[2,2,96,384]{3,2,1,0:T(8,128)(2,1)S(1)}, bf16[2,2,96,384]{3,2,1,0:T(8,128)(2,1)S(1)}, u32[]{:S(2)}, u32[]{:S(2)}) collective-permute-start(bf16[2,2,96,384]{3,2,1,0:T(8,128)(2,1)S(1)} %get-tuple-element.98), channel_id=1, source_target_pairs={{0,2},{1,3},{2,0},{3,1},{4,6},{5,7},{6,4},{7,5},{8,10},{9,11},{10,... | collective-permute-start | bytes 884744 | tf_op jit(solution)/shard_map/ppermute | solution.py:787
  42.8 15.2 %collective-permute-start.7 = (bf16[2,2,96,384]{3,2,1,0:T(8,128)(2,1)S(1)}, bf16[2,2,96,384]{3,2,1,0:T(8,128)(2,1)S(1)}, u32[]{:S(2)}, u32[]{:S(2)}) collective-permute-start(bf16[2,2,96,384]{3,2,1,0:T(8,128)(2,1)S(1)} %get-tuple-element.99), channel_id=1, source_target_pairs={{0,4},{1,5},{2,6},{3,7},{4,0},{5,1},{6,2},{7,3},{8,12},{9,13},{10,... | collective-permute-start | bytes 884744 | tf_op jit(solution)/shard_map/ppermute | solution.py:787
  58.1 13.3 %collective-permute-start.6 = (bf16[2,2,2,96,384]{4,3,1,0,2:T(8,128)(2,1)S(1)}, bf16[2,2,2,96,384]{4,3,1,0,2:T(8,128)(2,1)S(1)}, u32[]{:S(2)}, u32[]{:S(2)}) collective-permute-start(bf16[2,2,2,96,384]{4,3,1,0,2:T(8,128)(2,1)S(1)} %pad_maximum_fusion.18), channel_id=1, source_target_pairs={{0,4},{1,5},{2,6},{3,7},{4,0},{5,1},{6,2},{7,3},{8,12},{9,13},{10,... | collective-permute-start | bytes 1769480 | tf_op jit(solution)/shard_map/ppermute | solution.py:787
  59.8 11.8 %collective-permute-start.8 = (bf16[2,2,2,96,384]{4,3,2,1,0:T(8,128)(2,1)S(1)}, bf16[2,2,2,96,384]{4,3,2,1,0:T(8,128)(2,1)S(1)}, u32[]{:S(2)}, u32[]{:S(2)}) collective-permute-start(bf16[2,2,2,96,384]{4,3,2,1,0:T(8,128)(2,1)S(1)} %pad_maximum_fusion.19), channel_id=1, source_target_pairs={{0,2},{1,3},{2,0},{3,1},{4,6},{5,7},{6,4},{7,5},{8,10},{9,11},{10,... | collective-permute-start | bytes 1769480 | tf_op jit(solution)/shard_map/ppermute | solution.py:787
  73.4 16.4 %collective-permute-start.14 = (bf16[2,2,16,3072]{3,2,1,0:T(8,128)(2,1)S(1)}, bf16[2,2,16,3072]{3,2,1,0:T(8,128)(2,1)}, u32[]{:S(2)}, u32[]{:S(2)}) collective-permute-start(bf16[2,2,16,3072]{3,2,1,0:T(8,128)(2,1)S(1)} %slice.144), channel_id=1, source_target_pairs={{0,4},{1,5},{2,6},{3,7},{4,0},{5,1},{6,2},{7,3},{8,12},{9,13},{10,... | collective-permute-start | bytes 1179656 | tf_op jit(solution)/shard_map/ppermute | solution.py:787
  75.3 18.0 %collective-permute-start.13 = (bf16[2,2,16,3200]{3,2,1,0:T(8,128)(2,1)}, bf16[2,2,16,3200]{3,2,1,0:T(8,128)(2,1)S(1)}, u32[]{:S(2)}, u32[]{:S(2)}) collective-permute-start(bf16[2,2,16,3200]{3,2,1,0:T(8,128)(2,1)} %slice.143), channel_id=1, source_target_pairs={{0,2},{1,3},{2,0},{3,1},{4,6},{5,7},{6,4},{7,5},{8,10},{9,11},{10,... | collective-permute-start | bytes 1228808 | tf_op jit(solution)/shard_map/ppermute | solution.py:787
  77.1 17.5 %collective-permute-start.12 = (bf16[2,2,2,2,96,768]{5,4,3,2,1,0:T(8,128)(2,1)}, bf16[2,2,2,2,96,768]{5,4,3,2,1,0:T(8,128)(2,1)S(1)}, u32[]{:S(2)}, u32[]{:S(2)}) collective-permute-start(bf16[2,2,2,2,96,768]{5,4,3,2,1,0:T(8,128)(2,1)} %maximum_maximum_fusion.2), channel_id=1, source_target_pairs={{0,1},{1,0},{2,3},{3,2},{4,5},{5,4},{6,7},{7,6},{8,9},{9,8},{10,11... | collective-permute-start | bytes 7077896 | tf_op jit(solution)/shard_map/ppermute | solution.py:787
  119.2 27.7 %collective-permute-start.15 = (bf16[2,2,2,16,3200]{4,3,1,0,2:T(8,128)(2,1)S(1)}, bf16[2,2,2,16,3200]{4,3,1,0,2:T(8,128)(2,1)S(1)}, u32[]{:S(2)}, u32[]{:S(2)}) collective-permute-start(bf16[2,2,2,16,3200]{4,3,1,0,2:T(8,128)(2,1)S(1)} %copy-done.13), channel_id=1, source_target_pairs={{0,4},{1,5},{2,6},{3,7},{4,0},{5,1},{6,2},{7,3},{8,12},{9,13},{10,... | collective-permute-start | bytes 2457608 | tf_op jit(solution)/shard_map/ppermute | solution.py:787
  120.0 26.7 %collective-permute-start.16 = (bf16[2,2,2,16,3072]{4,3,2,1,0:T(8,128)(2,1)S(1)}, bf16[2,2,2,16,3072]{4,3,2,1,0:T(8,128)(2,1)S(1)}, u32[]{:S(2)}, u32[]{:S(2)}) collective-permute-start(bf16[2,2,2,16,3072]{4,3,2,1,0:T(8,128)(2,1)S(1)} %copy-done.14), channel_id=1, source_target_pairs={{0,2},{1,3},{2,0},{3,1},{4,6},{5,7},{6,4},{7,5},{8,10},{9,11},{10,... | collective-permute-start | bytes 2359304 | tf_op jit(solution)/shard_map/ppermute | solution.py:787
  149.8 15.1 %collective-permute-start.19 = (bf16[2,2,2,2,16,6272]{5,4,3,2,1,0:T(8,128)(2,1)}, bf16[2,2,2,2,16,6272]{5,4,3,2,1,0:T(8,128)(2,1)}, u32[]{:S(2)}, u32[]{:S(2)}) collective-permute-start(bf16[2,2,2,2,16,6272]{5,4,3,2,1,0:T(8,128)(2,1)} %maximum_maximum_fusion), channel_id=1, source_target_pairs={{0,1},{1,0},{2,3},{3,2},{4,5},{5,4},{6,7},{7,6},{8,9},{9,8},{10,11... | collective-permute-start | bytes 9633800 | tf_op jit(solution)/shard_map/ppermute | solution.py:787
  151.5 9.0 %collective-permute-start.17 = (bf16[2,128,512]{2,1,0:T(8,128)(2,1)}, bf16[2,128,512]{2,1,0:T(8,128)(2,1)}, u32[]{:S(2)}, u32[]{:S(2)}) collective-permute-start(bf16[2,128,512]{2,1,0:T(8,128)(2,1)} %dynamic-slice_bitcast_fusion.14), channel_id=1, source_target_pairs={{0,2},{1,3},{2,0},{3,1},{4,6},{5,7},{6,4},{7,5},{8,10},{9,11},{10,... | collective-permute-start | bytes 786440 | tf_op jit(solution)/shard_map/ppermute | solution.py:833
  273.2 12.4 %collective-permute-start.22 = (bf16[512,3200]{1,0:T(8,128)(2,1)}, bf16[512,3200]{1,0:T(8,128)(2,1)}, u32[]{:S(2)}, u32[]{:S(2)}) collective-permute-start(bf16[512,3200]{1,0:T(8,128)(2,1)} %get-tuple-element.122), channel_id=1, source_target_pairs={{0,1},{1,0},{2,3},{3,2},{4,5},{5,4},{6,7},{7,6},{8,9},{9,8},{10,11... | collective-permute-start | bytes 9830408 | tf_op jit(solution)/shard_map/ppermute | solution.py:703
  275.0 8.8 %collective-permute-start.21 = (bf16[2,128,512]{2,1,0:T(8,128)(2,1)}, bf16[2,128,512]{2,1,0:T(8,128)(2,1)S(1)}, u32[]{:S(2)}, u32[]{:S(2)}) collective-permute-start(bf16[2,128,512]{2,1,0:T(8,128)(2,1)} %dynamic-slice_bitcast_fusion.13), channel_id=1, source_target_pairs={{0,2},{1,3},{2,0},{3,1},{4,6},{5,7},{6,4},{7,5},{8,10},{9,11},{10,... | collective-permute-start | bytes 786440 | tf_op jit(solution)/shard_map/ppermute | solution.py:833
  288.9 23.2 %collective-permute-start.24 = (bf16[2,2,2,32,1664]{4,3,2,1,0:T(8,128)(2,1)S(1)}, bf16[2,2,2,32,1664]{4,3,2,1,0:T(8,128)(2,1)S(1)}, u32[]{:S(2)}, u32[]{:S(2)}) collective-permute-start(bf16[2,2,2,32,1664]{4,3,2,1,0:T(8,128)(2,1)S(1)} %dynamic-slice_bitcast_fusion.1), channel_id=1, source_target_pairs={{0,2},{1,3},{2,0},{3,1},{4,6},{5,7},{6,4},{7,5},{8,10},{9,11},{10,... | collective-permute-start | bytes 2555912 | tf_op jit(solution)/shard_map/ppermute | solution.py:740
  289.8 21.2 %collective-permute-start.23 = (bf16[2,2,2,32,1536]{4,3,1,0,2:T(8,128)(2,1)S(1)}, bf16[2,2,2,32,1536]{4,3,1,0,2:T(8,128)(2,1)S(1)}, u32[]{:S(2)}, u32[]{:S(2)}) collective-permute-start(bf16[2,2,2,32,1536]{4,3,1,0,2:T(8,128)(2,1)S(1)} %bitcast.327), channel_id=1, source_target_pairs={{0,4},{1,5},{2,6},{3,7},{4,0},{5,1},{6,2},{7,3},{8,12},{9,13},{10,... | collective-permute-start | bytes 2359304 | tf_op jit(solution)/shard_map/ppermute | solution.py:740
  312.4 22.6 %collective-permute-start.27 = (bf16[768,3072]{1,0:T(8,128)(2,1)}, bf16[768,3072]{1,0:T(8,128)(2,1)}, u32[]{:S(2)}, u32[]{:S(2)}) collective-permute-start(bf16[768,3072]{1,0:T(8,128)(2,1)} %get-tuple-element.144), channel_id=1, source_target_pairs={{0,1},{1,0},{2,3},{3,2},{4,5},{5,4},{6,7},{7,6},{8,9},{9,8},{10,11... | collective-permute-start | bytes 14155784 | tf_op jit(solution)/shard_map/ppermute | solution.py:703
  312.5 19.0 %collective-permute-start.25 = (bf16[2,2,32,1536]{3,2,1,0:T(8,128)(2,1)}, bf16[2,2,32,1536]{3,2,1,0:T(8,128)(2,1)}, u32[]{:S(2)}, u32[]{:S(2)}) collective-permute-start(bf16[2,2,32,1536]{3,2,1,0:T(8,128)(2,1)} %dynamic-slice_bitcast_fusion.8), channel_id=1, source_target_pairs={{0,2},{1,3},{2,0},{3,1},{4,6},{5,7},{6,4},{7,5},{8,10},{9,11},{10,... | collective-permute-start | bytes 1179656 | tf_op jit(solution)/shard_map/ppermute | solution.py:740
  314.1 18.6 %collective-permute-start.26 = (bf16[2,2,32,1664]{3,2,1,0:T(8,128)(2,1)S(1)}, bf16[2,2,32,1664]{3,2,1,0:T(8,128)(2,1)}, u32[]{:S(2)}, u32[]{:S(2)}) collective-permute-start(bf16[2,2,32,1664]{3,2,1,0:T(8,128)(2,1)S(1)} %dynamic-slice_bitcast_fusion.6), channel_id=1, source_target_pairs={{0,4},{1,5},{2,6},{3,7},{4,0},{5,1},{6,2},{7,3},{8,12},{9,13},{10,... | collective-permute-start | bytes 1277960 | tf_op jit(solution)/shard_map/ppermute | solution.py:740
  342.2 28.1 %collective-permute-start.32 = (bf16[2,2,2,48,1536]{4,3,2,1,0:T(8,128)(2,1)}, bf16[2,2,2,48,1536]{4,3,2,1,0:T(8,128)(2,1)}, u32[]{:S(2)}, u32[]{:S(2)}) collective-permute-start(bf16[2,2,2,48,1536]{4,3,2,1,0:T(8,128)(2,1)} %dynamic-slice_bitcast_fusion), channel_id=1, source_target_pairs={{0,2},{1,3},{2,0},{3,1},{4,6},{5,7},{6,4},{7,5},{8,10},{9,11},{10,... | collective-permute-start | bytes 3538952 | tf_op jit(solution)/shard_map/ppermute | solution.py:740
  342.9 10.4 %collective-permute-start.28 = (bf16[32,3200]{1,0:T(8,128)(2,1)}, bf16[32,3200]{1,0:T(8,128)(2,1)}, u32[]{:S(2)}, u32[]{:S(2)}) collective-permute-start(bf16[32,3200]{1,0:T(8,128)(2,1)} %get-tuple-element.147), channel_id=1, source_target_pairs={{0,8},{1,9},{2,10},{3,11},{4,12},{5,13},{6,14},{7,15},{8,0},{9,1},... | collective-permute-start | bytes 614408 | tf_op jit(solution)/shard_map/ppermute | solution.py:740
  342.9 18.0 %collective-permute-start.29 = (bf16[32,3200]{1,0:T(8,128)(2,1)}, bf16[32,3200]{1,0:T(8,128)(2,1)}, u32[]{:S(2)}, u32[]{:S(2)}) collective-permute-start(bf16[32,3200]{1,0:T(8,128)(2,1)} %get-tuple-element.148), channel_id=1, source_target_pairs={{0,16},{1,17},{2,18},{3,19},{4,20},{5,21},{6,22},{7,23},{8,24},{9,... | collective-permute-start | bytes 614408 | tf_op jit(solution)/shard_map/ppermute | solution.py:740
  345.7 15.2 %collective-permute-start.30 = (bf16[32,3200]{1,0:T(8,128)(2,1)}, bf16[32,3200]{1,0:T(8,128)(2,1)}, u32[]{:S(2)}, u32[]{:S(2)}) collective-permute-start(bf16[32,3200]{1,0:T(8,128)(2,1)} %get-tuple-element.149), channel_id=1, source_target_pairs={{0,24},{1,25},{2,26},{3,27},{4,28},{5,29},{6,30},{7,31},{8,16},{9,... | collective-permute-start | bytes 614408 | tf_op jit(solution)/shard_map/ppermute | solution.py:740
  347.3 26.8 %collective-permute-start.31 = (bf16[2,2,2,48,1536]{4,3,1,0,2:T(8,128)(2,1)}, bf16[2,2,2,48,1536]{4,3,1,0,2:T(8,128)(2,1)S(1)}, u32[]{:S(2)}, u32[]{:S(2)}) collective-permute-start(bf16[2,2,2,48,1536]{4,3,1,0,2:T(8,128)(2,1)} %bitcast.323), channel_id=1, source_target_pairs={{0,4},{1,5},{2,6},{3,7},{4,0},{5,1},{6,2},{7,3},{8,12},{9,13},{10,... | collective-permute-start | bytes 3538952 | tf_op jit(solution)/shard_map/ppermute | solution.py:740
  376.0 17.2 %collective-permute-start.33 = (bf16[768,1920]{1,0:T(8,128)(2,1)S(1)}, bf16[768,1920]{1,0:T(8,128)(2,1)S(1)}, u32[]{:S(2)}, u32[]{:S(2)}) collective-permute-start(bf16[768,1920]{1,0:T(8,128)(2,1)S(1)} %copy-done.18), channel_id=1, source_target_pairs={{0,1},{1,0},{2,3},{3,2},{4,5},{5,4},{6,7},{7,6},{8,9},{9,8},{10,11... | collective-permute-start | bytes 8847368 | tf_op jit(solution)/shard_map/ppermute | solution.py:703
  376.0 15.7 %collective-permute-start.34 = (bf16[2,2,48,1536]{3,2,1,0:T(8,128)(2,1)S(1)}, bf16[2,2,48,1536]{3,2,1,0:T(8,128)(2,1)S(1)}, u32[]{:S(2)}, u32[]{:S(2)}) collective-permute-start(bf16[2,2,48,1536]{3,2,1,0:T(8,128)(2,1)S(1)} %dynamic-slice_bitcast_fusion.4), channel_id=1, source_target_pairs={{0,2},{1,3},{2,0},{3,1},{4,6},{5,7},{6,4},{7,5},{8,10},{9,11},{10,... | collective-permute-start | bytes 1769480 | tf_op jit(solution)/shard_map/ppermute | solution.py:740
  377.4 15.5 %collective-permute-start.35 = (bf16[2,2,48,1536]{3,2,1,0:T(8,128)(2,1)S(1)}, bf16[2,2,48,1536]{3,2,1,0:T(8,128)(2,1)S(1)}, u32[]{:S(2)}, u32[]{:S(2)}) collective-permute-start(bf16[2,2,48,1536]{3,2,1,0:T(8,128)(2,1)S(1)} %dynamic-slice_bitcast_fusion.3), channel_id=1, source_target_pairs={{0,4},{1,5},{2,6},{3,7},{4,0},{5,1},{6,2},{7,3},{8,12},{9,13},{10,... | collective-permute-start | bytes 1769480 | tf_op jit(solution)/shard_map/ppermute | solution.py:740
  396.2 13.8 %collective-permute-start.37 = (bf16[48,3072]{1,0:T(8,128)(2,1)S(1)}, bf16[48,3072]{1,0:T(8,128)(2,1)S(1)}, u32[]{:S(2)}, u32[]{:S(2)}) collective-permute-start(bf16[48,3072]{1,0:T(8,128)(2,1)S(1)} %get-tuple-element.157), channel_id=1, source_target_pairs={{0,8},{1,9},{2,10},{3,11},{4,12},{5,13},{6,14},{7,15},{8,0},{9,1},... | collective-permute-start | bytes 884744 | tf_op jit(solution)/shard_map/ppermute | solution.py:740
  396.3 23.6 %collective-permute-start.38 = (bf16[48,3072]{1,0:T(8,128)(2,1)S(1)}, bf16[48,3072]{1,0:T(8,128)(2,1)S(1)}, u32[]{:S(2)}, u32[]{:S(2)}) collective-permute-start(bf16[48,3072]{1,0:T(8,128)(2,1)S(1)} %get-tuple-element.158), channel_id=1, source_target_pairs={{0,16},{1,17},{2,18},{3,19},{4,20},{5,21},{6,22},{7,23},{8,24},{9,... | collective-permute-start | bytes 884744 | tf_op jit(solution)/shard_map/ppermute | solution.py:740
  399.2 20.6 %collective-permute-start.39 = (bf16[48,3072]{1,0:T(8,128)(2,1)S(1)}, bf16[48,3072]{1,0:T(8,128)(2,1)S(1)}, u32[]{:S(2)}, u32[]{:S(2)}) collective-permute-start(bf16[48,3072]{1,0:T(8,128)(2,1)S(1)} %get-tuple-element.159), channel_id=1, source_target_pairs={{0,24},{1,25},{2,26},{3,27},{4,28},{5,29},{6,30},{7,31},{8,16},{9,... | collective-permute-start | bytes 884744 | tf_op jit(solution)/shard_map/ppermute | solution.py:740
  400.6 19.6 %collective-permute-start.40 = (bf16[2,2,2,48,1024]{4,3,2,1,0:T(8,128)(2,1)S(1)}, bf16[2,2,2,48,1024]{4,3,2,1,0:T(8,128)(2,1)S(1)}, u32[]{:S(2)}, u32[]{:S(2)}) collective-permute-start(bf16[2,2,2,48,1024]{4,3,2,1,0:T(8,128)(2,1)S(1)} %dynamic-slice_bitcast_fusion.2), channel_id=1, source_target_pairs={{0,2},{1,3},{2,0},{3,1},{4,6},{5,7},{6,4},{7,5},{8,10},{9,11},{10,... | collective-permute-start | bytes 2359304 | tf_op jit(solution)/shard_map/ppermute | solution.py:740
  401.4 18.6 %collective-permute-start.36 = (bf16[2,2,2,48,896]{4,3,1,0,2:T(8,128)(2,1)S(1)}, bf16[2,2,2,48,896]{4,3,1,0,2:T(8,128)(2,1)S(1)}, u32[]{:S(2)}, u32[]{:S(2)}) collective-permute-start(bf16[2,2,2,48,896]{4,3,1,0,2:T(8,128)(2,1)S(1)} %bitcast.328), channel_id=1, source_target_pairs={{0,4},{1,5},{2,6},{3,7},{4,0},{5,1},{6,2},{7,3},{8,12},{9,13},{10,... | collective-permute-start | bytes 2064392 | tf_op jit(solution)/shard_map/ppermute | solution.py:740
  430.5 21.9 %collective-permute-start.43 = (bf16[48,1920]{1,0:T(8,128)(2,1)S(1)}, bf16[48,1920]{1,0:T(8,128)(2,1)S(1)}, u32[]{:S(2)}, u32[]{:S(2)}) collective-permute-start(bf16[48,1920]{1,0:T(8,128)(2,1)S(1)} %get-tuple-element.242), channel_id=1, source_target_pairs={{0,8},{1,9},{2,10},{3,11},{4,12},{5,13},{6,14},{7,15},{8,0},{9,1},... | collective-permute-start | bytes 552968 | tf_op jit(solution)/shard_map/ppermute | solution.py:740
  437.9 23.3 %collective-permute-start.44 = (bf16[48,1920]{1,0:T(8,128)(2,1)S(1)}, bf16[48,1920]{1,0:T(8,128)(2,1)S(1)}, u32[]{:S(2)}, u32[]{:S(2)}) collective-permute-start(bf16[48,1920]{1,0:T(8,128)(2,1)S(1)} %get-tuple-element.244), channel_id=1, source_target_pairs={{0,16},{1,17},{2,18},{3,19},{4,20},{5,21},{6,22},{7,23},{8,24},{9,... | collective-permute-start | bytes 552968 | tf_op jit(solution)/shard_map/ppermute | solution.py:740
  438.6 22.6 %collective-permute-start.45 = (bf16[48,1920]{1,0:T(8,128)(2,1)S(1)}, bf16[48,1920]{1,0:T(8,128)(2,1)S(1)}, u32[]{:S(2)}, u32[]{:S(2)}) collective-permute-start(bf16[48,1920]{1,0:T(8,128)(2,1)S(1)} %get-tuple-element.243), channel_id=1, source_target_pairs={{0,24},{1,25},{2,26},{3,27},{4,28},{5,29},{6,30},{7,31},{8,16},{9,... | collective-permute-start | bytes 552968 | tf_op jit(solution)/shard_map/ppermute | solution.py:740
  461.3 10.1 %collective-permute-start.46 = (bf16[48,1920]{1,0:T(8,128)(2,1)S(1)}, bf16[48,1920]{1,0:T(8,128)(2,1)S(1)}, u32[]{:S(2)}, u32[]{:S(2)}) collective-permute-start(bf16[48,1920]{1,0:T(8,128)(2,1)S(1)} %fusion.20), channel_id=1, source_target_pairs={{0,24},{1,25},{2,26},{3,27},{4,28},{5,29},{6,30},{7,31},{8,16},{9,... | collective-permute-start | bytes 552968 | tf_op jit(solution)/shard_map/ppermute | solution.py:787
  462.9 35.0 %collective-permute-start.47 = (bf16[48,1920]{1,0:T(8,128)(2,1)S(1)}, bf16[48,1920]{1,0:T(8,128)(2,1)S(1)}, u32[]{:S(2)}, u32[]{:S(2)}) collective-permute-start(bf16[48,1920]{1,0:T(8,128)(2,1)S(1)} %fusion.20), channel_id=1, source_target_pairs={{0,16},{1,17},{2,18},{3,19},{4,20},{5,21},{6,22},{7,23},{8,24},{9,... | collective-permute-start | bytes 552968 | tf_op jit(solution)/shard_map/ppermute | solution.py:787
  468.2 29.7 %collective-permute-start.48 = (bf16[48,1920]{1,0:T(8,128)(2,1)S(1)}, bf16[48,1920]{1,0:T(8,128)(2,1)S(1)}, u32[]{:S(2)}, u32[]{:S(2)}) collective-permute-start(bf16[48,1920]{1,0:T(8,128)(2,1)S(1)} %fusion.20), channel_id=1, source_target_pairs={{0,8},{1,9},{2,10},{3,11},{4,12},{5,13},{6,14},{7,15},{8,0},{9,1},... | collective-permute-start | bytes 552968 | tf_op jit(solution)/shard_map/ppermute | solution.py:787
  499.6 17.8 %collective-permute-start.49 = (bf16[2,2,48,1024]{3,2,1,0:T(8,128)(2,1)S(1)}, bf16[2,2,48,1024]{3,2,1,0:T(8,128)(2,1)S(1)}, u32[]{:S(2)}, u32[]{:S(2)}) collective-permute-start(bf16[2,2,48,1024]{3,2,1,0:T(8,128)(2,1)S(1)} %slice.155), channel_id=1, source_target_pairs={{0,2},{1,3},{2,0},{3,1},{4,6},{5,7},{6,4},{7,5},{8,10},{9,11},{10,... | collective-permute-start | bytes 1179656 | tf_op jit(solution)/shard_map/ppermute | solution.py:787
  506.3 38.5 %collective-permute-start.52 = (bf16[2,2,2,48,896]{4,3,2,1,0:T(8,128)(2,1)S(1)}, bf16[2,2,2,48,896]{4,3,2,1,0:T(8,128)(2,1)S(1)}, u32[]{:S(2)}, u32[]{:S(2)}) collective-permute-start(bf16[2,2,2,48,896]{4,3,2,1,0:T(8,128)(2,1)S(1)} %pad_maximum_fusion.16), channel_id=1, source_target_pairs={{0,2},{1,3},{2,0},{3,1},{4,6},{5,7},{6,4},{7,5},{8,10},{9,11},{10,... | collective-permute-start | bytes 2064392 | tf_op jit(solution)/shard_map/ppermute | solution.py:787
  517.5 34.3 %collective-permute-start.50 = (bf16[2,2,2,48,1024]{4,3,1,0,2:T(8,128)(2,1)S(1)}, bf16[2,2,2,48,1024]{4,3,1,0,2:T(8,128)(2,1)S(1)}, u32[]{:S(2)}, u32[]{:S(2)}) collective-permute-start(bf16[2,2,2,48,1024]{4,3,1,0,2:T(8,128)(2,1)S(1)} %pad_maximum_fusion.13), channel_id=1, source_target_pairs={{0,4},{1,5},{2,6},{3,7},{4,0},{5,1},{6,2},{7,3},{8,12},{9,13},{10,... | collective-permute-start | bytes 2359304 | tf_op jit(solution)/shard_map/ppermute | solution.py:787
  (29 other events, 203.7 us)
Sparse Core Ops, SparseCore 0:
  12.3 106.8 all-gather.2
  421.6 153.5 all-gather.4

commit v6 on v5

--- a/solution.py
+++ b/solution.py
@@ -548,10 +548,11 @@
 
 
 def enc_blocks(pack, width, ff, sent):
+    up = 4 * width // FEED_CHUNK
     return (
         (pack, (width, 3 * width), 0),
         (pack, (width, width), 3),
-        (pack, (width, ff), 4 * width // ff),
+        (pack, (width, FEED_CHUNK), lambda i: (0, up + i)),
         (pack, (width, sent), (4 * width + ff) // sent),
         (pack, (width, LANES), (4 * width + ff + sent) // LANES),
     )
@@ -576,7 +577,6 @@
     ff, chunk = wd.shape[0], FEED_CHUNK
     _, _, up, proj, _ = blocks
     across, down = lambda i: (0, i), lambda i: (i, 0)
-    up = (up[0], (width, chunk), lambda i: (0, 4 * width // chunk + i))
     kept = ((m, ff), BF16, (m, chunk), across)
     outs = [((m, proj[1][1]), BF16), ((m, width), BF16), kept, kept]
     scratch = [((m, width), BF16), ((m, width), F32)]
@@ -589,7 +589,6 @@
     ff, chunk = wd.shape[0], FEED_CHUNK
     _, _, up, proj, _ = blocks
     across, down = lambda i: (0, i), lambda i: (i, 0)
-    up = (up[0], (width, chunk), lambda i: (0, 4 * width // chunk + i))
     half = ((width, ff), BF16, (width, chunk), across)
     outs = [(proj[1], BF16), half, half, ((m, width), F32), ((8, width), F32)]
     scratch = [((width, m), BF16), ((m, width), BF16), ((width, m), BF16), ((m, width), F32)]
@@ -700,9 +699,10 @@
         bits = total.bit_length() - 1
         self.total = total
         self.cut = keep.shape[1] // 256 * 128
-        got = lax.ppermute(give, AXES, partner_pairs(total, 1))
         rows = keep.shape[0] // (total // 2)
-        self.held = [add_low(keep, got).reshape((2,) * (bits - 1) + (rows, keep.shape[1]))]
+        self.shape = (2,) * (bits - 1) + (rows, keep.shape[1])
+        self.keep = [keep]
+        self.got = [lax.ppermute(give, AXES, partner_pairs(total, 1))]
         self.left = [list(range(bits - 1, 0, -1))]
         self.plan = [[[2], [1]], [[1], [2]]]
         rest = list(range(3, bits))
@@ -710,7 +710,16 @@
             self.plan.append([rest[:2]])
             rest = rest[2:]
 
+    def settle(self):
+        each = len(self.got) // len(self.keep)
+        self.held = [
+            add_low(keep, *self.got[i * each : (i + 1) * each]) for i, keep in enumerate(self.keep)
+        ]
+        if self.shape:
+            self.held, self.shape = [self.held[0].reshape(self.shape)], None
+
     def offers(self):
+        self.settle()
         me = lax.axis_index(AXES)
         groups = self.plan[0]
         if len(groups) > len(self.held):
@@ -736,19 +745,16 @@
         return gives
 
     def deliver(self, gives):
-        got = [
+        self.got = [
             lax.ppermute(give, AXES, partner_pairs(self.total, mask))
             for give, mask in zip(gives, self.masks)
         ]
-        each = len(got) // len(self.keep)
-        self.held = [
-            add_low(keep, *got[i * each : (i + 1) * each]) for i, keep in enumerate(self.keep)
-        ]
         self.plan = self.plan[1:]
 
     def finish(self):
         while self.plan:
             self.deliver(self.offers())
+        self.settle()
         return jnp.concatenate(self.held, axis=-1)
 
 
@@ -985,12 +991,15 @@
     keep, give, grad_visible = enc_attend_back(
         core, grad_middle, mixed, qkv, probs, visible, vecs, blocks, g_proj, g_vec
     )
-    keep, give, gives, feed_gives = together(keep, give, dec_run.offers(), feed_run.offers())
-    dec_run.deliver(gives)
+    keep, give, dec_run.got, feed_run.got = together(keep, give, dec_run.got, feed_run.got)
+    attend_run = RunningSum(keep, give, total)
+    feed_gives, dec_run.got, attend_run.got = together(
+        feed_run.offers(), dec_run.got, attend_run.got
+    )
     feed_run.deliver(feed_gives)
-    keep, give, dec_shard, feed_gives = together(keep, give, dec_run.finish(), feed_run.offers())
+    dec_run.deliver(dec_run.offers())
+    dec_shard, feed_gives = together(dec_run.finish(), feed_run.offers())
     feed_run.deliver(feed_gives)
-    attend_run = RunningSum(keep, give, total)
     feed_gives, gives = together(feed_run.offers(), attend_run.offers())
     feed_run.deliver(feed_gives)
     attend_run.deliver(gives)

time: 603 us -> 587 us (0.973)
  starting transfers between devices: 74.9 us -> 65.6 us
    ppermute x45, starting transfers between devices: 71.1 us -> 61.6 us  [deliver(): lax.ppermute(give, AXES, partner_pairs(self.total, mask))]
    unnamed x61 -> x49, local copies, waits for them, and re-layouts: 17.2 us -> 15 us
  transfers between devices with their start and end apart: 56 -> 56, of which waited for: 31 -> 31; matrix products, arithmetic and copies ran while one was open for 10% -> 10% of each run, Pallas kernels for 11% -> 12%
where the time goes in v6:
time: 587 us; the launch traced here: 580 us
  waiting for transfers between devices  233 us (40%)
  Pallas kernels  178 us (30%)
  starting transfers between devices  65.6 us (11%)
  other arithmetic  52.8 us (9%)
  local copies, waits for them, and re-layouts  35.7 us (6%)
  between operations  15.3 us (3%)
    ppermute x45, waiting for transfers between devices, deliver(): lax.ppermute(give, AXES, partner_pairs(self.total, mask))  198 us
    pallas_call x1, Pallas kernels, decoder_block(): pl.pallas_call(decoder_kernel, grid=(n_half // halves,), in_specs=[pl.Blo...  95.5 us
    pallas_call x4, Pallas kernels, whole_call(): pl.pallas_call(kernel, grid=(steps,), in_specs=specs, out_specs=out_specs...  62 us
    ppermute x45, starting transfers between devices, deliver(): lax.ppermute(give, AXES, partner_pairs(self.total, mask))  61.6 us
    all_gather x2, waiting for transfers between devices, gather_rows(): return lax.all_gather(shard, AXES, axis=0, tiled=True)  22.9 us
    pallas_call x2, Pallas kernels, unpack_sums(): pl.pallas_call(functools.partial(unpack_kernel, sections, pieces, talls,...  20.5 us
    another operation x28, other arithmetic, deliver(): held = jnp.stack(parts, axis=at)  16.2 us
    unnamed x49, local copies, waits for them, and re-layouts  15 us
  transfers between devices with their start and end apart: 56, of which 31 were waited for; matrix products, arithmetic and copies ran while one was open for 10% of the time, Pallas kernels for 12%

profile of v6, /device:TPU:0, one launch (start us, length us, event | category | flops | bytes accessed | tf_op | source)
XLA Modules:
  0.0 580.0 jit_solution(5541783011158800440)
XLA Ops:
  12.2 5.1 collective-permute-start.2
  28.3 7.2 %collective-permute-done.3 = bf16[96,768]{1,0:T(8,128)(2,1)S(1)} collective-permute-done((bf16[96,768]{1,0:T(8,128)(2,1)}, bf16[96,768]{1,0:T(8,128)(2,1)S(1)}, u32[]{:S(2)}, u32[]{:S(2)}) %collective-permute-start.3) | collective-permute-done | bytes 147488 | tf_op jit(solution)/shard_map/ppermute | solution.py:793
  36.8 4.3 collective-permute-start.11
  44.6 13.2 %collective-permute-done.10 = bf16[16,6272]{1,0:T(8,128)(2,1)S(1)} collective-permute-done((bf16[16,6272]{1,0:T(8,128)(2,1)S(1)}, bf16[16,6272]{1,0:T(8,128)(2,1)S(1)}, u32[]{:S(2)}, u32[]{:S(2)}) %collective-permute-start.10) | collective-permute-done | bytes 200736 | tf_op jit(solution)/shard_map/ppermute | solution.py:793
  59.8 2.8 collective-permute-start.8
  63.4 8.0 %collective-permute-done.6 = bf16[2,2,2,96,384]{4,3,1,0,2:T(8,128)(2,1)S(1)} collective-permute-done((bf16[2,2,2,96,384]{4,3,1,0,2:T(8,128)(2,1)S(1)}, bf16[2,2,2,96,384]{4,3,1,0,2:T(8,128)(2,1)S(1)}, u32[]{:S(2)}, u32[]{:S(2)}) %collective-permute-start.6) | collective-permute-done | bytes 589856 | tf_op jit(solution)/shard_map/ppermute | solution.py:793
  77.1 12.7 %collective-permute-done.14 = bf16[2,2,16,3072]{3,2,1,0:T(8,128)(2,1)} collective-permute-done((bf16[2,2,16,3072]{3,2,1,0:T(8,128)(2,1)S(1)}, bf16[2,2,16,3072]{3,2,1,0:T(8,128)(2,1)}, u32[]{:S(2)}, u32[]{:S(2)}) %collective-permute-start.14) | collective-permute-done | bytes 393248 | tf_op jit(solution)/shard_map/ppermute | solution.py:793
  95.8 2.6 pad_maximum_fusion.2
  98.4 20.8 %all-gather.3.cloned.1.call-done.small_ref.wqkv_ref.wo_ref.wu_ref.proj_ref = bf16[768,6784]{1,0:T(8,128)(2,1)} async-done(((bf16[24,6784]{1,0:T(8,128)(2,1)}), bf16[768,6784]{1,0:T(8,128)(2,1)}) %all-gather.3.cloned.1.call-update) | async-done | bytes 10420240 | tf_op jit(solution)/shard_map/all_gather | solution.py:819
  121.3 10.0 %enc_attend.1 = (bf16[512,2304]{1,0:T(8,128)(2,1)}, bf16[512,1536]{1,0:T(8,128)(2,1)}, bf16[512,768]{1,0:T(8,128)(2,1)}, f32[512,768]{1,0:T(8,128)}, f32[8,768]{1,0:T(8,128)}) custom-call(bf16[4,128,768]{2,1,0:T(8,128)(2,1)} %x_ref.3, f32[4,1,128]{2,1,0:T(1,128)} %compare_convert_fusion.mask_ref, ...), custom_call_target="tpu_custom_call" | custom-call | flops 10000000000 | bytes 16777216 | tf_op jit(solution)/shard_map/enc_attend/pallas_call | solution.py:535
  131.3 15.4 %enc_feed.1 = (bf16[512,512]{1,0:T(8,128)(2,1)}, bf16[512,768]{1,0:T(8,128)(2,1)}, bf16[512,3072]{1,0:T(8,128)(2,1)}, bf16[512,3072]{1,0:T(8,128)(2,1)}) custom-call(f32[512,768]{1,0:T(8,128)} %get-tuple-element.108.x2_ref, f32[8,768]{1,0:T(8,128)} %get-tuple-element.109.vec_ref, ...), custom_call_target="tpu_custom_call" | custom-call | flops 14000000000 | bytes 16777216 | tf_op jit(solution)/shard_map/enc_feed/pallas_call | solution.py:535
  154.0 4.0 reshape.367.cot_ref
  164.9 2.5 select_bitcast_fusion.1
  171.5 95.5 %decoder_block.1 = (bf16[8,256,512]{2,1,0:T(8,128)(2,1)}, bf16[8,128,512]{2,1,0:T(8,128)(2,1)}, bf16[512,3200]{1,0:T(8,128)(2,1)}, bf16[512,3200]{1,0:T(8,128)(2,1)}) custom-call(s32[1]{0:T(128)} %bitcast.core_ref, bf16[8,128,512]{2,1,0:T(8,128)(2,1)} %bitcast.322, s32[8,1,128]{2,1,0:T(1,128)} %bitcast.333, bf16[8,256,512]{2,1,0:T(8,128)(2,1)} %reshape.367.cot_ref, ...), custom_call_target="tpu_custom_call" | custom-call | flops 77309411328 | bytes 41943040 | tf_op jit(solution)/shard_map/decoder_block/pallas_call | solution.py:283
  269.0 2.1 collective-permute-done.20
  274.6 7.8 %collective-permute-done.21 = bf16[2,128,512]{2,1,0:T(8,128)(2,1)S(1)} collective-permute-done((bf16[2,128,512]{2,1,0:T(8,128)(2,1)}, bf16[2,128,512]{2,1,0:T(8,128)(2,1)S(1)}, u32[]{:S(2)}, u32[]{:S(2)}) %collective-permute-start.21) | collective-permute-done | bytes 262176 | tf_op jit(solution)/shard_map/ppermute | solution.py:839
  284.3 2.7 add_convert_fusion.1
  290.1 19.6 %enc_feed_back.1 = (bf16[768,512]{1,0:T(8,128)(2,1)}, bf16[768,3072]{1,0:T(8,128)(2,1)}, bf16[768,3072]{1,0:T(8,128)(2,1)}, f32[512,768]{1,0:T(8,128)}, f32[8,768]{1,0:T(8,128)}) custom-call(s32[1]{0:T(128)} %bitcast.core_ref, bf16[512,512]{1,0:T(8,128)(2,1)} %bitcast.329, bf16[512,768]{1,0:T(8,128)(2,1)} %get-tuple-element.125.enc_ref, ...), custom_call_target="tpu_custom_call" | custom-call | flops 17999998976 | bytes 16777216 | tf_op jit(solution)/shard_map/enc_feed_back/pallas_call | solution.py:535
  312.1 17.0 %enc_attend_back.1 = (bf16[768,1920]{1,0:T(8,128)(2,1)}, bf16[768,1920]{1,0:T(8,128)(2,1)}, bf16[4,128,768]{2,1,0:T(8,128)(2,1)}) custom-call(s32[1]{0:T(128)} %bitcast.core_ref, f32[512,768]{1,0:T(8,128)} %get-tuple-element.133.dx2_ref, bf16[512,768]{1,0:T(8,128)(2,1)} %get-tuple-element.134.o_ref, bf16[512,2304]{1,0:T(8,128)(2,1)} %get-tuple-element.135.qkv_ref, ...), custom_call_target="tpu_custom_call" | custom-call | flops 14000000000 | bytes 16777216 | tf_op jit(solution)/shard_map/enc_attend_back/pallas_call | solution.py:535
  329.2 5.7 add_convert_fusion
  337.6 2.6 add_convert_fusion.2
  343.4 2.9 collective-permute-start.31
  348.0 6.0 %collective-permute-done.30 = bf16[32,3200]{1,0:T(8,128)(2,1)S(1)} collective-permute-done((bf16[32,3200]{1,0:T(8,128)(2,1)S(1)}, bf16[32,3200]{1,0:T(8,128)(2,1)S(1)}, u32[]{:S(2)}, u32[]{:S(2)}) %collective-permute-start.30) | collective-permute-done | bytes 204832 | tf_op jit(solution)/shard_map/ppermute | solution.py:749
  353.9 7.1 %collective-permute-done.31 = bf16[32,3200]{1,0:T(8,128)(2,1)S(1)} collective-permute-done((bf16[32,3200]{1,0:T(8,128)(2,1)S(1)}, bf16[32,3200]{1,0:T(8,128)(2,1)S(1)}, u32[]{:S(2)}, u32[]{:S(2)}) %collective-permute-start.31) | collective-permute-done | bytes 204832 | tf_op jit(solution)/shard_map/ppermute | solution.py:749
  361.2 7.8 %collective-permute-done.33 = bf16[2,2,2,48,1536]{4,3,2,1,0:T(8,128)(2,1)S(1)} collective-permute-done((bf16[2,2,2,48,1536]{4,3,2,1,0:T(8,128)(2,1)S(1)}, bf16[2,2,2,48,1536]{4,3,2,1,0:T(8,128)(2,1)S(1)}, u32[]{:S(2)}, u32[]{:S(2)}) %collective-permute-start.33) | collective-permute-done | bytes 1179680 | tf_op jit(solution)/shard_map/ppermute | solution.py:749
  373.0 11.7 %collective-permute-done.34 = bf16[2,2,48,1536]{3,2,1,0:T(8,128)(2,1)S(1)} collective-permute-done((bf16[2,2,48,1536]{3,2,1,0:T(8,128)(2,1)S(1)}, bf16[2,2,48,1536]{3,2,1,0:T(8,128)(2,1)S(1)}, u32[]{:S(2)}, u32[]{:S(2)}) %collective-permute-start.34) | collective-permute-done | bytes 589856 | tf_op jit(solution)/shard_map/ppermute | solution.py:749
  386.1 2.8 collective-permute-start.38
  393.2 5.2 collective-permute-done.37
  398.4 11.3 %collective-permute-done.38 = bf16[48,3072]{1,0:T(8,128)(2,1)S(1)} collective-permute-done((bf16[48,3072]{1,0:T(8,128)(2,1)S(1)}, bf16[48,3072]{1,0:T(8,128)(2,1)S(1)}, u32[]{:S(2)}, u32[]{:S(2)}) %collective-permute-start.38) | collective-permute-done | bytes 294944 | tf_op jit(solution)/shard_map/ppermute | solution.py:749
  414.0 4.6 collective-permute-done.41
  420.3 5.1 collective-permute-start.43
  427.8 9.5 %collective-permute-done.43 = bf16[48,1920]{1,0:T(8,128)(2,1)S(1)} collective-permute-done((bf16[48,1920]{1,0:T(8,128)(2,1)S(1)}, bf16[48,1920]{1,0:T(8,128)(2,1)S(1)}, u32[]{:S(2)}, u32[]{:S(2)}) %collective-permute-start.43) | collective-permute-done | bytes 184352 | tf_op jit(solution)/shard_map/ppermute | solution.py:749
  437.3 13.1 %collective-permute-done.44 = bf16[48,1920]{1,0:T(8,128)(2,1)S(1)} collective-permute-done((bf16[48,1920]{1,0:T(8,128)(2,1)S(1)}, bf16[48,1920]{1,0:T(8,128)(2,1)S(1)}, u32[]{:S(2)}, u32[]{:S(2)}) %collective-permute-start.44) | collective-permute-done | bytes 184352 | tf_op jit(solution)/shard_map/ppermute | solution.py:749
  450.5 2.6 collective-permute-start.46
  453.1 2.5 collective-permute-start.47
  455.7 4.5 collective-permute-done.46
  460.2 26.1 %collective-permute-done.47 = bf16[48,1920]{1,0:T(8,128)(2,1)S(1)} collective-permute-done((bf16[48,1920]{1,0:T(8,128)(2,1)S(1)}, bf16[48,1920]{1,0:T(8,128)(2,1)S(1)}, u32[]{:S(2)}, u32[]{:S(2)}) %collective-permute-start.47) | collective-permute-done | bytes 184352 | tf_op jit(solution)/shard_map/ppermute | solution.py:793
  488.8 7.5 %collective-permute-done.51 = bf16[2,2,48,896]{3,2,1,0:T(8,128)(2,1)S(1)} collective-permute-done((bf16[2,2,48,896]{3,2,1,0:T(8,128)(2,1)S(1)}, bf16[2,2,48,896]{3,2,1,0:T(8,128)(2,1)S(1)}, u32[]{:S(2)}, u32[]{:S(2)}) %collective-permute-start.51) | collective-permute-done | bytes 344096 | tf_op jit(solution)/shard_map/ppermute | solution.py:793
  496.6 6.8 %collective-permute-done.49 = bf16[2,2,48,1024]{3,2,1,0:T(8,128)(2,1)S(1)} collective-permute-done((bf16[2,2,48,1024]{3,2,1,0:T(8,128)(2,1)S(1)}, bf16[2,2,48,1024]{3,2,1,0:T(8,128)(2,1)S(1)}, u32[]{:S(2)}, u32[]{:S(2)}) %collective-permute-start.49) | collective-permute-done | bytes 393248 | tf_op jit(solution)/shard_map/ppermute | solution.py:793
  503.6 22.4 %collective-permute-done.52 = bf16[2,2,2,48,896]{4,3,2,1,0:T(8,128)(2,1)S(1)} collective-permute-done((bf16[2,2,2,48,896]{4,3,2,1,0:T(8,128)(2,1)S(1)}, bf16[2,2,2,48,896]{4,3,2,1,0:T(8,128)(2,1)S(1)}, u32[]{:S(2)}, u32[]{:S(2)}) %collective-permute-start.52) | collective-permute-done | bytes 688160 | tf_op jit(solution)/shard_map/ppermute | solution.py:793
  526.1 7.7 %collective-permute-done.50 = bf16[2,2,2,48,1024]{4,3,1,0,2:T(8,128)(2,1)S(1)} collective-permute-done((bf16[2,2,2,48,1024]{4,3,1,0,2:T(8,128)(2,1)S(1)}, bf16[2,2,2,48,1024]{4,3,1,0,2:T(8,128)(2,1)S(1)}, u32[]{:S(2)}, u32[]{:S(2)}) %collective-permute-start.50) | collective-permute-done | bytes 786464 | tf_op jit(solution)/shard_map/ppermute | solution.py:793
  533.9 2.0 maximum_maximum_fusion.1
  536.0 4.0 reshape.373
  541.7 2.4 broadcast_select_fusion.1
  544.1 3.1 pad_maximum_fusion.1.packed_ref
  547.3 6.0 %unpack_sums.2 = (f32[768,2304]{1,0:T(8,128)}, f32[768,768]{1,0:T(8,128)}, f32[768,512]{1,0:T(8,128)}, f32[8,768]{1,0:T(8,128)}) custom-call(bf16[16,2,48,1920]{3,2,1,0:T(8,128)(2,1)} %pad_maximum_fusion.1.packed_ref), custom_call_target="tpu_custom_call" | custom-call | bytes 17694720 | tf_op jit(solution)/shard_map/unpack_sums/pallas_call | solution.py:672
  554.8 2.1 all-gather.5.cloned.1.call-done
  556.9 14.4 %unpack_sums.3 = (f32[512,1536]{1,0:T(8,128)}, f32[512,512]{1,0:T(8,128)}, f32[512,2048]{1,0:T(8,128)}, f32[2048,512]{1,0:T(8,128)}, f32[8,512]{1,0:T(8,128)}, /*index=5*/f32[768,3072]{1,0:T(8,128)}, f32[3072,768]{1,0:T(8,128)}) custom-call(bf16[16,2,16,15616]{3,2,1,0:T(8,128)(2,1)} %bitcast.286), custom_call_target="tpu_custom_call" | custom-call | bytes 47972352 | tf_op jit(solution)/shard_map/unpack_sums/pallas_call | solution.py:672
  (238 shorter events, 101.9 us)
Async XLA Ops:
  7.2 112.0 %all-gather.3.cloned.1.call-start = ((), (), s32[]{:S(2)}) async-start(), calls=%async_computation | async-start | bytes 10745856 | tf_op jit(solution)/shard_map/all_gather | solution.py:819
  12.2 544.8 %all-gather.5.cloned.1.call-start = ((), (), s32[]{:S(2)}) async-start(), calls=%async_computation.1 | async-start | bytes 16490496 | tf_op jit(solution)/shard_map/all_gather | solution.py:819
  12.2 16.1 %collective-permute-start.2 = (bf16[96,768]{1,0:T(8,128)(2,1)}, bf16[96,768]{1,0:T(8,128)(2,1)S(1)}, u32[]{:S(2)}, u32[]{:S(2)}) collective-permute-start(bf16[96,768]{1,0:T(8,128)(2,1)} %param.32), channel_id=1, source_target_pairs={{0,24},{1,25},{2,26},{3,27},{4,28},{5,29},{6,30},{7,31},{8,16},{9,... | collective-permute-start | bytes 442376 | tf_op jit(solution)/shard_map/ppermute | solution.py:793
  17.3 18.2 %collective-permute-start.3 = (bf16[96,768]{1,0:T(8,128)(2,1)}, bf16[96,768]{1,0:T(8,128)(2,1)S(1)}, u32[]{:S(2)}, u32[]{:S(2)}) collective-permute-start(bf16[96,768]{1,0:T(8,128)(2,1)} %param.32), channel_id=1, source_target_pairs={{0,16},{1,17},{2,18},{3,19},{4,20},{5,21},{6,22},{7,23},{8,24},{9,... | collective-permute-start | bytes 442376 | tf_op jit(solution)/shard_map/ppermute | solution.py:793
  17.3 18.2 %collective-permute-start.4 = (bf16[96,768]{1,0:T(8,128)(2,1)}, bf16[96,768]{1,0:T(8,128)(2,1)S(1)}, u32[]{:S(2)}, u32[]{:S(2)}) collective-permute-start(bf16[96,768]{1,0:T(8,128)(2,1)} %param.32), channel_id=1, source_target_pairs={{0,8},{1,9},{2,10},{3,11},{4,12},{5,13},{6,14},{7,15},{8,0},{9,1},... | collective-permute-start | bytes 442376 | tf_op jit(solution)/shard_map/ppermute | solution.py:793
  36.7 21.1 %collective-permute-start.10 = (bf16[16,6272]{1,0:T(8,128)(2,1)S(1)}, bf16[16,6272]{1,0:T(8,128)(2,1)S(1)}, u32[]{:S(2)}, u32[]{:S(2)}) collective-permute-start(bf16[16,6272]{1,0:T(8,128)(2,1)S(1)} %constant_dynamic-update-slice_fusion.5), channel_id=1, source_target_pairs={{0,16},{1,17},{2,18},{3,19},{4,20},{5,21},{6,22},{7,23},{8,24},{9,... | collective-permute-start | bytes 602120 | tf_op jit(solution)/shard_map/ppermute | solution.py:793
  36.8 21.0 %collective-permute-start.11 = (bf16[16,6272]{1,0:T(8,128)(2,1)S(1)}, bf16[16,6272]{1,0:T(8,128)(2,1)S(1)}, u32[]{:S(2)}, u32[]{:S(2)}) collective-permute-start(bf16[16,6272]{1,0:T(8,128)(2,1)S(1)} %constant_dynamic-update-slice_fusion.5), channel_id=1, source_target_pairs={{0,8},{1,9},{2,10},{3,11},{4,12},{5,13},{6,14},{7,15},{8,0},{9,1},... | collective-permute-start | bytes 602120 | tf_op jit(solution)/shard_map/ppermute | solution.py:793
  41.0 16.8 %collective-permute-start.9 = (bf16[16,6272]{1,0:T(8,128)(2,1)S(1)}, bf16[16,6272]{1,0:T(8,128)(2,1)S(1)}, u32[]{:S(2)}, u32[]{:S(2)}) collective-permute-start(bf16[16,6272]{1,0:T(8,128)(2,1)S(1)} %constant_dynamic-update-slice_fusion.5), channel_id=1, source_target_pairs={{0,24},{1,25},{2,26},{3,27},{4,28},{5,29},{6,30},{7,31},{8,16},{9,... | collective-permute-start | bytes 602120 | tf_op jit(solution)/shard_map/ppermute | solution.py:793
  41.1 16.8 %collective-permute-start.5 = (bf16[2,2,96,384]{3,2,1,0:T(8,128)(2,1)S(1)}, bf16[2,2,96,384]{3,2,1,0:T(8,128)(2,1)S(1)}, u32[]{:S(2)}, u32[]{:S(2)}) collective-permute-start(bf16[2,2,96,384]{3,2,1,0:T(8,128)(2,1)S(1)} %get-tuple-element.99), channel_id=1, source_target_pairs={{0,2},{1,3},{2,0},{3,1},{4,6},{5,7},{6,4},{7,5},{8,10},{9,11},{10,... | collective-permute-start | bytes 884744 | tf_op jit(solution)/shard_map/ppermute | solution.py:793
  42.8 15.2 %collective-permute-start.7 = (bf16[2,2,96,384]{3,2,1,0:T(8,128)(2,1)S(1)}, bf16[2,2,96,384]{3,2,1,0:T(8,128)(2,1)S(1)}, u32[]{:S(2)}, u32[]{:S(2)}) collective-permute-start(bf16[2,2,96,384]{3,2,1,0:T(8,128)(2,1)S(1)} %get-tuple-element.100), channel_id=1, source_target_pairs={{0,4},{1,5},{2,6},{3,7},{4,0},{5,1},{6,2},{7,3},{8,12},{9,13},{10,... | collective-permute-start | bytes 884744 | tf_op jit(solution)/shard_map/ppermute | solution.py:793
  58.1 13.3 %collective-permute-start.6 = (bf16[2,2,2,96,384]{4,3,1,0,2:T(8,128)(2,1)S(1)}, bf16[2,2,2,96,384]{4,3,1,0,2:T(8,128)(2,1)S(1)}, u32[]{:S(2)}, u32[]{:S(2)}) collective-permute-start(bf16[2,2,2,96,384]{4,3,1,0,2:T(8,128)(2,1)S(1)} %pad_maximum_fusion.18), channel_id=1, source_target_pairs={{0,4},{1,5},{2,6},{3,7},{4,0},{5,1},{6,2},{7,3},{8,12},{9,13},{10,... | collective-permute-start | bytes 1769480 | tf_op jit(solution)/shard_map/ppermute | solution.py:793
  59.8 11.8 %collective-permute-start.8 = (bf16[2,2,2,96,384]{4,3,2,1,0:T(8,128)(2,1)S(1)}, bf16[2,2,2,96,384]{4,3,2,1,0:T(8,128)(2,1)S(1)}, u32[]{:S(2)}, u32[]{:S(2)}) collective-permute-start(bf16[2,2,2,96,384]{4,3,2,1,0:T(8,128)(2,1)S(1)} %pad_maximum_fusion.19), channel_id=1, source_target_pairs={{0,2},{1,3},{2,0},{3,1},{4,6},{5,7},{6,4},{7,5},{8,10},{9,11},{10,... | collective-permute-start | bytes 1769480 | tf_op jit(solution)/shard_map/ppermute | solution.py:793
  73.4 16.4 %collective-permute-start.14 = (bf16[2,2,16,3072]{3,2,1,0:T(8,128)(2,1)S(1)}, bf16[2,2,16,3072]{3,2,1,0:T(8,128)(2,1)}, u32[]{:S(2)}, u32[]{:S(2)}) collective-permute-start(bf16[2,2,16,3072]{3,2,1,0:T(8,128)(2,1)S(1)} %slice.144), channel_id=1, source_target_pairs={{0,4},{1,5},{2,6},{3,7},{4,0},{5,1},{6,2},{7,3},{8,12},{9,13},{10,... | collective-permute-start | bytes 1179656 | tf_op jit(solution)/shard_map/ppermute | solution.py:793
  75.3 18.0 %collective-permute-start.13 = (bf16[2,2,16,3200]{3,2,1,0:T(8,128)(2,1)}, bf16[2,2,16,3200]{3,2,1,0:T(8,128)(2,1)S(1)}, u32[]{:S(2)}, u32[]{:S(2)}) collective-permute-start(bf16[2,2,16,3200]{3,2,1,0:T(8,128)(2,1)} %slice.143), channel_id=1, source_target_pairs={{0,2},{1,3},{2,0},{3,1},{4,6},{5,7},{6,4},{7,5},{8,10},{9,11},{10,... | collective-permute-start | bytes 1228808 | tf_op jit(solution)/shard_map/ppermute | solution.py:793
  77.1 17.5 %collective-permute-start.12 = (bf16[2,2,2,2,96,768]{5,4,3,2,1,0:T(8,128)(2,1)}, bf16[2,2,2,2,96,768]{5,4,3,2,1,0:T(8,128)(2,1)S(1)}, u32[]{:S(2)}, u32[]{:S(2)}) collective-permute-start(bf16[2,2,2,2,96,768]{5,4,3,2,1,0:T(8,128)(2,1)} %maximum_maximum_fusion.2), channel_id=1, source_target_pairs={{0,1},{1,0},{2,3},{3,2},{4,5},{5,4},{6,7},{7,6},{8,9},{9,8},{10,11... | collective-permute-start | bytes 7077896 | tf_op jit(solution)/shard_map/ppermute | solution.py:793
  119.2 27.6 %collective-permute-start.15 = (bf16[2,2,2,16,3200]{4,3,1,0,2:T(8,128)(2,1)S(1)}, bf16[2,2,2,16,3200]{4,3,1,0,2:T(8,128)(2,1)S(1)}, u32[]{:S(2)}, u32[]{:S(2)}) collective-permute-start(bf16[2,2,2,16,3200]{4,3,1,0,2:T(8,128)(2,1)S(1)} %copy-done.10), channel_id=1, source_target_pairs={{0,4},{1,5},{2,6},{3,7},{4,0},{5,1},{6,2},{7,3},{8,12},{9,13},{10,... | collective-permute-start | bytes 2457608 | tf_op jit(solution)/shard_map/ppermute | solution.py:793
  120.0 26.6 %collective-permute-start.16 = (bf16[2,2,2,16,3072]{4,3,2,1,0:T(8,128)(2,1)S(1)}, bf16[2,2,2,16,3072]{4,3,2,1,0:T(8,128)(2,1)S(1)}, u32[]{:S(2)}, u32[]{:S(2)}) collective-permute-start(bf16[2,2,2,16,3072]{4,3,2,1,0:T(8,128)(2,1)S(1)} %copy-done.11), channel_id=1, source_target_pairs={{0,2},{1,3},{2,0},{3,1},{4,6},{5,7},{6,4},{7,5},{8,10},{9,11},{10,... | collective-permute-start | bytes 2359304 | tf_op jit(solution)/shard_map/ppermute | solution.py:793
  149.8 15.1 %collective-permute-start.19 = (bf16[2,2,2,2,16,6272]{5,4,3,2,1,0:T(8,128)(2,1)}, bf16[2,2,2,2,16,6272]{5,4,3,2,1,0:T(8,128)(2,1)}, u32[]{:S(2)}, u32[]{:S(2)}) collective-permute-start(bf16[2,2,2,2,16,6272]{5,4,3,2,1,0:T(8,128)(2,1)} %maximum_maximum_fusion), channel_id=1, source_target_pairs={{0,1},{1,0},{2,3},{3,2},{4,5},{5,4},{6,7},{7,6},{8,9},{9,8},{10,11... | collective-permute-start | bytes 9633800 | tf_op jit(solution)/shard_map/ppermute | solution.py:793
  151.5 9.0 %collective-permute-start.17 = (bf16[2,128,512]{2,1,0:T(8,128)(2,1)}, bf16[2,128,512]{2,1,0:T(8,128)(2,1)}, u32[]{:S(2)}, u32[]{:S(2)}) collective-permute-start(bf16[2,128,512]{2,1,0:T(8,128)(2,1)} %dynamic-slice_bitcast_fusion.14), channel_id=1, source_target_pairs={{0,2},{1,3},{2,0},{3,1},{4,6},{5,7},{6,4},{7,5},{8,10},{9,11},{10,... | collective-permute-start | bytes 786440 | tf_op jit(solution)/shard_map/ppermute | solution.py:839
  272.4 11.9 %collective-permute-start.22 = (bf16[512,3200]{1,0:T(8,128)(2,1)}, bf16[512,3200]{1,0:T(8,128)(2,1)}, u32[]{:S(2)}, u32[]{:S(2)}) collective-permute-start(bf16[512,3200]{1,0:T(8,128)(2,1)} %get-tuple-element.123), channel_id=1, source_target_pairs={{0,1},{1,0},{2,3},{3,2},{4,5},{5,4},{6,7},{7,6},{8,9},{9,8},{10,11... | collective-permute-start | bytes 9830408 | tf_op jit(solution)/shard_map/ppermute | solution.py:705
  273.9 8.6 %collective-permute-start.21 = (bf16[2,128,512]{2,1,0:T(8,128)(2,1)}, bf16[2,128,512]{2,1,0:T(8,128)(2,1)S(1)}, u32[]{:S(2)}, u32[]{:S(2)}) collective-permute-start(bf16[2,128,512]{2,1,0:T(8,128)(2,1)} %dynamic-slice_bitcast_fusion.13), channel_id=1, source_target_pairs={{0,2},{1,3},{2,0},{3,1},{4,6},{5,7},{6,4},{7,5},{8,10},{9,11},{10,... | collective-permute-start | bytes 786440 | tf_op jit(solution)/shard_map/ppermute | solution.py:839
  287.6 22.3 %collective-permute-start.24 = (bf16[2,2,2,32,1664]{4,3,2,1,0:T(8,128)(2,1)S(1)}, bf16[2,2,2,32,1664]{4,3,2,1,0:T(8,128)(2,1)S(1)}, u32[]{:S(2)}, u32[]{:S(2)}) collective-permute-start(bf16[2,2,2,32,1664]{4,3,2,1,0:T(8,128)(2,1)S(1)} %dynamic-slice_bitcast_fusion.1), channel_id=1, source_target_pairs={{0,2},{1,3},{2,0},{3,1},{4,6},{5,7},{6,4},{7,5},{8,10},{9,11},{10,... | collective-permute-start | bytes 2555912 | tf_op jit(solution)/shard_map/ppermute | solution.py:749
  288.4 21.2 %collective-permute-start.23 = (bf16[2,2,2,32,1536]{4,3,1,0,2:T(8,128)(2,1)S(1)}, bf16[2,2,2,32,1536]{4,3,1,0,2:T(8,128)(2,1)S(1)}, u32[]{:S(2)}, u32[]{:S(2)}) collective-permute-start(bf16[2,2,2,32,1536]{4,3,1,0,2:T(8,128)(2,1)S(1)} %bitcast.325), channel_id=1, source_target_pairs={{0,4},{1,5},{2,6},{3,7},{4,0},{5,1},{6,2},{7,3},{8,12},{9,13},{10,... | collective-permute-start | bytes 2359304 | tf_op jit(solution)/shard_map/ppermute | solution.py:749
  310.2 18.9 %collective-permute-start.27 = (bf16[768,3072]{1,0:T(8,128)(2,1)}, bf16[768,3072]{1,0:T(8,128)(2,1)}, u32[]{:S(2)}, u32[]{:S(2)}) collective-permute-start(bf16[768,3072]{1,0:T(8,128)(2,1)} %get-tuple-element.144), channel_id=1, source_target_pairs={{0,1},{1,0},{2,3},{3,2},{4,5},{5,4},{6,7},{7,6},{8,9},{9,8},{10,11... | collective-permute-start | bytes 14155784 | tf_op jit(solution)/shard_map/ppermute | solution.py:705
  310.3 18.8 %collective-permute-start.26 = (bf16[2,2,32,1664]{3,2,1,0:T(8,128)(2,1)S(1)}, bf16[2,2,32,1664]{3,2,1,0:T(8,128)(2,1)S(1)}, u32[]{:S(2)}, u32[]{:S(2)}) collective-permute-start(bf16[2,2,32,1664]{3,2,1,0:T(8,128)(2,1)S(1)} %dynamic-slice_bitcast_fusion.6), channel_id=1, source_target_pairs={{0,4},{1,5},{2,6},{3,7},{4,0},{5,1},{6,2},{7,3},{8,12},{9,13},{10,... | collective-permute-start | bytes 1277960 | tf_op jit(solution)/shard_map/ppermute | solution.py:749
  310.8 18.4 %collective-permute-start.25 = (bf16[2,2,32,1536]{3,2,1,0:T(8,128)(2,1)S(1)}, bf16[2,2,32,1536]{3,2,1,0:T(8,128)(2,1)S(1)}, u32[]{:S(2)}, u32[]{:S(2)}) collective-permute-start(bf16[2,2,32,1536]{3,2,1,0:T(8,128)(2,1)S(1)} %dynamic-slice_bitcast_fusion.8), channel_id=1, source_target_pairs={{0,2},{1,3},{2,0},{3,1},{4,6},{5,7},{6,4},{7,5},{8,10},{9,11},{10,... | collective-permute-start | bytes 1179656 | tf_op jit(solution)/shard_map/ppermute | solution.py:749
  340.5 28.4 %collective-permute-start.33 = (bf16[2,2,2,48,1536]{4,3,2,1,0:T(8,128)(2,1)S(1)}, bf16[2,2,2,48,1536]{4,3,2,1,0:T(8,128)(2,1)S(1)}, u32[]{:S(2)}, u32[]{:S(2)}) collective-permute-start(bf16[2,2,2,48,1536]{4,3,2,1,0:T(8,128)(2,1)S(1)} %dynamic-slice_bitcast_fusion), channel_id=1, source_target_pairs={{0,2},{1,3},{2,0},{3,1},{4,6},{5,7},{6,4},{7,5},{8,10},{9,11},{10,... | collective-permute-start | bytes 3538952 | tf_op jit(solution)/shard_map/ppermute | solution.py:749
  341.3 28.1 %collective-permute-start.29 = (bf16[2,2,2,48,1536]{4,3,1,0,2:T(8,128)(2,1)S(1)}, bf16[2,2,2,48,1536]{4,3,1,0,2:T(8,128)(2,1)S(1)}, u32[]{:S(2)}, u32[]{:S(2)}) collective-permute-start(bf16[2,2,2,48,1536]{4,3,1,0,2:T(8,128)(2,1)S(1)} %bitcast.321), channel_id=1, source_target_pairs={{0,4},{1,5},{2,6},{3,7},{4,0},{5,1},{6,2},{7,3},{8,12},{9,13},{10,... | collective-permute-start | bytes 3538952 | tf_op jit(solution)/shard_map/ppermute | solution.py:749
  343.3 10.7 %collective-permute-start.30 = (bf16[32,3200]{1,0:T(8,128)(2,1)S(1)}, bf16[32,3200]{1,0:T(8,128)(2,1)S(1)}, u32[]{:S(2)}, u32[]{:S(2)}) collective-permute-start(bf16[32,3200]{1,0:T(8,128)(2,1)S(1)} %get-tuple-element.229), channel_id=1, source_target_pairs={{0,8},{1,9},{2,10},{3,11},{4,12},{5,13},{6,14},{7,15},{8,0},{9,1},... | collective-permute-start | bytes 614408 | tf_op jit(solution)/shard_map/ppermute | solution.py:749
  343.4 17.7 %collective-permute-start.31 = (bf16[32,3200]{1,0:T(8,128)(2,1)S(1)}, bf16[32,3200]{1,0:T(8,128)(2,1)S(1)}, u32[]{:S(2)}, u32[]{:S(2)}) collective-permute-start(bf16[32,3200]{1,0:T(8,128)(2,1)S(1)} %get-tuple-element.231), channel_id=1, source_target_pairs={{0,16},{1,17},{2,18},{3,19},{4,20},{5,21},{6,22},{7,23},{8,24},{9,... | collective-permute-start | bytes 614408 | tf_op jit(solution)/shard_map/ppermute | solution.py:749
  346.2 14.8 %collective-permute-start.32 = (bf16[32,3200]{1,0:T(8,128)(2,1)S(1)}, bf16[32,3200]{1,0:T(8,128)(2,1)S(1)}, u32[]{:S(2)}, u32[]{:S(2)}) collective-permute-start(bf16[32,3200]{1,0:T(8,128)(2,1)S(1)} %get-tuple-element.230), channel_id=1, source_target_pairs={{0,24},{1,25},{2,26},{3,27},{4,28},{5,29},{6,30},{7,31},{8,16},{9,... | collective-permute-start | bytes 614408 | tf_op jit(solution)/shard_map/ppermute | solution.py:749
  369.8 14.9 %collective-permute-start.34 = (bf16[2,2,48,1536]{3,2,1,0:T(8,128)(2,1)S(1)}, bf16[2,2,48,1536]{3,2,1,0:T(8,128)(2,1)S(1)}, u32[]{:S(2)}, u32[]{:S(2)}) collective-permute-start(bf16[2,2,48,1536]{3,2,1,0:T(8,128)(2,1)S(1)} %dynamic-slice_bitcast_fusion.4), channel_id=1, source_target_pairs={{0,2},{1,3},{2,0},{3,1},{4,6},{5,7},{6,4},{7,5},{8,10},{9,11},{10,... | collective-permute-start | bytes 1769480 | tf_op jit(solution)/shard_map/ppermute | solution.py:749
  371.2 14.4 %collective-permute-start.35 = (bf16[2,2,48,1536]{3,2,1,0:T(8,128)(2,1)S(1)}, bf16[2,2,48,1536]{3,2,1,0:T(8,128)(2,1)S(1)}, u32[]{:S(2)}, u32[]{:S(2)}) collective-permute-start(bf16[2,2,48,1536]{3,2,1,0:T(8,128)(2,1)S(1)} %dynamic-slice_bitcast_fusion.3), channel_id=1, source_target_pairs={{0,4},{1,5},{2,6},{3,7},{4,0},{5,1},{6,2},{7,3},{8,12},{9,13},{10,... | collective-permute-start | bytes 1769480 | tf_op jit(solution)/shard_map/ppermute | solution.py:749
  386.0 12.3 %collective-permute-start.37 = (bf16[48,3072]{1,0:T(8,128)(2,1)S(1)}, bf16[48,3072]{1,0:T(8,128)(2,1)S(1)}, u32[]{:S(2)}, u32[]{:S(2)}) collective-permute-start(bf16[48,3072]{1,0:T(8,128)(2,1)S(1)} %get-tuple-element.159), channel_id=1, source_target_pairs={{0,8},{1,9},{2,10},{3,11},{4,12},{5,13},{6,14},{7,15},{8,0},{9,1},... | collective-permute-start | bytes 884744 | tf_op jit(solution)/shard_map/ppermute | solution.py:749
  386.1 23.6 %collective-permute-start.38 = (bf16[48,3072]{1,0:T(8,128)(2,1)S(1)}, bf16[48,3072]{1,0:T(8,128)(2,1)S(1)}, u32[]{:S(2)}, u32[]{:S(2)}) collective-permute-start(bf16[48,3072]{1,0:T(8,128)(2,1)S(1)} %get-tuple-element.160), channel_id=1, source_target_pairs={{0,16},{1,17},{2,18},{3,19},{4,20},{5,21},{6,22},{7,23},{8,24},{9,... | collective-permute-start | bytes 884744 | tf_op jit(solution)/shard_map/ppermute | solution.py:749
  388.9 20.7 %collective-permute-start.39 = (bf16[48,3072]{1,0:T(8,128)(2,1)S(1)}, bf16[48,3072]{1,0:T(8,128)(2,1)S(1)}, u32[]{:S(2)}, u32[]{:S(2)}) collective-permute-start(bf16[48,3072]{1,0:T(8,128)(2,1)S(1)} %get-tuple-element.161), channel_id=1, source_target_pairs={{0,24},{1,25},{2,26},{3,27},{4,28},{5,29},{6,30},{7,31},{8,16},{9,... | collective-permute-start | bytes 884744 | tf_op jit(solution)/shard_map/ppermute | solution.py:749
  390.5 19.6 %collective-permute-start.40 = (bf16[2,2,2,48,1024]{4,3,2,1,0:T(8,128)(2,1)S(1)}, bf16[2,2,2,48,1024]{4,3,2,1,0:T(8,128)(2,1)S(1)}, u32[]{:S(2)}, u32[]{:S(2)}) collective-permute-start(bf16[2,2,2,48,1024]{4,3,2,1,0:T(8,128)(2,1)S(1)} %dynamic-slice_bitcast_fusion.2), channel_id=1, source_target_pairs={{0,2},{1,3},{2,0},{3,1},{4,6},{5,7},{6,4},{7,5},{8,10},{9,11},{10,... | collective-permute-start | bytes 2359304 | tf_op jit(solution)/shard_map/ppermute | solution.py:749
  391.4 18.4 %collective-permute-start.36 = (bf16[2,2,2,48,896]{4,3,1,0,2:T(8,128)(2,1)S(1)}, bf16[2,2,2,48,896]{4,3,1,0,2:T(8,128)(2,1)S(1)}, u32[]{:S(2)}, u32[]{:S(2)}) collective-permute-start(bf16[2,2,2,48,896]{4,3,1,0,2:T(8,128)(2,1)S(1)} %bitcast.326), channel_id=1, source_target_pairs={{0,4},{1,5},{2,6},{3,7},{4,0},{5,1},{6,2},{7,3},{8,12},{9,13},{10,... | collective-permute-start | bytes 2064392 | tf_op jit(solution)/shard_map/ppermute | solution.py:749
  420.3 17.0 %collective-permute-start.43 = (bf16[48,1920]{1,0:T(8,128)(2,1)S(1)}, bf16[48,1920]{1,0:T(8,128)(2,1)S(1)}, u32[]{:S(2)}, u32[]{:S(2)}) collective-permute-start(bf16[48,1920]{1,0:T(8,128)(2,1)S(1)} %get-tuple-element.244), channel_id=1, source_target_pairs={{0,8},{1,9},{2,10},{3,11},{4,12},{5,13},{6,14},{7,15},{8,0},{9,1},... | collective-permute-start | bytes 552968 | tf_op jit(solution)/shard_map/ppermute | solution.py:749
  425.4 25.0 %collective-permute-start.44 = (bf16[48,1920]{1,0:T(8,128)(2,1)S(1)}, bf16[48,1920]{1,0:T(8,128)(2,1)S(1)}, u32[]{:S(2)}, u32[]{:S(2)}) collective-permute-start(bf16[48,1920]{1,0:T(8,128)(2,1)S(1)} %get-tuple-element.246), channel_id=1, source_target_pairs={{0,16},{1,17},{2,18},{3,19},{4,20},{5,21},{6,22},{7,23},{8,24},{9,... | collective-permute-start | bytes 552968 | tf_op jit(solution)/shard_map/ppermute | solution.py:749
  426.3 24.1 %collective-permute-start.45 = (bf16[48,1920]{1,0:T(8,128)(2,1)S(1)}, bf16[48,1920]{1,0:T(8,128)(2,1)S(1)}, u32[]{:S(2)}, u32[]{:S(2)}) collective-permute-start(bf16[48,1920]{1,0:T(8,128)(2,1)S(1)} %get-tuple-element.245), channel_id=1, source_target_pairs={{0,24},{1,25},{2,26},{3,27},{4,28},{5,29},{6,30},{7,31},{8,16},{9,... | collective-permute-start | bytes 552968 | tf_op jit(solution)/shard_map/ppermute | solution.py:749
  450.5 9.6 %collective-permute-start.46 = (bf16[48,1920]{1,0:T(8,128)(2,1)S(1)}, bf16[48,1920]{1,0:T(8,128)(2,1)S(1)}, u32[]{:S(2)}, u32[]{:S(2)}) collective-permute-start(bf16[48,1920]{1,0:T(8,128)(2,1)S(1)} %fusion.20), channel_id=1, source_target_pairs={{0,24},{1,25},{2,26},{3,27},{4,28},{5,29},{6,30},{7,31},{8,16},{9,... | collective-permute-start | bytes 552968 | tf_op jit(solution)/shard_map/ppermute | solution.py:793
  453.1 33.2 %collective-permute-start.47 = (bf16[48,1920]{1,0:T(8,128)(2,1)S(1)}, bf16[48,1920]{1,0:T(8,128)(2,1)S(1)}, u32[]{:S(2)}, u32[]{:S(2)}) collective-permute-start(bf16[48,1920]{1,0:T(8,128)(2,1)S(1)} %fusion.20), channel_id=1, source_target_pairs={{0,16},{1,17},{2,18},{3,19},{4,20},{5,21},{6,22},{7,23},{8,24},{9,... | collective-permute-start | bytes 552968 | tf_op jit(solution)/shard_map/ppermute | solution.py:793
  455.7 30.6 %collective-permute-start.48 = (bf16[48,1920]{1,0:T(8,128)(2,1)S(1)}, bf16[48,1920]{1,0:T(8,128)(2,1)S(1)}, u32[]{:S(2)}, u32[]{:S(2)}) collective-permute-start(bf16[48,1920]{1,0:T(8,128)(2,1)S(1)} %fusion.20), channel_id=1, source_target_pairs={{0,8},{1,9},{2,10},{3,11},{4,12},{5,13},{6,14},{7,15},{8,0},{9,1},... | collective-permute-start | bytes 552968 | tf_op jit(solution)/shard_map/ppermute | solution.py:793
  486.6 9.8 %collective-permute-start.51 = (bf16[2,2,48,896]{3,2,1,0:T(8,128)(2,1)S(1)}, bf16[2,2,48,896]{3,2,1,0:T(8,128)(2,1)S(1)}, u32[]{:S(2)}, u32[]{:S(2)}) collective-permute-start(bf16[2,2,48,896]{3,2,1,0:T(8,128)(2,1)S(1)} %slice.156), channel_id=1, source_target_pairs={{0,4},{1,5},{2,6},{3,7},{4,0},{5,1},{6,2},{7,3},{8,12},{9,13},{10,... | collective-permute-start | bytes 1032200 | tf_op jit(solution)/shard_map/ppermute | solution.py:793
  488.4 14.9 %collective-permute-start.49 = (bf16[2,2,48,1024]{3,2,1,0:T(8,128)(2,1)S(1)}, bf16[2,2,48,1024]{3,2,1,0:T(8,128)(2,1)S(1)}, u32[]{:S(2)}, u32[]{:S(2)}) collective-permute-start(bf16[2,2,48,1024]{3,2,1,0:T(8,128)(2,1)S(1)} %slice.155), channel_id=1, source_target_pairs={{0,2},{1,3},{2,0},{3,1},{4,6},{5,7},{6,4},{7,5},{8,10},{9,11},{10,... | collective-permute-start | bytes 1179656 | tf_op jit(solution)/shard_map/ppermute | solution.py:793
  496.5 29.4 %collective-permute-start.52 = (bf16[2,2,2,48,896]{4,3,2,1,0:T(8,128)(2,1)S(1)}, bf16[2,2,2,48,896]{4,3,2,1,0:T(8,128)(2,1)S(1)}, u32[]{:S(2)}, u32[]{:S(2)}) collective-permute-start(bf16[2,2,2,48,896]{4,3,2,1,0:T(8,128)(2,1)S(1)} %pad_maximum_fusion.16), channel_id=1, source_target_pairs={{0,2},{1,3},{2,0},{3,1},{4,6},{5,7},{6,4},{7,5},{8,10},{9,11},{10,... | collective-permute-start | bytes 2064392 | tf_op jit(solution)/shard_map/ppermute | solution.py:793
  503.5 30.4 %collective-permute-start.50 = (bf16[2,2,2,48,1024]{4,3,1,0,2:T(8,128)(2,1)S(1)}, bf16[2,2,2,48,1024]{4,3,1,0,2:T(8,128)(2,1)S(1)}, u32[]{:S(2)}, u32[]{:S(2)}) collective-permute-start(bf16[2,2,2,48,1024]{4,3,1,0,2:T(8,128)(2,1)S(1)} %pad_maximum_fusion.13), channel_id=1, source_target_pairs={{0,4},{1,5},{2,6},{3,7},{4,0},{5,1},{6,2},{7,3},{8,12},{9,13},{10,... | collective-permute-start | bytes 2359304 | tf_op jit(solution)/shard_map/ppermute | solution.py:793
  (23 other events, 138.7 us)
Sparse Core Ops, SparseCore 0:
  12.3 106.8 all-gather.2
  411.4 145.4 all-gather.4

commit v7 on v6

--- a/solution.py
+++ b/solution.py
@@ -108,7 +108,7 @@
 
 def decoder_kernel(
     core_ref, rows_ref, idx_ref, cot_ref, pos_ref, mask_ref, small_ref, wqkv_ref, wo_ref, wu_ref, wd_ref,
-    out_ref, ret_ref, keep_ref, give_ref,
+    out_ref, own_ref, other_ref, keep_ref, give_ref,
     acc_qkv, acc_o, acc_u, acc_d, gvec_ref, vec_ref,
     x_s, qkv_s, p_s, o_s, a2_s, a2t_s, dzt_s, da_s, y_s, dqkv_s,
 ):
@@ -248,7 +248,16 @@
         dx_h = dx[h * cells : (h + 1) * cells, :]
         gvec_ref[4:5, :] += jnp.sum(unseen[h] * dx_h, axis=0, keepdims=True)
         place = place_of(h).astype(F32).T.astype(BF16)
-        ret_ref[h] = mm(place, dx_h.astype(BF16)).astype(BF16)
+        back = mm(place, dx_h.astype(BF16)).astype(BF16)
+        ours = core_ref[0] == lax.rem(step, 2)
+
+        @pl.when(ours)
+        def _(back=back, h=h):
+            own_ref[h] = back
+
+        @pl.when(jnp.logical_not(ours))
+        def _(back=back, h=h):
+            other_ref[h] = back
 
     @pl.when(step == last)
     def _():
@@ -298,13 +307,15 @@
         ],
         out_specs=[
             pl.BlockSpec((halves, cells, width), lambda i: (i, 0, 0)),
-            pl.BlockSpec((halves, slots, width), lambda i: (i, 0, 0)),
+            pl.BlockSpec((halves, slots, width), lambda i: (i // 2, 0, 0)),
+            pl.BlockSpec((halves, slots, width), lambda i: (i // 2, 0, 0)),
             whole(width, half_wide),
             whole(width, half_wide),
         ],
         out_shape=[
             jax.ShapeDtypeStruct((n_half, cells, width), BF16),
-            jax.ShapeDtypeStruct((n_half, slots, width), BF16),
+            jax.ShapeDtypeStruct((n_half // 2, slots, width), BF16),
+            jax.ShapeDtypeStruct((n_half // 2, slots, width), BF16),
             jax.ShapeDtypeStruct((width, half_wide), BF16),
             jax.ShapeDtypeStruct((width, half_wide), BF16),
         ],
@@ -379,7 +390,9 @@
 
 
 def enc_feed_kernel(
-    x2_ref, vec_ref, wu_ref, wd_ref, proj_ref, sent_ref, enc_ref, h_ref, gp_ref, a2_s, y_s
+    half_ref, x2_ref, vec_ref, wu_ref, wd_ref, proj_ref,
+    own_ref, other_ref, enc_ref, h_ref, gp_ref,
+    a2_s, y_s,
 ):
     step = pl.program_id(0)
 
@@ -400,7 +413,11 @@
     def _():
         encoded = y_s[...].astype(BF16)
         enc_ref[...] = encoded
-        sent_ref[...] = mm(encoded, proj_ref[...]).astype(BF16)
+        sent = mm(encoded, proj_ref[...]).astype(BF16)
+        rows = own_ref.shape[0]
+        first = half_ref[0] == 0
+        own_ref[...] = jnp.where(first, sent[:rows], sent[rows:])
+        other_ref[...] = jnp.where(first, sent[rows:], sent[:rows])
 
 
 def enc_feed_back_kernel(
@@ -572,15 +589,16 @@
     return whole_call(enc_attend_kernel, (x, mask, small, qkv, out), outs, [], "enc_attend", 10**10)
 
 
-def enc_feed(x2, vecs, blocks, wd):
+def enc_feed(half, x2, vecs, blocks, wd):
     m, width = x2.shape
     ff, chunk = wd.shape[0], FEED_CHUNK
     _, _, up, proj, _ = blocks
     across, down = lambda i: (0, i), lambda i: (i, 0)
     kept = ((m, ff), BF16, (m, chunk), across)
-    outs = [((m, proj[1][1]), BF16), ((m, width), BF16), kept, kept]
+    sent = ((m // 2, proj[1][1]), BF16)
+    outs = [sent, sent, ((m, width), BF16), kept, kept]
     scratch = [((m, width), BF16), ((m, width), F32)]
-    args = (x2, vecs, up, (wd, (chunk, width), down), proj)
+    args = (half, x2, vecs, up, (wd, (chunk, width), down), proj)
     return whole_call(enc_feed_kernel, args, outs, scratch, "enc_feed", 14 * 10**9, ff // chunk)
 
 
@@ -839,20 +857,13 @@
     return lax.ppermute(array, "band", [(i, i ^ bit) for i in range(4)])
 
 
-def owners_to_bands(array):
+def owners_to_bands(own, other):
     band = lax.axis_index("band")
     half, side = band // 2, band % 2
-    own = lax.dynamic_index_in_dim(array, half, 0, keepdims=False)
-    got = swap_band(lax.dynamic_index_in_dim(array, 1 - half, 0, keepdims=False), 2)
+    got = swap_band(other, 2)
     pair = jnp.stack([jnp.where(half == 0, own, got), jnp.where(half == 0, got, own)])
     other = swap_band(pair, 1)
     return jnp.stack([jnp.where(side == 0, pair, other), jnp.where(side == 0, other, pair)], axis=1)
-
-
-def join_bands(array):
-    side = lax.axis_index("band") % 2
-    own = lax.dynamic_index_in_dim(array, side, 1, keepdims=False)
-    return own + swap_band(lax.dynamic_index_in_dim(array, 1 - side, 1, keepdims=False), 1)
 
 
 def bands_to_owners(pair):
@@ -912,7 +923,10 @@
     valid_rows = slot_ids[None, :] < visible_count[:, None]
     valid_mask = valid_rows.astype(F32)[:, None, :]
     cell_number = jnp.where(valid_rows, keep_index, -1).reshape(2, half_clips, slot_total)
-    cell_number = owners_to_bands(cell_number).reshape(-1, slot_total)
+    half = lax.axis_index("band") // 2
+    own = lax.dynamic_index_in_dim(cell_number, half, 0, keepdims=False)
+    other = lax.dynamic_index_in_dim(cell_number, 1 - half, 0, keepdims=False)
+    cell_number = owners_to_bands(own, other).reshape(-1, slot_total)
 
     dec_small = columns_of([dec_gain1, dec_shift1, dec_gain2, dec_shift2, mask_token])
     dec_tall = blocks_beside(dec_down, dec_out.shape[0])
@@ -939,14 +953,17 @@
 
     blocks = enc_blocks(enc_pack, enc_wide, enc_ff, dec_wide)
     qkv, probs, mixed, middle, vecs = enc_attend(visible, valid_mask, blocks)
-    sent_rows, encoded, hidden, slope = enc_feed(middle, vecs, blocks, whole_down)
-    sent_rows, gives = together(sent_rows, dec_run.offers())
+    own, other, encoded, hidden, slope = enc_feed(
+        half.reshape(1), middle, vecs, blocks, whole_down
+    )
+    own, other, gives = together(own, other, dec_run.offers())
     dec_run.deliver(gives)
     dec_pack = dec_run.finish().reshape(-1, dec_pack.shape[1])
     dec_end = 4 * dec_wide + dec_ff
     dec_whole_down = blocks_below(dec_pack[:, dec_end : dec_end + dec_ff], total, dec_wide)
     dec_whole_down = dec_whole_down.reshape(-1, dec_wide)
-    arrived_rows = owners_to_bands(sent_rows.reshape(2, half_clips, slot_total, dec_wide))
+    parted = (half_clips, slot_total, dec_wide)
+    arrived_rows = owners_to_bands(own.reshape(parted), other.reshape(parted))
     half_total = 4 * half_clips
 
     cell_count = TIME * band_height
@@ -964,7 +981,7 @@
 
     cells_in = WINDOW * WINDOW
     allowed = (query // cells_in == key // cells_in) & (label(query) == label(key))
-    decoded, returning, keep, give = decoder_block(
+    decoded, own, other, keep, give = decoder_block(
         core,
         arrived_rows.reshape(half_total, slot_total, dec_wide),
         arrived_index,
@@ -976,7 +993,7 @@
     )
     decoded_out = decoded.reshape(cotangent.shape)
 
-    returning = join_bands(returning.reshape(2, 2, half_clips, slot_total, dec_wide))
+    returning = (own + swap_band(other, 1)).reshape(2, half_clips, slot_total, dec_wide)
     returning, keep, give = together(returning, keep, give)
     dec_run = RunningSum(keep, give, total)
     grad_sent = bands_to_owners(returning).reshape(-1, dec_wide)

time: 587 us -> 584 us (level)
  no operation moved by 1% of the time
where the time goes in v7:
time: 584 us; the launch traced here: 577 us
  waiting for transfers between devices  233 us (40%)
  Pallas kernels  179 us (31%)
  starting transfers between devices  65.7 us (11%)
  other arithmetic  52.7 us (9%)
  local copies, waits for them, and re-layouts  32.1 us (5%)
  between operations  15.3 us (3%)
    ppermute x45, waiting for transfers between devices, deliver(): lax.ppermute(give, AXES, partner_pairs(self.total, mask))  198 us
    pallas_call x1, Pallas kernels, decoder_block(): pl.pallas_call(decoder_kernel, grid=(n_half // halves,), in_specs=[pl.Blo...  96.1 us
    pallas_call x4, Pallas kernels, whole_call(): pl.pallas_call(kernel, grid=(steps,), in_specs=specs, out_specs=out_specs...  62 us
    ppermute x45, starting transfers between devices, deliver(): lax.ppermute(give, AXES, partner_pairs(self.total, mask))  61.6 us
    all_gather x2, waiting for transfers between devices, gather_rows(): return lax.all_gather(shard, AXES, axis=0, tiled=True)  22.9 us
    pallas_call x2, Pallas kernels, unpack_sums(): pl.pallas_call(functools.partial(unpack_kernel, sections, pieces, talls,...  20.5 us
    another operation x28, other arithmetic, deliver(): held = jnp.stack(parts, axis=at)  16.2 us
    unnamed x49, local copies, waits for them, and re-layouts  15 us
  transfers between devices with their start and end apart: 56, of which 31 were waited for; matrix products, arithmetic and copies ran while one was open for 10% of the time, Pallas kernels for 12%

profile of v7, /device:TPU:0, one launch (start us, length us, event | category | flops | bytes accessed | tf_op | source)
XLA Modules:
  0.0 577.0 jit_solution(14245955171857208853)
XLA Ops:
  12.2 5.1 collective-permute-start.2
  28.3 7.2 %collective-permute-done.3 = bf16[96,768]{1,0:T(8,128)(2,1)S(1)} collective-permute-done((bf16[96,768]{1,0:T(8,128)(2,1)}, bf16[96,768]{1,0:T(8,128)(2,1)S(1)}, u32[]{:S(2)}, u32[]{:S(2)}) %collective-permute-start.3) | collective-permute-done | bytes 147488 | tf_op jit(solution)/shard_map/ppermute | solution.py:811
  36.8 4.3 collective-permute-start.11
  44.6 13.2 %collective-permute-done.10 = bf16[16,6272]{1,0:T(8,128)(2,1)S(1)} collective-permute-done((bf16[16,6272]{1,0:T(8,128)(2,1)S(1)}, bf16[16,6272]{1,0:T(8,128)(2,1)S(1)}, u32[]{:S(2)}, u32[]{:S(2)}) %collective-permute-start.10) | collective-permute-done | bytes 200736 | tf_op jit(solution)/shard_map/ppermute | solution.py:811
  59.8 2.8 collective-permute-start.8
  63.4 8.0 %collective-permute-done.6 = bf16[2,2,2,96,384]{4,3,1,0,2:T(8,128)(2,1)S(1)} collective-permute-done((bf16[2,2,2,96,384]{4,3,1,0,2:T(8,128)(2,1)S(1)}, bf16[2,2,2,96,384]{4,3,1,0,2:T(8,128)(2,1)S(1)}, u32[]{:S(2)}, u32[]{:S(2)}) %collective-permute-start.6) | collective-permute-done | bytes 589856 | tf_op jit(solution)/shard_map/ppermute | solution.py:811
  77.1 12.7 %collective-permute-done.14 = bf16[2,2,16,3072]{3,2,1,0:T(8,128)(2,1)} collective-permute-done((bf16[2,2,16,3072]{3,2,1,0:T(8,128)(2,1)S(1)}, bf16[2,2,16,3072]{3,2,1,0:T(8,128)(2,1)}, u32[]{:S(2)}, u32[]{:S(2)}) %collective-permute-start.14) | collective-permute-done | bytes 393248 | tf_op jit(solution)/shard_map/ppermute | solution.py:811
  95.8 2.6 pad_maximum_fusion.2
  98.4 20.8 %all-gather.3.cloned.1.call-done.small_ref.wqkv_ref.wo_ref.wu_ref.proj_ref = bf16[768,6784]{1,0:T(8,128)(2,1)} async-done(((bf16[24,6784]{1,0:T(8,128)(2,1)}), bf16[768,6784]{1,0:T(8,128)(2,1)}) %all-gather.3.cloned.1.call-update) | async-done | bytes 10420240 | tf_op jit(solution)/shard_map/all_gather | solution.py:837
  121.3 10.0 %enc_attend.1 = (bf16[512,2304]{1,0:T(8,128)(2,1)}, bf16[512,1536]{1,0:T(8,128)(2,1)}, bf16[512,768]{1,0:T(8,128)(2,1)}, f32[512,768]{1,0:T(8,128)}, f32[8,768]{1,0:T(8,128)}) custom-call(bf16[4,128,768]{2,1,0:T(8,128)(2,1)} %x_ref.3, f32[4,1,128]{2,1,0:T(1,128)} %compare_convert_fusion.mask_ref, ...), custom_call_target="tpu_custom_call" | custom-call | flops 10000000000 | bytes 16777216 | tf_op jit(solution)/shard_map/enc_attend/pallas_call | solution.py:552
  131.3 15.4 %enc_feed.1 = (bf16[256,512]{1,0:T(8,128)(2,1)}, bf16[256,512]{1,0:T(8,128)(2,1)}, bf16[512,768]{1,0:T(8,128)(2,1)}, bf16[512,3072]{1,0:T(8,128)(2,1)}, bf16[512,3072]{1,0:T(8,128)(2,1)}) custom-call(s32[1]{0:T(128)} %bitcast.1.half_ref, f32[512,768]{1,0:T(8,128)} %get-tuple-element.111.x2_ref, f32[8,768]{1,0:T(8,128)} %get-tuple-element.112.vec_ref, ...), custom_call_target="tpu_custom_call" | custom-call | flops 14000000000 | bytes 16777216 | tf_op jit(solution)/shard_map/enc_feed/pallas_call | solution.py:552
  152.4 4.0 reshape.375.cot_ref
  163.3 2.5 select_bitcast_fusion.1
  169.9 96.1 %decoder_block.1 = (bf16[8,256,512]{2,1,0:T(8,128)(2,1)}, bf16[4,128,512]{2,1,0:T(8,128)(2,1)}, bf16[4,128,512]{2,1,0:T(8,128)(2,1)}, bf16[512,3200]{1,0:T(8,128)(2,1)}, bf16[512,3200]{1,0:T(8,128)(2,1)}) custom-call(s32[1]{0:T(128)} %bitcast.core_ref, bf16[8,128,512]{2,1,0:T(8,128)(2,1)} %bitcast.313, s32[8,1,128]{2,1,0:T(1,128)} %bitcast.321, ...), custom_call_target="tpu_custom_call" | custom-call | flops 77309411328 | bytes 41943040 | tf_op jit(solution)/shard_map/decoder_block/pallas_call | solution.py:292
  266.2 1.9 collective-permute-done.20
  271.6 7.8 %collective-permute-done.21 = bf16[2,128,512]{2,1,0:T(8,128)(2,1)S(1)} collective-permute-done((bf16[2,128,512]{2,1,0:T(8,128)(2,1)}, bf16[2,128,512]{2,1,0:T(8,128)(2,1)S(1)}, u32[]{:S(2)}, u32[]{:S(2)}) %collective-permute-start.21) | collective-permute-done | bytes 262176 | tf_op jit(solution)/shard_map/ppermute | solution.py:857
  281.3 2.7 add_convert_fusion.1
  287.1 19.6 %enc_feed_back.1 = (bf16[768,512]{1,0:T(8,128)(2,1)}, bf16[768,3072]{1,0:T(8,128)(2,1)}, bf16[768,3072]{1,0:T(8,128)(2,1)}, f32[512,768]{1,0:T(8,128)}, f32[8,768]{1,0:T(8,128)}) custom-call(s32[1]{0:T(128)} %bitcast.core_ref, bf16[512,512]{1,0:T(8,128)(2,1)} %bitcast.316, bf16[512,768]{1,0:T(8,128)(2,1)} %get-tuple-element.131.enc_ref, ...), custom_call_target="tpu_custom_call" | custom-call | flops 17999998976 | bytes 16777216 | tf_op jit(solution)/shard_map/enc_feed_back/pallas_call | solution.py:552
  309.1 17.0 %enc_attend_back.1 = (bf16[768,1920]{1,0:T(8,128)(2,1)}, bf16[768,1920]{1,0:T(8,128)(2,1)}, bf16[4,128,768]{2,1,0:T(8,128)(2,1)}) custom-call(s32[1]{0:T(128)} %bitcast.core_ref, f32[512,768]{1,0:T(8,128)} %get-tuple-element.139.dx2_ref, bf16[512,768]{1,0:T(8,128)(2,1)} %get-tuple-element.140.o_ref, bf16[512,2304]{1,0:T(8,128)(2,1)} %get-tuple-element.141.qkv_ref, ...), custom_call_target="tpu_custom_call" | custom-call | flops 14000000000 | bytes 16777216 | tf_op jit(solution)/shard_map/enc_attend_back/pallas_call | solution.py:552
  326.2 5.7 add_convert_fusion
  334.6 2.6 add_convert_fusion.2
  340.4 2.8 collective-permute-start.31
  345.0 5.9 %collective-permute-done.30 = bf16[32,3200]{1,0:T(8,128)(2,1)S(1)} collective-permute-done((bf16[32,3200]{1,0:T(8,128)(2,1)S(1)}, bf16[32,3200]{1,0:T(8,128)(2,1)S(1)}, u32[]{:S(2)}, u32[]{:S(2)}) %collective-permute-start.30) | collective-permute-done | bytes 204832 | tf_op jit(solution)/shard_map/ppermute | solution.py:767
  350.9 7.1 %collective-permute-done.31 = bf16[32,3200]{1,0:T(8,128)(2,1)S(1)} collective-permute-done((bf16[32,3200]{1,0:T(8,128)(2,1)S(1)}, bf16[32,3200]{1,0:T(8,128)(2,1)S(1)}, u32[]{:S(2)}, u32[]{:S(2)}) %collective-permute-start.31) | collective-permute-done | bytes 204832 | tf_op jit(solution)/shard_map/ppermute | solution.py:767
  358.2 7.7 %collective-permute-done.33 = bf16[2,2,2,48,1536]{4,3,2,1,0:T(8,128)(2,1)S(1)} collective-permute-done((bf16[2,2,2,48,1536]{4,3,2,1,0:T(8,128)(2,1)S(1)}, bf16[2,2,2,48,1536]{4,3,2,1,0:T(8,128)(2,1)S(1)}, u32[]{:S(2)}, u32[]{:S(2)}) %collective-permute-start.33) | collective-permute-done | bytes 1179680 | tf_op jit(solution)/shard_map/ppermute | solution.py:767
  370.0 11.7 %collective-permute-done.34 = bf16[2,2,48,1536]{3,2,1,0:T(8,128)(2,1)S(1)} collective-permute-done((bf16[2,2,48,1536]{3,2,1,0:T(8,128)(2,1)S(1)}, bf16[2,2,48,1536]{3,2,1,0:T(8,128)(2,1)S(1)}, u32[]{:S(2)}, u32[]{:S(2)}) %collective-permute-start.34) | collective-permute-done | bytes 589856 | tf_op jit(solution)/shard_map/ppermute | solution.py:767
  383.1 2.8 collective-permute-start.38
  390.2 5.2 collective-permute-done.37
  395.3 11.3 %collective-permute-done.38 = bf16[48,3072]{1,0:T(8,128)(2,1)S(1)} collective-permute-done((bf16[48,3072]{1,0:T(8,128)(2,1)S(1)}, bf16[48,3072]{1,0:T(8,128)(2,1)S(1)}, u32[]{:S(2)}, u32[]{:S(2)}) %collective-permute-start.38) | collective-permute-done | bytes 294944 | tf_op jit(solution)/shard_map/ppermute | solution.py:767
  411.0 4.6 collective-permute-done.41
  417.3 5.1 collective-permute-start.43
  424.8 9.4 %collective-permute-done.43 = bf16[48,1920]{1,0:T(8,128)(2,1)S(1)} collective-permute-done((bf16[48,1920]{1,0:T(8,128)(2,1)S(1)}, bf16[48,1920]{1,0:T(8,128)(2,1)S(1)}, u32[]{:S(2)}, u32[]{:S(2)}) %collective-permute-start.43) | collective-permute-done | bytes 184352 | tf_op jit(solution)/shard_map/ppermute | solution.py:767
  434.2 13.2 %collective-permute-done.44 = bf16[48,1920]{1,0:T(8,128)(2,1)S(1)} collective-permute-done((bf16[48,1920]{1,0:T(8,128)(2,1)S(1)}, bf16[48,1920]{1,0:T(8,128)(2,1)S(1)}, u32[]{:S(2)}, u32[]{:S(2)}) %collective-permute-start.44) | collective-permute-done | bytes 184352 | tf_op jit(solution)/shard_map/ppermute | solution.py:767
  447.5 2.6 collective-permute-start.46
  450.1 2.5 collective-permute-start.47
  452.6 4.5 collective-permute-done.46
  457.1 26.2 %collective-permute-done.47 = bf16[48,1920]{1,0:T(8,128)(2,1)S(1)} collective-permute-done((bf16[48,1920]{1,0:T(8,128)(2,1)S(1)}, bf16[48,1920]{1,0:T(8,128)(2,1)S(1)}, u32[]{:S(2)}, u32[]{:S(2)}) %collective-permute-start.47) | collective-permute-done | bytes 184352 | tf_op jit(solution)/shard_map/ppermute | solution.py:811
  485.8 7.5 %collective-permute-done.51 = bf16[2,2,48,896]{3,2,1,0:T(8,128)(2,1)S(1)} collective-permute-done((bf16[2,2,48,896]{3,2,1,0:T(8,128)(2,1)S(1)}, bf16[2,2,48,896]{3,2,1,0:T(8,128)(2,1)S(1)}, u32[]{:S(2)}, u32[]{:S(2)}) %collective-permute-start.51) | collective-permute-done | bytes 344096 | tf_op jit(solution)/shard_map/ppermute | solution.py:811
  493.6 6.8 %collective-permute-done.49 = bf16[2,2,48,1024]{3,2,1,0:T(8,128)(2,1)S(1)} collective-permute-done((bf16[2,2,48,1024]{3,2,1,0:T(8,128)(2,1)S(1)}, bf16[2,2,48,1024]{3,2,1,0:T(8,128)(2,1)S(1)}, u32[]{:S(2)}, u32[]{:S(2)}) %collective-permute-start.49) | collective-permute-done | bytes 393248 | tf_op jit(solution)/shard_map/ppermute | solution.py:811
  500.6 22.4 %collective-permute-done.52 = bf16[2,2,2,48,896]{4,3,2,1,0:T(8,128)(2,1)S(1)} collective-permute-done((bf16[2,2,2,48,896]{4,3,2,1,0:T(8,128)(2,1)S(1)}, bf16[2,2,2,48,896]{4,3,2,1,0:T(8,128)(2,1)S(1)}, u32[]{:S(2)}, u32[]{:S(2)}) %collective-permute-start.52) | collective-permute-done | bytes 688160 | tf_op jit(solution)/shard_map/ppermute | solution.py:811
  523.1 7.8 %collective-permute-done.50 = bf16[2,2,2,48,1024]{4,3,1,0,2:T(8,128)(2,1)S(1)} collective-permute-done((bf16[2,2,2,48,1024]{4,3,1,0,2:T(8,128)(2,1)S(1)}, bf16[2,2,2,48,1024]{4,3,1,0,2:T(8,128)(2,1)S(1)}, u32[]{:S(2)}, u32[]{:S(2)}) %collective-permute-start.50) | collective-permute-done | bytes 786464 | tf_op jit(solution)/shard_map/ppermute | solution.py:811
  530.9 2.0 maximum_maximum_fusion.1
  533.0 4.0 reshape.381
  538.7 2.4 broadcast_select_fusion.1
  541.1 3.1 pad_maximum_fusion.1.packed_ref
  544.3 6.0 %unpack_sums.2 = (f32[768,2304]{1,0:T(8,128)}, f32[768,768]{1,0:T(8,128)}, f32[768,512]{1,0:T(8,128)}, f32[8,768]{1,0:T(8,128)}) custom-call(bf16[16,2,48,1920]{3,2,1,0:T(8,128)(2,1)} %pad_maximum_fusion.1.packed_ref), custom_call_target="tpu_custom_call" | custom-call | bytes 17694720 | tf_op jit(solution)/shard_map/unpack_sums/pallas_call | solution.py:690
  551.8 2.1 all-gather.5.cloned.1.call-done
  553.9 14.4 %unpack_sums.3 = (f32[512,1536]{1,0:T(8,128)}, f32[512,512]{1,0:T(8,128)}, f32[512,2048]{1,0:T(8,128)}, f32[2048,512]{1,0:T(8,128)}, f32[8,512]{1,0:T(8,128)}, /*index=5*/f32[768,3072]{1,0:T(8,128)}, f32[3072,768]{1,0:T(8,128)}) custom-call(bf16[16,2,16,15616]{3,2,1,0:T(8,128)(2,1)} %bitcast.275), custom_call_target="tpu_custom_call" | custom-call | bytes 47972352 | tf_op jit(solution)/shard_map/unpack_sums/pallas_call | solution.py:690
  (236 shorter events, 98.5 us)
Async XLA Ops:
  7.2 112.0 %all-gather.3.cloned.1.call-start = ((), (), s32[]{:S(2)}) async-start(), calls=%async_computation | async-start | bytes 10745856 | tf_op jit(solution)/shard_map/all_gather | solution.py:837
  12.2 541.8 %all-gather.5.cloned.1.call-start = ((), (), s32[]{:S(2)}) async-start(), calls=%async_computation.1 | async-start | bytes 16490496 | tf_op jit(solution)/shard_map/all_gather | solution.py:837
  12.2 16.1 %collective-permute-start.2 = (bf16[96,768]{1,0:T(8,128)(2,1)}, bf16[96,768]{1,0:T(8,128)(2,1)S(1)}, u32[]{:S(2)}, u32[]{:S(2)}) collective-permute-start(bf16[96,768]{1,0:T(8,128)(2,1)} %param.32), channel_id=1, source_target_pairs={{0,24},{1,25},{2,26},{3,27},{4,28},{5,29},{6,30},{7,31},{8,16},{9,... | collective-permute-start | bytes 442376 | tf_op jit(solution)/shard_map/ppermute | solution.py:811
  17.3 18.2 %collective-permute-start.3 = (bf16[96,768]{1,0:T(8,128)(2,1)}, bf16[96,768]{1,0:T(8,128)(2,1)S(1)}, u32[]{:S(2)}, u32[]{:S(2)}) collective-permute-start(bf16[96,768]{1,0:T(8,128)(2,1)} %param.32), channel_id=1, source_target_pairs={{0,16},{1,17},{2,18},{3,19},{4,20},{5,21},{6,22},{7,23},{8,24},{9,... | collective-permute-start | bytes 442376 | tf_op jit(solution)/shard_map/ppermute | solution.py:811
  17.3 18.2 %collective-permute-start.4 = (bf16[96,768]{1,0:T(8,128)(2,1)}, bf16[96,768]{1,0:T(8,128)(2,1)S(1)}, u32[]{:S(2)}, u32[]{:S(2)}) collective-permute-start(bf16[96,768]{1,0:T(8,128)(2,1)} %param.32), channel_id=1, source_target_pairs={{0,8},{1,9},{2,10},{3,11},{4,12},{5,13},{6,14},{7,15},{8,0},{9,1},... | collective-permute-start | bytes 442376 | tf_op jit(solution)/shard_map/ppermute | solution.py:811
  36.7 21.1 %collective-permute-start.10 = (bf16[16,6272]{1,0:T(8,128)(2,1)S(1)}, bf16[16,6272]{1,0:T(8,128)(2,1)S(1)}, u32[]{:S(2)}, u32[]{:S(2)}) collective-permute-start(bf16[16,6272]{1,0:T(8,128)(2,1)S(1)} %constant_dynamic-update-slice_fusion.5), channel_id=1, source_target_pairs={{0,16},{1,17},{2,18},{3,19},{4,20},{5,21},{6,22},{7,23},{8,24},{9,... | collective-permute-start | bytes 602120 | tf_op jit(solution)/shard_map/ppermute | solution.py:811
  36.8 21.0 %collective-permute-start.11 = (bf16[16,6272]{1,0:T(8,128)(2,1)S(1)}, bf16[16,6272]{1,0:T(8,128)(2,1)S(1)}, u32[]{:S(2)}, u32[]{:S(2)}) collective-permute-start(bf16[16,6272]{1,0:T(8,128)(2,1)S(1)} %constant_dynamic-update-slice_fusion.5), channel_id=1, source_target_pairs={{0,8},{1,9},{2,10},{3,11},{4,12},{5,13},{6,14},{7,15},{8,0},{9,1},... | collective-permute-start | bytes 602120 | tf_op jit(solution)/shard_map/ppermute | solution.py:811
  41.0 16.8 %collective-permute-start.9 = (bf16[16,6272]{1,0:T(8,128)(2,1)S(1)}, bf16[16,6272]{1,0:T(8,128)(2,1)S(1)}, u32[]{:S(2)}, u32[]{:S(2)}) collective-permute-start(bf16[16,6272]{1,0:T(8,128)(2,1)S(1)} %constant_dynamic-update-slice_fusion.5), channel_id=1, source_target_pairs={{0,24},{1,25},{2,26},{3,27},{4,28},{5,29},{6,30},{7,31},{8,16},{9,... | collective-permute-start | bytes 602120 | tf_op jit(solution)/shard_map/ppermute | solution.py:811
  41.1 16.8 %collective-permute-start.5 = (bf16[2,2,96,384]{3,2,1,0:T(8,128)(2,1)S(1)}, bf16[2,2,96,384]{3,2,1,0:T(8,128)(2,1)S(1)}, u32[]{:S(2)}, u32[]{:S(2)}) collective-permute-start(bf16[2,2,96,384]{3,2,1,0:T(8,128)(2,1)S(1)} %get-tuple-element.102), channel_id=1, source_target_pairs={{0,2},{1,3},{2,0},{3,1},{4,6},{5,7},{6,4},{7,5},{8,10},{9,11},{10,... | collective-permute-start | bytes 884744 | tf_op jit(solution)/shard_map/ppermute | solution.py:811
  42.8 15.2 %collective-permute-start.7 = (bf16[2,2,96,384]{3,2,1,0:T(8,128)(2,1)S(1)}, bf16[2,2,96,384]{3,2,1,0:T(8,128)(2,1)S(1)}, u32[]{:S(2)}, u32[]{:S(2)}) collective-permute-start(bf16[2,2,96,384]{3,2,1,0:T(8,128)(2,1)S(1)} %get-tuple-element.103), channel_id=1, source_target_pairs={{0,4},{1,5},{2,6},{3,7},{4,0},{5,1},{6,2},{7,3},{8,12},{9,13},{10,... | collective-permute-start | bytes 884744 | tf_op jit(solution)/shard_map/ppermute | solution.py:811
  58.1 13.3 %collective-permute-start.6 = (bf16[2,2,2,96,384]{4,3,1,0,2:T(8,128)(2,1)S(1)}, bf16[2,2,2,96,384]{4,3,1,0,2:T(8,128)(2,1)S(1)}, u32[]{:S(2)}, u32[]{:S(2)}) collective-permute-start(bf16[2,2,2,96,384]{4,3,1,0,2:T(8,128)(2,1)S(1)} %pad_maximum_fusion.18), channel_id=1, source_target_pairs={{0,4},{1,5},{2,6},{3,7},{4,0},{5,1},{6,2},{7,3},{8,12},{9,13},{10,... | collective-permute-start | bytes 1769480 | tf_op jit(solution)/shard_map/ppermute | solution.py:811
  59.8 11.8 %collective-permute-start.8 = (bf16[2,2,2,96,384]{4,3,2,1,0:T(8,128)(2,1)S(1)}, bf16[2,2,2,96,384]{4,3,2,1,0:T(8,128)(2,1)S(1)}, u32[]{:S(2)}, u32[]{:S(2)}) collective-permute-start(bf16[2,2,2,96,384]{4,3,2,1,0:T(8,128)(2,1)S(1)} %pad_maximum_fusion.19), channel_id=1, source_target_pairs={{0,2},{1,3},{2,0},{3,1},{4,6},{5,7},{6,4},{7,5},{8,10},{9,11},{10,... | collective-permute-start | bytes 1769480 | tf_op jit(solution)/shard_map/ppermute | solution.py:811
  73.4 16.4 %collective-permute-start.14 = (bf16[2,2,16,3072]{3,2,1,0:T(8,128)(2,1)S(1)}, bf16[2,2,16,3072]{3,2,1,0:T(8,128)(2,1)}, u32[]{:S(2)}, u32[]{:S(2)}) collective-permute-start(bf16[2,2,16,3072]{3,2,1,0:T(8,128)(2,1)S(1)} %slice.144), channel_id=1, source_target_pairs={{0,4},{1,5},{2,6},{3,7},{4,0},{5,1},{6,2},{7,3},{8,12},{9,13},{10,... | collective-permute-start | bytes 1179656 | tf_op jit(solution)/shard_map/ppermute | solution.py:811
  75.3 18.0 %collective-permute-start.13 = (bf16[2,2,16,3200]{3,2,1,0:T(8,128)(2,1)}, bf16[2,2,16,3200]{3,2,1,0:T(8,128)(2,1)S(1)}, u32[]{:S(2)}, u32[]{:S(2)}) collective-permute-start(bf16[2,2,16,3200]{3,2,1,0:T(8,128)(2,1)} %slice.143), channel_id=1, source_target_pairs={{0,2},{1,3},{2,0},{3,1},{4,6},{5,7},{6,4},{7,5},{8,10},{9,11},{10,... | collective-permute-start | bytes 1228808 | tf_op jit(solution)/shard_map/ppermute | solution.py:811
  77.1 17.5 %collective-permute-start.12 = (bf16[2,2,2,2,96,768]{5,4,3,2,1,0:T(8,128)(2,1)}, bf16[2,2,2,2,96,768]{5,4,3,2,1,0:T(8,128)(2,1)S(1)}, u32[]{:S(2)}, u32[]{:S(2)}) collective-permute-start(bf16[2,2,2,2,96,768]{5,4,3,2,1,0:T(8,128)(2,1)} %maximum_maximum_fusion.2), channel_id=1, source_target_pairs={{0,1},{1,0},{2,3},{3,2},{4,5},{5,4},{6,7},{7,6},{8,9},{9,8},{10,11... | collective-permute-start | bytes 7077896 | tf_op jit(solution)/shard_map/ppermute | solution.py:811
  119.2 27.7 %collective-permute-start.15 = (bf16[2,2,2,16,3200]{4,3,1,0,2:T(8,128)(2,1)S(1)}, bf16[2,2,2,16,3200]{4,3,1,0,2:T(8,128)(2,1)S(1)}, u32[]{:S(2)}, u32[]{:S(2)}) collective-permute-start(bf16[2,2,2,16,3200]{4,3,1,0,2:T(8,128)(2,1)S(1)} %copy-done.10), channel_id=1, source_target_pairs={{0,4},{1,5},{2,6},{3,7},{4,0},{5,1},{6,2},{7,3},{8,12},{9,13},{10,... | collective-permute-start | bytes 2457608 | tf_op jit(solution)/shard_map/ppermute | solution.py:811
  120.0 26.7 %collective-permute-start.16 = (bf16[2,2,2,16,3072]{4,3,2,1,0:T(8,128)(2,1)S(1)}, bf16[2,2,2,16,3072]{4,3,2,1,0:T(8,128)(2,1)S(1)}, u32[]{:S(2)}, u32[]{:S(2)}) collective-permute-start(bf16[2,2,2,16,3072]{4,3,2,1,0:T(8,128)(2,1)S(1)} %copy-done.11), channel_id=1, source_target_pairs={{0,2},{1,3},{2,0},{3,1},{4,6},{5,7},{6,4},{7,5},{8,10},{9,11},{10,... | collective-permute-start | bytes 2359304 | tf_op jit(solution)/shard_map/ppermute | solution.py:811
  149.8 13.5 %collective-permute-start.19 = (bf16[2,2,2,2,16,6272]{5,4,3,2,1,0:T(8,128)(2,1)}, bf16[2,2,2,2,16,6272]{5,4,3,2,1,0:T(8,128)(2,1)}, u32[]{:S(2)}, u32[]{:S(2)}) collective-permute-start(bf16[2,2,2,2,16,6272]{5,4,3,2,1,0:T(8,128)(2,1)} %maximum_maximum_fusion), channel_id=1, source_target_pairs={{0,1},{1,0},{2,3},{3,2},{4,5},{5,4},{6,7},{7,6},{8,9},{9,8},{10,11... | collective-permute-start | bytes 9633800 | tf_op jit(solution)/shard_map/ppermute | solution.py:811
  149.9 9.1 %collective-permute-start.17 = (bf16[2,128,512]{2,1,0:T(8,128)(2,1)}, bf16[2,128,512]{2,1,0:T(8,128)(2,1)}, u32[]{:S(2)}, u32[]{:S(2)}) collective-permute-start(bf16[2,128,512]{2,1,0:T(8,128)(2,1)} %bitcast.55), channel_id=1, source_target_pairs={{0,2},{1,3},{2,0},{3,1},{4,6},{5,7},{6,4},{7,5},{8,10},{9,11},{10,... | collective-permute-start | bytes 786440 | tf_op jit(solution)/shard_map/ppermute | solution.py:857
  269.4 12.0 %collective-permute-start.22 = (bf16[512,3200]{1,0:T(8,128)(2,1)}, bf16[512,3200]{1,0:T(8,128)(2,1)}, u32[]{:S(2)}, u32[]{:S(2)}) collective-permute-start(bf16[512,3200]{1,0:T(8,128)(2,1)} %get-tuple-element.129), channel_id=1, source_target_pairs={{0,1},{1,0},{2,3},{3,2},{4,5},{5,4},{6,7},{7,6},{8,9},{9,8},{10,11... | collective-permute-start | bytes 9830408 | tf_op jit(solution)/shard_map/ppermute | solution.py:723
  270.9 8.6 %collective-permute-start.21 = (bf16[2,128,512]{2,1,0:T(8,128)(2,1)}, bf16[2,128,512]{2,1,0:T(8,128)(2,1)S(1)}, u32[]{:S(2)}, u32[]{:S(2)}) collective-permute-start(bf16[2,128,512]{2,1,0:T(8,128)(2,1)} %dynamic-slice_bitcast_fusion.12), channel_id=1, source_target_pairs={{0,2},{1,3},{2,0},{3,1},{4,6},{5,7},{6,4},{7,5},{8,10},{9,11},{10,... | collective-permute-start | bytes 786440 | tf_op jit(solution)/shard_map/ppermute | solution.py:857
  284.6 22.3 %collective-permute-start.24 = (bf16[2,2,2,32,1664]{4,3,2,1,0:T(8,128)(2,1)S(1)}, bf16[2,2,2,32,1664]{4,3,2,1,0:T(8,128)(2,1)S(1)}, u32[]{:S(2)}, u32[]{:S(2)}) collective-permute-start(bf16[2,2,2,32,1664]{4,3,2,1,0:T(8,128)(2,1)S(1)} %dynamic-slice_bitcast_fusion.1), channel_id=1, source_target_pairs={{0,2},{1,3},{2,0},{3,1},{4,6},{5,7},{6,4},{7,5},{8,10},{9,11},{10,... | collective-permute-start | bytes 2555912 | tf_op jit(solution)/shard_map/ppermute | solution.py:767
  285.4 21.2 %collective-permute-start.23 = (bf16[2,2,2,32,1536]{4,3,1,0,2:T(8,128)(2,1)S(1)}, bf16[2,2,2,32,1536]{4,3,1,0,2:T(8,128)(2,1)S(1)}, u32[]{:S(2)}, u32[]{:S(2)}) collective-permute-start(bf16[2,2,2,32,1536]{4,3,1,0,2:T(8,128)(2,1)S(1)} %bitcast.314), channel_id=1, source_target_pairs={{0,4},{1,5},{2,6},{3,7},{4,0},{5,1},{6,2},{7,3},{8,12},{9,13},{10,... | collective-permute-start | bytes 2359304 | tf_op jit(solution)/shard_map/ppermute | solution.py:767
  307.2 18.9 %collective-permute-start.27 = (bf16[768,3072]{1,0:T(8,128)(2,1)}, bf16[768,3072]{1,0:T(8,128)(2,1)}, u32[]{:S(2)}, u32[]{:S(2)}) collective-permute-start(bf16[768,3072]{1,0:T(8,128)(2,1)} %get-tuple-element.150), channel_id=1, source_target_pairs={{0,1},{1,0},{2,3},{3,2},{4,5},{5,4},{6,7},{7,6},{8,9},{9,8},{10,11... | collective-permute-start | bytes 14155784 | tf_op jit(solution)/shard_map/ppermute | solution.py:723
  307.3 18.8 %collective-permute-start.26 = (bf16[2,2,32,1664]{3,2,1,0:T(8,128)(2,1)S(1)}, bf16[2,2,32,1664]{3,2,1,0:T(8,128)(2,1)S(1)}, u32[]{:S(2)}, u32[]{:S(2)}) collective-permute-start(bf16[2,2,32,1664]{3,2,1,0:T(8,128)(2,1)S(1)} %dynamic-slice_bitcast_fusion.5), channel_id=1, source_target_pairs={{0,4},{1,5},{2,6},{3,7},{4,0},{5,1},{6,2},{7,3},{8,12},{9,13},{10,... | collective-permute-start | bytes 1277960 | tf_op jit(solution)/shard_map/ppermute | solution.py:767
  307.8 18.3 %collective-permute-start.25 = (bf16[2,2,32,1536]{3,2,1,0:T(8,128)(2,1)S(1)}, bf16[2,2,32,1536]{3,2,1,0:T(8,128)(2,1)S(1)}, u32[]{:S(2)}, u32[]{:S(2)}) collective-permute-start(bf16[2,2,32,1536]{3,2,1,0:T(8,128)(2,1)S(1)} %dynamic-slice_bitcast_fusion.7), channel_id=1, source_target_pairs={{0,2},{1,3},{2,0},{3,1},{4,6},{5,7},{6,4},{7,5},{8,10},{9,11},{10,... | collective-permute-start | bytes 1179656 | tf_op jit(solution)/shard_map/ppermute | solution.py:767
  337.5 28.4 %collective-permute-start.33 = (bf16[2,2,2,48,1536]{4,3,2,1,0:T(8,128)(2,1)S(1)}, bf16[2,2,2,48,1536]{4,3,2,1,0:T(8,128)(2,1)S(1)}, u32[]{:S(2)}, u32[]{:S(2)}) collective-permute-start(bf16[2,2,2,48,1536]{4,3,2,1,0:T(8,128)(2,1)S(1)} %dynamic-slice_bitcast_fusion), channel_id=1, source_target_pairs={{0,2},{1,3},{2,0},{3,1},{4,6},{5,7},{6,4},{7,5},{8,10},{9,11},{10,... | collective-permute-start | bytes 3538952 | tf_op jit(solution)/shard_map/ppermute | solution.py:767
  338.3 28.1 %collective-permute-start.29 = (bf16[2,2,2,48,1536]{4,3,1,0,2:T(8,128)(2,1)S(1)}, bf16[2,2,2,48,1536]{4,3,1,0,2:T(8,128)(2,1)S(1)}, u32[]{:S(2)}, u32[]{:S(2)}) collective-permute-start(bf16[2,2,2,48,1536]{4,3,1,0,2:T(8,128)(2,1)S(1)} %bitcast.312), channel_id=1, source_target_pairs={{0,4},{1,5},{2,6},{3,7},{4,0},{5,1},{6,2},{7,3},{8,12},{9,13},{10,... | collective-permute-start | bytes 3538952 | tf_op jit(solution)/shard_map/ppermute | solution.py:767
  340.3 10.7 %collective-permute-start.30 = (bf16[32,3200]{1,0:T(8,128)(2,1)S(1)}, bf16[32,3200]{1,0:T(8,128)(2,1)S(1)}, u32[]{:S(2)}, u32[]{:S(2)}) collective-permute-start(bf16[32,3200]{1,0:T(8,128)(2,1)S(1)} %get-tuple-element.235), channel_id=1, source_target_pairs={{0,8},{1,9},{2,10},{3,11},{4,12},{5,13},{6,14},{7,15},{8,0},{9,1},... | collective-permute-start | bytes 614408 | tf_op jit(solution)/shard_map/ppermute | solution.py:767
  340.4 17.7 %collective-permute-start.31 = (bf16[32,3200]{1,0:T(8,128)(2,1)S(1)}, bf16[32,3200]{1,0:T(8,128)(2,1)S(1)}, u32[]{:S(2)}, u32[]{:S(2)}) collective-permute-start(bf16[32,3200]{1,0:T(8,128)(2,1)S(1)} %get-tuple-element.237), channel_id=1, source_target_pairs={{0,16},{1,17},{2,18},{3,19},{4,20},{5,21},{6,22},{7,23},{8,24},{9,... | collective-permute-start | bytes 614408 | tf_op jit(solution)/shard_map/ppermute | solution.py:767
  343.2 14.9 %collective-permute-start.32 = (bf16[32,3200]{1,0:T(8,128)(2,1)S(1)}, bf16[32,3200]{1,0:T(8,128)(2,1)S(1)}, u32[]{:S(2)}, u32[]{:S(2)}) collective-permute-start(bf16[32,3200]{1,0:T(8,128)(2,1)S(1)} %get-tuple-element.236), channel_id=1, source_target_pairs={{0,24},{1,25},{2,26},{3,27},{4,28},{5,29},{6,30},{7,31},{8,16},{9,... | collective-permute-start | bytes 614408 | tf_op jit(solution)/shard_map/ppermute | solution.py:767
  366.8 14.9 %collective-permute-start.34 = (bf16[2,2,48,1536]{3,2,1,0:T(8,128)(2,1)S(1)}, bf16[2,2,48,1536]{3,2,1,0:T(8,128)(2,1)S(1)}, u32[]{:S(2)}, u32[]{:S(2)}) collective-permute-start(bf16[2,2,48,1536]{3,2,1,0:T(8,128)(2,1)S(1)} %dynamic-slice_bitcast_fusion.4), channel_id=1, source_target_pairs={{0,2},{1,3},{2,0},{3,1},{4,6},{5,7},{6,4},{7,5},{8,10},{9,11},{10,... | collective-permute-start | bytes 1769480 | tf_op jit(solution)/shard_map/ppermute | solution.py:767
  368.2 14.4 %collective-permute-start.35 = (bf16[2,2,48,1536]{3,2,1,0:T(8,128)(2,1)S(1)}, bf16[2,2,48,1536]{3,2,1,0:T(8,128)(2,1)S(1)}, u32[]{:S(2)}, u32[]{:S(2)}) collective-permute-start(bf16[2,2,48,1536]{3,2,1,0:T(8,128)(2,1)S(1)} %dynamic-slice_bitcast_fusion.3), channel_id=1, source_target_pairs={{0,4},{1,5},{2,6},{3,7},{4,0},{5,1},{6,2},{7,3},{8,12},{9,13},{10,... | collective-permute-start | bytes 1769480 | tf_op jit(solution)/shard_map/ppermute | solution.py:767
  383.0 12.3 %collective-permute-start.37 = (bf16[48,3072]{1,0:T(8,128)(2,1)S(1)}, bf16[48,3072]{1,0:T(8,128)(2,1)S(1)}, u32[]{:S(2)}, u32[]{:S(2)}) collective-permute-start(bf16[48,3072]{1,0:T(8,128)(2,1)S(1)} %get-tuple-element.165), channel_id=1, source_target_pairs={{0,8},{1,9},{2,10},{3,11},{4,12},{5,13},{6,14},{7,15},{8,0},{9,1},... | collective-permute-start | bytes 884744 | tf_op jit(solution)/shard_map/ppermute | solution.py:767
  383.1 23.6 %collective-permute-start.38 = (bf16[48,3072]{1,0:T(8,128)(2,1)S(1)}, bf16[48,3072]{1,0:T(8,128)(2,1)S(1)}, u32[]{:S(2)}, u32[]{:S(2)}) collective-permute-start(bf16[48,3072]{1,0:T(8,128)(2,1)S(1)} %get-tuple-element.166), channel_id=1, source_target_pairs={{0,16},{1,17},{2,18},{3,19},{4,20},{5,21},{6,22},{7,23},{8,24},{9,... | collective-permute-start | bytes 884744 | tf_op jit(solution)/shard_map/ppermute | solution.py:767
  385.9 20.7 %collective-permute-start.39 = (bf16[48,3072]{1,0:T(8,128)(2,1)S(1)}, bf16[48,3072]{1,0:T(8,128)(2,1)S(1)}, u32[]{:S(2)}, u32[]{:S(2)}) collective-permute-start(bf16[48,3072]{1,0:T(8,128)(2,1)S(1)} %get-tuple-element.167), channel_id=1, source_target_pairs={{0,24},{1,25},{2,26},{3,27},{4,28},{5,29},{6,30},{7,31},{8,16},{9,... | collective-permute-start | bytes 884744 | tf_op jit(solution)/shard_map/ppermute | solution.py:767
  387.5 19.6 %collective-permute-start.40 = (bf16[2,2,2,48,1024]{4,3,2,1,0:T(8,128)(2,1)S(1)}, bf16[2,2,2,48,1024]{4,3,2,1,0:T(8,128)(2,1)S(1)}, u32[]{:S(2)}, u32[]{:S(2)}) collective-permute-start(bf16[2,2,2,48,1024]{4,3,2,1,0:T(8,128)(2,1)S(1)} %dynamic-slice_bitcast_fusion.2), channel_id=1, source_target_pairs={{0,2},{1,3},{2,0},{3,1},{4,6},{5,7},{6,4},{7,5},{8,10},{9,11},{10,... | collective-permute-start | bytes 2359304 | tf_op jit(solution)/shard_map/ppermute | solution.py:767
  388.4 18.4 %collective-permute-start.36 = (bf16[2,2,2,48,896]{4,3,1,0,2:T(8,128)(2,1)S(1)}, bf16[2,2,2,48,896]{4,3,1,0,2:T(8,128)(2,1)S(1)}, u32[]{:S(2)}, u32[]{:S(2)}) collective-permute-start(bf16[2,2,2,48,896]{4,3,1,0,2:T(8,128)(2,1)S(1)} %bitcast.315), channel_id=1, source_target_pairs={{0,4},{1,5},{2,6},{3,7},{4,0},{5,1},{6,2},{7,3},{8,12},{9,13},{10,... | collective-permute-start | bytes 2064392 | tf_op jit(solution)/shard_map/ppermute | solution.py:767
  417.3 16.9 %collective-permute-start.43 = (bf16[48,1920]{1,0:T(8,128)(2,1)S(1)}, bf16[48,1920]{1,0:T(8,128)(2,1)S(1)}, u32[]{:S(2)}, u32[]{:S(2)}) collective-permute-start(bf16[48,1920]{1,0:T(8,128)(2,1)S(1)} %get-tuple-element.248), channel_id=1, source_target_pairs={{0,8},{1,9},{2,10},{3,11},{4,12},{5,13},{6,14},{7,15},{8,0},{9,1},... | collective-permute-start | bytes 552968 | tf_op jit(solution)/shard_map/ppermute | solution.py:767
  422.4 25.0 %collective-permute-start.44 = (bf16[48,1920]{1,0:T(8,128)(2,1)S(1)}, bf16[48,1920]{1,0:T(8,128)(2,1)S(1)}, u32[]{:S(2)}, u32[]{:S(2)}) collective-permute-start(bf16[48,1920]{1,0:T(8,128)(2,1)S(1)} %get-tuple-element.250), channel_id=1, source_target_pairs={{0,16},{1,17},{2,18},{3,19},{4,20},{5,21},{6,22},{7,23},{8,24},{9,... | collective-permute-start | bytes 552968 | tf_op jit(solution)/shard_map/ppermute | solution.py:767
  423.3 24.1 %collective-permute-start.45 = (bf16[48,1920]{1,0:T(8,128)(2,1)S(1)}, bf16[48,1920]{1,0:T(8,128)(2,1)S(1)}, u32[]{:S(2)}, u32[]{:S(2)}) collective-permute-start(bf16[48,1920]{1,0:T(8,128)(2,1)S(1)} %get-tuple-element.249), channel_id=1, source_target_pairs={{0,24},{1,25},{2,26},{3,27},{4,28},{5,29},{6,30},{7,31},{8,16},{9,... | collective-permute-start | bytes 552968 | tf_op jit(solution)/shard_map/ppermute | solution.py:767
  447.5 9.6 %collective-permute-start.46 = (bf16[48,1920]{1,0:T(8,128)(2,1)S(1)}, bf16[48,1920]{1,0:T(8,128)(2,1)S(1)}, u32[]{:S(2)}, u32[]{:S(2)}) collective-permute-start(bf16[48,1920]{1,0:T(8,128)(2,1)S(1)} %fusion.20), channel_id=1, source_target_pairs={{0,24},{1,25},{2,26},{3,27},{4,28},{5,29},{6,30},{7,31},{8,16},{9,... | collective-permute-start | bytes 552968 | tf_op jit(solution)/shard_map/ppermute | solution.py:811
  450.1 33.2 %collective-permute-start.47 = (bf16[48,1920]{1,0:T(8,128)(2,1)S(1)}, bf16[48,1920]{1,0:T(8,128)(2,1)S(1)}, u32[]{:S(2)}, u32[]{:S(2)}) collective-permute-start(bf16[48,1920]{1,0:T(8,128)(2,1)S(1)} %fusion.20), channel_id=1, source_target_pairs={{0,16},{1,17},{2,18},{3,19},{4,20},{5,21},{6,22},{7,23},{8,24},{9,... | collective-permute-start | bytes 552968 | tf_op jit(solution)/shard_map/ppermute | solution.py:811
  452.6 30.6 %collective-permute-start.48 = (bf16[48,1920]{1,0:T(8,128)(2,1)S(1)}, bf16[48,1920]{1,0:T(8,128)(2,1)S(1)}, u32[]{:S(2)}, u32[]{:S(2)}) collective-permute-start(bf16[48,1920]{1,0:T(8,128)(2,1)S(1)} %fusion.20), channel_id=1, source_target_pairs={{0,8},{1,9},{2,10},{3,11},{4,12},{5,13},{6,14},{7,15},{8,0},{9,1},... | collective-permute-start | bytes 552968 | tf_op jit(solution)/shard_map/ppermute | solution.py:811
  483.6 9.8 %collective-permute-start.51 = (bf16[2,2,48,896]{3,2,1,0:T(8,128)(2,1)S(1)}, bf16[2,2,48,896]{3,2,1,0:T(8,128)(2,1)S(1)}, u32[]{:S(2)}, u32[]{:S(2)}) collective-permute-start(bf16[2,2,48,896]{3,2,1,0:T(8,128)(2,1)S(1)} %slice.156), channel_id=1, source_target_pairs={{0,4},{1,5},{2,6},{3,7},{4,0},{5,1},{6,2},{7,3},{8,12},{9,13},{10,... | collective-permute-start | bytes 1032200 | tf_op jit(solution)/shard_map/ppermute | solution.py:811
  485.4 14.9 %collective-permute-start.49 = (bf16[2,2,48,1024]{3,2,1,0:T(8,128)(2,1)S(1)}, bf16[2,2,48,1024]{3,2,1,0:T(8,128)(2,1)S(1)}, u32[]{:S(2)}, u32[]{:S(2)}) collective-permute-start(bf16[2,2,48,1024]{3,2,1,0:T(8,128)(2,1)S(1)} %slice.155), channel_id=1, source_target_pairs={{0,2},{1,3},{2,0},{3,1},{4,6},{5,7},{6,4},{7,5},{8,10},{9,11},{10,... | collective-permute-start | bytes 1179656 | tf_op jit(solution)/shard_map/ppermute | solution.py:811
  493.5 29.4 %collective-permute-start.52 = (bf16[2,2,2,48,896]{4,3,2,1,0:T(8,128)(2,1)S(1)}, bf16[2,2,2,48,896]{4,3,2,1,0:T(8,128)(2,1)S(1)}, u32[]{:S(2)}, u32[]{:S(2)}) collective-permute-start(bf16[2,2,2,48,896]{4,3,2,1,0:T(8,128)(2,1)S(1)} %pad_maximum_fusion.16), channel_id=1, source_target_pairs={{0,2},{1,3},{2,0},{3,1},{4,6},{5,7},{6,4},{7,5},{8,10},{9,11},{10,... | collective-permute-start | bytes 2064392 | tf_op jit(solution)/shard_map/ppermute | solution.py:811
  500.5 30.4 %collective-permute-start.50 = (bf16[2,2,2,48,1024]{4,3,1,0,2:T(8,128)(2,1)S(1)}, bf16[2,2,2,48,1024]{4,3,1,0,2:T(8,128)(2,1)S(1)}, u32[]{:S(2)}, u32[]{:S(2)}) collective-permute-start(bf16[2,2,2,48,1024]{4,3,1,0,2:T(8,128)(2,1)S(1)} %pad_maximum_fusion.13), channel_id=1, source_target_pairs={{0,4},{1,5},{2,6},{3,7},{4,0},{5,1},{6,2},{7,3},{8,12},{9,13},{10,... | collective-permute-start | bytes 2359304 | tf_op jit(solution)/shard_map/ppermute | solution.py:811
  (23 other events, 138.5 us)
Sparse Core Ops, SparseCore 0:
  12.3 106.8 all-gather.2
  408.4 145.4 all-gather.4

commit v8 on v7

--- a/solution.py
+++ b/solution.py
@@ -124,7 +124,7 @@
     blocks = m_rows // block
     scale = head_dim ** (-0.5)
     ff = wu_ref.shape[1]
-    chunk = 512
+    chunk = 1024
 
     @pl.when(step == 0)
     def _():
@@ -206,9 +206,9 @@
         h = (u * cdf).astype(BF16)
         du = ((cdf + bump) * dh).astype(BF16)
         y_s[...] += mm(h, wd_ref[at, :])
+        da_s[...] += mm_t(du, wu_ref[:, at])
         acc_d[:, at] += mm(dzt_s[...], h)
         acc_u[:, at] += mm(a2t_s[...], du)
-        da_s[...] += mm_t(du, wu_ref[:, at])
 
     out_ref[...] = y_s[...].reshape(halves, cells, width).astype(BF16)
     da2 = da_s[...]
@@ -528,7 +528,7 @@
     by_core(core_ref, fill, keep_ref, give_ref)
 
 
-FEED_CHUNK = 512
+FEED_CHUNK = 768
 
 
 def whole_call(kernel, args, outs, scratch, name, flops, steps=1):

time: 584 us -> 577 us (0.988)
  Pallas kernels: 179 us -> 173 us
where the time goes in v8:
time: 577 us; the launch traced here: 571 us
  waiting for transfers between devices  232 us (40%)
  Pallas kernels  173 us (30%)
  starting transfers between devices  65.7 us (11%)
  other arithmetic  52.7 us (9%)
  local copies, waits for them, and re-layouts  32.1 us (6%)
  between operations  15.3 us (3%)
    ppermute x45, waiting for transfers between devices, deliver(): lax.ppermute(give, AXES, partner_pairs(self.total, mask))  197 us
    pallas_call x1, Pallas kernels, decoder_block(): pl.pallas_call(decoder_kernel, grid=(n_half // halves,), in_specs=[pl.Blo...  90.7 us
    ppermute x45, starting transfers between devices, deliver(): lax.ppermute(give, AXES, partner_pairs(self.total, mask))  61.7 us
    pallas_call x4, Pallas kernels, whole_call(): pl.pallas_call(kernel, grid=(steps,), in_specs=specs, out_specs=out_specs...  61.4 us
    all_gather x2, waiting for transfers between devices, gather_rows(): return lax.all_gather(shard, AXES, axis=0, tiled=True)  23 us
    pallas_call x2, Pallas kernels, unpack_sums(): pl.pallas_call(functools.partial(unpack_kernel, sections, pieces, talls,...  20.7 us
    another operation x28, other arithmetic, deliver(): held = jnp.stack(parts, axis=at)  16.2 us
    unnamed x49, local copies, waits for them, and re-layouts  15 us
  transfers between devices with their start and end apart: 56, of which 31 were waited for; matrix products, arithmetic and copies ran while one was open for 10% of the time, Pallas kernels for 12%

profile of v8, /device:TPU:0, one launch (start us, length us, event | category | flops | bytes accessed | tf_op | source)
XLA Modules:
  0.0 571.0 jit_solution(16174459061346424265)
XLA Ops:
  12.2 5.1 collective-permute-start.2
  28.3 7.2 %collective-permute-done.3 = bf16[96,768]{1,0:T(8,128)(2,1)S(1)} collective-permute-done((bf16[96,768]{1,0:T(8,128)(2,1)}, bf16[96,768]{1,0:T(8,128)(2,1)S(1)}, u32[]{:S(2)}, u32[]{:S(2)}) %collective-permute-start.3) | collective-permute-done | bytes 147488 | tf_op jit(solution)/shard_map/ppermute | solution.py:811
  36.8 4.3 collective-permute-start.11
  44.6 13.2 %collective-permute-done.10 = bf16[16,6272]{1,0:T(8,128)(2,1)S(1)} collective-permute-done((bf16[16,6272]{1,0:T(8,128)(2,1)S(1)}, bf16[16,6272]{1,0:T(8,128)(2,1)S(1)}, u32[]{:S(2)}, u32[]{:S(2)}) %collective-permute-start.10) | collective-permute-done | bytes 200736 | tf_op jit(solution)/shard_map/ppermute | solution.py:811
  59.8 2.8 collective-permute-start.8
  63.4 8.0 %collective-permute-done.6 = bf16[2,2,2,96,384]{4,3,1,0,2:T(8,128)(2,1)S(1)} collective-permute-done((bf16[2,2,2,96,384]{4,3,1,0,2:T(8,128)(2,1)S(1)}, bf16[2,2,2,96,384]{4,3,1,0,2:T(8,128)(2,1)S(1)}, u32[]{:S(2)}, u32[]{:S(2)}) %collective-permute-start.6) | collective-permute-done | bytes 589856 | tf_op jit(solution)/shard_map/ppermute | solution.py:811
  77.1 12.7 %collective-permute-done.14 = bf16[2,2,16,3072]{3,2,1,0:T(8,128)(2,1)} collective-permute-done((bf16[2,2,16,3072]{3,2,1,0:T(8,128)(2,1)S(1)}, bf16[2,2,16,3072]{3,2,1,0:T(8,128)(2,1)}, u32[]{:S(2)}, u32[]{:S(2)}) %collective-permute-start.14) | collective-permute-done | bytes 393248 | tf_op jit(solution)/shard_map/ppermute | solution.py:811
  95.8 2.6 pad_maximum_fusion.2
  98.4 20.8 %all-gather.3.cloned.1.call-done.small_ref.wqkv_ref.wo_ref.wu_ref.proj_ref = bf16[768,6784]{1,0:T(8,128)(2,1)} async-done(((bf16[24,6784]{1,0:T(8,128)(2,1)}), bf16[768,6784]{1,0:T(8,128)(2,1)}) %all-gather.3.cloned.1.call-update) | async-done | bytes 10420240 | tf_op jit(solution)/shard_map/all_gather | solution.py:837
  121.3 10.0 %enc_attend.1 = (bf16[512,2304]{1,0:T(8,128)(2,1)}, bf16[512,1536]{1,0:T(8,128)(2,1)}, bf16[512,768]{1,0:T(8,128)(2,1)}, f32[512,768]{1,0:T(8,128)}, f32[8,768]{1,0:T(8,128)}) custom-call(bf16[4,128,768]{2,1,0:T(8,128)(2,1)} %x_ref.3, f32[4,1,128]{2,1,0:T(1,128)} %compare_convert_fusion.mask_ref, ...), custom_call_target="tpu_custom_call" | custom-call | flops 10000000000 | bytes 16777216 | tf_op jit(solution)/shard_map/enc_attend/pallas_call | solution.py:552
  131.3 15.3 %enc_feed.1 = (bf16[256,512]{1,0:T(8,128)(2,1)}, bf16[256,512]{1,0:T(8,128)(2,1)}, bf16[512,768]{1,0:T(8,128)(2,1)}, bf16[512,3072]{1,0:T(8,128)(2,1)}, bf16[512,3072]{1,0:T(8,128)(2,1)}) custom-call(s32[1]{0:T(128)} %bitcast.1.half_ref, f32[512,768]{1,0:T(8,128)} %get-tuple-element.111.x2_ref, f32[8,768]{1,0:T(8,128)} %get-tuple-element.112.vec_ref, ...), custom_call_target="tpu_custom_call" | custom-call | flops 14000000000 | bytes 16777216 | tf_op jit(solution)/shard_map/enc_feed/pallas_call | solution.py:552
  152.3 4.0 reshape.375.cot_ref
  163.2 2.5 select_bitcast_fusion.1
  169.7 90.7 %decoder_block.1 = (bf16[8,256,512]{2,1,0:T(8,128)(2,1)}, bf16[4,128,512]{2,1,0:T(8,128)(2,1)}, bf16[4,128,512]{2,1,0:T(8,128)(2,1)}, bf16[512,3200]{1,0:T(8,128)(2,1)}, bf16[512,3200]{1,0:T(8,128)(2,1)}) custom-call(s32[1]{0:T(128)} %bitcast.core_ref, bf16[8,128,512]{2,1,0:T(8,128)(2,1)} %bitcast.313, s32[8,1,128]{2,1,0:T(1,128)} %bitcast.321, ...), custom_call_target="tpu_custom_call" | custom-call | flops 77309411328 | bytes 41943040 | tf_op jit(solution)/shard_map/decoder_block/pallas_call | solution.py:292
  260.7 2.0 collective-permute-done.20
  266.1 7.8 %collective-permute-done.21 = bf16[2,128,512]{2,1,0:T(8,128)(2,1)S(1)} collective-permute-done((bf16[2,128,512]{2,1,0:T(8,128)(2,1)}, bf16[2,128,512]{2,1,0:T(8,128)(2,1)S(1)}, u32[]{:S(2)}, u32[]{:S(2)}) %collective-permute-start.21) | collective-permute-done | bytes 262176 | tf_op jit(solution)/shard_map/ppermute | solution.py:857
  275.8 2.7 add_convert_fusion.1
  281.5 19.1 %enc_feed_back.1 = (bf16[768,512]{1,0:T(8,128)(2,1)}, bf16[768,3072]{1,0:T(8,128)(2,1)}, bf16[768,3072]{1,0:T(8,128)(2,1)}, f32[512,768]{1,0:T(8,128)}, f32[8,768]{1,0:T(8,128)}) custom-call(s32[1]{0:T(128)} %bitcast.core_ref, bf16[512,512]{1,0:T(8,128)(2,1)} %bitcast.316, bf16[512,768]{1,0:T(8,128)(2,1)} %get-tuple-element.131.enc_ref, ...), custom_call_target="tpu_custom_call" | custom-call | flops 17999998976 | bytes 16777216 | tf_op jit(solution)/shard_map/enc_feed_back/pallas_call | solution.py:552
  303.0 17.0 %enc_attend_back.1 = (bf16[768,1920]{1,0:T(8,128)(2,1)}, bf16[768,1920]{1,0:T(8,128)(2,1)}, bf16[4,128,768]{2,1,0:T(8,128)(2,1)}) custom-call(s32[1]{0:T(128)} %bitcast.core_ref, f32[512,768]{1,0:T(8,128)} %get-tuple-element.139.dx2_ref, bf16[512,768]{1,0:T(8,128)(2,1)} %get-tuple-element.140.o_ref, bf16[512,2304]{1,0:T(8,128)(2,1)} %get-tuple-element.141.qkv_ref, ...), custom_call_target="tpu_custom_call" | custom-call | flops 14000000000 | bytes 16777216 | tf_op jit(solution)/shard_map/enc_attend_back/pallas_call | solution.py:552
  320.2 5.7 add_convert_fusion
  328.6 2.6 add_convert_fusion.2
  334.4 2.8 collective-permute-start.31
  339.0 5.9 %collective-permute-done.30 = bf16[32,3200]{1,0:T(8,128)(2,1)S(1)} collective-permute-done((bf16[32,3200]{1,0:T(8,128)(2,1)S(1)}, bf16[32,3200]{1,0:T(8,128)(2,1)S(1)}, u32[]{:S(2)}, u32[]{:S(2)}) %collective-permute-start.30) | collective-permute-done | bytes 204832 | tf_op jit(solution)/shard_map/ppermute | solution.py:767
  344.9 7.1 %collective-permute-done.31 = bf16[32,3200]{1,0:T(8,128)(2,1)S(1)} collective-permute-done((bf16[32,3200]{1,0:T(8,128)(2,1)S(1)}, bf16[32,3200]{1,0:T(8,128)(2,1)S(1)}, u32[]{:S(2)}, u32[]{:S(2)}) %collective-permute-start.31) | collective-permute-done | bytes 204832 | tf_op jit(solution)/shard_map/ppermute | solution.py:767
  352.2 7.7 %collective-permute-done.33 = bf16[2,2,2,48,1536]{4,3,2,1,0:T(8,128)(2,1)S(1)} collective-permute-done((bf16[2,2,2,48,1536]{4,3,2,1,0:T(8,128)(2,1)S(1)}, bf16[2,2,2,48,1536]{4,3,2,1,0:T(8,128)(2,1)S(1)}, u32[]{:S(2)}, u32[]{:S(2)}) %collective-permute-start.33) | collective-permute-done | bytes 1179680 | tf_op jit(solution)/shard_map/ppermute | solution.py:767
  364.0 11.7 %collective-permute-done.34 = bf16[2,2,48,1536]{3,2,1,0:T(8,128)(2,1)S(1)} collective-permute-done((bf16[2,2,48,1536]{3,2,1,0:T(8,128)(2,1)S(1)}, bf16[2,2,48,1536]{3,2,1,0:T(8,128)(2,1)S(1)}, u32[]{:S(2)}, u32[]{:S(2)}) %collective-permute-start.34) | collective-permute-done | bytes 589856 | tf_op jit(solution)/shard_map/ppermute | solution.py:767
  377.1 2.8 collective-permute-start.38
  384.2 5.2 collective-permute-done.37
  389.4 11.2 %collective-permute-done.38 = bf16[48,3072]{1,0:T(8,128)(2,1)S(1)} collective-permute-done((bf16[48,3072]{1,0:T(8,128)(2,1)S(1)}, bf16[48,3072]{1,0:T(8,128)(2,1)S(1)}, u32[]{:S(2)}, u32[]{:S(2)}) %collective-permute-start.38) | collective-permute-done | bytes 294944 | tf_op jit(solution)/shard_map/ppermute | solution.py:767
  405.0 4.6 collective-permute-done.41
  411.3 5.1 collective-permute-start.43
  418.9 9.8 %collective-permute-done.43 = bf16[48,1920]{1,0:T(8,128)(2,1)S(1)} collective-permute-done((bf16[48,1920]{1,0:T(8,128)(2,1)S(1)}, bf16[48,1920]{1,0:T(8,128)(2,1)S(1)}, u32[]{:S(2)}, u32[]{:S(2)}) %collective-permute-start.43) | collective-permute-done | bytes 184352 | tf_op jit(solution)/shard_map/ppermute | solution.py:767
  428.7 12.8 %collective-permute-done.44 = bf16[48,1920]{1,0:T(8,128)(2,1)S(1)} collective-permute-done((bf16[48,1920]{1,0:T(8,128)(2,1)S(1)}, bf16[48,1920]{1,0:T(8,128)(2,1)S(1)}, u32[]{:S(2)}, u32[]{:S(2)}) %collective-permute-start.44) | collective-permute-done | bytes 184352 | tf_op jit(solution)/shard_map/ppermute | solution.py:767
  441.5 2.6 collective-permute-start.46
  444.2 2.6 collective-permute-start.47
  446.7 4.5 collective-permute-done.46
  451.2 26.0 %collective-permute-done.47 = bf16[48,1920]{1,0:T(8,128)(2,1)S(1)} collective-permute-done((bf16[48,1920]{1,0:T(8,128)(2,1)S(1)}, bf16[48,1920]{1,0:T(8,128)(2,1)S(1)}, u32[]{:S(2)}, u32[]{:S(2)}) %collective-permute-start.47) | collective-permute-done | bytes 184352 | tf_op jit(solution)/shard_map/ppermute | solution.py:811
  479.8 9.3 %collective-permute-done.51 = bf16[2,2,48,896]{3,2,1,0:T(8,128)(2,1)S(1)} collective-permute-done((bf16[2,2,48,896]{3,2,1,0:T(8,128)(2,1)S(1)}, bf16[2,2,48,896]{3,2,1,0:T(8,128)(2,1)S(1)}, u32[]{:S(2)}, u32[]{:S(2)}) %collective-permute-start.51) | collective-permute-done | bytes 344096 | tf_op jit(solution)/shard_map/ppermute | solution.py:811
  489.3 4.4 collective-permute-done.49
  494.0 21.9 %collective-permute-done.52 = bf16[2,2,2,48,896]{4,3,2,1,0:T(8,128)(2,1)S(1)} collective-permute-done((bf16[2,2,2,48,896]{4,3,2,1,0:T(8,128)(2,1)S(1)}, bf16[2,2,2,48,896]{4,3,2,1,0:T(8,128)(2,1)S(1)}, u32[]{:S(2)}, u32[]{:S(2)}) %collective-permute-start.52) | collective-permute-done | bytes 688160 | tf_op jit(solution)/shard_map/ppermute | solution.py:811
  516.0 8.4 %collective-permute-done.50 = bf16[2,2,2,48,1024]{4,3,1,0,2:T(8,128)(2,1)S(1)} collective-permute-done((bf16[2,2,2,48,1024]{4,3,1,0,2:T(8,128)(2,1)S(1)}, bf16[2,2,2,48,1024]{4,3,1,0,2:T(8,128)(2,1)S(1)}, u32[]{:S(2)}, u32[]{:S(2)}) %collective-permute-start.50) | collective-permute-done | bytes 786464 | tf_op jit(solution)/shard_map/ppermute | solution.py:811
  524.5 2.0 maximum_maximum_fusion.1
  526.5 4.0 reshape.381
  532.3 2.4 broadcast_select_fusion.1
  534.7 3.1 pad_maximum_fusion.1.packed_ref
  537.9 6.3 %unpack_sums.2 = (f32[768,2304]{1,0:T(8,128)}, f32[768,768]{1,0:T(8,128)}, f32[768,512]{1,0:T(8,128)}, f32[8,768]{1,0:T(8,128)}) custom-call(bf16[16,2,48,1920]{3,2,1,0:T(8,128)(2,1)} %pad_maximum_fusion.1.packed_ref), custom_call_target="tpu_custom_call" | custom-call | bytes 17694720 | tf_op jit(solution)/shard_map/unpack_sums/pallas_call | solution.py:690
  545.6 2.2 all-gather.5.cloned.1.call-done
  547.9 14.4 %unpack_sums.3 = (f32[512,1536]{1,0:T(8,128)}, f32[512,512]{1,0:T(8,128)}, f32[512,2048]{1,0:T(8,128)}, f32[2048,512]{1,0:T(8,128)}, f32[8,512]{1,0:T(8,128)}, /*index=5*/f32[768,3072]{1,0:T(8,128)}, f32[3072,768]{1,0:T(8,128)}) custom-call(bf16[16,2,16,15616]{3,2,1,0:T(8,128)(2,1)} %bitcast.275), custom_call_target="tpu_custom_call" | custom-call | bytes 47972352 | tf_op jit(solution)/shard_map/unpack_sums/pallas_call | solution.py:690
  (236 shorter events, 98.5 us)
Async XLA Ops:
  7.2 112.0 %all-gather.3.cloned.1.call-start = ((), (), s32[]{:S(2)}) async-start(), calls=%async_computation | async-start | bytes 10745856 | tf_op jit(solution)/shard_map/all_gather | solution.py:837
  12.2 535.7 %all-gather.5.cloned.1.call-start = ((), (), s32[]{:S(2)}) async-start(), calls=%async_computation.1 | async-start | bytes 16490496 | tf_op jit(solution)/shard_map/all_gather | solution.py:837
  12.2 16.1 %collective-permute-start.2 = (bf16[96,768]{1,0:T(8,128)(2,1)}, bf16[96,768]{1,0:T(8,128)(2,1)S(1)}, u32[]{:S(2)}, u32[]{:S(2)}) collective-permute-start(bf16[96,768]{1,0:T(8,128)(2,1)} %param.32), channel_id=1, source_target_pairs={{0,24},{1,25},{2,26},{3,27},{4,28},{5,29},{6,30},{7,31},{8,16},{9,... | collective-permute-start | bytes 442376 | tf_op jit(solution)/shard_map/ppermute | solution.py:811
  17.3 18.2 %collective-permute-start.3 = (bf16[96,768]{1,0:T(8,128)(2,1)}, bf16[96,768]{1,0:T(8,128)(2,1)S(1)}, u32[]{:S(2)}, u32[]{:S(2)}) collective-permute-start(bf16[96,768]{1,0:T(8,128)(2,1)} %param.32), channel_id=1, source_target_pairs={{0,16},{1,17},{2,18},{3,19},{4,20},{5,21},{6,22},{7,23},{8,24},{9,... | collective-permute-start | bytes 442376 | tf_op jit(solution)/shard_map/ppermute | solution.py:811
  17.3 18.2 %collective-permute-start.4 = (bf16[96,768]{1,0:T(8,128)(2,1)}, bf16[96,768]{1,0:T(8,128)(2,1)S(1)}, u32[]{:S(2)}, u32[]{:S(2)}) collective-permute-start(bf16[96,768]{1,0:T(8,128)(2,1)} %param.32), channel_id=1, source_target_pairs={{0,8},{1,9},{2,10},{3,11},{4,12},{5,13},{6,14},{7,15},{8,0},{9,1},... | collective-permute-start | bytes 442376 | tf_op jit(solution)/shard_map/ppermute | solution.py:811
  36.7 21.1 %collective-permute-start.10 = (bf16[16,6272]{1,0:T(8,128)(2,1)S(1)}, bf16[16,6272]{1,0:T(8,128)(2,1)S(1)}, u32[]{:S(2)}, u32[]{:S(2)}) collective-permute-start(bf16[16,6272]{1,0:T(8,128)(2,1)S(1)} %constant_dynamic-update-slice_fusion.5), channel_id=1, source_target_pairs={{0,16},{1,17},{2,18},{3,19},{4,20},{5,21},{6,22},{7,23},{8,24},{9,... | collective-permute-start | bytes 602120 | tf_op jit(solution)/shard_map/ppermute | solution.py:811
  36.8 21.0 %collective-permute-start.11 = (bf16[16,6272]{1,0:T(8,128)(2,1)S(1)}, bf16[16,6272]{1,0:T(8,128)(2,1)S(1)}, u32[]{:S(2)}, u32[]{:S(2)}) collective-permute-start(bf16[16,6272]{1,0:T(8,128)(2,1)S(1)} %constant_dynamic-update-slice_fusion.5), channel_id=1, source_target_pairs={{0,8},{1,9},{2,10},{3,11},{4,12},{5,13},{6,14},{7,15},{8,0},{9,1},... | collective-permute-start | bytes 602120 | tf_op jit(solution)/shard_map/ppermute | solution.py:811
  41.0 16.8 %collective-permute-start.9 = (bf16[16,6272]{1,0:T(8,128)(2,1)S(1)}, bf16[16,6272]{1,0:T(8,128)(2,1)S(1)}, u32[]{:S(2)}, u32[]{:S(2)}) collective-permute-start(bf16[16,6272]{1,0:T(8,128)(2,1)S(1)} %constant_dynamic-update-slice_fusion.5), channel_id=1, source_target_pairs={{0,24},{1,25},{2,26},{3,27},{4,28},{5,29},{6,30},{7,31},{8,16},{9,... | collective-permute-start | bytes 602120 | tf_op jit(solution)/shard_map/ppermute | solution.py:811
  41.1 16.8 %collective-permute-start.5 = (bf16[2,2,96,384]{3,2,1,0:T(8,128)(2,1)S(1)}, bf16[2,2,96,384]{3,2,1,0:T(8,128)(2,1)S(1)}, u32[]{:S(2)}, u32[]{:S(2)}) collective-permute-start(bf16[2,2,96,384]{3,2,1,0:T(8,128)(2,1)S(1)} %get-tuple-element.102), channel_id=1, source_target_pairs={{0,2},{1,3},{2,0},{3,1},{4,6},{5,7},{6,4},{7,5},{8,10},{9,11},{10,... | collective-permute-start | bytes 884744 | tf_op jit(solution)/shard_map/ppermute | solution.py:811
  42.8 15.2 %collective-permute-start.7 = (bf16[2,2,96,384]{3,2,1,0:T(8,128)(2,1)S(1)}, bf16[2,2,96,384]{3,2,1,0:T(8,128)(2,1)S(1)}, u32[]{:S(2)}, u32[]{:S(2)}) collective-permute-start(bf16[2,2,96,384]{3,2,1,0:T(8,128)(2,1)S(1)} %get-tuple-element.103), channel_id=1, source_target_pairs={{0,4},{1,5},{2,6},{3,7},{4,0},{5,1},{6,2},{7,3},{8,12},{9,13},{10,... | collective-permute-start | bytes 884744 | tf_op jit(solution)/shard_map/ppermute | solution.py:811
  58.1 13.3 %collective-permute-start.6 = (bf16[2,2,2,96,384]{4,3,1,0,2:T(8,128)(2,1)S(1)}, bf16[2,2,2,96,384]{4,3,1,0,2:T(8,128)(2,1)S(1)}, u32[]{:S(2)}, u32[]{:S(2)}) collective-permute-start(bf16[2,2,2,96,384]{4,3,1,0,2:T(8,128)(2,1)S(1)} %pad_maximum_fusion.18), channel_id=1, source_target_pairs={{0,4},{1,5},{2,6},{3,7},{4,0},{5,1},{6,2},{7,3},{8,12},{9,13},{10,... | collective-permute-start | bytes 1769480 | tf_op jit(solution)/shard_map/ppermute | solution.py:811
  59.8 11.8 %collective-permute-start.8 = (bf16[2,2,2,96,384]{4,3,2,1,0:T(8,128)(2,1)S(1)}, bf16[2,2,2,96,384]{4,3,2,1,0:T(8,128)(2,1)S(1)}, u32[]{:S(2)}, u32[]{:S(2)}) collective-permute-start(bf16[2,2,2,96,384]{4,3,2,1,0:T(8,128)(2,1)S(1)} %pad_maximum_fusion.19), channel_id=1, source_target_pairs={{0,2},{1,3},{2,0},{3,1},{4,6},{5,7},{6,4},{7,5},{8,10},{9,11},{10,... | collective-permute-start | bytes 1769480 | tf_op jit(solution)/shard_map/ppermute | solution.py:811
  73.4 16.4 %collective-permute-start.14 = (bf16[2,2,16,3072]{3,2,1,0:T(8,128)(2,1)S(1)}, bf16[2,2,16,3072]{3,2,1,0:T(8,128)(2,1)}, u32[]{:S(2)}, u32[]{:S(2)}) collective-permute-start(bf16[2,2,16,3072]{3,2,1,0:T(8,128)(2,1)S(1)} %slice.144), channel_id=1, source_target_pairs={{0,4},{1,5},{2,6},{3,7},{4,0},{5,1},{6,2},{7,3},{8,12},{9,13},{10,... | collective-permute-start | bytes 1179656 | tf_op jit(solution)/shard_map/ppermute | solution.py:811
  75.3 18.0 %collective-permute-start.13 = (bf16[2,2,16,3200]{3,2,1,0:T(8,128)(2,1)}, bf16[2,2,16,3200]{3,2,1,0:T(8,128)(2,1)S(1)}, u32[]{:S(2)}, u32[]{:S(2)}) collective-permute-start(bf16[2,2,16,3200]{3,2,1,0:T(8,128)(2,1)} %slice.143), channel_id=1, source_target_pairs={{0,2},{1,3},{2,0},{3,1},{4,6},{5,7},{6,4},{7,5},{8,10},{9,11},{10,... | collective-permute-start | bytes 1228808 | tf_op jit(solution)/shard_map/ppermute | solution.py:811
  77.1 17.5 %collective-permute-start.12 = (bf16[2,2,2,2,96,768]{5,4,3,2,1,0:T(8,128)(2,1)}, bf16[2,2,2,2,96,768]{5,4,3,2,1,0:T(8,128)(2,1)S(1)}, u32[]{:S(2)}, u32[]{:S(2)}) collective-permute-start(bf16[2,2,2,2,96,768]{5,4,3,2,1,0:T(8,128)(2,1)} %maximum_maximum_fusion.2), channel_id=1, source_target_pairs={{0,1},{1,0},{2,3},{3,2},{4,5},{5,4},{6,7},{7,6},{8,9},{9,8},{10,11... | collective-permute-start | bytes 7077896 | tf_op jit(solution)/shard_map/ppermute | solution.py:811
  119.2 27.5 %collective-permute-start.15 = (bf16[2,2,2,16,3200]{4,3,1,0,2:T(8,128)(2,1)S(1)}, bf16[2,2,2,16,3200]{4,3,1,0,2:T(8,128)(2,1)S(1)}, u32[]{:S(2)}, u32[]{:S(2)}) collective-permute-start(bf16[2,2,2,16,3200]{4,3,1,0,2:T(8,128)(2,1)S(1)} %copy-done.10), channel_id=1, source_target_pairs={{0,4},{1,5},{2,6},{3,7},{4,0},{5,1},{6,2},{7,3},{8,12},{9,13},{10,... | collective-permute-start | bytes 2457608 | tf_op jit(solution)/shard_map/ppermute | solution.py:811
  120.0 26.5 %collective-permute-start.16 = (bf16[2,2,2,16,3072]{4,3,2,1,0:T(8,128)(2,1)S(1)}, bf16[2,2,2,16,3072]{4,3,2,1,0:T(8,128)(2,1)S(1)}, u32[]{:S(2)}, u32[]{:S(2)}) collective-permute-start(bf16[2,2,2,16,3072]{4,3,2,1,0:T(8,128)(2,1)S(1)} %copy-done.11), channel_id=1, source_target_pairs={{0,2},{1,3},{2,0},{3,1},{4,6},{5,7},{6,4},{7,5},{8,10},{9,11},{10,... | collective-permute-start | bytes 2359304 | tf_op jit(solution)/shard_map/ppermute | solution.py:811
  149.7 13.5 %collective-permute-start.19 = (bf16[2,2,2,2,16,6272]{5,4,3,2,1,0:T(8,128)(2,1)}, bf16[2,2,2,2,16,6272]{5,4,3,2,1,0:T(8,128)(2,1)}, u32[]{:S(2)}, u32[]{:S(2)}) collective-permute-start(bf16[2,2,2,2,16,6272]{5,4,3,2,1,0:T(8,128)(2,1)} %maximum_maximum_fusion), channel_id=1, source_target_pairs={{0,1},{1,0},{2,3},{3,2},{4,5},{5,4},{6,7},{7,6},{8,9},{9,8},{10,11... | collective-permute-start | bytes 9633800 | tf_op jit(solution)/shard_map/ppermute | solution.py:811
  149.7 9.1 %collective-permute-start.17 = (bf16[2,128,512]{2,1,0:T(8,128)(2,1)}, bf16[2,128,512]{2,1,0:T(8,128)(2,1)}, u32[]{:S(2)}, u32[]{:S(2)}) collective-permute-start(bf16[2,128,512]{2,1,0:T(8,128)(2,1)} %bitcast.55), channel_id=1, source_target_pairs={{0,2},{1,3},{2,0},{3,1},{4,6},{5,7},{6,4},{7,5},{8,10},{9,11},{10,... | collective-permute-start | bytes 786440 | tf_op jit(solution)/shard_map/ppermute | solution.py:857
  263.8 11.9 %collective-permute-start.22 = (bf16[512,3200]{1,0:T(8,128)(2,1)}, bf16[512,3200]{1,0:T(8,128)(2,1)}, u32[]{:S(2)}, u32[]{:S(2)}) collective-permute-start(bf16[512,3200]{1,0:T(8,128)(2,1)} %get-tuple-element.129), channel_id=1, source_target_pairs={{0,1},{1,0},{2,3},{3,2},{4,5},{5,4},{6,7},{7,6},{8,9},{9,8},{10,11... | collective-permute-start | bytes 9830408 | tf_op jit(solution)/shard_map/ppermute | solution.py:723
  265.3 8.6 %collective-permute-start.21 = (bf16[2,128,512]{2,1,0:T(8,128)(2,1)}, bf16[2,128,512]{2,1,0:T(8,128)(2,1)S(1)}, u32[]{:S(2)}, u32[]{:S(2)}) collective-permute-start(bf16[2,128,512]{2,1,0:T(8,128)(2,1)} %dynamic-slice_bitcast_fusion.12), channel_id=1, source_target_pairs={{0,2},{1,3},{2,0},{3,1},{4,6},{5,7},{6,4},{7,5},{8,10},{9,11},{10,... | collective-permute-start | bytes 786440 | tf_op jit(solution)/shard_map/ppermute | solution.py:857
  279.1 21.9 %collective-permute-start.24 = (bf16[2,2,2,32,1664]{4,3,2,1,0:T(8,128)(2,1)S(1)}, bf16[2,2,2,32,1664]{4,3,2,1,0:T(8,128)(2,1)S(1)}, u32[]{:S(2)}, u32[]{:S(2)}) collective-permute-start(bf16[2,2,2,32,1664]{4,3,2,1,0:T(8,128)(2,1)S(1)} %dynamic-slice_bitcast_fusion.1), channel_id=1, source_target_pairs={{0,2},{1,3},{2,0},{3,1},{4,6},{5,7},{6,4},{7,5},{8,10},{9,11},{10,... | collective-permute-start | bytes 2555912 | tf_op jit(solution)/shard_map/ppermute | solution.py:767
  279.9 20.8 %collective-permute-start.23 = (bf16[2,2,2,32,1536]{4,3,1,0,2:T(8,128)(2,1)S(1)}, bf16[2,2,2,32,1536]{4,3,1,0,2:T(8,128)(2,1)S(1)}, u32[]{:S(2)}, u32[]{:S(2)}) collective-permute-start(bf16[2,2,2,32,1536]{4,3,1,0,2:T(8,128)(2,1)S(1)} %bitcast.314), channel_id=1, source_target_pairs={{0,4},{1,5},{2,6},{3,7},{4,0},{5,1},{6,2},{7,3},{8,12},{9,13},{10,... | collective-permute-start | bytes 2359304 | tf_op jit(solution)/shard_map/ppermute | solution.py:767
  301.2 18.9 %collective-permute-start.27 = (bf16[768,3072]{1,0:T(8,128)(2,1)}, bf16[768,3072]{1,0:T(8,128)(2,1)}, u32[]{:S(2)}, u32[]{:S(2)}) collective-permute-start(bf16[768,3072]{1,0:T(8,128)(2,1)} %get-tuple-element.150), channel_id=1, source_target_pairs={{0,1},{1,0},{2,3},{3,2},{4,5},{5,4},{6,7},{7,6},{8,9},{9,8},{10,11... | collective-permute-start | bytes 14155784 | tf_op jit(solution)/shard_map/ppermute | solution.py:723
  301.3 18.8 %collective-permute-start.26 = (bf16[2,2,32,1664]{3,2,1,0:T(8,128)(2,1)S(1)}, bf16[2,2,32,1664]{3,2,1,0:T(8,128)(2,1)S(1)}, u32[]{:S(2)}, u32[]{:S(2)}) collective-permute-start(bf16[2,2,32,1664]{3,2,1,0:T(8,128)(2,1)S(1)} %dynamic-slice_bitcast_fusion.5), channel_id=1, source_target_pairs={{0,4},{1,5},{2,6},{3,7},{4,0},{5,1},{6,2},{7,3},{8,12},{9,13},{10,... | collective-permute-start | bytes 1277960 | tf_op jit(solution)/shard_map/ppermute | solution.py:767
  301.7 18.4 %collective-permute-start.25 = (bf16[2,2,32,1536]{3,2,1,0:T(8,128)(2,1)S(1)}, bf16[2,2,32,1536]{3,2,1,0:T(8,128)(2,1)S(1)}, u32[]{:S(2)}, u32[]{:S(2)}) collective-permute-start(bf16[2,2,32,1536]{3,2,1,0:T(8,128)(2,1)S(1)} %dynamic-slice_bitcast_fusion.7), channel_id=1, source_target_pairs={{0,2},{1,3},{2,0},{3,1},{4,6},{5,7},{6,4},{7,5},{8,10},{9,11},{10,... | collective-permute-start | bytes 1179656 | tf_op jit(solution)/shard_map/ppermute | solution.py:767
  331.5 28.4 %collective-permute-start.33 = (bf16[2,2,2,48,1536]{4,3,2,1,0:T(8,128)(2,1)S(1)}, bf16[2,2,2,48,1536]{4,3,2,1,0:T(8,128)(2,1)S(1)}, u32[]{:S(2)}, u32[]{:S(2)}) collective-permute-start(bf16[2,2,2,48,1536]{4,3,2,1,0:T(8,128)(2,1)S(1)} %dynamic-slice_bitcast_fusion), channel_id=1, source_target_pairs={{0,2},{1,3},{2,0},{3,1},{4,6},{5,7},{6,4},{7,5},{8,10},{9,11},{10,... | collective-permute-start | bytes 3538952 | tf_op jit(solution)/shard_map/ppermute | solution.py:767
  332.3 28.1 %collective-permute-start.29 = (bf16[2,2,2,48,1536]{4,3,1,0,2:T(8,128)(2,1)S(1)}, bf16[2,2,2,48,1536]{4,3,1,0,2:T(8,128)(2,1)S(1)}, u32[]{:S(2)}, u32[]{:S(2)}) collective-permute-start(bf16[2,2,2,48,1536]{4,3,1,0,2:T(8,128)(2,1)S(1)} %bitcast.312), channel_id=1, source_target_pairs={{0,4},{1,5},{2,6},{3,7},{4,0},{5,1},{6,2},{7,3},{8,12},{9,13},{10,... | collective-permute-start | bytes 3538952 | tf_op jit(solution)/shard_map/ppermute | solution.py:767
  334.3 10.7 %collective-permute-start.30 = (bf16[32,3200]{1,0:T(8,128)(2,1)S(1)}, bf16[32,3200]{1,0:T(8,128)(2,1)S(1)}, u32[]{:S(2)}, u32[]{:S(2)}) collective-permute-start(bf16[32,3200]{1,0:T(8,128)(2,1)S(1)} %get-tuple-element.235), channel_id=1, source_target_pairs={{0,8},{1,9},{2,10},{3,11},{4,12},{5,13},{6,14},{7,15},{8,0},{9,1},... | collective-permute-start | bytes 614408 | tf_op jit(solution)/shard_map/ppermute | solution.py:767
  334.4 17.7 %collective-permute-start.31 = (bf16[32,3200]{1,0:T(8,128)(2,1)S(1)}, bf16[32,3200]{1,0:T(8,128)(2,1)S(1)}, u32[]{:S(2)}, u32[]{:S(2)}) collective-permute-start(bf16[32,3200]{1,0:T(8,128)(2,1)S(1)} %get-tuple-element.237), channel_id=1, source_target_pairs={{0,16},{1,17},{2,18},{3,19},{4,20},{5,21},{6,22},{7,23},{8,24},{9,... | collective-permute-start | bytes 614408 | tf_op jit(solution)/shard_map/ppermute | solution.py:767
  337.2 14.9 %collective-permute-start.32 = (bf16[32,3200]{1,0:T(8,128)(2,1)S(1)}, bf16[32,3200]{1,0:T(8,128)(2,1)S(1)}, u32[]{:S(2)}, u32[]{:S(2)}) collective-permute-start(bf16[32,3200]{1,0:T(8,128)(2,1)S(1)} %get-tuple-element.236), channel_id=1, source_target_pairs={{0,24},{1,25},{2,26},{3,27},{4,28},{5,29},{6,30},{7,31},{8,16},{9,... | collective-permute-start | bytes 614408 | tf_op jit(solution)/shard_map/ppermute | solution.py:767
  360.7 14.9 %collective-permute-start.34 = (bf16[2,2,48,1536]{3,2,1,0:T(8,128)(2,1)S(1)}, bf16[2,2,48,1536]{3,2,1,0:T(8,128)(2,1)S(1)}, u32[]{:S(2)}, u32[]{:S(2)}) collective-permute-start(bf16[2,2,48,1536]{3,2,1,0:T(8,128)(2,1)S(1)} %dynamic-slice_bitcast_fusion.4), channel_id=1, source_target_pairs={{0,2},{1,3},{2,0},{3,1},{4,6},{5,7},{6,4},{7,5},{8,10},{9,11},{10,... | collective-permute-start | bytes 1769480 | tf_op jit(solution)/shard_map/ppermute | solution.py:767
  362.2 14.4 %collective-permute-start.35 = (bf16[2,2,48,1536]{3,2,1,0:T(8,128)(2,1)S(1)}, bf16[2,2,48,1536]{3,2,1,0:T(8,128)(2,1)S(1)}, u32[]{:S(2)}, u32[]{:S(2)}) collective-permute-start(bf16[2,2,48,1536]{3,2,1,0:T(8,128)(2,1)S(1)} %dynamic-slice_bitcast_fusion.3), channel_id=1, source_target_pairs={{0,4},{1,5},{2,6},{3,7},{4,0},{5,1},{6,2},{7,3},{8,12},{9,13},{10,... | collective-permute-start | bytes 1769480 | tf_op jit(solution)/shard_map/ppermute | solution.py:767
  377.0 12.4 %collective-permute-start.37 = (bf16[48,3072]{1,0:T(8,128)(2,1)S(1)}, bf16[48,3072]{1,0:T(8,128)(2,1)S(1)}, u32[]{:S(2)}, u32[]{:S(2)}) collective-permute-start(bf16[48,3072]{1,0:T(8,128)(2,1)S(1)} %get-tuple-element.165), channel_id=1, source_target_pairs={{0,8},{1,9},{2,10},{3,11},{4,12},{5,13},{6,14},{7,15},{8,0},{9,1},... | collective-permute-start | bytes 884744 | tf_op jit(solution)/shard_map/ppermute | solution.py:767
  377.1 23.6 %collective-permute-start.38 = (bf16[48,3072]{1,0:T(8,128)(2,1)S(1)}, bf16[48,3072]{1,0:T(8,128)(2,1)S(1)}, u32[]{:S(2)}, u32[]{:S(2)}) collective-permute-start(bf16[48,3072]{1,0:T(8,128)(2,1)S(1)} %get-tuple-element.166), channel_id=1, source_target_pairs={{0,16},{1,17},{2,18},{3,19},{4,20},{5,21},{6,22},{7,23},{8,24},{9,... | collective-permute-start | bytes 884744 | tf_op jit(solution)/shard_map/ppermute | solution.py:767
  379.9 20.8 %collective-permute-start.39 = (bf16[48,3072]{1,0:T(8,128)(2,1)S(1)}, bf16[48,3072]{1,0:T(8,128)(2,1)S(1)}, u32[]{:S(2)}, u32[]{:S(2)}) collective-permute-start(bf16[48,3072]{1,0:T(8,128)(2,1)S(1)} %get-tuple-element.167), channel_id=1, source_target_pairs={{0,24},{1,25},{2,26},{3,27},{4,28},{5,29},{6,30},{7,31},{8,16},{9,... | collective-permute-start | bytes 884744 | tf_op jit(solution)/shard_map/ppermute | solution.py:767
  381.5 19.6 %collective-permute-start.40 = (bf16[2,2,2,48,1024]{4,3,2,1,0:T(8,128)(2,1)S(1)}, bf16[2,2,2,48,1024]{4,3,2,1,0:T(8,128)(2,1)S(1)}, u32[]{:S(2)}, u32[]{:S(2)}) collective-permute-start(bf16[2,2,2,48,1024]{4,3,2,1,0:T(8,128)(2,1)S(1)} %dynamic-slice_bitcast_fusion.2), channel_id=1, source_target_pairs={{0,2},{1,3},{2,0},{3,1},{4,6},{5,7},{6,4},{7,5},{8,10},{9,11},{10,... | collective-permute-start | bytes 2359304 | tf_op jit(solution)/shard_map/ppermute | solution.py:767
  382.4 18.4 %collective-permute-start.36 = (bf16[2,2,2,48,896]{4,3,1,0,2:T(8,128)(2,1)S(1)}, bf16[2,2,2,48,896]{4,3,1,0,2:T(8,128)(2,1)S(1)}, u32[]{:S(2)}, u32[]{:S(2)}) collective-permute-start(bf16[2,2,2,48,896]{4,3,1,0,2:T(8,128)(2,1)S(1)} %bitcast.315), channel_id=1, source_target_pairs={{0,4},{1,5},{2,6},{3,7},{4,0},{5,1},{6,2},{7,3},{8,12},{9,13},{10,... | collective-permute-start | bytes 2064392 | tf_op jit(solution)/shard_map/ppermute | solution.py:767
  411.3 17.4 %collective-permute-start.43 = (bf16[48,1920]{1,0:T(8,128)(2,1)S(1)}, bf16[48,1920]{1,0:T(8,128)(2,1)S(1)}, u32[]{:S(2)}, u32[]{:S(2)}) collective-permute-start(bf16[48,1920]{1,0:T(8,128)(2,1)S(1)} %get-tuple-element.248), channel_id=1, source_target_pairs={{0,8},{1,9},{2,10},{3,11},{4,12},{5,13},{6,14},{7,15},{8,0},{9,1},... | collective-permute-start | bytes 552968 | tf_op jit(solution)/shard_map/ppermute | solution.py:767
  416.4 25.0 %collective-permute-start.44 = (bf16[48,1920]{1,0:T(8,128)(2,1)S(1)}, bf16[48,1920]{1,0:T(8,128)(2,1)S(1)}, u32[]{:S(2)}, u32[]{:S(2)}) collective-permute-start(bf16[48,1920]{1,0:T(8,128)(2,1)S(1)} %get-tuple-element.250), channel_id=1, source_target_pairs={{0,16},{1,17},{2,18},{3,19},{4,20},{5,21},{6,22},{7,23},{8,24},{9,... | collective-permute-start | bytes 552968 | tf_op jit(solution)/shard_map/ppermute | solution.py:767
  417.3 24.2 %collective-permute-start.45 = (bf16[48,1920]{1,0:T(8,128)(2,1)S(1)}, bf16[48,1920]{1,0:T(8,128)(2,1)S(1)}, u32[]{:S(2)}, u32[]{:S(2)}) collective-permute-start(bf16[48,1920]{1,0:T(8,128)(2,1)S(1)} %get-tuple-element.249), channel_id=1, source_target_pairs={{0,24},{1,25},{2,26},{3,27},{4,28},{5,29},{6,30},{7,31},{8,16},{9,... | collective-permute-start | bytes 552968 | tf_op jit(solution)/shard_map/ppermute | solution.py:767
  441.5 9.7 %collective-permute-start.46 = (bf16[48,1920]{1,0:T(8,128)(2,1)S(1)}, bf16[48,1920]{1,0:T(8,128)(2,1)S(1)}, u32[]{:S(2)}, u32[]{:S(2)}) collective-permute-start(bf16[48,1920]{1,0:T(8,128)(2,1)S(1)} %fusion.20), channel_id=1, source_target_pairs={{0,24},{1,25},{2,26},{3,27},{4,28},{5,29},{6,30},{7,31},{8,16},{9,... | collective-permute-start | bytes 552968 | tf_op jit(solution)/shard_map/ppermute | solution.py:811
  444.2 33.1 %collective-permute-start.47 = (bf16[48,1920]{1,0:T(8,128)(2,1)S(1)}, bf16[48,1920]{1,0:T(8,128)(2,1)S(1)}, u32[]{:S(2)}, u32[]{:S(2)}) collective-permute-start(bf16[48,1920]{1,0:T(8,128)(2,1)S(1)} %fusion.20), channel_id=1, source_target_pairs={{0,16},{1,17},{2,18},{3,19},{4,20},{5,21},{6,22},{7,23},{8,24},{9,... | collective-permute-start | bytes 552968 | tf_op jit(solution)/shard_map/ppermute | solution.py:811
  446.7 30.5 %collective-permute-start.48 = (bf16[48,1920]{1,0:T(8,128)(2,1)S(1)}, bf16[48,1920]{1,0:T(8,128)(2,1)S(1)}, u32[]{:S(2)}, u32[]{:S(2)}) collective-permute-start(bf16[48,1920]{1,0:T(8,128)(2,1)S(1)} %fusion.20), channel_id=1, source_target_pairs={{0,8},{1,9},{2,10},{3,11},{4,12},{5,13},{6,14},{7,15},{8,0},{9,1},... | collective-permute-start | bytes 552968 | tf_op jit(solution)/shard_map/ppermute | solution.py:811
  477.5 11.6 %collective-permute-start.51 = (bf16[2,2,48,896]{3,2,1,0:T(8,128)(2,1)S(1)}, bf16[2,2,48,896]{3,2,1,0:T(8,128)(2,1)S(1)}, u32[]{:S(2)}, u32[]{:S(2)}) collective-permute-start(bf16[2,2,48,896]{3,2,1,0:T(8,128)(2,1)S(1)} %slice.156), channel_id=1, source_target_pairs={{0,4},{1,5},{2,6},{3,7},{4,0},{5,1},{6,2},{7,3},{8,12},{9,13},{10,... | collective-permute-start | bytes 1032200 | tf_op jit(solution)/shard_map/ppermute | solution.py:811
  479.4 14.3 %collective-permute-start.49 = (bf16[2,2,48,1024]{3,2,1,0:T(8,128)(2,1)S(1)}, bf16[2,2,48,1024]{3,2,1,0:T(8,128)(2,1)S(1)}, u32[]{:S(2)}, u32[]{:S(2)}) collective-permute-start(bf16[2,2,48,1024]{3,2,1,0:T(8,128)(2,1)S(1)} %slice.155), channel_id=1, source_target_pairs={{0,2},{1,3},{2,0},{3,1},{4,6},{5,7},{6,4},{7,5},{8,10},{9,11},{10,... | collective-permute-start | bytes 1179656 | tf_op jit(solution)/shard_map/ppermute | solution.py:811
  489.3 26.6 %collective-permute-start.52 = (bf16[2,2,2,48,896]{4,3,2,1,0:T(8,128)(2,1)S(1)}, bf16[2,2,2,48,896]{4,3,2,1,0:T(8,128)(2,1)S(1)}, u32[]{:S(2)}, u32[]{:S(2)}) collective-permute-start(bf16[2,2,2,48,896]{4,3,2,1,0:T(8,128)(2,1)S(1)} %pad_maximum_fusion.16), channel_id=1, source_target_pairs={{0,2},{1,3},{2,0},{3,1},{4,6},{5,7},{6,4},{7,5},{8,10},{9,11},{10,... | collective-permute-start | bytes 2064392 | tf_op jit(solution)/shard_map/ppermute | solution.py:811
  493.9 30.5 %collective-permute-start.50 = (bf16[2,2,2,48,1024]{4,3,1,0,2:T(8,128)(2,1)S(1)}, bf16[2,2,2,48,1024]{4,3,1,0,2:T(8,128)(2,1)S(1)}, u32[]{:S(2)}, u32[]{:S(2)}) collective-permute-start(bf16[2,2,2,48,1024]{4,3,1,0,2:T(8,128)(2,1)S(1)} %pad_maximum_fusion.13), channel_id=1, source_target_pairs={{0,4},{1,5},{2,6},{3,7},{4,0},{5,1},{6,2},{7,3},{8,12},{9,13},{10,... | collective-permute-start | bytes 2359304 | tf_op jit(solution)/shard_map/ppermute | solution.py:811
  (23 other events, 138.3 us)
Sparse Core Ops, SparseCore 0:
  12.3 106.8 all-gather.2
  402.4 145.4 all-gather.4
